TPU v7x, 32 devices: a whole 2x2x4 slice. The times are simulated.
32 devices in a mesh: sec: 2 (over core), row: 8 (over z, y), col: 2 (over x).
Axes of the slice: x: 2, y: 2, z: 4, core: 2. Of those that a mesh axis runs over, the one named last changes fastest.
Arguments:
- grid_terms: float32 [768, 1536, 128], P(('row', 'col'), 'sec'), may hold values from -6 to 6
- pair_orders: int32 [32], replicated, may hold values from 0 to 31, each once
- legendre: bfloat16 [32, 65, 768], P(('sec', 'row', 'col')), may hold values from -0.21875 to 0.21875
- state: bfloat16 [32, 65, 256], P(('sec', 'row', 'col')), may hold values from -6 to 6
- kappa: float32 [128], replicated, may hold values from 0.05 to 5
- right_op: bfloat16 [128, 128], replicated, may hold values from -0.5 to 0.5
- left_op: bfloat16 [128, 128], replicated, may hold values from -0.5 to 0.5
Outputs:
- evolved: float32 [768, 1536, 128], P(('row', 'col'), 'sec')
- new_state: bfloat16 [32, 65, 256], P(('sec', 'row', 'col'))
Inputs may be any that keep to these rules, and one draw needn't show every extreme that they name: pair_orders is a permutation: each order below 32 is the lower order of exactly one pair.
All inputs are finite; a program needn't handle non-finite values.
Results may differ from a plain program's by a relative error of at most 0.0085.
Values may be sent and summed in bfloat16 or wider, within the bound.
No kernel may reach another device: no remote copies, remote signals or barrier semaphores. Data moves between devices by JAX's collectives and lax.ppermute only.
A program may use at most 128 MiB of HBM per device.

v0:
```python
import math

import jax
import jax.numpy as jnp
from jax import lax
from jax.sharding import PartitionSpec as P

time_step = 0.5
filter_strength = 36.0
filter_power = 36.0


def slot_orders_of(pair_orders):
    order_total = 2 * pair_orders.shape[0]
    return jnp.stack([pair_orders, order_total - 1 - pair_orders], axis=1).reshape(order_total)


def fourier_table(orders, phi_start, phi_count, longitudes):
    longitude = phi_start + lax.iota(jnp.int32, phi_count)
    phase_turns = longitude[:, None] * orders[None, :] % longitudes
    phase_angle = phase_turns.astype(jnp.float32) * (2.0 * math.pi / longitudes)
    norm_scale = 1.0 / math.sqrt(longitudes)
    return jnp.stack(
        [jnp.cos(phase_angle) * norm_scale, -jnp.sin(phase_angle) * norm_scale], axis=-1
    )


def on_device(grid_terms, pair_orders, legendre, state, kappa, right_op, left_op):
    lat_rows, phi_count, radial = grid_terms.shape
    pairs_here = legendre.shape[0]
    degrees = legendre.shape[1] - 1
    latitudes = legendre.shape[2]
    sections = lax.axis_size("sec")
    longitudes = phi_count * sections
    columns = 2 * radial
    section_slots = degrees // sections
    orders = slot_orders_of(pair_orders)
    sec_index = lax.axis_index("sec")
    highest = lax.Precision.HIGHEST
    phi_start = sec_index * phi_count
    sub_orders = orders
    phase_table = fourier_table(sub_orders, phi_start, phi_count, longitudes)
    term = jnp.einsum(
        "tpr,psc->stcr",
        grid_terms,
        phase_table,
        precision=highest,
        preferred_element_type=jnp.float32,
    )
    spectral = lax.psum_scatter(
        term.reshape(section_slots * lax.axis_size("sec"), lat_rows, columns),
        "sec",
        scatter_dimension=0,
        tiled=True,
    ).astype(jnp.bfloat16)
    device = lax.axis_index(("sec", "row", "col"))
    local_orders = lax.dynamic_slice_in_dim(pair_orders, device * pairs_here, pairs_here)
    row_index = lax.iota(jnp.int32, degrees + 1)
    leading = row_index[None, :] < (degrees - local_orders)[:, None]
    degree = jnp.where(leading, local_orders[:, None] + row_index[None, :], row_index[None, :] - 1)
    received = lax.all_to_all(spectral, ("row", "col"), split_axis=0, concat_axis=1, tiled=True)
    item_count = received.shape[2]
    paired = received.reshape(pairs_here, 2, latitudes, item_count)
    both_orders = jnp.einsum("pit,potx->piox", legendre, paired, preferred_element_type=jnp.float32)
    coefficient = jnp.where(leading[:, :, None], both_orders[:, :, 0], both_orders[:, :, 1])
    right_side = (state.astype(jnp.float32) + time_step * coefficient).astype(jnp.bfloat16)
    right_side = right_side.reshape(pairs_here, degrees + 1, 2, radial)
    eigen_part = jnp.einsum(
        "picr,rk->pick", right_side, right_op, preferred_element_type=jnp.float32
    )
    radial_mode = lax.iota(jnp.float32, radial) / radial
    damping = jnp.exp(-filter_strength * radial_mode**filter_power)
    degree_wide = degree.astype(jnp.float32)
    degree_term = degree_wide * (degree_wide + 1.0) / (degrees * degrees)
    factor = damping[None, None, :] / (1.0 + kappa[None, None, :] + degree_term[:, :, None])
    scaled = (eigen_part * factor[:, :, None, :]).astype(jnp.bfloat16)
    new_state = jnp.einsum("pick,kr->picr", scaled, left_op, preferred_element_type=jnp.float32)
    new_state = new_state.astype(jnp.bfloat16).reshape(pairs_here, degrees + 1, columns)
    zero_rows = jnp.zeros_like(new_state)
    split_state = jnp.stack(
        [
            jnp.where(leading[:, :, None], new_state, zero_rows),
            jnp.where(leading[:, :, None], zero_rows, new_state),
        ],
        axis=1,
    )
    synthesis_wide = jnp.einsum(
        "pit,poix->potx", legendre, split_state, preferred_element_type=jnp.float32
    )
    synthesis = synthesis_wide.astype(jnp.bfloat16).reshape(2 * pairs_here, latitudes, columns)
    returned = lax.all_to_all(synthesis, ("row", "col"), split_axis=1, concat_axis=0, tiled=True)
    sub_orders = lax.dynamic_slice_in_dim(orders, sec_index * section_slots, section_slots)
    phase_table = fourier_table(sub_orders, 0, longitudes, longitudes)
    values = returned.astype(jnp.float32).reshape(section_slots, lat_rows, 2, radial)
    partial_value = jnp.einsum(
        "stcr,psc->tpr", values, phase_table, precision=highest, preferred_element_type=jnp.float32
    )
    evolved = lax.psum_scatter(
        partial_value.astype(jnp.bfloat16), "sec", scatter_dimension=1, tiled=True
    ).astype(jnp.float32)
    return (evolved, new_state)


def solution(mesh):
    return jax.shard_map(
        on_device,
        mesh=mesh,
        in_specs=(
            P(("row", "col"), "sec", None),
            P(),
            P(("sec", "row", "col"), None, None),
            P(("sec", "row", "col"), None, None),
            P(),
            P(),
            P(),
        ),
        out_specs=(P(("row", "col"), "sec", None), P(("sec", "row", "col"), None, None)),
        check_vma=False,
    )
```

profile of v0, /device:TPU:0, one launch (start us, length us, event | category | flops | bytes accessed | tf_op | source)
XLA Modules:
  0.0 164.9 jit_solution(17537406543758473047)
XLA Ops:
  7.2 0.7 subtract_bitcast_fusion
  7.9 0.7 pad_add_fusion
  8.6 0.1 copy.28
  8.7 0.1 reshape.494
  8.8 0.9 cosine_multiply_fusion
  9.7 13.3 %fusion.3 = f32[64,48,2,128]{3,0,1,2:T(8,128)S(1)} fusion(f32[48,768,128]{2,1,0:T(8,128)} %param.7, f32[768,64,1]{0,1,2:T(8,128)S(1)} %get-tuple-element.5, f32[768,64,1]{0,1,2:T(8,128)S(1)} %get-tuple-element.4), kind=kOutput, calls=%fused_computation.4 | convolution fusion | flops 7247855616 | bytes 22413312 | tf_op jit(solution)/shard_map/tpr,psc->stcr/dot_general | solution.py:43
  23.0 2.4 %copy.29 = f32[64,48,2,128]{3,2,1,0:T(2,128)S(1)} copy(f32[64,48,2,128]{3,0,1,2:T(8,128)S(1)} %fusion.3) | data formatting | bytes 6291456 | tf_op jit(solution)/shard_map/tpr,psc->stcr/transpose | solution.py:43
  25.4 3.6 %reshape.495 = f32[64,48,256]{2,1,0:T(8,128)} reshape(f32[64,48,2,128]{3,2,1,0:T(2,128)S(1)} %copy.29) | data formatting | bytes 6291456 | tf_op jit(solution)/shard_map/reshape | solution.py:51
  29.1 13.8 %reduce-scatter.3.cloned.1.call-done = f32[32,48,256]{2,1,0:T(8,128)} async-done(((f32[64,48,256]{2,1,0:T(8,128)}), f32[32,48,256]{2,1,0:T(8,128)}) %reduce-scatter.3.cloned.1.call-update) | async-done | bytes 1572880 | tf_op jit(solution)/shard_map/reduce_scatter | solution.py:50
  42.9 2.4 %convert_element_type.76 = bf16[32,48,256]{2,1,0:T(8,128)(2,1)} convert(f32[32,48,256]{2,1,0:T(8,128)} %reduce-scatter.3.cloned.1.call-done) | non-fusion elementwise | flops 393216 | bytes 2359296 | tf_op jit(solution)/shard_map/convert_element_type | solution.py:55
  45.2 6.7 %all-to-all-start = ((bf16[32,48,256]{2,1,0:T(8,128)(2,1)}), bf16[32,48,256]{2,1,0:T(8,128)(2,1)S(1)}, u32[]{:S(2)}, u32[]{:S(2)}) async-start(bf16[32,48,256]{2,1,0:T(8,128)(2,1)} %convert_element_type.76), calls=%async_computation.1 | async-start | bytes 1572864 | tf_op jit(solution)/shard_map/all_to_all | solution.py:61
  52.0 0.6 dynamic_slice.7
  53.3 0.7 fusion.37
  53.9 0.1 add_divide_fusion
  54.0 18.0 %all-to-all-done = bf16[32,48,256]{2,1,0:T(8,128)(2,1)S(1)} async-done(((bf16[32,48,256]{2,1,0:T(8,128)(2,1)}), bf16[32,48,256]{2,1,0:T(8,128)(2,1)S(1)}, u32[]{:S(2)}, u32[]{:S(2)}) %all-to-all-start) | async-done | bytes 786464 | tf_op jit(solution)/shard_map/all_to_all | solution.py:61
  72.1 0.3 convolution_bitcast_fusion
  72.4 0.1 fusion.28
  72.6 0.3 convolution_convert_fusion.1
  73.0 0.1 broadcast_select_fusion.1
  73.0 0.4 fusion.6
  73.4 1.8 %copy.33 = bf16[2,768,256]{2,0,1:T(2,128)(2,1)} copy(bf16[2,768,256]{1,2,0:T(8,128)(2,1)S(1)} %fusion.6) | data formatting | bytes 1572864 | tf_op jit(solution)/shard_map/reshape | solution.py:90
  75.2 5.1 %all-to-all-start.1 = ((bf16[2,768,256]{2,0,1:T(2,128)(2,1)}), bf16[2,768,256]{2,0,1:T(2,128)(2,1)S(1)}, u32[]{:S(2)}, u32[]{:S(2)}) async-start(bf16[2,768,256]{2,0,1:T(2,128)(2,1)} %copy.33), calls=%async_computation.2 | async-start | bytes 1572864 | tf_op jit(solution)/shard_map/all_to_all | solution.py:91
  80.3 0.2 reduce-scatter.5.cloned.1.call-start
  80.6 0.1 dynamic_slice.6
  80.6 0.9 cosine_multiply_fusion.1
  81.5 17.6 %all-to-all-done.1 = bf16[2,768,256]{2,0,1:T(2,128)(2,1)S(1)} async-done(((bf16[2,768,256]{2,0,1:T(2,128)(2,1)}), bf16[2,768,256]{2,0,1:T(2,128)(2,1)S(1)}, u32[]{:S(2)}, u32[]{:S(2)}) %all-to-all-start.1) | async-done | bytes 786464 | tf_op jit(solution)/shard_map/all_to_all | solution.py:91
  99.2 0.1 copy.34
  99.4 0.2 reshape.502
  99.6 17.9 %fusion = bf16[48,1536,128]{2,1,0:T(8,128)(2,1)} fusion(bf16[32,48,2,128]{3,2,1,0:T(2,128)(2,1)S(1)} %reshape.502, f32[1536,32,1]{0,1,2:T(8,128)S(1)} %get-tuple-element.7, f32[1536,32,1]{0,1,2:T(8,128)S(1)} %get-tuple-element.6), kind=kOutput, calls=%fused_computation.1 | convolution fusion | flops 7257292800 | bytes 20054016 | tf_op jit(solution)/shard_map/stcr,psc->tpr/dot_general | solution.py:95
  117.5 0.7 reshape.503
  118.2 27.0 %reduce-scatter.5.cloned.1.call-done = bf16[48,768,128]{2,1,0:T(8,128)(2,1)} async-done(((bf16[48,1536,128]{2,1,0:T(8,128)(2,1)}), bf16[48,768,128]{2,1,0:T(8,128)(2,1)}) %reduce-scatter.5.cloned.1.call-update) | async-done | bytes 9437200 | tf_op jit(solution)/shard_map/reduce_scatter | solution.py:98
  145.2 12.9 %convert_element_type.86 = f32[48,768,128]{2,1,0:T(8,128)} convert(bf16[48,768,128]{2,1,0:T(8,128)(2,1)} %reduce-scatter.5.cloned.1.call-done) | non-fusion elementwise | flops 4718592 | bytes 28311552 | tf_op jit(solution)/shard_map/convert_element_type | solution.py:100
  (25 shorter events, 0.4 us)
Async XLA Ops:
  7.2 65.0 %copy-start = (bf16[1,65,768]{2,1,0:T(8,128)(2,1)S(1)}, bf16[1,65,768]{2,1,0:T(8,128)(2,1)}, u32[]{:S(2)}) copy-start(bf16[1,65,768]{2,1,0:T(8,128)(2,1)} %param.9) | copy-start | bytes 299524
  7.2 35.7 %reduce-scatter.3.cloned.1.call-start = ((), (), s32[]{:S(2)}) async-start(), calls=%async_computation.4 | async-start | bytes 4718592 | tf_op jit(solution)/shard_map/reduce_scatter | solution.py:50
  9.7 42.3 %copy-start.5 = (s32[32]{0:T(128)S(1)}, s32[32]{0:T(128)}, u32[]{:S(2)}) copy-start(s32[32]{0:T(128)} %param.8) | copy-start | bytes 388
  9.7 44.2 %copy-start.6 = (f32[128]{0:T(128)S(1)}, f32[128]{0:T(128)}, u32[]{:S(2)}) copy-start(f32[128]{0:T(128)} %param.11) | copy-start | bytes 1540
  9.7 62.7 %copy-start.2 = (bf16[1,65,256]{2,1,0:T(8,128)(2,1)S(1)}, bf16[1,65,256]{2,1,0:T(8,128)(2,1)}, u32[]{:S(2)}) copy-start(bf16[1,65,256]{2,1,0:T(8,128)(2,1)} %param.10) | copy-start | bytes 99844
  9.7 62.8 %copy-start.3 = (bf16[128,128]{1,0:T(8,128)(2,1)S(1)}, bf16[128,128]{1,0:T(8,128)(2,1)}, u32[]{:S(2)}) copy-start(bf16[128,128]{1,0:T(8,128)(2,1)} %param.13) | copy-start | bytes 98308
  9.7 62.8 %copy-start.4 = (bf16[128,128]{1,0:T(8,128)(2,1)S(1)}, bf16[128,128]{1,0:T(8,128)(2,1)}, u32[]{:S(2)}) copy-start(bf16[128,128]{1,0:T(8,128)(2,1)} %param.12) | copy-start | bytes 98308
  45.2 26.8 %all-to-all-start = ((bf16[32,48,256]{2,1,0:T(8,128)(2,1)}), bf16[32,48,256]{2,1,0:T(8,128)(2,1)S(1)}, u32[]{:S(2)}, u32[]{:S(2)}) async-start(bf16[32,48,256]{2,1,0:T(8,128)(2,1)} %convert_element_type.76), calls=%async_computation.1 | async-start | bytes 1572864 | tf_op jit(solution)/shard_map/all_to_all | solution.py:61
  75.2 23.9 %all-to-all-start.1 = ((bf16[2,768,256]{2,0,1:T(2,128)(2,1)}), bf16[2,768,256]{2,0,1:T(2,128)(2,1)S(1)}, u32[]{:S(2)}, u32[]{:S(2)}) async-start(bf16[2,768,256]{2,0,1:T(2,128)(2,1)} %copy.33), calls=%async_computation.2 | async-start | bytes 1572864 | tf_op jit(solution)/shard_map/all_to_all | solution.py:91
  80.3 64.9 %reduce-scatter.5.cloned.1.call-start = ((), (), s32[]{:S(2)}) async-start(), calls=%async_computation.5 | async-start | bytes 28311552 | tf_op jit(solution)/shard_map/reduce_scatter | solution.py:98
  117.5 40.6 %copy-start.1 = (bf16[1,65,768]{2,1,0:T(8,128)(2,1)S(1)}, bf16[1,65,768]{2,1,0:T(8,128)(2,1)}, u32[]{:S(2)}) copy-start(bf16[1,65,768]{2,1,0:T(8,128)(2,1)} %param.9) | copy-start | bytes 299524
Sparse Core Ops, SparseCore 0:
  29.2 13.6 reduce-scatter.2
  117.6 27.5 reduce-scatter.4
where the time goes:
time: 165 us
  waiting for transfers between devices  76.5 us (46%)
  matrix products  32.1 us (19%)
  other arithmetic  19.3 us (12%)
  between operations  14.9 us (9%)
  starting transfers between devices  12.1 us (7%)
  local copies, waits for them, and re-layouts  9.99 us (6%)
    reduce_scatter x1, waiting for transfers between devices, on_device(): lax.psum_scatter(partial_value.astype(jnp.bfloat16), 'sec', scatter_dimen...  27 us
    all_to_all x1, waiting for transfers between devices, on_device(): lax.all_to_all(spectral, ('row', 'col'), split_axis=0, concat_axis=1, til...  18 us
    dot_general x1, matrix products, on_device(): jnp.einsum('stcr,psc->tpr', values, phase_table, precision=highest, prefe...  17.9 us
    all_to_all x1, waiting for transfers between devices, on_device(): lax.all_to_all(synthesis, ('row', 'col'), split_axis=1, concat_axis=0, ti...  17.6 us
    reduce_scatter x1, waiting for transfers between devices, on_device(): lax.psum_scatter(term.reshape(section_slots * lax.axis_size('sec'), lat_r...  13.8 us
    dot_general x1, matrix products, on_device(): jnp.einsum('tpr,psc->stcr', grid_terms, phase_table, precision=highest, p...  13.3 us
    convert_element_type x1, other arithmetic, on_device(): evolved = lax.psum_scatter(partial_value.astype(jnp.bfloat16), 'sec', sca...  12.9 us
    all_to_all x1, starting transfers between devices, on_device(): lax.all_to_all(spectral, ('row', 'col'), split_axis=0, concat_axis=1, til...  6.75 us
  transfers between devices with their start and end apart: 4, of which 4 were waited for; matrix products, arithmetic and copies ran while one was open for 2% of the time, Pallas kernels for 0%

commit v1 on v0

--- a/solution.py
+++ b/solution.py
@@ -1,8 +1,12 @@
+import functools
 import math
 
 import jax
 import jax.numpy as jnp
+import numpy as np
 from jax import lax
+from jax.experimental import pallas as pl
+from jax.experimental.pallas import tpu as pltpu
 from jax.sharding import PartitionSpec as P
 
 time_step = 0.5
@@ -25,7 +29,7 @@
     )
 
 
-def on_device(grid_terms, pair_orders, legendre, state, kappa, right_op, left_op):
+def on_device_wide(grid_terms, pair_orders, legendre, state, kappa, right_op, left_op):
     lat_rows, phi_count, radial = grid_terms.shape
     pairs_here = legendre.shape[0]
     degrees = legendre.shape[1] - 1
@@ -101,6 +105,319 @@
     return (evolved, new_state)
 
 
+def natural_table(pair_total, sections, phi_count):
+    slots = 2 * pair_total
+    longitudes = sections * phi_count
+    low = np.arange(pair_total)
+    orders = np.stack([low, slots - 1 - low], axis=1).reshape(slots)
+    turns = orders[:, None] * np.arange(longitudes)[None, :] % longitudes
+    angle = turns * (2.0 * np.pi / longitudes)
+    table = np.concatenate([np.cos(angle), -np.sin(angle)], axis=0) / np.sqrt(longitudes)
+    return table.reshape(2 * slots, sections, phi_count).transpose(1, 0, 2).astype(np.float32)
+
+
+def params(mib, **more):
+    return pltpu.CompilerParams(vmem_limit_bytes=mib * 1024 * 1024, **more)
+
+
+def whole(memory_space=pltpu.VMEM):
+    return pl.BlockSpec(memory_space=memory_space)
+
+
+def forward_kernel(table_ref, grid_ref, out_ref, held):
+    step = pl.program_id(0)
+    lat_block, _, radial = grid_ref.shape
+    blocks, rows = held.shape[0], held.shape[1]
+    slots = rows // 2
+    table = table_ref[lax.axis_index("sec")]
+    for at in range(0, lat_block, 2):
+        two = jnp.concatenate(
+            [grid_ref[at].astype(jnp.bfloat16), grid_ref[at + 1].astype(jnp.bfloat16)], axis=1
+        )
+        sums = jnp.dot(table, two, preferred_element_type=jnp.float32)
+        held[step, :, at, :] = sums[:, :radial]
+        held[step, :, at + 1, :] = sums[:, radial:]
+
+    @pl.when(step == blocks - 1)
+    def _():
+        for block in range(0, blocks, 2):
+            for part in range(2):
+                rows_of = pl.ds(part * slots, slots)
+                both = jnp.concatenate([held[block, rows_of], held[block + 1, rows_of]], axis=1)
+                out_ref[:, pl.ds(block * lat_block, 2 * lat_block), pl.ds(part * radial, radial)] = (
+                    both.astype(jnp.bfloat16)
+                )
+
+
+def forward_sums(table, grid_terms, lat_block):
+    sections, rows, phi_count = table.shape
+    lat_rows, _, radial = grid_terms.shape
+    blocks = lat_rows // lat_block
+    return pl.pallas_call(
+        forward_kernel,
+        grid=(blocks,),
+        in_specs=[
+            pl.BlockSpec((sections, rows, phi_count), lambda step: (0, 0, 0)),
+            pl.BlockSpec((lat_block, phi_count, radial), lambda step: (step, 0, 0)),
+        ],
+        out_specs=pl.BlockSpec((rows // 2, lat_rows, 2 * radial), lambda step: (0, 0, 0)),
+        out_shape=jax.ShapeDtypeStruct((rows // 2, lat_rows, 2 * radial), jnp.bfloat16),
+        scratch_shapes=[pltpu.VMEM((blocks, rows, lat_block, radial), jnp.float32)],
+        compiler_params=params(40),
+        cost_estimate=pl.CostEstimate(
+            flops=2 * rows * phi_count * lat_rows * radial,
+            bytes_accessed=4 * lat_rows * phi_count * radial,
+            transcendentals=0,
+        ),
+    )(table, grid_terms)
+
+
+def degrees_kernel(turn, orders_ref, legendre_ref, fourier_ref, out_ref):
+    count, rows = out_ref.shape[0], out_ref.shape[1]
+    sections = lax.axis_size("sec")
+    first = lax.rem(lax.axis_index("sec") + turn, sections) * count
+    row_index = lax.broadcasted_iota(jnp.int32, (rows, legendre_ref.shape[2]), 0)
+    for at in range(count):
+        order = orders_ref[first + at]
+        weights = legendre_ref[first + at]
+        leading = row_index < rows - 1 - order
+        zero = jnp.zeros_like(weights)
+        total = jnp.dot(
+            jnp.where(leading, weights, zero),
+            fourier_ref[2 * order],
+            preferred_element_type=jnp.float32,
+        ) + jnp.dot(
+            jnp.where(leading, zero, weights),
+            fourier_ref[2 * order + 1],
+            preferred_element_type=jnp.float32,
+        )
+        out_ref[at] = total.astype(out_ref.dtype)
+
+
+def degree_sums(turn, pair_orders, legendre, fourier, count):
+    pair_total, rows, lat_rows = legendre.shape
+    columns = fourier.shape[2]
+    return pl.pallas_call(
+        functools.partial(degrees_kernel, turn),
+        in_specs=[whole(pltpu.SMEM), whole(), whole()],
+        out_specs=whole(),
+        out_shape=jax.ShapeDtypeStruct((count, rows, columns), jnp.bfloat16),
+        compiler_params=params(24),
+        cost_estimate=pl.CostEstimate(
+            flops=4 * count * rows * lat_rows * columns,
+            bytes_accessed=fourier.size * 2 + count * rows * columns * 2,
+            transcendentals=0,
+        ),
+    )(pair_orders, legendre, fourier)
+
+
+def plane_kernel(plane, kept_ref, taken_ref, *out_refs):
+    side_y, side_x = plane
+    here_y = lax.rem(lax.axis_index("row"), side_y)
+    here_x = lax.axis_index("col")
+    at = 0
+    for step_y in range(side_y):
+        for step_x in range(side_x):
+            to = lax.rem(here_y + step_y, side_y) * side_x + lax.rem(here_x + step_x, side_x)
+            for deep in range(kept_ref.shape[0]):
+                total = kept_ref[deep, to].astype(jnp.float32) + taken_ref[deep, to].astype(jnp.float32)
+                out_refs[at][deep] = total.astype(jnp.bfloat16)
+            at += 1
+
+
+def depth_kernel(side_y, depth, *refs):
+    takes, outs = refs[: len(refs) - depth], refs[len(refs) - depth :]
+    here = lax.axis_index("row") // side_y
+    for step in range(depth):
+        to = lax.rem(here + step, depth)
+        total = takes[0][to].astype(jnp.float32)
+        for other in takes[1:]:
+            total += other[to].astype(jnp.float32)
+        outs[step][...] = total.astype(outs[step].dtype)
+
+
+def solve_kernel(parts, *refs):
+    takes = refs[:parts]
+    orders_ref, state_ref, degree_free_ref, damping_ref, right_ref, left_ref, out_ref = refs[parts:]
+    rows = state_ref.shape[1]
+    radial = right_ref.shape[0]
+    degrees = rows - 1
+    sec, row, col = (lax.axis_index(name) for name in ("sec", "row", "col"))
+    pair = (sec * lax.axis_size("row") + row) * lax.axis_size("col") + col
+    order = orders_ref[pair]
+    coefficient = takes[0][...].astype(jnp.float32)
+    for other in takes[1:]:
+        coefficient += other[...].astype(jnp.float32)
+    right_side = (state_ref[0].astype(jnp.float32) + time_step * coefficient).astype(jnp.bfloat16)
+    row_index = lax.broadcasted_iota(jnp.int32, (rows, radial), 0)
+    degree = jnp.where(row_index < degrees - order, order + row_index, row_index - 1)
+    degree = degree.astype(jnp.float32)
+    factor = damping_ref[...] / (
+        1.0 + degree_free_ref[...] + degree * (degree + 1.0) / (degrees * degrees)
+    )
+    for part in range(2):
+        columns = pl.ds(part * radial, radial)
+        eigen = jnp.dot(
+            right_side[:, part * radial : (part + 1) * radial],
+            right_ref[...],
+            preferred_element_type=jnp.float32,
+        )
+        scaled = (eigen * factor).astype(jnp.bfloat16)
+        out_ref[0, :, columns] = jnp.dot(
+            scaled, left_ref[...], preferred_element_type=jnp.float32
+        ).astype(jnp.bfloat16)
+
+
+def inverse_kernel(orders_ref, legendre_ref, state_ref, table_ref, out_ref, held):
+    step = pl.program_id(0)
+    pair_total, rows, lat_rows = legendre_ref.shape
+    blocks, slot_rows, lat_block, radial = held.shape
+    slots = slot_rows // 2
+
+    @pl.when(step == 0)
+    def _():
+        row_index = lax.broadcasted_iota(jnp.int32, (rows, lat_rows), 0)
+        for pair in range(pair_total):
+            order = orders_ref[pair]
+            weights = legendre_ref[pair]
+            leading = row_index < rows - 1 - order
+            zero = jnp.zeros_like(weights)
+            fields = state_ref[pair]
+            for half in range(2):
+                kept = jnp.where(leading, weights, zero) if half == 0 else jnp.where(leading, zero, weights)
+                rebuilt = lax.dot_general(
+                    kept, fields, (((0,), (0,)), ((), ())), preferred_element_type=jnp.float32
+                )
+                for part in range(2):
+                    held[:, part * slots + 2 * order + half] = rebuilt[
+                        :, part * radial : (part + 1) * radial
+                    ].reshape(blocks, lat_block, radial)
+
+    table = table_ref[lax.axis_index("sec")]
+    for at in range(0, lat_block, 2):
+        two = jnp.concatenate(
+            [
+                held[step, :, at, :].astype(jnp.bfloat16),
+                held[step, :, at + 1, :].astype(jnp.bfloat16),
+            ],
+            axis=1,
+        )
+        values = jnp.dot(table, two, preferred_element_type=jnp.float32)
+        out_ref[at] = values[:, :radial]
+        out_ref[at + 1] = values[:, radial:]
+
+
+def inverse_values(pair_orders, legendre, new_states, table, lat_block):
+    pair_total, rows, lat_rows = legendre.shape
+    sections, phi_count, slot_rows = table.shape
+    radial = new_states.shape[2] // 2
+    blocks = lat_rows // lat_block
+    return pl.pallas_call(
+        inverse_kernel,
+        grid=(blocks,),
+        in_specs=[
+            whole(pltpu.SMEM),
+            pl.BlockSpec((pair_total, rows, lat_rows), lambda step: (0, 0, 0)),
+            pl.BlockSpec(new_states.shape, lambda step: (0, 0, 0)),
+            pl.BlockSpec(table.shape, lambda step: (0, 0, 0)),
+        ],
+        out_specs=pl.BlockSpec((lat_block, phi_count, radial), lambda step: (step, 0, 0)),
+        out_shape=jax.ShapeDtypeStruct((lat_rows, phi_count, radial), jnp.float32),
+        scratch_shapes=[pltpu.VMEM((blocks, slot_rows, lat_block, radial), jnp.float32)],
+        compiler_params=params(40),
+        cost_estimate=pl.CostEstimate(
+            flops=2 * slot_rows * phi_count * lat_rows * radial,
+            bytes_accessed=4 * lat_rows * phi_count * radial,
+            transcendentals=0,
+        ),
+    )(pair_orders, legendre, new_states, table)
+
+
+names = ("sec", "row", "col")
+
+
+def shifted(sizes, shift):
+    pairs = []
+    for source in np.ndindex(*sizes):
+        target = tuple((at + by) % size for at, by, size in zip(source, shift, sizes))
+        pairs.append((int(np.ravel_multi_index(source, sizes)), int(np.ravel_multi_index(target, sizes))))
+    return pairs
+
+
+def on_device_compact(grid_terms, pair_orders, legendre, state, kappa, right_op, left_op):
+    lat_rows, phi_count, radial = grid_terms.shape
+    rows = legendre.shape[1]
+    columns = 2 * radial
+    pair_total = pair_orders.shape[0]
+    sections, side_row, side_x = (lax.axis_size(name) for name in names)
+    side_y = 2 if side_row % 2 == 0 else 1
+    depth = side_row // side_y
+    plane = side_y * side_x
+    sizes = (sections, depth, side_y, side_x)
+    lat_block = 8
+    table = natural_table(pair_total, sections, phi_count)
+    forward_table = jnp.asarray(table, jnp.bfloat16)
+    inverse_table = jnp.asarray(table.transpose(0, 2, 1), jnp.bfloat16)
+
+    cut = legendre.reshape(rows, side_row * side_x, lat_rows).transpose(1, 0, 2)
+    cut = jnp.concatenate([cut] * sections, axis=0)
+    legendre_here = lax.all_to_all(cut, names, split_axis=0, concat_axis=0, tiled=True)
+
+    fourier = forward_sums(forward_table, grid_terms, lat_block)
+    count = pair_total // sections
+    sent = degree_sums(1, pair_orders, legendre_here, fourier, count)
+    taken = lax.ppermute(sent, names, shifted(sizes, (1, 0, 0, 0)))
+    kept = degree_sums(0, pair_orders, legendre_here, fourier, count)
+
+    block = jax.ShapeDtypeStruct((depth, rows, columns), jnp.bfloat16)
+    slabs = pl.pallas_call(
+        functools.partial(plane_kernel, (side_y, side_x)),
+        in_specs=[whole()] * 2,
+        out_specs=[whole()] * plane,
+        out_shape=[block] * plane,
+        compiler_params=params(16),
+    )(
+        kept.reshape(depth, plane, rows, columns),
+        taken.reshape(depth, plane, rows, columns),
+    )
+    moved = [slabs[0]]
+    for at in range(1, plane):
+        moved.append(lax.ppermute(slabs[at], names, shifted(sizes, (0, 0, at // side_x, at % side_x))))
+
+    single = jax.ShapeDtypeStruct((rows, columns), jnp.bfloat16)
+    lines = pl.pallas_call(
+        functools.partial(depth_kernel, side_y, depth),
+        in_specs=[whole()] * plane,
+        out_specs=[whole()] * depth,
+        out_shape=[jax.ShapeDtypeStruct((rows, columns), jnp.float32)] + [single] * (depth - 1),
+        compiler_params=params(16),
+    )(*moved)
+    parts = [lines[0]]
+    for at in range(1, depth):
+        parts.append(lax.ppermute(lines[at], names, shifted(sizes, (0, at, 0, 0))))
+
+    radial_mode = np.arange(radial, dtype=np.float32) / np.float32(radial)
+    damping = np.exp(-filter_strength * radial_mode**filter_power).astype(np.float32)
+    new_state = pl.pallas_call(
+        functools.partial(solve_kernel, len(parts)),
+        in_specs=[whole()] * len(parts) + [whole(pltpu.SMEM)] + [whole()] * 5,
+        out_specs=whole(),
+        out_shape=jax.ShapeDtypeStruct((1, rows, columns), jnp.bfloat16),
+        compiler_params=params(16),
+    )(*parts, pair_orders, state, kappa[None, :], jnp.asarray(damping)[None, :], right_op, left_op)
+    new_states = lax.all_gather(new_state, names, axis=0, tiled=True)
+    evolved = inverse_values(pair_orders, legendre_here, new_states, inverse_table, lat_block)
+    return (evolved, new_state)
+
+
+def on_device(*args):
+    lat_rows = args[0].shape[0]
+    rows = args[2].shape[1]
+    if args[2].shape[0] == 1 and lat_rows % 16 == 0 and rows <= 2 * lat_rows:
+        return on_device_compact(*args)
+    return on_device_wide(*args)
+
+
 def solution(mesh):
     return jax.shard_map(
         on_device,

time: 165 us -> 125 us (0.76)
  matrix products: 32.1 us -> 0 us
  Pallas kernels: 0 us -> 22.5 us
  other arithmetic: 19.3 us -> 0.11 us
  waiting for transfers between devices: 76.5 us -> 68.3 us
  local copies, waits for them, and re-layouts: 9.99 us -> 4.51 us
  starting transfers between devices: 12.1 us -> 14.8 us
    all_gather x0 -> x1, waiting for transfers between devices: none -> 54.3 us  [on_device_compact(): new_states = lax.all_gather(new_state, names, axis=0, tiled=True)]
    reduce_scatter x2 -> x0, waiting for transfers between devices: 40.8 us -> none  [the longest x1 27 us: on_device(): lax.psum_scatter(partial_value.astype(jnp.bfloat16), 'sec', scatter_dimen...]
    dot_general x5 -> x0, matrix products: 32.1 us -> none  [the longest x1 17.9 us: on_device(): jnp.einsum('stcr,psc->tpr', values, phase_table, precision=highest, prefe...]
    all_to_all x2 -> x1, waiting for transfers between devices: 35.7 us -> 5.04 us  [on_device_compact(): lax.all_to_all(cut, names, split_axis=0, concat_axis=0, tiled=True)]
    pallas_call x0 -> x7, Pallas kernels: none -> 22.5 us  [the longest x1 9.88 us: inverse_values(): pl.pallas_call(inverse_kernel, grid=(blocks,), in_specs=[whole(pltpu.SMEM...]
    convert_element_type x3 -> x0, other arithmetic: 15.3 us -> none  [the longest x1 12.9 us: on_device(): evolved = lax.psum_scatter(partial_value.astype(jnp.bfloat16), 'sec', sca...]
    ppermute x0 -> x7, waiting for transfers between devices: none -> 8.95 us  [the longest x3 5.64 us: on_device_compact(): lax.ppermute(slabs[at], names, shifted(sizes, (0, 0, at // side_x, at % s...]
    ppermute x0 -> x7, starting transfers between devices: none -> 7.5 us  [the longest x3 3.88 us: on_device_compact(): parts.append(lax.ppermute(lines[at], names, shifted(sizes, (0, at, 0, 0))))]
  transfers between devices with their start and end apart: 4 -> 9, of which waited for: 4 -> 7; matrix products, arithmetic and copies ran while one was open for 2% -> 0% of each run, Pallas kernels for 0% -> 8%
where the time goes in v1:
time: 125 us
  waiting for transfers between devices  68.3 us (55%)
  Pallas kernels  22.5 us (18%)
  starting transfers between devices  14.8 us (12%)
  between operations  14.2 us (11%)
  local copies, waits for them, and re-layouts  4.51 us (4%)
    all_gather x1, waiting for transfers between devices, on_device_compact(): new_states = lax.all_gather(new_state, names, axis=0, tiled=True)  54.3 us
    pallas_call x1, Pallas kernels, inverse_values(): pl.pallas_call(inverse_kernel, grid=(blocks,), in_specs=[whole(pltpu.SMEM...  9.88 us
    pallas_call x1, Pallas kernels, forward_sums(): pl.pallas_call(forward_kernel, grid=(blocks,), in_specs=[pl.BlockSpec((se...  8.91 us
    all_to_all x1, starting transfers between devices, on_device_compact(): lax.all_to_all(cut, names, split_axis=0, concat_axis=0, tiled=True)  7.3 us
    ppermute x3, waiting for transfers between devices, on_device_compact(): lax.ppermute(slabs[at], names, shifted(sizes, (0, 0, at // side_x, at % s...  5.64 us
    all_to_all x1, waiting for transfers between devices, on_device_compact(): lax.all_to_all(cut, names, split_axis=0, concat_axis=0, tiled=True)  5.04 us
    ppermute x3, starting transfers between devices, on_device_compact(): parts.append(lax.ppermute(lines[at], names, shifted(sizes, (0, at, 0, 0))))  3.88 us
    ppermute x3, starting transfers between devices, on_device_compact(): lax.ppermute(slabs[at], names, shifted(sizes, (0, 0, at // side_x, at % s...  3.55 us
  transfers between devices with their start and end apart: 9, of which 7 were waited for; matrix products, arithmetic and copies ran while one was open for 0% of the time, Pallas kernels for 8%

profile of v1, /device:TPU:0, one launch (start us, length us, event | category | flops | bytes accessed | tf_op | source)
XLA Modules:
  0.0 124.6 jit_solution(12702082006391628523)
XLA Ops:
  7.2 1.2 reshape.13
  8.4 0.0 copy-start.2
  8.4 0.1 pad_maximum_fusion
  8.5 1.4 %copy.13 = bf16[32,65,48]{1,2,0:T(8,128)(2,1)} copy(bf16[32,65,48]{2,0,1:T(8,128)(2,1)S(1)} %pad_maximum_fusion) | data formatting | bytes 399360 | tf_op jit(solution)/shard_map/concatenate | solution.py:363
  9.9 7.3 %all-to-all-start = ((bf16[32,65,48]{1,2,0:T(8,128)(2,1)}), bf16[32,65,48]{1,2,0:T(8,128)(2,1)S(1)}, u32[]{:S(2)}, u32[]{:S(2)}) async-start(bf16[32,65,48]{1,2,0:T(8,128)(2,1)} %copy.13), calls=%async_computation | async-start | bytes 786432 | tf_op jit(solution)/shard_map/all_to_all | solution.py:364
  17.2 0.0 all-gather.2.cloned.1.call-start
  17.3 8.9 %shard_map.113.fourier_ref = bf16[64,48,256]{2,1,0:T(8,128)(2,1)S(1)} custom-call(bf16[2,128,768]{2,1,0:T(8,128)(2,1)S(1)} %copy-done.2, f32[48,768,128]{2,1,0:T(8,128)} %grid_ref.1), custom_call_target="tpu_custom_call" | custom-call | flops 1207959552 | bytes 18874368 | tf_op jit(solution)/shard_map/pallas_call | solution.py:156
  26.2 5.0 %all-to-all-done = bf16[32,65,48]{1,2,0:T(8,128)(2,1)S(1)} async-done(((bf16[32,65,48]{1,2,0:T(8,128)(2,1)}), bf16[32,65,48]{1,2,0:T(8,128)(2,1)S(1)}, u32[]{:S(2)}, u32[]{:S(2)}) %all-to-all-start) | async-done | bytes 199712 | tf_op jit(solution)/shard_map/all_to_all | solution.py:364
  31.2 0.3 copy.18.legendre_ref
  31.6 1.0 shard_map.115
  32.6 0.1 copy.16
  32.7 0.1 collective-permute-start
  32.8 1.0 shard_map.114
  33.9 0.8 collective-permute-done
  34.7 0.2 copy.17
  34.9 0.2 shard_map.116
  35.0 0.2 collective-permute-start.1
  35.3 0.8 collective-permute-start.2
  36.1 2.5 %collective-permute-start.3 = (bf16[4,65,256]{2,1,0:T(8,128)(2,1)S(1)}, bf16[4,65,256]{2,1,0:T(8,128)(2,1)S(1)}, u32[]{:S(2)}, u32[]{:S(2)}) collective-permute-start(bf16[4,65,256]{2,1,0:T(8,128)(2,1)S(1)} %get-tuple-element.13), channel_id=1, source_target_pairs={{0,3},{1,2},{2,1},{3,0},{4,7},{5,6},{6,5},{7,4},{8,11},{9,10},{10,... | collective-permute-start | bytes 399368 | tf_op jit(solution)/shard_map/ppermute | solution.py:385
  38.6 3.2 %collective-permute-done.1.refs_1_ = bf16[4,65,256]{2,1,0:T(8,128)(2,1)S(1)} collective-permute-done((bf16[4,65,256]{2,1,0:T(8,128)(2,1)S(1)}, bf16[4,65,256]{2,1,0:T(8,128)(2,1)S(1)}, u32[]{:S(2)}, u32[]{:S(2)}) %collective-permute-start.1) | collective-permute-done | bytes 133152 | tf_op jit(solution)/shard_map/ppermute | solution.py:385
  41.8 2.4 %collective-permute-done.2.refs_2_ = bf16[4,65,256]{2,1,0:T(8,128)(2,1)S(1)} collective-permute-done((bf16[4,65,256]{2,1,0:T(8,128)(2,1)S(1)}, bf16[4,65,256]{2,1,0:T(8,128)(2,1)S(1)}, u32[]{:S(2)}, u32[]{:S(2)}) %collective-permute-start.2) | collective-permute-done | bytes 133152 | tf_op jit(solution)/shard_map/ppermute | solution.py:385
  44.2 0.1 shard_map.117
  44.3 0.6 collective-permute-start.4
  44.9 1.1 collective-permute-start.5
  46.0 2.2 %collective-permute-start.6 = (bf16[65,256]{1,0:T(8,128)(2,1)S(1)}, bf16[65,256]{1,0:T(8,128)(2,1)S(1)}, u32[]{:S(2)}, u32[]{:S(2)}) collective-permute-start(bf16[65,256]{1,0:T(8,128)(2,1)S(1)} %get-tuple-element.17), channel_id=1, source_target_pairs={{0,12},{1,13},{2,14},{3,15},{4,0},{5,1},{6,2},{7,3},{8,4},{9,5},{1... | collective-permute-start | bytes 99848 | tf_op jit(solution)/shard_map/ppermute | solution.py:397
  48.2 1.9 %collective-permute-done.4.refs_1_ = bf16[65,256]{1,0:T(8,128)(2,1)S(1)} collective-permute-done((bf16[65,256]{1,0:T(8,128)(2,1)S(1)}, bf16[65,256]{1,0:T(8,128)(2,1)S(1)}, u32[]{:S(2)}, u32[]{:S(2)}) %collective-permute-start.4) | collective-permute-done | bytes 33312 | tf_op jit(solution)/shard_map/ppermute | solution.py:397
  50.1 0.6 collective-permute-done.6.refs_3_
  50.7 1.5 %shard_map.118 = bf16[1,65,256]{2,1,0:T(8,128)(2,1)} custom-call(f32[65,256]{1,0:T(8,128)S(1)} %get-tuple-element.14.refs_0_, bf16[65,256]{1,0:T(8,128)(2,1)S(1)} %collective-permute-done.4.refs_1_, bf16[65,256]{1,0:T(8,128)(2,1)S(1)} %collective-permute-done.5.refs_2_, bf16[65,256]{1,0:T(8,128)(2,1)S(1)} %collective-permute-done.6.refs_3_, ...), custom_call_target="tpu_custom_call" | custom-call | tf_op jit(solution)/shard_map/pallas_call | solution.py:401
  52.2 0.0 all-gather.2.cloned.1.call-update
  52.2 54.3 %all-gather.2.cloned.1.call-done.state_ref = bf16[32,65,256]{2,1,0:T(8,128)(2,1)} async-done(((bf16[1,65,256]{2,1,0:T(8,128)(2,1)}), bf16[32,65,256]{2,1,0:T(8,128)(2,1)}) %all-gather.2.cloned.1.call-update) | async-done | bytes 1064976 | tf_op jit(solution)/shard_map/all_gather | solution.py:408
  106.6 1.3 %copy-done = bf16[32,65,256]{2,1,0:T(8,128)(2,1)S(1)} copy-done((bf16[32,65,256]{2,1,0:T(8,128)(2,1)S(1)}, bf16[32,65,256]{2,1,0:T(8,128)(2,1)}, u32[]{:S(2)}) %copy-start) | copy-done | bytes 1064984
  107.8 9.9 %shard_map.119 = f32[48,768,128]{2,1,0:T(8,128)} custom-call(s32[32]{0:T(128)S(1)} %copy-done.6, bf16[32,65,48]{2,1,0:T(8,128)(2,1)S(1)} %copy.18.legendre_ref, bf16[32,65,256]{2,1,0:T(8,128)(2,1)S(1)} %copy-done, bf16[2,768,128]{2,1,0:T(8,128)(2,1)S(1)} %copy-done.1), custom_call_target="tpu_custom_call" | custom-call | flops 1207959552 | bytes 18874368 | tf_op jit(solution)/shard_map/pallas_call | solution.py:315
  (18 shorter events, 0.1 us)
Async XLA Ops:
  8.4 8.9 %copy-start.2 = (bf16[2,128,768]{2,1,0:T(8,128)(2,1)S(1)}, bf16[2,128,768]{2,1,0:T(8,128)(2,1)}, u32[]{:S(2)}) copy-start(bf16[2,128,768]{2,1,0:T(8,128)(2,1)} %constant.6.clone.table_ref) | copy-start | bytes 1179652
  9.9 21.3 %all-to-all-start = ((bf16[32,65,48]{1,2,0:T(8,128)(2,1)}), bf16[32,65,48]{1,2,0:T(8,128)(2,1)S(1)}, u32[]{:S(2)}, u32[]{:S(2)}) async-start(bf16[32,65,48]{1,2,0:T(8,128)(2,1)} %copy.13), calls=%async_computation | async-start | bytes 786432 | tf_op jit(solution)/shard_map/all_to_all | solution.py:364
  17.2 14.4 %copy-start.6 = (s32[32]{0:T(128)S(1)}, s32[32]{0:T(128)}, u32[]{:S(2)}) copy-start(s32[32]{0:T(128)} %orders_ref.5) | copy-start | bytes 388
  17.2 89.3 %all-gather.2.cloned.1.call-start = ((), (), s32[]{:S(2)}) async-start(), calls=%async_computation.1 | async-start | bytes 1216512 | tf_op jit(solution)/shard_map/all_gather | solution.py:408
  32.7 2.0 %collective-permute-start = (bf16[16,65,256]{2,0,1:T(8,128)(2,1)S(1)}, bf16[16,65,256]{2,0,1:T(8,128)(2,1)S(1)}, u32[]{:S(2)}, u32[]{:S(2)}) collective-permute-start(bf16[16,65,256]{2,0,1:T(8,128)(2,1)S(1)} %copy.16), channel_id=1, source_target_pairs={{0,16},{1,17},{2,18},{3,19},{4,20},{5,21},{6,22},{7,23},{8,24},{9,... | collective-permute-start | bytes 1597448 | tf_op jit(solution)/shard_map/ppermute | solution.py:369
  33.8 16.9 %copy-start.3 = (bf16[1,65,256]{2,1,0:T(8,128)(2,1)S(1)}, bf16[1,65,256]{2,1,0:T(8,128)(2,1)}, u32[]{:S(2)}) copy-start(bf16[1,65,256]{2,1,0:T(8,128)(2,1)} %refs_5_.1) | copy-start | bytes 99844
  33.8 16.9 %copy-start.4 = (bf16[128,128]{1,0:T(8,128)(2,1)S(1)}, bf16[128,128]{1,0:T(8,128)(2,1)}, u32[]{:S(2)}) copy-start(bf16[128,128]{1,0:T(8,128)(2,1)} %refs_8_.1) | copy-start | bytes 98308
  33.8 16.9 %copy-start.5 = (bf16[128,128]{1,0:T(8,128)(2,1)S(1)}, bf16[128,128]{1,0:T(8,128)(2,1)}, u32[]{:S(2)}) copy-start(bf16[128,128]{1,0:T(8,128)(2,1)} %refs_9_.1) | copy-start | bytes 98308
  33.9 16.8 %copy-start.7 = (f32[128]{0:T(128)S(1)}, f32[128]{0:T(128)}, u32[]{:S(2)}) copy-start(f32[128]{0:T(128)} %param.14) | copy-start | bytes 1540
  33.9 16.8 %copy-start.8 = (f32[1,128]{1,0:T(1,128)S(1)}, f32[1,128]{1,0:T(1,128)}, u32[]{:S(2)}) copy-start(f32[1,128]{1,0:T(1,128)} %constant.11.refs_7_) | copy-start | bytes 1540
  34.9 71.7 %copy-start.1 = (bf16[2,768,128]{2,1,0:T(8,128)(2,1)S(1)}, bf16[2,768,128]{2,1,0:T(8,128)(2,1)}, u32[]{:S(2)}) copy-start(bf16[2,768,128]{2,1,0:T(8,128)(2,1)} %constant.7.clone.table_ref) | copy-start | bytes 1179652
  35.0 6.8 %collective-permute-start.1 = (bf16[4,65,256]{2,1,0:T(8,128)(2,1)S(1)}, bf16[4,65,256]{2,1,0:T(8,128)(2,1)S(1)}, u32[]{:S(2)}, u32[]{:S(2)}) collective-permute-start(bf16[4,65,256]{2,1,0:T(8,128)(2,1)S(1)} %get-tuple-element.11), channel_id=1, source_target_pairs={{0,1},{1,0},{2,3},{3,2},{4,5},{5,4},{6,7},{7,6},{8,9},{9,8},{10,11... | collective-permute-start | bytes 399368 | tf_op jit(solution)/shard_map/ppermute | solution.py:385
  35.3 9.0 %collective-permute-start.2 = (bf16[4,65,256]{2,1,0:T(8,128)(2,1)S(1)}, bf16[4,65,256]{2,1,0:T(8,128)(2,1)S(1)}, u32[]{:S(2)}, u32[]{:S(2)}) collective-permute-start(bf16[4,65,256]{2,1,0:T(8,128)(2,1)S(1)} %get-tuple-element.12), channel_id=1, source_target_pairs={{0,2},{1,3},{2,0},{3,1},{4,6},{5,7},{6,4},{7,5},{8,10},{9,11},{10,... | collective-permute-start | bytes 399368 | tf_op jit(solution)/shard_map/ppermute | solution.py:385
  36.1 8.2 %collective-permute-start.3 = (bf16[4,65,256]{2,1,0:T(8,128)(2,1)S(1)}, bf16[4,65,256]{2,1,0:T(8,128)(2,1)S(1)}, u32[]{:S(2)}, u32[]{:S(2)}) collective-permute-start(bf16[4,65,256]{2,1,0:T(8,128)(2,1)S(1)} %get-tuple-element.13), channel_id=1, source_target_pairs={{0,3},{1,2},{2,1},{3,0},{4,7},{5,6},{6,5},{7,4},{8,11},{9,10},{10,... | collective-permute-start | bytes 399368 | tf_op jit(solution)/shard_map/ppermute | solution.py:385
  44.3 5.8 %collective-permute-start.4 = (bf16[65,256]{1,0:T(8,128)(2,1)S(1)}, bf16[65,256]{1,0:T(8,128)(2,1)S(1)}, u32[]{:S(2)}, u32[]{:S(2)}) collective-permute-start(bf16[65,256]{1,0:T(8,128)(2,1)S(1)} %get-tuple-element.15), channel_id=1, source_target_pairs={{0,4},{1,5},{2,6},{3,7},{4,8},{5,9},{6,10},{7,11},{8,12},{9,13},{1... | collective-permute-start | bytes 99848 | tf_op jit(solution)/shard_map/ppermute | solution.py:397
  44.9 5.3 %collective-permute-start.5 = (bf16[65,256]{1,0:T(8,128)(2,1)S(1)}, bf16[65,256]{1,0:T(8,128)(2,1)S(1)}, u32[]{:S(2)}, u32[]{:S(2)}) collective-permute-start(bf16[65,256]{1,0:T(8,128)(2,1)S(1)} %get-tuple-element.16), channel_id=1, source_target_pairs={{0,8},{1,9},{2,10},{3,11},{4,12},{5,13},{6,14},{7,15},{8,0},{9,1},... | collective-permute-start | bytes 99848 | tf_op jit(solution)/shard_map/ppermute | solution.py:397
  46.0 4.7 %collective-permute-start.6 = (bf16[65,256]{1,0:T(8,128)(2,1)S(1)}, bf16[65,256]{1,0:T(8,128)(2,1)S(1)}, u32[]{:S(2)}, u32[]{:S(2)}) collective-permute-start(bf16[65,256]{1,0:T(8,128)(2,1)S(1)} %get-tuple-element.17), channel_id=1, source_target_pairs={{0,12},{1,13},{2,14},{3,15},{4,0},{5,1},{6,2},{7,3},{8,4},{9,5},{1... | collective-permute-start | bytes 99848 | tf_op jit(solution)/shard_map/ppermute | solution.py:397
  106.6 1.3 %copy-start = (bf16[32,65,256]{2,1,0:T(8,128)(2,1)S(1)}, bf16[32,65,256]{2,1,0:T(8,128)(2,1)}, u32[]{:S(2)}) copy-start(bf16[32,65,256]{2,1,0:T(8,128)(2,1)} %all-gather.2.cloned.1.call-done.state_ref) | copy-start | bytes 3194884
Sparse Core Ops, SparseCore 0:
  52.3 54.1 all-gather.1

commit v2 on v0

--- a/solution.py
+++ b/solution.py
@@ -1,8 +1,12 @@
+import functools
 import math
 
 import jax
 import jax.numpy as jnp
+import numpy as np
 from jax import lax
+from jax.experimental import pallas as pl
+from jax.experimental.pallas import tpu as pltpu
 from jax.sharding import PartitionSpec as P
 
 time_step = 0.5
@@ -25,7 +29,7 @@
     )
 
 
-def on_device(grid_terms, pair_orders, legendre, state, kappa, right_op, left_op):
+def on_device_wide(grid_terms, pair_orders, legendre, state, kappa, right_op, left_op):
     lat_rows, phi_count, radial = grid_terms.shape
     pairs_here = legendre.shape[0]
     degrees = legendre.shape[1] - 1
@@ -101,6 +105,409 @@
     return (evolved, new_state)
 
 
+names = ("sec", "row", "col")
+
+
+def natural_table(pair_total, sections, phi_count):
+    slots = 2 * pair_total
+    longitudes = sections * phi_count
+    low = np.arange(pair_total)
+    orders = np.stack([low, slots - 1 - low], axis=1).reshape(slots)
+    turns = orders[:, None] * np.arange(longitudes)[None, :] % longitudes
+    angle = turns * (2.0 * np.pi / longitudes)
+    table = np.concatenate([np.cos(angle), -np.sin(angle)], axis=0) / np.sqrt(longitudes)
+    return table.reshape(2 * slots, sections, phi_count).transpose(1, 0, 2).astype(np.float32)
+
+
+def params(mib):
+    return pltpu.CompilerParams(vmem_limit_bytes=mib * 1024 * 1024)
+
+
+def vmem():
+    return pl.BlockSpec(memory_space=pltpu.VMEM)
+
+
+def smem():
+    return pl.BlockSpec(memory_space=pltpu.SMEM)
+
+
+def anywhere():
+    return pl.BlockSpec(memory_space=pl.ANY)
+
+
+def call(kernel, operands, out_shapes, mib=16, scalars=0, cost=None):
+    single = not isinstance(out_shapes, (list, tuple))
+    return pl.pallas_call(
+        kernel,
+        in_specs=[smem()] * scalars + [vmem()] * (len(operands) - scalars),
+        out_specs=vmem() if single else [vmem()] * len(out_shapes),
+        out_shape=out_shapes,
+        compiler_params=params(mib),
+        cost_estimate=cost,
+    )(*operands)
+
+
+class Places:
+    def __init__(self):
+        self.sections, side_row, self.side_x = (lax.axis_size(name) for name in names)
+        self.side_y = 2 if side_row % 2 == 0 else 1
+        self.depth = side_row // self.side_y
+        self.sizes = (self.sections, self.depth, self.side_y, self.side_x)
+
+    def pair(self, sec, deep, y, x):
+        at_sec = lax.axis_index("sec") ^ sec
+        at_row = lax.axis_index("row") ^ (deep * self.side_y + y)
+        at_col = lax.axis_index("col") ^ x
+        return (at_sec * (self.depth * self.side_y) + at_row) * self.side_x + at_col
+
+    def move(self, array, sec=0, deep=0, y=0, x=0):
+        shift = (sec, deep, y, x)
+        pairs = []
+        for source in np.ndindex(*self.sizes):
+            target = tuple(at ^ by for at, by in zip(source, shift))
+            pairs.append(
+                (
+                    int(np.ravel_multi_index(source, self.sizes)),
+                    int(np.ravel_multi_index(target, self.sizes)),
+                )
+            )
+        return lax.ppermute(array, names, pairs)
+
+
+def cut_kernel(legendre_ref, out_ref):
+    copies, lat_rows, rows = out_ref.shape
+    turned = jnp.pad(
+        legendre_ref[0].astype(jnp.float32), ((0, rows - legendre_ref.shape[1]), (0, 0))
+    ).T.astype(jnp.bfloat16)
+    parts = turned.shape[0] // lat_rows
+    for at in range(copies):
+        begin = at % parts * lat_rows
+        out_ref[at] = turned[begin : begin + lat_rows]
+
+
+def forward_kernel(table_ref, grid_ref, out_ref, buffer, held, sems):
+    blocks, rows, lat_block, radial = held.shape
+    slots = rows // 2
+    chunks = sems.shape[0]
+
+    def chunk(at):
+        return pltpu.make_async_copy(
+            grid_ref.at[pl.ds(2 * at, 2)], buffer.at[pl.ds(2 * at, 2)], sems.at[at]
+        )
+
+    for at in range(chunks):
+        chunk(at).start()
+    table = table_ref[lax.axis_index("sec")]
+
+    def one_block(block, carry):
+        for at in range(0, lat_block, 2):
+            lat = block * lat_block + at
+            chunk(lat // 2).wait()
+            two = jnp.concatenate(
+                [buffer[lat].astype(jnp.bfloat16), buffer[lat + 1].astype(jnp.bfloat16)], axis=1
+            )
+            sums = jnp.dot(table, two, preferred_element_type=jnp.float32)
+            held[block, :, at, :] = sums[:, :radial]
+            held[block, :, at + 1, :] = sums[:, radial:]
+        return carry
+
+    lax.fori_loop(0, blocks, one_block, 0)
+    for block in range(0, blocks, 2):
+        for part in range(2):
+            rows_of = pl.ds(part * slots, slots)
+            both = jnp.concatenate([held[block, rows_of], held[block + 1, rows_of]], axis=1)
+            out_ref[:, pl.ds(block * lat_block, 2 * lat_block), pl.ds(part * radial, radial)] = (
+                both.astype(jnp.bfloat16)
+            )
+
+
+def forward_sums(table, grid_terms, lat_block):
+    sections, rows, phi_count = table.shape
+    lat_rows, _, radial = grid_terms.shape
+    blocks = lat_rows // lat_block
+    return pl.pallas_call(
+        forward_kernel,
+        in_specs=[vmem(), anywhere()],
+        out_specs=vmem(),
+        out_shape=jax.ShapeDtypeStruct((rows // 2, lat_rows, 2 * radial), jnp.bfloat16),
+        scratch_shapes=[
+            pltpu.VMEM(grid_terms.shape, jnp.float32),
+            pltpu.VMEM((blocks, rows, lat_block, radial), jnp.float32),
+            pltpu.SemaphoreType.DMA((lat_rows // 2,)),
+        ],
+        compiler_params=params(36),
+        cost_estimate=pl.CostEstimate(
+            flops=2 * rows * phi_count * lat_rows * radial,
+            bytes_accessed=4 * lat_rows * phi_count * radial,
+            transcendentals=0,
+        ),
+    )(table, grid_terms)
+
+
+def masked(weights, order, degrees):
+    row_index = lax.broadcasted_iota(jnp.int32, weights.shape, 1)
+    leading = row_index < degrees - order
+    zero = jnp.zeros_like(weights)
+    return jnp.where(leading, weights, zero), jnp.where(leading, zero, weights)
+
+
+def degrees_kernel(places, sec, degrees, orders_ref, legendre_ref, fourier_ref, out_ref):
+    side_x, side_y = places.side_x, places.side_y
+    contract = (((0,), (0,)), ((), ()))
+    for deep, y, x in np.ndindex(places.depth, side_y, side_x):
+        pair = places.pair(sec, int(deep), int(y), int(x))
+        order = orders_ref[pair]
+        lower, upper = masked(legendre_ref[pair], order, degrees)
+        total = lax.dot_general(
+            lower, fourier_ref[2 * order], contract, preferred_element_type=jnp.float32
+        ) + lax.dot_general(
+            upper, fourier_ref[2 * order + 1], contract, preferred_element_type=jnp.float32
+        )
+        out_ref[y, x, deep] = total.astype(out_ref.dtype)
+
+
+def plane_kernel(kept_ref, taken_ref, keep_a, send_a, keep_b, send_b):
+    radial = keep_a.shape[-1]
+    for y in range(2):
+        for x in range(2):
+            total = kept_ref[y, x] + taken_ref[y, x].astype(jnp.float32)
+            part_a, part_b = total[..., :radial], total[..., radial:]
+            if x == 0:
+                keep_a[y] = part_a
+            else:
+                send_a[y] = part_a.astype(jnp.bfloat16)
+            if y == 0:
+                keep_b[x] = part_b
+            else:
+                send_b[x] = part_b.astype(jnp.bfloat16)
+
+
+def cross_kernel(keep_a, take_a, keep_b, take_b, keep_a2, send_a2, keep_b2, send_b2):
+    keep_a2[...] = keep_a[0] + take_a[0].astype(jnp.float32)
+    send_a2[...] = (keep_a[1] + take_a[1].astype(jnp.float32)).astype(jnp.bfloat16)
+    keep_b2[...] = keep_b[0] + take_b[0].astype(jnp.float32)
+    send_b2[...] = (keep_b[1] + take_b[1].astype(jnp.float32)).astype(jnp.bfloat16)
+
+
+def depth_kernel(keep_a, take_a, keep_b, take_b, *outs):
+    radial = keep_a.shape[-1]
+    for deep, out in enumerate(outs):
+        out[:, :radial] = (keep_a[deep] + take_a[deep].astype(jnp.float32)).astype(out.dtype)
+        out[:, radial:] = (keep_b[deep] + take_b[deep].astype(jnp.float32)).astype(out.dtype)
+
+
+def solve_kernel(places, orders_ref, *refs):
+    takes = refs[: places.depth]
+    state_ref, kappa_ref, damping_ref, right_ref, left_ref, out_ref, sent_ref = refs[places.depth :]
+    rows = state_ref.shape[1]
+    radial = right_ref.shape[0]
+    degrees = rows - 1
+    order = orders_ref[places.pair(0, 0, 0, 0)]
+    coefficient = takes[0][...].astype(jnp.float32)
+    for other in takes[1:]:
+        coefficient += other[...].astype(jnp.float32)
+    right_side = state_ref[0].astype(jnp.float32) + time_step * coefficient[:rows]
+    right_side = right_side.astype(jnp.bfloat16)
+    row_index = lax.broadcasted_iota(jnp.int32, (rows, radial), 0)
+    degree = jnp.where(row_index < degrees - order, order + row_index, row_index - 1)
+    degree = degree.astype(jnp.float32)
+    factor = damping_ref[...] / (
+        1.0 + kappa_ref[...] + degree * (degree + 1.0) / (degrees * degrees)
+    )
+    sent_ref[...] = jnp.zeros_like(sent_ref)
+    for part in range(2):
+        columns = pl.ds(part * radial, radial)
+        eigen = jnp.dot(
+            right_side[:, part * radial : (part + 1) * radial],
+            right_ref[...],
+            preferred_element_type=jnp.float32,
+        )
+        scaled = (eigen * factor).astype(jnp.bfloat16)
+        field = jnp.dot(scaled, left_ref[...], preferred_element_type=jnp.float32)
+        field = field.astype(jnp.bfloat16)
+        out_ref[0, :, columns] = field
+        sent_ref[pl.ds(0, rows), columns] = field
+
+
+def spread_kernel(*refs):
+    fields, (out_a, out_b) = refs[:-2], refs[-2:]
+    radial = out_a.shape[-1]
+    for deep, field in enumerate(fields):
+        out_a[deep] = field[:, :radial]
+        out_b[deep] = field[:, radial:]
+
+
+def join_kernel(own_a, take_a, own_b, take_b, out_a, out_b):
+    out_a[0] = own_a[...]
+    out_a[1] = take_a[...]
+    out_b[0] = own_b[...]
+    out_b[1] = take_b[...]
+
+
+def inverse_kernel(places, degrees, orders_ref, legendre_ref, table_ref, *refs):
+    fields, (out_ref, buffer, held, sems) = refs[:-4], refs[-4:]
+    blocks, slot_rows, lat_block, radial = held.shape
+    slots = slot_rows // 2
+    per_section = len(fields) // places.sections
+
+    for sec in range(places.sections):
+        own_a, far_a, own_b, far_b = fields[sec * per_section : (sec + 1) * per_section]
+        for deep, y, x in np.ndindex(places.depth, places.side_y, places.side_x):
+            deep, y, x = int(deep), int(y), int(x)
+            pair = places.pair(sec, deep, y, x)
+            order = orders_ref[pair]
+            weights = masked(legendre_ref[pair], order, degrees)
+            both = ((far_a if y else own_a)[x, deep], (far_b if x else own_b)[y, deep])
+            field = jnp.concatenate(both, axis=1)
+            for half in range(2):
+                rebuilt = jnp.dot(weights[half], field, preferred_element_type=jnp.float32)
+                for part in range(2):
+                    held[:, part * slots + 2 * order + half] = rebuilt[
+                        :, part * radial : (part + 1) * radial
+                    ].reshape(blocks, lat_block, radial)
+
+    table = table_ref[lax.axis_index("sec")]
+
+    def chunk(at):
+        return pltpu.make_async_copy(
+            buffer.at[pl.ds(2 * at, 2)], out_ref.at[pl.ds(2 * at, 2)], sems.at[at]
+        )
+
+    def one_block(block, carry):
+        for at in range(0, lat_block, 2):
+            two = jnp.concatenate(
+                [
+                    held[block, :, at, :].astype(jnp.bfloat16),
+                    held[block, :, at + 1, :].astype(jnp.bfloat16),
+                ],
+                axis=1,
+            )
+            values = jnp.dot(table, two, preferred_element_type=jnp.float32)
+            lat = block * lat_block + at
+            buffer[lat] = values[:, :radial]
+            buffer[lat + 1] = values[:, radial:]
+            chunk(lat // 2).start()
+        return carry
+
+    lax.fori_loop(0, blocks, one_block, 0)
+    for at in range(sems.shape[0]):
+        chunk(at).wait()
+
+
+def inverse_values(places, degrees, pair_orders, legendre, table, fields, lat_rows, lat_block):
+    _, phi_count, slot_rows = table.shape
+    radial = fields[0].shape[-1]
+    blocks = lat_rows // lat_block
+    out = jax.ShapeDtypeStruct((lat_rows, phi_count, radial), jnp.float32)
+    return pl.pallas_call(
+        functools.partial(inverse_kernel, places, degrees),
+        in_specs=[smem()] + [vmem()] * (2 + len(fields)),
+        out_specs=anywhere(),
+        out_shape=out,
+        scratch_shapes=[
+            pltpu.VMEM(out.shape, jnp.float32),
+            pltpu.VMEM((blocks, slot_rows, lat_block, radial), jnp.float32),
+            pltpu.SemaphoreType.DMA((lat_rows // 2,)),
+        ],
+        compiler_params=params(36),
+        cost_estimate=pl.CostEstimate(
+            flops=2 * slot_rows * phi_count * lat_rows * radial,
+            bytes_accessed=4 * lat_rows * phi_count * radial,
+            transcendentals=0,
+        ),
+    )(pair_orders, legendre, table, *fields)
+
+
+def on_device_compact(grid_terms, pair_orders, legendre, state, kappa, right_op, left_op):
+    lat_rows, phi_count, radial = grid_terms.shape
+    rows = legendre.shape[1]
+    degrees = rows - 1
+    padded = -(-rows // 8) * 8
+    columns = 2 * radial
+    pair_total = pair_orders.shape[0]
+    places = Places()
+    depth = places.depth
+    lat_block = 8
+    table = natural_table(pair_total, places.sections, phi_count)
+    forward_table = jnp.asarray(table, jnp.bfloat16)
+    inverse_table = jnp.asarray(table.transpose(0, 2, 1), jnp.bfloat16)
+
+    def shape(*sizes, dtype=jnp.bfloat16):
+        return jax.ShapeDtypeStruct(sizes, dtype)
+
+    cut = call(cut_kernel, [legendre], shape(pair_total, lat_rows, padded))
+    legendre_here = lax.all_to_all(cut, names, split_axis=0, concat_axis=0, tiled=True)
+
+    fourier = forward_sums(forward_table, grid_terms, lat_block)
+
+    def partial_sums(sec, dtype):
+        return call(
+            functools.partial(degrees_kernel, places, sec, degrees),
+            [pair_orders, legendre_here, fourier],
+            shape(2, 2, depth, padded, columns, dtype=dtype),
+            mib=24,
+            scalars=1,
+            cost=pl.CostEstimate(
+                flops=4 * pair_total * rows * lat_rows * columns // places.sections,
+                bytes_accessed=fourier.size * 2,
+                transcendentals=0,
+            ),
+        )
+
+    taken = places.move(partial_sums(1, jnp.bfloat16), sec=1)
+    kept = partial_sums(0, jnp.float32)
+    wide = shape(2, depth, padded, radial, dtype=jnp.float32)
+    half = shape(2, depth, padded, radial)
+    keep_a, send_a, keep_b, send_b = call(plane_kernel, [kept, taken], [wide, half, wide, half])
+    take_a, take_b = places.move(send_a, x=1), places.move(send_b, y=1)
+    wide = shape(depth, padded, radial, dtype=jnp.float32)
+    half = shape(depth, padded, radial)
+    keep_a, send_a, keep_b, send_b = call(
+        cross_kernel, [keep_a, take_a, keep_b, take_b], [wide, half, wide, half]
+    )
+    take_a, take_b = places.move(send_a, y=1), places.move(send_b, x=1)
+    lines = call(
+        depth_kernel,
+        [keep_a, take_a, keep_b, take_b],
+        [shape(padded, columns, dtype=jnp.float32)] + [shape(padded, columns)] * (depth - 1),
+    )
+    parts = [lines[0]] + [places.move(lines[deep], deep=deep) for deep in range(1, depth)]
+
+    radial_mode = np.arange(radial, dtype=np.float32) / np.float32(radial)
+    damping = np.exp(-filter_strength * radial_mode**filter_power).astype(np.float32)
+    new_state, field = call(
+        functools.partial(solve_kernel, places),
+        [pair_orders, *parts, state, kappa[None, :], jnp.asarray(damping)[None, :], right_op, left_op],
+        [shape(1, rows, columns), shape(padded, columns)],
+        scalars=1,
+    )
+
+    fields = [field] + [places.move(field, deep=deep) for deep in range(1, depth)]
+    own_a, own_b = call(spread_kernel, fields, [half, half])
+    take_a, take_b = places.move(own_a, x=1), places.move(own_b, y=1)
+    both = shape(2, depth, padded, radial)
+    own_a, own_b = call(join_kernel, [own_a, take_a, own_b, take_b], [both, both])
+    far_a, far_b = places.move(own_a, y=1), places.move(own_b, x=1)
+    here = [own_a, far_a, own_b, far_b]
+    there = [places.move(part, sec=1) for part in (own_a, own_b)]
+    there += [places.move(part, sec=1) for part in (far_a, far_b)]
+    gathered = here + [there[0], there[2], there[1], there[3]]
+    evolved = inverse_values(
+        places, degrees, pair_orders, legendre_here, inverse_table, gathered, lat_rows, lat_block
+    )
+    return (evolved, new_state)
+
+
+def on_device(*args):
+    lat_rows = args[0].shape[0]
+    rows = args[2].shape[1]
+    sections, side_row, side_x = (lax.axis_size(name) for name in names)
+    fits = args[2].shape[0] == 1 and lat_rows % 16 == 0 and rows <= 2 * lat_rows
+    fits = fits and args[0].size * 4 <= 24 * 1024 * 1024
+    fits = fits and sections == 2 and side_x == 2 and side_row in (2, 4, 8, 16)
+    return on_device_compact(*args) if fits else on_device_wide(*args)
+
+
 def solution(mesh):
     return jax.shard_map(
         on_device,

time: 165 us -> 78.2 us (0.47)
  waiting for transfers between devices: 76.5 us -> 27.7 us
  matrix products: 32.1 us -> 0 us
  Pallas kernels: 0 us -> 22.4 us
  other arithmetic: 19.3 us -> 0 us
  between operations: 14.9 us -> 0.79 us
  starting transfers between devices: 12.1 us -> 25.1 us
  local copies, waits for them, and re-layouts: 9.99 us -> 1.96 us
    reduce_scatter x2 -> x0, waiting for transfers between devices: 40.8 us -> none  [the longest x1 27 us: on_device(): lax.psum_scatter(partial_value.astype(jnp.bfloat16), 'sec', scatter_dimen...]
    dot_general x5 -> x0, matrix products: 32.1 us -> none  [the longest x1 17.9 us: on_device(): jnp.einsum('stcr,psc->tpr', values, phase_table, precision=highest, prefe...]
    all_to_all x2 -> x1, waiting for transfers between devices: 35.7 us -> 4.3 us  [on_device_compact(): lax.all_to_all(cut, names, split_axis=0, concat_axis=0, tiled=True)]
    ppermute x0 -> x19, waiting for transfers between devices: none -> 23.4 us  [move(): return lax.ppermute(array, names, pairs)]
    pallas_call x0 -> x11, Pallas kernels: none -> 22.4 us  [the longest x1 8.94 us: inverse_values(): pl.pallas_call(functools.partial(inverse_kernel, places, degrees), in_spe...]
    ppermute x0 -> x19, starting transfers between devices: none -> 17.8 us  [move(): return lax.ppermute(array, names, pairs)]
    convert_element_type x3 -> x0, other arithmetic: 15.3 us -> none  [the longest x1 12.9 us: on_device(): evolved = lax.psum_scatter(partial_value.astype(jnp.bfloat16), 'sec', sca...]
    reshape x6 -> x0, local copies, waits for them, and re-layouts: 6.47 us -> none  [the longest x1 3.63 us: on_device(): term.reshape(section_slots * lax.axis_size('sec'), lat_rows, columns)]
  transfers between devices with their start and end apart: 4 -> 20, of which waited for: 4 -> 15; matrix products, arithmetic and copies ran while one was open for 2% -> 0% of each run, Pallas kernels for 0% -> 13%
where the time goes in v2:
time: 78.2 us; the launch traced here: 77.9 us
  waiting for transfers between devices  27.7 us (35%)
  starting transfers between devices  25.1 us (32%)
  Pallas kernels  22.4 us (29%)
  local copies, waits for them, and re-layouts  1.96 us (3%)
  between operations  0.79 us (1%)
    ppermute x19, waiting for transfers between devices, move(): return lax.ppermute(array, names, pairs)  23.4 us
    ppermute x19, starting transfers between devices, move(): return lax.ppermute(array, names, pairs)  17.8 us
    pallas_call x1, Pallas kernels, inverse_values(): pl.pallas_call(functools.partial(inverse_kernel, places, degrees), in_spe...  8.94 us
    pallas_call x1, Pallas kernels, forward_sums(): pl.pallas_call(forward_kernel, in_specs=[vmem(), anywhere()], out_specs=v...  8.71 us
    all_to_all x1, starting transfers between devices, on_device_compact(): lax.all_to_all(cut, names, split_axis=0, concat_axis=0, tiled=True)  7.3 us
    pallas_call x9, Pallas kernels, call(): pl.pallas_call(kernel, in_specs=[smem()] * scalars + [vmem()] * (len(oper...  4.78 us
    all_to_all x1, waiting for transfers between devices, on_device_compact(): lax.all_to_all(cut, names, split_axis=0, concat_axis=0, tiled=True)  4.3 us
    unnamed x18, local copies, waits for them, and re-layouts  1.96 us
  transfers between devices with their start and end apart: 20, of which 15 were waited for; matrix products, arithmetic and copies ran while one was open for 0% of the time, Pallas kernels for 13%

profile of v2, /device:TPU:0, one launch (start us, length us, event | category | flops | bytes accessed | tf_op | source)
XLA Modules:
  0.0 77.9 jit_solution(11568768147105329866)
XLA Ops:
  0.7 0.9 %copy-done.2 = bf16[1,65,768]{2,1,0:T(8,128)(2,1)S(1)} copy-done((bf16[1,65,768]{2,1,0:T(8,128)(2,1)S(1)}, bf16[1,65,768]{2,1,0:T(8,128)(2,1)}, u32[]{:S(2)}) %copy-start.2) | copy-done | bytes 99864
  1.6 0.9 %shard_map.113 = bf16[32,48,72]{2,1,0:T(8,128)(2,1)} custom-call(bf16[1,65,768]{2,1,0:T(8,128)(2,1)S(1)} %copy-done.2), custom_call_target="tpu_custom_call" | custom-call | tf_op jit(solution)/shard_map/pallas_call | solution.py:140
  2.5 7.3 %all-to-all-start = ((bf16[32,48,72]{2,1,0:T(8,128)(2,1)}), bf16[32,48,72]{2,1,0:T(8,128)(2,1)S(1)}, u32[]{:S(2)}, u32[]{:S(2)}) async-start(bf16[32,48,72]{2,1,0:T(8,128)(2,1)} %shard_map.113), calls=%async_computation | async-start | bytes 786432 | tf_op jit(solution)/shard_map/all_to_all | solution.py:439
  9.8 1.0 %copy-done.1 = bf16[2,128,768]{2,1,0:T(8,128)(2,1)S(1)} copy-done((bf16[2,128,768]{2,1,0:T(8,128)(2,1)S(1)}, bf16[2,128,768]{2,1,0:T(8,128)(2,1)}, u32[]{:S(2)}) %copy-start.1) | copy-done | bytes 393240
  10.8 8.7 %shard_map.114.fourier_ref = bf16[64,48,256]{2,1,0:T(8,128)(2,1)S(1)} custom-call(bf16[2,128,768]{2,1,0:T(8,128)(2,1)S(1)} %copy-done.1, f32[48,768,128]{2,1,0:T(8,128)} %grid_ref.1), custom_call_target="tpu_custom_call" | custom-call | flops 1207959552 | bytes 18874368 | tf_op jit(solution)/shard_map/pallas_call | solution.py:228
  19.5 4.3 %all-to-all-done.legendre_ref = bf16[32,48,72]{2,1,0:T(8,128)(2,1)S(1)} async-done(((bf16[32,48,72]{2,1,0:T(8,128)(2,1)}), bf16[32,48,72]{2,1,0:T(8,128)(2,1)S(1)}, u32[]{:S(2)}, u32[]{:S(2)}) %all-to-all-start) | async-done | bytes 221216 | tf_op jit(solution)/shard_map/all_to_all | solution.py:439
  23.8 1.1 %shard_map.116 = bf16[2,2,4,72,256]{4,3,2,1,0:T(8,128)(2,1)S(1)} custom-call(s32[32]{0:T(128)S(1)} %copy-done.6, bf16[32,48,72]{2,1,0:T(8,128)(2,1)S(1)} %all-to-all-done.legendre_ref, bf16[64,48,256]{2,1,0:T(8,128)(2,1)S(1)} %shard_map.114.fourier_ref), custom_call_target="tpu_custom_call" | custom-call | flops 51118080 | bytes 1572864 | tf_op jit(solution)/shard_map/pallas_call | solution.py:140
  25.0 1.1 %shard_map.115.kept_ref = f32[2,2,4,72,256]{4,3,2,1,0:T(8,128)S(1)} custom-call(s32[32]{0:T(128)S(1)} %copy-done.6, bf16[32,48,72]{2,1,0:T(8,128)(2,1)S(1)} %all-to-all-done.legendre_ref, bf16[64,48,256]{2,1,0:T(8,128)(2,1)S(1)} %shard_map.114.fourier_ref), custom_call_target="tpu_custom_call" | custom-call | flops 51118080 | bytes 1572864 | tf_op jit(solution)/shard_map/pallas_call | solution.py:140
  26.1 0.9 %collective-permute-done.taken_ref = bf16[2,2,4,72,256]{4,3,2,1,0:T(8,128)(2,1)S(1)} collective-permute-done((bf16[2,2,4,72,256]{4,3,2,1,0:T(8,128)(2,1)S(1)}, bf16[2,2,4,72,256]{4,3,2,1,0:T(8,128)(2,1)S(1)}, u32[]{:S(2)}, u32[]{:S(2)}) %collective-permute-start) | collective-permute-done | bytes 589856 | tf_op jit(solution)/shard_map/ppermute | solution.py:174
  27.4 0.8 %collective-permute-start.2 = (bf16[2,4,72,128]{3,2,1,0:T(8,128)(2,1)S(1)}, bf16[2,4,72,128]{3,2,1,0:T(8,128)(2,1)S(1)}, u32[]{:S(2)}, u32[]{:S(2)}) collective-permute-start(bf16[2,4,72,128]{3,2,1,0:T(8,128)(2,1)S(1)} %get-tuple-element.23), channel_id=1, source_target_pairs={{0,2},{1,3},{2,0},{3,1},{4,6},{5,7},{6,4},{7,5},{8,10},{9,11},{10,... | collective-permute-start | bytes 442376 | tf_op jit(solution)/shard_map/ppermute | solution.py:174
  28.2 4.9 %collective-permute-done.1.take_a = bf16[2,4,72,128]{3,2,1,0:T(8,128)(2,1)S(1)} collective-permute-done((bf16[2,4,72,128]{3,2,1,0:T(8,128)(2,1)S(1)}, bf16[2,4,72,128]{3,2,1,0:T(8,128)(2,1)S(1)}, u32[]{:S(2)}, u32[]{:S(2)}) %collective-permute-start.1) | collective-permute-done | bytes 147488 | tf_op jit(solution)/shard_map/ppermute | solution.py:174
  33.2 0.7 collective-permute-start.3
  33.9 1.3 %collective-permute-start.4 = (bf16[4,72,128]{2,1,0:T(8,128)(2,1)S(1)}, bf16[4,72,128]{2,1,0:T(8,128)(2,1)S(1)}, u32[]{:S(2)}, u32[]{:S(2)}) collective-permute-start(bf16[4,72,128]{2,1,0:T(8,128)(2,1)S(1)} %get-tuple-element.27), channel_id=1, source_target_pairs={{0,1},{1,0},{2,3},{3,2},{4,5},{5,4},{6,7},{7,6},{8,9},{9,8},{10,11... | collective-permute-start | bytes 221192 | tf_op jit(solution)/shard_map/ppermute | solution.py:174
  35.2 2.4 %collective-permute-done.3.take_a = bf16[4,72,128]{2,1,0:T(8,128)(2,1)S(1)} collective-permute-done((bf16[4,72,128]{2,1,0:T(8,128)(2,1)S(1)}, bf16[4,72,128]{2,1,0:T(8,128)(2,1)S(1)}, u32[]{:S(2)}, u32[]{:S(2)}) %collective-permute-start.3) | collective-permute-done | bytes 73760 | tf_op jit(solution)/shard_map/ppermute | solution.py:174
  37.6 0.6 collective-permute-done.4.take_b
  38.7 1.6 %collective-permute-start.6 = (bf16[72,256]{1,0:T(8,128)(2,1)S(1)}, bf16[72,256]{1,0:T(8,128)(2,1)S(1)}, u32[]{:S(2)}, u32[]{:S(2)}) collective-permute-start(bf16[72,256]{1,0:T(8,128)(2,1)S(1)} %get-tuple-element.30), channel_id=1, source_target_pairs={{0,8},{1,9},{2,10},{3,11},{4,12},{5,13},{6,14},{7,15},{8,0},{9,1},... | collective-permute-start | bytes 110600 | tf_op jit(solution)/shard_map/ppermute | solution.py:174
  40.3 2.5 %collective-permute-start.7 = (bf16[72,256]{1,0:T(8,128)(2,1)S(1)}, bf16[72,256]{1,0:T(8,128)(2,1)S(1)}, u32[]{:S(2)}, u32[]{:S(2)}) collective-permute-start(bf16[72,256]{1,0:T(8,128)(2,1)S(1)} %get-tuple-element.31), channel_id=1, source_target_pairs={{0,12},{1,13},{2,14},{3,15},{4,8},{5,9},{6,10},{7,11},{8,4},{9,5},... | collective-permute-start | bytes 110600 | tf_op jit(solution)/shard_map/ppermute | solution.py:174
  42.8 0.8 collective-permute-done.6.refs_2_
  43.5 2.5 %collective-permute-done.7.refs_3_ = bf16[72,256]{1,0:T(8,128)(2,1)S(1)} collective-permute-done((bf16[72,256]{1,0:T(8,128)(2,1)S(1)}, bf16[72,256]{1,0:T(8,128)(2,1)S(1)}, u32[]{:S(2)}, u32[]{:S(2)}) %collective-permute-start.7) | collective-permute-done | bytes 36896 | tf_op jit(solution)/shard_map/ppermute | solution.py:174
  46.1 1.5 %shard_map.120 = (bf16[1,65,256]{2,1,0:T(8,128)(2,1)}, bf16[72,256]{1,0:T(8,128)(2,1)S(1)}) custom-call(s32[32]{0:T(128)S(1)} %copy-done.6, f32[72,256]{1,0:T(8,128)S(1)} %get-tuple-element.28.refs_0_, bf16[72,256]{1,0:T(8,128)(2,1)S(1)} %collective-permute-done.5.refs_1_, bf16[72,256]{1,0:T(8,128)(2,1)S(1)} %collective-permute-done.6.refs_2_, ...), custom_call_target="tpu_custom_call" | custom-call | tf_op jit(solution)/shard_map/pallas_call | solution.py:140
  47.5 2.5 %collective-permute-start.10 = (bf16[72,256]{1,0:T(8,128)(2,1)S(1)}, bf16[72,256]{1,0:T(8,128)(2,1)S(1)}, u32[]{:S(2)}, u32[]{:S(2)}) collective-permute-start(bf16[72,256]{1,0:T(8,128)(2,1)S(1)} %get-tuple-element.32.refs_0_), channel_id=1, source_target_pairs={{0,12},{1,13},{2,14},{3,15},{4,8},{5,9},{6,10},{7,11},{8,4},{9,5},... | collective-permute-start | bytes 110600 | tf_op jit(solution)/shard_map/ppermute | solution.py:174
  50.0 1.9 %collective-permute-start.8 = (bf16[72,256]{1,0:T(8,128)(2,1)S(1)}, bf16[72,256]{1,0:T(8,128)(2,1)S(1)}, u32[]{:S(2)}, u32[]{:S(2)}) collective-permute-start(bf16[72,256]{1,0:T(8,128)(2,1)S(1)} %get-tuple-element.32.refs_0_), channel_id=1, source_target_pairs={{0,4},{1,5},{2,6},{3,7},{4,0},{5,1},{6,2},{7,3},{8,12},{9,13},{10,... | collective-permute-start | bytes 110600 | tf_op jit(solution)/shard_map/ppermute | solution.py:174
  51.9 1.4 %collective-permute-done.10.refs_3_ = bf16[72,256]{1,0:T(8,128)(2,1)S(1)} collective-permute-done((bf16[72,256]{1,0:T(8,128)(2,1)S(1)}, bf16[72,256]{1,0:T(8,128)(2,1)S(1)}, u32[]{:S(2)}, u32[]{:S(2)}) %collective-permute-start.10) | collective-permute-done | bytes 36896 | tf_op jit(solution)/shard_map/ppermute | solution.py:174
  53.3 1.6 %collective-permute-done.9.refs_2_ = bf16[72,256]{1,0:T(8,128)(2,1)S(1)} collective-permute-done((bf16[72,256]{1,0:T(8,128)(2,1)S(1)}, bf16[72,256]{1,0:T(8,128)(2,1)S(1)}, u32[]{:S(2)}, u32[]{:S(2)}) %collective-permute-start.9) | collective-permute-done | bytes 36896 | tf_op jit(solution)/shard_map/ppermute | solution.py:174
  54.9 1.4 %collective-permute-start.11 = (bf16[4,72,128]{2,1,0:T(8,128)(2,1)S(1)}, bf16[4,72,128]{2,1,0:T(8,128)(2,1)S(1)}, u32[]{:S(2)}, u32[]{:S(2)}) collective-permute-start(bf16[4,72,128]{2,1,0:T(8,128)(2,1)S(1)} %get-tuple-element.33.own_a), channel_id=1, source_target_pairs={{0,1},{1,0},{2,3},{3,2},{4,5},{5,4},{6,7},{7,6},{8,9},{9,8},{10,11... | collective-permute-start | bytes 221192 | tf_op jit(solution)/shard_map/ppermute | solution.py:174
  56.3 1.7 %collective-permute-start.12 = (bf16[4,72,128]{2,1,0:T(8,128)(2,1)S(1)}, bf16[4,72,128]{2,1,0:T(8,128)(2,1)S(1)}, u32[]{:S(2)}, u32[]{:S(2)}) collective-permute-start(bf16[4,72,128]{2,1,0:T(8,128)(2,1)S(1)} %get-tuple-element.34.own_b), channel_id=1, source_target_pairs={{0,2},{1,3},{2,0},{3,1},{4,6},{5,7},{6,4},{7,5},{8,10},{9,11},{10,... | collective-permute-start | bytes 221192 | tf_op jit(solution)/shard_map/ppermute | solution.py:174
  58.0 2.0 %collective-permute-done.11.take_a = bf16[4,72,128]{2,1,0:T(8,128)(2,1)S(1)} collective-permute-done((bf16[4,72,128]{2,1,0:T(8,128)(2,1)S(1)}, bf16[4,72,128]{2,1,0:T(8,128)(2,1)S(1)}, u32[]{:S(2)}, u32[]{:S(2)}) %collective-permute-start.11) | collective-permute-done | bytes 73760 | tf_op jit(solution)/shard_map/ppermute | solution.py:174
  60.7 1.8 %collective-permute-start.13 = (bf16[2,4,72,128]{3,2,1,0:T(8,128)(2,1)S(1)}, bf16[2,4,72,128]{3,2,1,0:T(8,128)(2,1)S(1)}, u32[]{:S(2)}, u32[]{:S(2)}) collective-permute-start(bf16[2,4,72,128]{3,2,1,0:T(8,128)(2,1)S(1)} %get-tuple-element.35.refs_0_), channel_id=1, source_target_pairs={{0,2},{1,3},{2,0},{3,1},{4,6},{5,7},{6,4},{7,5},{8,10},{9,11},{10,... | collective-permute-start | bytes 442376 | tf_op jit(solution)/shard_map/ppermute | solution.py:174
  63.3 2.5 %collective-permute-done.13.refs_1_ = bf16[2,4,72,128]{3,2,1,0:T(8,128)(2,1)S(1)} collective-permute-done((bf16[2,4,72,128]{3,2,1,0:T(8,128)(2,1)S(1)}, bf16[2,4,72,128]{3,2,1,0:T(8,128)(2,1)S(1)}, u32[]{:S(2)}, u32[]{:S(2)}) %collective-permute-start.13) | collective-permute-done | bytes 147488 | tf_op jit(solution)/shard_map/ppermute | solution.py:174
  65.9 1.7 %collective-permute-done.14.refs_3_ = bf16[2,4,72,128]{3,2,1,0:T(8,128)(2,1)S(1)} collective-permute-done((bf16[2,4,72,128]{3,2,1,0:T(8,128)(2,1)S(1)}, bf16[2,4,72,128]{3,2,1,0:T(8,128)(2,1)S(1)}, u32[]{:S(2)}, u32[]{:S(2)}) %collective-permute-start.14) | collective-permute-done | bytes 147488 | tf_op jit(solution)/shard_map/ppermute | solution.py:174
  67.6 1.3 %collective-permute-done.18.refs_7_ = bf16[2,4,72,128]{3,2,1,0:T(8,128)(2,1)S(1)} collective-permute-done((bf16[2,4,72,128]{3,2,1,0:T(8,128)(2,1)S(1)}, bf16[2,4,72,128]{3,2,1,0:T(8,128)(2,1)S(1)}, u32[]{:S(2)}, u32[]{:S(2)}) %collective-permute-start.18) | collective-permute-done | bytes 147488 | tf_op jit(solution)/shard_map/ppermute | solution.py:174
  69.0 8.9 %shard_map.123 = f32[48,768,128]{2,1,0:T(8,128)} custom-call(s32[32]{0:T(128)S(1)} %copy-done.6, bf16[32,48,72]{2,1,0:T(8,128)(2,1)S(1)} %all-to-all-done.legendre_ref, bf16[2,768,128]{2,1,0:T(8,128)(2,1)S(1)} %copy-done, bf16[2,4,72,128]{3,2,1,0:T(8,128)(2,1)S(1)} %get-tuple-element.35.refs_0_, bf16[2,4,72,128]{3,2,1,0:T(8,128)(2,1)S(1)} %collective-permute-done.13.refs_1_, ...), custom_call_target="tpu_custom_call" | custom-call | flops 1207959552 | bytes 18874368 | tf_op jit(solution)/shard_map/pallas_call | solution.py:402
  (37 shorter events, 2.5 us)
Async XLA Ops:
  0.6 45.4 %copy-start.8 = (f32[1,128]{1,0:T(1,128)S(1)}, f32[1,128]{1,0:T(1,128)}, u32[]{:S(2)}) copy-start(f32[1,128]{1,0:T(1,128)} %constant.11.refs_6_) | copy-start | bytes 1540
  0.6 68.4 %copy-start = (bf16[2,768,128]{2,1,0:T(8,128)(2,1)S(1)}, bf16[2,768,128]{2,1,0:T(8,128)(2,1)}, u32[]{:S(2)}) copy-start(bf16[2,768,128]{2,1,0:T(8,128)(2,1)} %constant.7.clone.table_ref) | copy-start | bytes 1179652
  0.7 0.9 %copy-start.2 = (bf16[1,65,768]{2,1,0:T(8,128)(2,1)S(1)}, bf16[1,65,768]{2,1,0:T(8,128)(2,1)}, u32[]{:S(2)}) copy-start(bf16[1,65,768]{2,1,0:T(8,128)(2,1)} %legendre_ref.1) | copy-start | bytes 299524
  1.6 22.2 %copy-start.6 = (s32[32]{0:T(128)S(1)}, s32[32]{0:T(128)}, u32[]{:S(2)}) copy-start(s32[32]{0:T(128)} %orders_ref.7) | copy-start | bytes 388
  1.6 44.4 %copy-start.3 = (bf16[1,65,256]{2,1,0:T(8,128)(2,1)S(1)}, bf16[1,65,256]{2,1,0:T(8,128)(2,1)}, u32[]{:S(2)}) copy-start(bf16[1,65,256]{2,1,0:T(8,128)(2,1)} %refs_4_.1) | copy-start | bytes 99844
  1.6 44.4 %copy-start.4 = (bf16[128,128]{1,0:T(8,128)(2,1)S(1)}, bf16[128,128]{1,0:T(8,128)(2,1)}, u32[]{:S(2)}) copy-start(bf16[128,128]{1,0:T(8,128)(2,1)} %refs_7_.1) | copy-start | bytes 98308
  1.6 44.4 %copy-start.5 = (bf16[128,128]{1,0:T(8,128)(2,1)S(1)}, bf16[128,128]{1,0:T(8,128)(2,1)}, u32[]{:S(2)}) copy-start(bf16[128,128]{1,0:T(8,128)(2,1)} %refs_8_.1) | copy-start | bytes 98308
  1.6 44.4 %copy-start.7 = (f32[128]{0:T(128)S(1)}, f32[128]{0:T(128)}, u32[]{:S(2)}) copy-start(f32[128]{0:T(128)} %param.14) | copy-start | bytes 1540
  2.5 21.3 %all-to-all-start = ((bf16[32,48,72]{2,1,0:T(8,128)(2,1)}), bf16[32,48,72]{2,1,0:T(8,128)(2,1)S(1)}, u32[]{:S(2)}, u32[]{:S(2)}) async-start(bf16[32,48,72]{2,1,0:T(8,128)(2,1)} %shard_map.113), calls=%async_computation | async-start | bytes 786432 | tf_op jit(solution)/shard_map/all_to_all | solution.py:439
  9.8 1.0 %copy-start.1 = (bf16[2,128,768]{2,1,0:T(8,128)(2,1)S(1)}, bf16[2,128,768]{2,1,0:T(8,128)(2,1)}, u32[]{:S(2)}) copy-start(bf16[2,128,768]{2,1,0:T(8,128)(2,1)} %constant.6.clone.table_ref) | copy-start | bytes 1179652
  24.9 2.1 %collective-permute-start = (bf16[2,2,4,72,256]{4,3,2,1,0:T(8,128)(2,1)S(1)}, bf16[2,2,4,72,256]{4,3,2,1,0:T(8,128)(2,1)S(1)}, u32[]{:S(2)}, u32[]{:S(2)}) collective-permute-start(bf16[2,2,4,72,256]{4,3,2,1,0:T(8,128)(2,1)S(1)} %shard_map.116), channel_id=1, source_target_pairs={{0,16},{1,17},{2,18},{3,19},{4,20},{5,21},{6,22},{7,23},{8,24},{9,... | collective-permute-start | bytes 1769480 | tf_op jit(solution)/shard_map/ppermute | solution.py:174
  27.1 6.0 %collective-permute-start.1 = (bf16[2,4,72,128]{3,2,1,0:T(8,128)(2,1)S(1)}, bf16[2,4,72,128]{3,2,1,0:T(8,128)(2,1)S(1)}, u32[]{:S(2)}, u32[]{:S(2)}) collective-permute-start(bf16[2,4,72,128]{3,2,1,0:T(8,128)(2,1)S(1)} %get-tuple-element.21), channel_id=1, source_target_pairs={{0,1},{1,0},{2,3},{3,2},{4,5},{5,4},{6,7},{7,6},{8,9},{9,8},{10,11... | collective-permute-start | bytes 442376 | tf_op jit(solution)/shard_map/ppermute | solution.py:174
  27.4 5.8 %collective-permute-start.2 = (bf16[2,4,72,128]{3,2,1,0:T(8,128)(2,1)S(1)}, bf16[2,4,72,128]{3,2,1,0:T(8,128)(2,1)S(1)}, u32[]{:S(2)}, u32[]{:S(2)}) collective-permute-start(bf16[2,4,72,128]{3,2,1,0:T(8,128)(2,1)S(1)} %get-tuple-element.23), channel_id=1, source_target_pairs={{0,2},{1,3},{2,0},{3,1},{4,6},{5,7},{6,4},{7,5},{8,10},{9,11},{10,... | collective-permute-start | bytes 442376 | tf_op jit(solution)/shard_map/ppermute | solution.py:174
  33.2 4.4 %collective-permute-start.3 = (bf16[4,72,128]{2,1,0:T(8,128)(2,1)S(1)}, bf16[4,72,128]{2,1,0:T(8,128)(2,1)S(1)}, u32[]{:S(2)}, u32[]{:S(2)}) collective-permute-start(bf16[4,72,128]{2,1,0:T(8,128)(2,1)S(1)} %get-tuple-element.25), channel_id=1, source_target_pairs={{0,2},{1,3},{2,0},{3,1},{4,6},{5,7},{6,4},{7,5},{8,10},{9,11},{10,... | collective-permute-start | bytes 221192 | tf_op jit(solution)/shard_map/ppermute | solution.py:174
  33.9 4.4 %collective-permute-start.4 = (bf16[4,72,128]{2,1,0:T(8,128)(2,1)S(1)}, bf16[4,72,128]{2,1,0:T(8,128)(2,1)S(1)}, u32[]{:S(2)}, u32[]{:S(2)}) collective-permute-start(bf16[4,72,128]{2,1,0:T(8,128)(2,1)S(1)} %get-tuple-element.27), channel_id=1, source_target_pairs={{0,1},{1,0},{2,3},{3,2},{4,5},{5,4},{6,7},{7,6},{8,9},{9,8},{10,11... | collective-permute-start | bytes 221192 | tf_op jit(solution)/shard_map/ppermute | solution.py:174
  38.3 4.5 %collective-permute-start.5 = (bf16[72,256]{1,0:T(8,128)(2,1)S(1)}, bf16[72,256]{1,0:T(8,128)(2,1)S(1)}, u32[]{:S(2)}, u32[]{:S(2)}) collective-permute-start(bf16[72,256]{1,0:T(8,128)(2,1)S(1)} %get-tuple-element.29), channel_id=1, source_target_pairs={{0,4},{1,5},{2,6},{3,7},{4,0},{5,1},{6,2},{7,3},{8,12},{9,13},{10,... | collective-permute-start | bytes 110600 | tf_op jit(solution)/shard_map/ppermute | solution.py:174
  38.7 4.9 %collective-permute-start.6 = (bf16[72,256]{1,0:T(8,128)(2,1)S(1)}, bf16[72,256]{1,0:T(8,128)(2,1)S(1)}, u32[]{:S(2)}, u32[]{:S(2)}) collective-permute-start(bf16[72,256]{1,0:T(8,128)(2,1)S(1)} %get-tuple-element.30), channel_id=1, source_target_pairs={{0,8},{1,9},{2,10},{3,11},{4,12},{5,13},{6,14},{7,15},{8,0},{9,1},... | collective-permute-start | bytes 110600 | tf_op jit(solution)/shard_map/ppermute | solution.py:174
  40.3 5.8 %collective-permute-start.7 = (bf16[72,256]{1,0:T(8,128)(2,1)S(1)}, bf16[72,256]{1,0:T(8,128)(2,1)S(1)}, u32[]{:S(2)}, u32[]{:S(2)}) collective-permute-start(bf16[72,256]{1,0:T(8,128)(2,1)S(1)} %get-tuple-element.31), channel_id=1, source_target_pairs={{0,12},{1,13},{2,14},{3,15},{4,8},{5,9},{6,10},{7,11},{8,4},{9,5},... | collective-permute-start | bytes 110600 | tf_op jit(solution)/shard_map/ppermute | solution.py:174
  47.5 5.8 %collective-permute-start.10 = (bf16[72,256]{1,0:T(8,128)(2,1)S(1)}, bf16[72,256]{1,0:T(8,128)(2,1)S(1)}, u32[]{:S(2)}, u32[]{:S(2)}) collective-permute-start(bf16[72,256]{1,0:T(8,128)(2,1)S(1)} %get-tuple-element.32.refs_0_), channel_id=1, source_target_pairs={{0,12},{1,13},{2,14},{3,15},{4,8},{5,9},{6,10},{7,11},{8,4},{9,5},... | collective-permute-start | bytes 110600 | tf_op jit(solution)/shard_map/ppermute | solution.py:174
  50.0 4.9 %collective-permute-start.9 = (bf16[72,256]{1,0:T(8,128)(2,1)S(1)}, bf16[72,256]{1,0:T(8,128)(2,1)S(1)}, u32[]{:S(2)}, u32[]{:S(2)}) collective-permute-start(bf16[72,256]{1,0:T(8,128)(2,1)S(1)} %get-tuple-element.32.refs_0_), channel_id=1, source_target_pairs={{0,8},{1,9},{2,10},{3,11},{4,12},{5,13},{6,14},{7,15},{8,0},{9,1},... | collective-permute-start | bytes 110600 | tf_op jit(solution)/shard_map/ppermute | solution.py:174
  50.0 4.9 %collective-permute-start.8 = (bf16[72,256]{1,0:T(8,128)(2,1)S(1)}, bf16[72,256]{1,0:T(8,128)(2,1)S(1)}, u32[]{:S(2)}, u32[]{:S(2)}) collective-permute-start(bf16[72,256]{1,0:T(8,128)(2,1)S(1)} %get-tuple-element.32.refs_0_), channel_id=1, source_target_pairs={{0,4},{1,5},{2,6},{3,7},{4,0},{5,1},{6,2},{7,3},{8,12},{9,13},{10,... | collective-permute-start | bytes 110600 | tf_op jit(solution)/shard_map/ppermute | solution.py:174
  54.9 5.2 %collective-permute-start.11 = (bf16[4,72,128]{2,1,0:T(8,128)(2,1)S(1)}, bf16[4,72,128]{2,1,0:T(8,128)(2,1)S(1)}, u32[]{:S(2)}, u32[]{:S(2)}) collective-permute-start(bf16[4,72,128]{2,1,0:T(8,128)(2,1)S(1)} %get-tuple-element.33.own_a), channel_id=1, source_target_pairs={{0,1},{1,0},{2,3},{3,2},{4,5},{5,4},{6,7},{7,6},{8,9},{9,8},{10,11... | collective-permute-start | bytes 221192 | tf_op jit(solution)/shard_map/ppermute | solution.py:174
  56.3 4.4 %collective-permute-start.12 = (bf16[4,72,128]{2,1,0:T(8,128)(2,1)S(1)}, bf16[4,72,128]{2,1,0:T(8,128)(2,1)S(1)}, u32[]{:S(2)}, u32[]{:S(2)}) collective-permute-start(bf16[4,72,128]{2,1,0:T(8,128)(2,1)S(1)} %get-tuple-element.34.own_b), channel_id=1, source_target_pairs={{0,2},{1,3},{2,0},{3,1},{4,6},{5,7},{6,4},{7,5},{8,10},{9,11},{10,... | collective-permute-start | bytes 221192 | tf_op jit(solution)/shard_map/ppermute | solution.py:174
  60.7 5.2 %collective-permute-start.13 = (bf16[2,4,72,128]{3,2,1,0:T(8,128)(2,1)S(1)}, bf16[2,4,72,128]{3,2,1,0:T(8,128)(2,1)S(1)}, u32[]{:S(2)}, u32[]{:S(2)}) collective-permute-start(bf16[2,4,72,128]{3,2,1,0:T(8,128)(2,1)S(1)} %get-tuple-element.35.refs_0_), channel_id=1, source_target_pairs={{0,2},{1,3},{2,0},{3,1},{4,6},{5,7},{6,4},{7,5},{8,10},{9,11},{10,... | collective-permute-start | bytes 442376 | tf_op jit(solution)/shard_map/ppermute | solution.py:174
  62.5 5.1 %collective-permute-start.14 = (bf16[2,4,72,128]{3,2,1,0:T(8,128)(2,1)S(1)}, bf16[2,4,72,128]{3,2,1,0:T(8,128)(2,1)S(1)}, u32[]{:S(2)}, u32[]{:S(2)}) collective-permute-start(bf16[2,4,72,128]{3,2,1,0:T(8,128)(2,1)S(1)} %get-tuple-element.36.refs_2_), channel_id=1, source_target_pairs={{0,1},{1,0},{2,3},{3,2},{4,5},{5,4},{6,7},{7,6},{8,9},{9,8},{10,11... | collective-permute-start | bytes 442376 | tf_op jit(solution)/shard_map/ppermute | solution.py:174
  62.8 4.8 %collective-permute-start.15 = (bf16[2,4,72,128]{3,2,1,0:T(8,128)(2,1)S(1)}, bf16[2,4,72,128]{3,2,1,0:T(8,128)(2,1)S(1)}, u32[]{:S(2)}, u32[]{:S(2)}) collective-permute-start(bf16[2,4,72,128]{3,2,1,0:T(8,128)(2,1)S(1)} %get-tuple-element.35.refs_0_), channel_id=1, source_target_pairs={{0,16},{1,17},{2,18},{3,19},{4,20},{5,21},{6,22},{7,23},{8,24},{9,... | collective-permute-start | bytes 442376 | tf_op jit(solution)/shard_map/ppermute | solution.py:174
  62.8 4.8 %collective-permute-start.17 = (bf16[2,4,72,128]{3,2,1,0:T(8,128)(2,1)S(1)}, bf16[2,4,72,128]{3,2,1,0:T(8,128)(2,1)S(1)}, u32[]{:S(2)}, u32[]{:S(2)}) collective-permute-start(bf16[2,4,72,128]{3,2,1,0:T(8,128)(2,1)S(1)} %get-tuple-element.36.refs_2_), channel_id=1, source_target_pairs={{0,16},{1,17},{2,18},{3,19},{4,20},{5,21},{6,22},{7,23},{8,24},{9,... | collective-permute-start | bytes 442376 | tf_op jit(solution)/shard_map/ppermute | solution.py:174
  65.9 1.8 %collective-permute-start.16 = (bf16[2,4,72,128]{3,2,1,0:T(8,128)(2,1)S(1)}, bf16[2,4,72,128]{3,2,1,0:T(8,128)(2,1)S(1)}, u32[]{:S(2)}, u32[]{:S(2)}) collective-permute-start(bf16[2,4,72,128]{3,2,1,0:T(8,128)(2,1)S(1)} %collective-permute-done.13.refs_1_), channel_id=1, source_target_pairs={{0,16},{1,17},{2,18},{3,19},{4,20},{5,21},{6,22},{7,23},{8,24},{9,... | collective-permute-start | bytes 442376 | tf_op jit(solution)/shard_map/ppermute | solution.py:174
  67.6 1.4 %collective-permute-start.18 = (bf16[2,4,72,128]{3,2,1,0:T(8,128)(2,1)S(1)}, bf16[2,4,72,128]{3,2,1,0:T(8,128)(2,1)S(1)}, u32[]{:S(2)}, u32[]{:S(2)}) collective-permute-start(bf16[2,4,72,128]{3,2,1,0:T(8,128)(2,1)S(1)} %collective-permute-done.14.refs_3_), channel_id=1, source_target_pairs={{0,16},{1,17},{2,18},{3,19},{4,20},{5,21},{6,22},{7,23},{8,24},{9,... | collective-permute-start | bytes 442376 | tf_op jit(solution)/shard_map/ppermute | solution.py:174

commit v3 on v2

--- a/solution.py
+++ b/solution.py
@@ -135,13 +135,14 @@
     return pl.BlockSpec(memory_space=pl.ANY)
 
 
-def call(kernel, operands, out_shapes, mib=16, scalars=0, cost=None):
+def call(kernel, operands, out_shapes, mib=16, scalars=0, cost=None, scratch=()):
     single = not isinstance(out_shapes, (list, tuple))
     return pl.pallas_call(
         kernel,
         in_specs=[smem()] * scalars + [vmem()] * (len(operands) - scalars),
         out_specs=vmem() if single else [vmem()] * len(out_shapes),
         out_shape=out_shapes,
+        scratch_shapes=scratch,
         compiler_params=params(mib),
         cost_estimate=cost,
     )(*operands)
@@ -153,6 +154,9 @@
         self.side_y = 2 if side_row % 2 == 0 else 1
         self.depth = side_row // self.side_y
         self.sizes = (self.sections, self.depth, self.side_y, self.side_x)
+
+    def row(self):
+        return lax.axis_index("row")
 
     def pair(self, sec, deep, y, x):
         at_sec = lax.axis_index("sec") ^ sec
@@ -174,37 +178,43 @@
         return lax.ppermute(array, names, pairs)
 
 
-def cut_kernel(legendre_ref, out_ref):
-    copies, lat_rows, rows = out_ref.shape
-    turned = jnp.pad(
+def cut_kernel(places, legendre_ref, *refs):
+    outs, turned = refs[:-1], refs[-1]
+    parts, lat_rows, rows = turned.shape
+    plane = parts // len(outs)
+    whole = jnp.pad(
         legendre_ref[0].astype(jnp.float32), ((0, rows - legendre_ref.shape[1]), (0, 0))
     ).T.astype(jnp.bfloat16)
-    parts = turned.shape[0] // lat_rows
-    for at in range(copies):
-        begin = at % parts * lat_rows
-        out_ref[at] = turned[begin : begin + lat_rows]
-
-
-def forward_kernel(table_ref, grid_ref, out_ref, buffer, held, sems):
+    for at in range(parts):
+        turned[at] = whole[at * lat_rows : (at + 1) * lat_rows]
+    for deep, out in enumerate(outs):
+        begin = (places.row() ^ (deep * places.side_y)) // places.side_y * plane
+        out[...] = turned[pl.ds(begin, plane)]
+
+
+def turn_kernel(places, *refs):
+    takes, outs = refs[: places.depth], refs[places.depth :]
+    own = places.row() % places.side_y * places.side_x + lax.axis_index("col")
+    for at, out in enumerate(outs):
+        for deep, take in enumerate(takes):
+            out[deep] = take[own ^ at]
+
+
+def stack_kernel(*refs):
+    for at, take in enumerate(refs[:-1]):
+        refs[-1][at] = take[...]
+
+
+def forward_kernel(table_ref, grid_ref, out_ref, held):
     blocks, rows, lat_block, radial = held.shape
     slots = rows // 2
-    chunks = sems.shape[0]
-
-    def chunk(at):
-        return pltpu.make_async_copy(
-            grid_ref.at[pl.ds(2 * at, 2)], buffer.at[pl.ds(2 * at, 2)], sems.at[at]
-        )
-
-    for at in range(chunks):
-        chunk(at).start()
     table = table_ref[lax.axis_index("sec")]
 
     def one_block(block, carry):
         for at in range(0, lat_block, 2):
             lat = block * lat_block + at
-            chunk(lat // 2).wait()
             two = jnp.concatenate(
-                [buffer[lat].astype(jnp.bfloat16), buffer[lat + 1].astype(jnp.bfloat16)], axis=1
+                [grid_ref[lat].astype(jnp.bfloat16), grid_ref[lat + 1].astype(jnp.bfloat16)], axis=1
             )
             sums = jnp.dot(table, two, preferred_element_type=jnp.float32)
             held[block, :, at, :] = sums[:, :radial]
@@ -227,21 +237,17 @@
     blocks = lat_rows // lat_block
     return pl.pallas_call(
         forward_kernel,
-        in_specs=[vmem(), anywhere()],
+        in_specs=[vmem(), vmem()],
         out_specs=vmem(),
         out_shape=jax.ShapeDtypeStruct((rows // 2, lat_rows, 2 * radial), jnp.bfloat16),
-        scratch_shapes=[
-            pltpu.VMEM(grid_terms.shape, jnp.float32),
-            pltpu.VMEM((blocks, rows, lat_block, radial), jnp.float32),
-            pltpu.SemaphoreType.DMA((lat_rows // 2,)),
-        ],
-        compiler_params=params(36),
+        scratch_shapes=[pltpu.VMEM((blocks, rows, lat_block, radial), jnp.float32)],
+        compiler_params=params(8),
         cost_estimate=pl.CostEstimate(
             flops=2 * rows * phi_count * lat_rows * radial,
             bytes_accessed=4 * lat_rows * phi_count * radial,
             transcendentals=0,
         ),
-    )(table, grid_terms)
+    )(table, pltpu.with_memory_space_constraint(grid_terms, pltpu.VMEM))
 
 
 def masked(weights, order, degrees):
@@ -257,7 +263,7 @@
     for deep, y, x in np.ndindex(places.depth, side_y, side_x):
         pair = places.pair(sec, int(deep), int(y), int(x))
         order = orders_ref[pair]
-        lower, upper = masked(legendre_ref[pair], order, degrees)
+        lower, upper = masked(legendre_ref[2 * y + x, deep], order, degrees)
         total = lax.dot_general(
             lower, fourier_ref[2 * order], contract, preferred_element_type=jnp.float32
         ) + lax.dot_general(
@@ -298,7 +304,7 @@
 
 def solve_kernel(places, orders_ref, *refs):
     takes = refs[: places.depth]
-    state_ref, kappa_ref, damping_ref, right_ref, left_ref, out_ref, sent_ref = refs[places.depth :]
+    state_ref, kappa_ref, damping_ref, right_ref, left_ref, sent_ref = refs[places.depth :]
     rows = state_ref.shape[1]
     radial = right_ref.shape[0]
     degrees = rows - 1
@@ -325,7 +331,6 @@
         scaled = (eigen * factor).astype(jnp.bfloat16)
         field = jnp.dot(scaled, left_ref[...], preferred_element_type=jnp.float32)
         field = field.astype(jnp.bfloat16)
-        out_ref[0, :, columns] = field
         sent_ref[pl.ds(0, rows), columns] = field
 
 
@@ -344,7 +349,7 @@
     out_b[1] = take_b[...]
 
 
-def inverse_kernel(places, degrees, orders_ref, legendre_ref, table_ref, *refs):
+def inverse_kernel(places, degrees, orders_ref, here_ref, there_ref, table_ref, *refs):
     fields, (out_ref, buffer, held, sems) = refs[:-4], refs[-4:]
     blocks, slot_rows, lat_block, radial = held.shape
     slots = slot_rows // 2
@@ -356,7 +361,7 @@
             deep, y, x = int(deep), int(y), int(x)
             pair = places.pair(sec, deep, y, x)
             order = orders_ref[pair]
-            weights = masked(legendre_ref[pair], order, degrees)
+            weights = masked((there_ref if sec else here_ref)[2 * y + x, deep], order, degrees)
             both = ((far_a if y else own_a)[x, deep], (far_b if x else own_b)[y, deep])
             field = jnp.concatenate(both, axis=1)
             for half in range(2):
@@ -401,7 +406,7 @@
     out = jax.ShapeDtypeStruct((lat_rows, phi_count, radial), jnp.float32)
     return pl.pallas_call(
         functools.partial(inverse_kernel, places, degrees),
-        in_specs=[smem()] + [vmem()] * (2 + len(fields)),
+        in_specs=[smem()] + [vmem()] * (1 + len(legendre) + len(fields)),
         out_specs=anywhere(),
         out_shape=out,
         scratch_shapes=[
@@ -415,7 +420,7 @@
             bytes_accessed=4 * lat_rows * phi_count * radial,
             transcendentals=0,
         ),
-    )(pair_orders, legendre, table, *fields)
+    )(pair_orders, *legendre, table, *fields)
 
 
 def on_device_compact(grid_terms, pair_orders, legendre, state, kappa, right_op, left_op):
@@ -435,15 +440,28 @@
     def shape(*sizes, dtype=jnp.bfloat16):
         return jax.ShapeDtypeStruct(sizes, dtype)
 
-    cut = call(cut_kernel, [legendre], shape(pair_total, lat_rows, padded))
-    legendre_here = lax.all_to_all(cut, names, split_axis=0, concat_axis=0, tiled=True)
+    part = shape(places.side_y * places.side_x, lat_rows, padded)
+    cuts = call(
+        functools.partial(cut_kernel, places),
+        [legendre],
+        [part] * depth,
+        scratch=[pltpu.VMEM((depth * part.shape[0], lat_rows, padded), jnp.bfloat16)],
+        cost=pl.CostEstimate(flops=int(1.3e10), bytes_accessed=0, transcendentals=0),
+    )
+    cuts = [cuts[0]] + [places.move(cuts[deep], deep=deep) for deep in range(1, depth)]
+    part = shape(depth, lat_rows, padded)
+    cuts = call(functools.partial(turn_kernel, places), cuts, [part] * 4)
+    cuts = [cuts[0]] + [places.move(cuts[at], y=at // 2, x=at % 2) for at in range(1, 4)]
+    legendre_here = call(stack_kernel, cuts, shape(4, depth, lat_rows, padded))
+    legendre_there = places.move(legendre_here, sec=1)
+    legendres = (legendre_here, legendre_there)
 
     fourier = forward_sums(forward_table, grid_terms, lat_block)
 
     def partial_sums(sec, dtype):
         return call(
             functools.partial(degrees_kernel, places, sec, degrees),
-            [pair_orders, legendre_here, fourier],
+            [pair_orders, legendres[sec], fourier],
             shape(2, 2, depth, padded, columns, dtype=dtype),
             mib=24,
             scalars=1,
@@ -475,12 +493,13 @@
 
     radial_mode = np.arange(radial, dtype=np.float32) / np.float32(radial)
     damping = np.exp(-filter_strength * radial_mode**filter_power).astype(np.float32)
-    new_state, field = call(
+    field = call(
         functools.partial(solve_kernel, places),
         [pair_orders, *parts, state, kappa[None, :], jnp.asarray(damping)[None, :], right_op, left_op],
-        [shape(1, rows, columns), shape(padded, columns)],
+        shape(padded, columns),
         scalars=1,
     )
+    new_state = field[None, :rows]
 
     fields = [field] + [places.move(field, deep=deep) for deep in range(1, depth)]
     own_a, own_b = call(spread_kernel, fields, [half, half])
@@ -493,7 +512,7 @@
     there += [places.move(part, sec=1) for part in (far_a, far_b)]
     gathered = here + [there[0], there[2], there[1], there[3]]
     evolved = inverse_values(
-        places, degrees, pair_orders, legendre_here, inverse_table, gathered, lat_rows, lat_block
+        places, degrees, pair_orders, legendres, inverse_table, gathered, lat_rows, lat_block
     )
     return (evolved, new_state)
 

time: 78.2 us -> 79.3 us (1.014)
  Pallas kernels: 22.4 us -> 15.9 us
  waiting for transfers between devices: 27.7 us -> 33 us
  starting transfers between devices: 25.1 us -> 27.6 us
    ppermute x19 -> x26, starting transfers between devices: 17.8 us -> 27.6 us  [move(): return lax.ppermute(array, names, pairs)]
    ppermute x19 -> x26, waiting for transfers between devices: 23.4 us -> 33 us  [move(): return lax.ppermute(array, names, pairs)]
    all_to_all x1 -> x0, starting transfers between devices: 7.3 us -> none  [on_device_compact(): lax.all_to_all(cut, names, split_axis=0, concat_axis=0, tiled=True)]
    pallas_call x1, Pallas kernels: 8.71 us -> 3.46 us  [forward_sums(): pl.pallas_call(forward_kernel, in_specs=[vmem(), vmem()], out_specs=vmem(...]
    all_to_all x1 -> x0, waiting for transfers between devices: 4.3 us -> none  [on_device_compact(): lax.all_to_all(cut, names, split_axis=0, concat_axis=0, tiled=True)]
    pallas_call x9 -> x11, Pallas kernels: 4.78 us -> 3.52 us  [call(): pl.pallas_call(kernel, in_specs=[smem()] * scalars + [vmem()] * (len(oper...]
    unnamed x18 -> x20, local copies, waits for them, and re-layouts: 1.96 us -> 1.1 us
  transfers between devices with their start and end apart: 20 -> 26, of which waited for: 15 -> 19; matrix products, arithmetic and copies ran while one was open for 0% -> 1% of each run, Pallas kernels for 13% -> 6%
where the time goes in v3:
time: 79.3 us; the launch traced here: 79.2 us
  waiting for transfers between devices  33 us (42%)
  starting transfers between devices  27.6 us (35%)
  Pallas kernels  15.9 us (20%)
  local copies, waits for them, and re-layouts  1.72 us (2%)
  between operations  0.87 us (1%)
    ppermute x26, waiting for transfers between devices, move(): return lax.ppermute(array, names, pairs)  33 us
    ppermute x26, starting transfers between devices, move(): return lax.ppermute(array, names, pairs)  27.6 us
    pallas_call x1, Pallas kernels, inverse_values(): pl.pallas_call(functools.partial(inverse_kernel, places, degrees), in_spe...  8.97 us
    pallas_call x11, Pallas kernels, call(): pl.pallas_call(kernel, in_specs=[smem()] * scalars + [vmem()] * (len(oper...  3.52 us
    pallas_call x1, Pallas kernels, forward_sums(): pl.pallas_call(forward_kernel, in_specs=[vmem(), vmem()], out_specs=vmem(...  3.46 us
  transfers between devices with their start and end apart: 26, of which 19 were waited for; matrix products, arithmetic and copies ran while one was open for 1% of the time, Pallas kernels for 6%

profile of v3, /device:TPU:0, one launch (start us, length us, event | category | flops | bytes accessed | tf_op | source)
XLA Modules:
  0.0 79.2 jit_solution(15340352939075510059)
XLA Ops:
  0.7 1.0 %copy-done.9 = bf16[1,65,768]{2,1,0:T(8,128)(2,1)S(1)} copy-done((bf16[1,65,768]{2,1,0:T(8,128)(2,1)S(1)}, bf16[1,65,768]{2,1,0:T(8,128)(2,1)}, u32[]{:S(2)}) %copy-start.9) | copy-done | bytes 99864
  2.0 3.1 %collective-permute-start = (bf16[4,48,72]{2,1,0:T(8,128)(2,1)S(1)}, bf16[4,48,72]{2,1,0:T(8,128)(2,1)S(1)}, u32[]{:S(2)}, u32[]{:S(2)}) collective-permute-start(bf16[4,48,72]{2,1,0:T(8,128)(2,1)S(1)} %get-tuple-element.27), channel_id=1, source_target_pairs={{0,4},{1,5},{2,6},{3,7},{4,0},{5,1},{6,2},{7,3},{8,12},{9,13},{10,... | collective-permute-start | bytes 82952 | tf_op jit(solution)/shard_map/ppermute | solution.py:178
  5.1 2.6 %collective-permute-start.1 = (bf16[4,48,72]{2,1,0:T(8,128)(2,1)S(1)}, bf16[4,48,72]{2,1,0:T(8,128)(2,1)S(1)}, u32[]{:S(2)}, u32[]{:S(2)}) collective-permute-start(bf16[4,48,72]{2,1,0:T(8,128)(2,1)S(1)} %get-tuple-element.28), channel_id=1, source_target_pairs={{0,8},{1,9},{2,10},{3,11},{4,12},{5,13},{6,14},{7,15},{8,0},{9,1},... | collective-permute-start | bytes 82952 | tf_op jit(solution)/shard_map/ppermute | solution.py:178
  7.7 3.3 %collective-permute-done.1.refs_2_ = bf16[4,48,72]{2,1,0:T(8,128)(2,1)S(1)} collective-permute-done((bf16[4,48,72]{2,1,0:T(8,128)(2,1)S(1)}, bf16[4,48,72]{2,1,0:T(8,128)(2,1)S(1)}, u32[]{:S(2)}, u32[]{:S(2)}) %collective-permute-start.1) | collective-permute-done | bytes 27680 | tf_op jit(solution)/shard_map/ppermute | solution.py:178
  11.0 2.6 %collective-permute-done.2.refs_3_ = bf16[4,48,72]{2,1,0:T(8,128)(2,1)S(1)} collective-permute-done((bf16[4,48,72]{2,1,0:T(8,128)(2,1)S(1)}, bf16[4,48,72]{2,1,0:T(8,128)(2,1)S(1)}, u32[]{:S(2)}, u32[]{:S(2)}) %collective-permute-start.2) | collective-permute-done | bytes 27680 | tf_op jit(solution)/shard_map/ppermute | solution.py:178
  13.6 1.6 %collective-permute-start.3 = (bf16[4,48,72]{2,1,0:T(8,128)(2,1)S(1)}, bf16[4,48,72]{2,1,0:T(8,128)(2,1)S(1)}, u32[]{:S(2)}, u32[]{:S(2)}) collective-permute-start(bf16[4,48,72]{2,1,0:T(8,128)(2,1)S(1)} %get-tuple-element.31), channel_id=1, source_target_pairs={{0,1},{1,0},{2,3},{3,2},{4,5},{5,4},{6,7},{7,6},{8,9},{9,8},{10,11... | collective-permute-start | bytes 82952 | tf_op jit(solution)/shard_map/ppermute | solution.py:178
  15.1 1.5 %collective-permute-start.4 = (bf16[4,48,72]{2,1,0:T(8,128)(2,1)S(1)}, bf16[4,48,72]{2,1,0:T(8,128)(2,1)S(1)}, u32[]{:S(2)}, u32[]{:S(2)}) collective-permute-start(bf16[4,48,72]{2,1,0:T(8,128)(2,1)S(1)} %get-tuple-element.32), channel_id=1, source_target_pairs={{0,2},{1,3},{2,0},{3,1},{4,6},{5,7},{6,4},{7,5},{8,10},{9,11},{10,... | collective-permute-start | bytes 82952 | tf_op jit(solution)/shard_map/ppermute | solution.py:178
  17.1 0.8 collective-permute-done.3.refs_1_
  17.9 1.3 %collective-permute-done.4.refs_2_ = bf16[4,48,72]{2,1,0:T(8,128)(2,1)S(1)} collective-permute-done((bf16[4,48,72]{2,1,0:T(8,128)(2,1)S(1)}, bf16[4,48,72]{2,1,0:T(8,128)(2,1)S(1)}, u32[]{:S(2)}, u32[]{:S(2)}) %collective-permute-start.4) | collective-permute-done | bytes 27680 | tf_op jit(solution)/shard_map/ppermute | solution.py:178
  19.2 2.4 %collective-permute-done.5.refs_3_ = bf16[4,48,72]{2,1,0:T(8,128)(2,1)S(1)} collective-permute-done((bf16[4,48,72]{2,1,0:T(8,128)(2,1)S(1)}, bf16[4,48,72]{2,1,0:T(8,128)(2,1)S(1)}, u32[]{:S(2)}, u32[]{:S(2)}) %collective-permute-start.5) | collective-permute-done | bytes 27680 | tf_op jit(solution)/shard_map/ppermute | solution.py:178
  21.8 3.5 %shard_map.116.fourier_ref = bf16[64,48,256]{2,1,0:T(8,128)(2,1)S(1)} custom-call(bf16[2,128,768]{2,1,0:T(8,128)(2,1)S(1)} %copy-done.2, f32[48,768,128]{2,1,0:T(8,128)S(1)} %copy-done), custom_call_target="tpu_custom_call" | custom-call | flops 1207959552 | bytes 18874368 | tf_op jit(solution)/shard_map/pallas_call | solution.py:238
  25.3 1.1 %shard_map.118 = bf16[2,2,4,72,256]{4,3,2,1,0:T(8,128)(2,1)S(1)} custom-call(s32[32]{0:T(128)S(1)} %copy-done.6, bf16[4,4,48,72]{3,2,1,0:T(8,128)(2,1)S(1)} %collective-permute-done.6.legendre_ref.there_ref, bf16[64,48,256]{2,1,0:T(8,128)(2,1)S(1)} %shard_map.116.fourier_ref), custom_call_target="tpu_custom_call" | custom-call | flops 51118080 | bytes 1572864 | tf_op jit(solution)/shard_map/pallas_call | solution.py:140
  26.9 1.1 %shard_map.117.kept_ref = f32[2,2,4,72,256]{4,3,2,1,0:T(8,128)S(1)} custom-call(s32[32]{0:T(128)S(1)} %copy-done.6, bf16[4,4,48,72]{3,2,1,0:T(8,128)(2,1)S(1)} %shard_map.115.legendre_ref.here_ref, bf16[64,48,256]{2,1,0:T(8,128)(2,1)S(1)} %shard_map.116.fourier_ref), custom_call_target="tpu_custom_call" | custom-call | flops 51118080 | bytes 1572864 | tf_op jit(solution)/shard_map/pallas_call | solution.py:140
  29.8 5.1 %collective-permute-done.8.take_a = bf16[2,4,72,128]{3,2,1,0:T(8,128)(2,1)S(1)} collective-permute-done((bf16[2,4,72,128]{3,2,1,0:T(8,128)(2,1)S(1)}, bf16[2,4,72,128]{3,2,1,0:T(8,128)(2,1)S(1)}, u32[]{:S(2)}, u32[]{:S(2)}) %collective-permute-start.8) | collective-permute-done | bytes 147488 | tf_op jit(solution)/shard_map/ppermute | solution.py:178
  35.7 1.5 %collective-permute-start.11 = (bf16[4,72,128]{2,1,0:T(8,128)(2,1)S(1)}, bf16[4,72,128]{2,1,0:T(8,128)(2,1)S(1)}, u32[]{:S(2)}, u32[]{:S(2)}) collective-permute-start(bf16[4,72,128]{2,1,0:T(8,128)(2,1)S(1)} %get-tuple-element.41), channel_id=1, source_target_pairs={{0,1},{1,0},{2,3},{3,2},{4,5},{5,4},{6,7},{7,6},{8,9},{9,8},{10,11... | collective-permute-start | bytes 221192 | tf_op jit(solution)/shard_map/ppermute | solution.py:178
  37.2 2.4 %collective-permute-done.10.take_a = bf16[4,72,128]{2,1,0:T(8,128)(2,1)S(1)} collective-permute-done((bf16[4,72,128]{2,1,0:T(8,128)(2,1)S(1)}, bf16[4,72,128]{2,1,0:T(8,128)(2,1)S(1)}, u32[]{:S(2)}, u32[]{:S(2)}) %collective-permute-start.10) | collective-permute-done | bytes 73760 | tf_op jit(solution)/shard_map/ppermute | solution.py:178
  40.2 1.3 %collective-permute-start.13 = (bf16[72,256]{1,0:T(8,128)(2,1)S(1)}, bf16[72,256]{1,0:T(8,128)(2,1)S(1)}, u32[]{:S(2)}, u32[]{:S(2)}) collective-permute-start(bf16[72,256]{1,0:T(8,128)(2,1)S(1)} %get-tuple-element.44), channel_id=1, source_target_pairs={{0,8},{1,9},{2,10},{3,11},{4,12},{5,13},{6,14},{7,15},{8,0},{9,1},... | collective-permute-start | bytes 110600 | tf_op jit(solution)/shard_map/ppermute | solution.py:178
  41.5 3.1 %collective-permute-start.14 = (bf16[72,256]{1,0:T(8,128)(2,1)S(1)}, bf16[72,256]{1,0:T(8,128)(2,1)S(1)}, u32[]{:S(2)}, u32[]{:S(2)}) collective-permute-start(bf16[72,256]{1,0:T(8,128)(2,1)S(1)} %get-tuple-element.45), channel_id=1, source_target_pairs={{0,12},{1,13},{2,14},{3,15},{4,8},{5,9},{6,10},{7,11},{8,4},{9,5},... | collective-permute-start | bytes 110600 | tf_op jit(solution)/shard_map/ppermute | solution.py:178
  45.1 2.2 %collective-permute-done.14.refs_3_ = bf16[72,256]{1,0:T(8,128)(2,1)S(1)} collective-permute-done((bf16[72,256]{1,0:T(8,128)(2,1)S(1)}, bf16[72,256]{1,0:T(8,128)(2,1)S(1)}, u32[]{:S(2)}, u32[]{:S(2)}) %collective-permute-start.14) | collective-permute-done | bytes 36896 | tf_op jit(solution)/shard_map/ppermute | solution.py:178
  47.3 0.8 %shard_map.122.refs_0_ = bf16[72,256]{1,0:T(8,128)(2,1)S(1)} custom-call(s32[32]{0:T(128)S(1)} %copy-done.6, f32[72,256]{1,0:T(8,128)S(1)} %get-tuple-element.42.refs_0_, bf16[72,256]{1,0:T(8,128)(2,1)S(1)} %collective-permute-done.12.refs_1_, bf16[72,256]{1,0:T(8,128)(2,1)S(1)} %collective-permute-done.13.refs_2_, ...), custom_call_target="tpu_custom_call" | custom-call | tf_op jit(solution)/shard_map/pallas_call | solution.py:140
  48.2 3.1 %collective-permute-start.17 = (bf16[72,256]{1,0:T(8,128)(2,1)S(1)}, bf16[72,256]{1,0:T(8,128)(2,1)S(1)}, u32[]{:S(2)}, u32[]{:S(2)}) collective-permute-start(bf16[72,256]{1,0:T(8,128)(2,1)S(1)} %shard_map.122.refs_0_), channel_id=1, source_target_pairs={{0,12},{1,13},{2,14},{3,15},{4,8},{5,9},{6,10},{7,11},{8,4},{9,5},... | collective-permute-start | bytes 110600 | tf_op jit(solution)/shard_map/ppermute | solution.py:178
  51.3 1.3 %collective-permute-start.15 = (bf16[72,256]{1,0:T(8,128)(2,1)S(1)}, bf16[72,256]{1,0:T(8,128)(2,1)S(1)}, u32[]{:S(2)}, u32[]{:S(2)}) collective-permute-start(bf16[72,256]{1,0:T(8,128)(2,1)S(1)} %shard_map.122.refs_0_), channel_id=1, source_target_pairs={{0,4},{1,5},{2,6},{3,7},{4,0},{5,1},{6,2},{7,3},{8,12},{9,13},{10,... | collective-permute-start | bytes 110600 | tf_op jit(solution)/shard_map/ppermute | solution.py:178
  52.6 1.4 %collective-permute-done.17.refs_3_ = bf16[72,256]{1,0:T(8,128)(2,1)S(1)} collective-permute-done((bf16[72,256]{1,0:T(8,128)(2,1)S(1)}, bf16[72,256]{1,0:T(8,128)(2,1)S(1)}, u32[]{:S(2)}, u32[]{:S(2)}) %collective-permute-start.17) | collective-permute-done | bytes 36896 | tf_op jit(solution)/shard_map/ppermute | solution.py:178
  54.0 2.2 %collective-permute-done.16.refs_2_ = bf16[72,256]{1,0:T(8,128)(2,1)S(1)} collective-permute-done((bf16[72,256]{1,0:T(8,128)(2,1)S(1)}, bf16[72,256]{1,0:T(8,128)(2,1)S(1)}, u32[]{:S(2)}, u32[]{:S(2)}) %collective-permute-start.16) | collective-permute-done | bytes 36896 | tf_op jit(solution)/shard_map/ppermute | solution.py:178
  56.2 1.6 %collective-permute-start.18 = (bf16[4,72,128]{2,1,0:T(8,128)(2,1)S(1)}, bf16[4,72,128]{2,1,0:T(8,128)(2,1)S(1)}, u32[]{:S(2)}, u32[]{:S(2)}) collective-permute-start(bf16[4,72,128]{2,1,0:T(8,128)(2,1)S(1)} %get-tuple-element.46.own_a), channel_id=1, source_target_pairs={{0,1},{1,0},{2,3},{3,2},{4,5},{5,4},{6,7},{7,6},{8,9},{9,8},{10,11... | collective-permute-start | bytes 221192 | tf_op jit(solution)/shard_map/ppermute | solution.py:178
  57.7 1.5 %collective-permute-start.19 = (bf16[4,72,128]{2,1,0:T(8,128)(2,1)S(1)}, bf16[4,72,128]{2,1,0:T(8,128)(2,1)S(1)}, u32[]{:S(2)}, u32[]{:S(2)}) collective-permute-start(bf16[4,72,128]{2,1,0:T(8,128)(2,1)S(1)} %get-tuple-element.47.own_b), channel_id=1, source_target_pairs={{0,2},{1,3},{2,0},{3,1},{4,6},{5,7},{6,4},{7,5},{8,10},{9,11},{10,... | collective-permute-start | bytes 221192 | tf_op jit(solution)/shard_map/ppermute | solution.py:178
  59.2 1.9 %collective-permute-done.18.take_a = bf16[4,72,128]{2,1,0:T(8,128)(2,1)S(1)} collective-permute-done((bf16[4,72,128]{2,1,0:T(8,128)(2,1)S(1)}, bf16[4,72,128]{2,1,0:T(8,128)(2,1)S(1)}, u32[]{:S(2)}, u32[]{:S(2)}) %collective-permute-start.18) | collective-permute-done | bytes 73760 | tf_op jit(solution)/shard_map/ppermute | solution.py:178
  61.1 1.0 %collective-permute-done.19.take_b = bf16[4,72,128]{2,1,0:T(8,128)(2,1)S(1)} collective-permute-done((bf16[4,72,128]{2,1,0:T(8,128)(2,1)S(1)}, bf16[4,72,128]{2,1,0:T(8,128)(2,1)S(1)}, u32[]{:S(2)}, u32[]{:S(2)}) %collective-permute-start.19) | collective-permute-done | bytes 73760 | tf_op jit(solution)/shard_map/ppermute | solution.py:178
  62.1 1.6 %collective-permute-start.20 = (bf16[2,4,72,128]{3,2,1,0:T(8,128)(2,1)S(1)}, bf16[2,4,72,128]{3,2,1,0:T(8,128)(2,1)S(1)}, u32[]{:S(2)}, u32[]{:S(2)}) collective-permute-start(bf16[2,4,72,128]{3,2,1,0:T(8,128)(2,1)S(1)} %get-tuple-element.48.refs_0_), channel_id=1, source_target_pairs={{0,2},{1,3},{2,0},{3,1},{4,6},{5,7},{6,4},{7,5},{8,10},{9,11},{10,... | collective-permute-start | bytes 442376 | tf_op jit(solution)/shard_map/ppermute | solution.py:178
  64.7 2.6 %collective-permute-done.20.refs_1_ = bf16[2,4,72,128]{3,2,1,0:T(8,128)(2,1)S(1)} collective-permute-done((bf16[2,4,72,128]{3,2,1,0:T(8,128)(2,1)S(1)}, bf16[2,4,72,128]{3,2,1,0:T(8,128)(2,1)S(1)}, u32[]{:S(2)}, u32[]{:S(2)}) %collective-permute-start.20) | collective-permute-done | bytes 147488 | tf_op jit(solution)/shard_map/ppermute | solution.py:178
  67.3 1.5 %collective-permute-done.21.refs_3_ = bf16[2,4,72,128]{3,2,1,0:T(8,128)(2,1)S(1)} collective-permute-done((bf16[2,4,72,128]{3,2,1,0:T(8,128)(2,1)S(1)}, bf16[2,4,72,128]{3,2,1,0:T(8,128)(2,1)S(1)}, u32[]{:S(2)}, u32[]{:S(2)}) %collective-permute-start.21) | collective-permute-done | bytes 147488 | tf_op jit(solution)/shard_map/ppermute | solution.py:178
  70.2 9.0 %shard_map.125 = f32[48,768,128]{2,1,0:T(8,128)} custom-call(s32[32]{0:T(128)S(1)} %copy-done.6, bf16[4,4,48,72]{3,2,1,0:T(8,128)(2,1)S(1)} %shard_map.115.legendre_ref.here_ref, bf16[4,4,48,72]{3,2,1,0:T(8,128)(2,1)S(1)} %collective-permute-done.6.legendre_ref.there_ref, bf16[2,768,128]{2,1,0:T(8,128)(2,1)S(1)} %copy-done.1, ...), custom_call_target="tpu_custom_call" | custom-call | flops 1207959552 | bytes 18874368 | tf_op jit(solution)/shard_map/pallas_call | solution.py:407
  (54 shorter events, 7.7 us)
Async XLA Ops:
  1.9 45.4 %copy-start.3 = (bf16[1,65,256]{2,1,0:T(8,128)(2,1)S(1)}, bf16[1,65,256]{2,1,0:T(8,128)(2,1)}, u32[]{:S(2)}) copy-start(bf16[1,65,256]{2,1,0:T(8,128)(2,1)} %refs_4_.1) | copy-start | bytes 99844
  1.9 45.4 %copy-start.4 = (bf16[128,128]{1,0:T(8,128)(2,1)S(1)}, bf16[128,128]{1,0:T(8,128)(2,1)}, u32[]{:S(2)}) copy-start(bf16[128,128]{1,0:T(8,128)(2,1)} %refs_7_.1) | copy-start | bytes 98308
  1.9 45.4 %copy-start.5 = (bf16[128,128]{1,0:T(8,128)(2,1)S(1)}, bf16[128,128]{1,0:T(8,128)(2,1)}, u32[]{:S(2)}) copy-start(bf16[128,128]{1,0:T(8,128)(2,1)} %refs_8_.1) | copy-start | bytes 98308
  1.9 45.4 %copy-start.7 = (f32[128]{0:T(128)S(1)}, f32[128]{0:T(128)}, u32[]{:S(2)}) copy-start(f32[128]{0:T(128)} %param.14) | copy-start | bytes 1540
  1.9 45.4 %copy-start.8 = (f32[1,128]{1,0:T(1,128)S(1)}, f32[1,128]{1,0:T(1,128)}, u32[]{:S(2)}) copy-start(f32[1,128]{1,0:T(1,128)} %constant.11.refs_6_) | copy-start | bytes 1540
  1.9 68.3 %copy-start.1 = (bf16[2,768,128]{2,1,0:T(8,128)(2,1)S(1)}, bf16[2,768,128]{2,1,0:T(8,128)(2,1)}, u32[]{:S(2)}) copy-start(bf16[2,768,128]{2,1,0:T(8,128)(2,1)} %constant.7.clone.table_ref) | copy-start | bytes 1179652
  2.0 5.7 %collective-permute-start = (bf16[4,48,72]{2,1,0:T(8,128)(2,1)S(1)}, bf16[4,48,72]{2,1,0:T(8,128)(2,1)S(1)}, u32[]{:S(2)}, u32[]{:S(2)}) collective-permute-start(bf16[4,48,72]{2,1,0:T(8,128)(2,1)S(1)} %get-tuple-element.27), channel_id=1, source_target_pairs={{0,4},{1,5},{2,6},{3,7},{4,0},{5,1},{6,2},{7,3},{8,12},{9,13},{10,... | collective-permute-start | bytes 82952 | tf_op jit(solution)/shard_map/ppermute | solution.py:178
  5.1 5.9 %collective-permute-start.1 = (bf16[4,48,72]{2,1,0:T(8,128)(2,1)S(1)}, bf16[4,48,72]{2,1,0:T(8,128)(2,1)S(1)}, u32[]{:S(2)}, u32[]{:S(2)}) collective-permute-start(bf16[4,48,72]{2,1,0:T(8,128)(2,1)S(1)} %get-tuple-element.28), channel_id=1, source_target_pairs={{0,8},{1,9},{2,10},{3,11},{4,12},{5,13},{6,14},{7,15},{8,0},{9,1},... | collective-permute-start | bytes 82952 | tf_op jit(solution)/shard_map/ppermute | solution.py:178
  7.6 5.9 %collective-permute-start.2 = (bf16[4,48,72]{2,1,0:T(8,128)(2,1)S(1)}, bf16[4,48,72]{2,1,0:T(8,128)(2,1)S(1)}, u32[]{:S(2)}, u32[]{:S(2)}) collective-permute-start(bf16[4,48,72]{2,1,0:T(8,128)(2,1)S(1)} %get-tuple-element.29), channel_id=1, source_target_pairs={{0,12},{1,13},{2,14},{3,15},{4,8},{5,9},{6,10},{7,11},{8,4},{9,5},... | collective-permute-start | bytes 82952 | tf_op jit(solution)/shard_map/ppermute | solution.py:178
  13.6 4.3 %collective-permute-start.3 = (bf16[4,48,72]{2,1,0:T(8,128)(2,1)S(1)}, bf16[4,48,72]{2,1,0:T(8,128)(2,1)S(1)}, u32[]{:S(2)}, u32[]{:S(2)}) collective-permute-start(bf16[4,48,72]{2,1,0:T(8,128)(2,1)S(1)} %get-tuple-element.31), channel_id=1, source_target_pairs={{0,1},{1,0},{2,3},{3,2},{4,5},{5,4},{6,7},{7,6},{8,9},{9,8},{10,11... | collective-permute-start | bytes 82952 | tf_op jit(solution)/shard_map/ppermute | solution.py:178
  15.1 4.1 %collective-permute-start.4 = (bf16[4,48,72]{2,1,0:T(8,128)(2,1)S(1)}, bf16[4,48,72]{2,1,0:T(8,128)(2,1)S(1)}, u32[]{:S(2)}, u32[]{:S(2)}) collective-permute-start(bf16[4,48,72]{2,1,0:T(8,128)(2,1)S(1)} %get-tuple-element.32), channel_id=1, source_target_pairs={{0,2},{1,3},{2,0},{3,1},{4,6},{5,7},{6,4},{7,5},{8,10},{9,11},{10,... | collective-permute-start | bytes 82952 | tf_op jit(solution)/shard_map/ppermute | solution.py:178
  16.6 5.0 %collective-permute-start.5 = (bf16[4,48,72]{2,1,0:T(8,128)(2,1)S(1)}, bf16[4,48,72]{2,1,0:T(8,128)(2,1)S(1)}, u32[]{:S(2)}, u32[]{:S(2)}) collective-permute-start(bf16[4,48,72]{2,1,0:T(8,128)(2,1)S(1)} %get-tuple-element.33), channel_id=1, source_target_pairs={{0,3},{1,2},{2,1},{3,0},{4,7},{5,6},{6,5},{7,4},{8,11},{9,10},{10,... | collective-permute-start | bytes 82952 | tf_op jit(solution)/shard_map/ppermute | solution.py:178
  21.7 3.6 %collective-permute-start.6 = (bf16[4,4,48,72]{3,2,1,0:T(8,128)(2,1)S(1)}, bf16[4,4,48,72]{3,2,1,0:T(8,128)(2,1)S(1)}, u32[]{:S(2)}, u32[]{:S(2)}) collective-permute-start(bf16[4,4,48,72]{3,2,1,0:T(8,128)(2,1)S(1)} %shard_map.115.legendre_ref.here_ref), channel_id=1, source_target_pairs={{0,16},{1,17},{2,18},{3,19},{4,20},{5,21},{6,22},{7,23},{8,24},{9,... | collective-permute-start | bytes 331784 | tf_op jit(solution)/shard_map/ppermute | solution.py:178
  26.4 2.2 %collective-permute-start.7 = (bf16[2,2,4,72,256]{4,3,2,1,0:T(8,128)(2,1)S(1)}, bf16[2,2,4,72,256]{4,3,2,1,0:T(8,128)(2,1)S(1)}, u32[]{:S(2)}, u32[]{:S(2)}) collective-permute-start(bf16[2,2,4,72,256]{4,3,2,1,0:T(8,128)(2,1)S(1)} %shard_map.118), channel_id=1, source_target_pairs={{0,16},{1,17},{2,18},{3,19},{4,20},{5,21},{6,22},{7,23},{8,24},{9,... | collective-permute-start | bytes 1769480 | tf_op jit(solution)/shard_map/ppermute | solution.py:178
  28.7 6.2 %collective-permute-start.8 = (bf16[2,4,72,128]{3,2,1,0:T(8,128)(2,1)S(1)}, bf16[2,4,72,128]{3,2,1,0:T(8,128)(2,1)S(1)}, u32[]{:S(2)}, u32[]{:S(2)}) collective-permute-start(bf16[2,4,72,128]{3,2,1,0:T(8,128)(2,1)S(1)} %get-tuple-element.35), channel_id=1, source_target_pairs={{0,1},{1,0},{2,3},{3,2},{4,5},{5,4},{6,7},{7,6},{8,9},{9,8},{10,11... | collective-permute-start | bytes 442376 | tf_op jit(solution)/shard_map/ppermute | solution.py:178
  29.3 5.8 %collective-permute-start.9 = (bf16[2,4,72,128]{3,2,1,0:T(8,128)(2,1)S(1)}, bf16[2,4,72,128]{3,2,1,0:T(8,128)(2,1)S(1)}, u32[]{:S(2)}, u32[]{:S(2)}) collective-permute-start(bf16[2,4,72,128]{3,2,1,0:T(8,128)(2,1)S(1)} %get-tuple-element.37), channel_id=1, source_target_pairs={{0,2},{1,3},{2,0},{3,1},{4,6},{5,7},{6,4},{7,5},{8,10},{9,11},{10,... | collective-permute-start | bytes 442376 | tf_op jit(solution)/shard_map/ppermute | solution.py:178
  35.2 4.4 %collective-permute-start.10 = (bf16[4,72,128]{2,1,0:T(8,128)(2,1)S(1)}, bf16[4,72,128]{2,1,0:T(8,128)(2,1)S(1)}, u32[]{:S(2)}, u32[]{:S(2)}) collective-permute-start(bf16[4,72,128]{2,1,0:T(8,128)(2,1)S(1)} %get-tuple-element.39), channel_id=1, source_target_pairs={{0,2},{1,3},{2,0},{3,1},{4,6},{5,7},{6,4},{7,5},{8,10},{9,11},{10,... | collective-permute-start | bytes 221192 | tf_op jit(solution)/shard_map/ppermute | solution.py:178
  35.7 4.4 %collective-permute-start.11 = (bf16[4,72,128]{2,1,0:T(8,128)(2,1)S(1)}, bf16[4,72,128]{2,1,0:T(8,128)(2,1)S(1)}, u32[]{:S(2)}, u32[]{:S(2)}) collective-permute-start(bf16[4,72,128]{2,1,0:T(8,128)(2,1)S(1)} %get-tuple-element.41), channel_id=1, source_target_pairs={{0,1},{1,0},{2,3},{3,2},{4,5},{5,4},{6,7},{7,6},{8,9},{9,8},{10,11... | collective-permute-start | bytes 221192 | tf_op jit(solution)/shard_map/ppermute | solution.py:178
  40.1 4.5 %collective-permute-start.12 = (bf16[72,256]{1,0:T(8,128)(2,1)S(1)}, bf16[72,256]{1,0:T(8,128)(2,1)S(1)}, u32[]{:S(2)}, u32[]{:S(2)}) collective-permute-start(bf16[72,256]{1,0:T(8,128)(2,1)S(1)} %get-tuple-element.43), channel_id=1, source_target_pairs={{0,4},{1,5},{2,6},{3,7},{4,0},{5,1},{6,2},{7,3},{8,12},{9,13},{10,... | collective-permute-start | bytes 110600 | tf_op jit(solution)/shard_map/ppermute | solution.py:178
  40.2 4.9 %collective-permute-start.13 = (bf16[72,256]{1,0:T(8,128)(2,1)S(1)}, bf16[72,256]{1,0:T(8,128)(2,1)S(1)}, u32[]{:S(2)}, u32[]{:S(2)}) collective-permute-start(bf16[72,256]{1,0:T(8,128)(2,1)S(1)} %get-tuple-element.44), channel_id=1, source_target_pairs={{0,8},{1,9},{2,10},{3,11},{4,12},{5,13},{6,14},{7,15},{8,0},{9,1},... | collective-permute-start | bytes 110600 | tf_op jit(solution)/shard_map/ppermute | solution.py:178
  41.5 5.8 %collective-permute-start.14 = (bf16[72,256]{1,0:T(8,128)(2,1)S(1)}, bf16[72,256]{1,0:T(8,128)(2,1)S(1)}, u32[]{:S(2)}, u32[]{:S(2)}) collective-permute-start(bf16[72,256]{1,0:T(8,128)(2,1)S(1)} %get-tuple-element.45), channel_id=1, source_target_pairs={{0,12},{1,13},{2,14},{3,15},{4,8},{5,9},{6,10},{7,11},{8,4},{9,5},... | collective-permute-start | bytes 110600 | tf_op jit(solution)/shard_map/ppermute | solution.py:178
  48.2 5.8 %collective-permute-start.17 = (bf16[72,256]{1,0:T(8,128)(2,1)S(1)}, bf16[72,256]{1,0:T(8,128)(2,1)S(1)}, u32[]{:S(2)}, u32[]{:S(2)}) collective-permute-start(bf16[72,256]{1,0:T(8,128)(2,1)S(1)} %shard_map.122.refs_0_), channel_id=1, source_target_pairs={{0,12},{1,13},{2,14},{3,15},{4,8},{5,9},{6,10},{7,11},{8,4},{9,5},... | collective-permute-start | bytes 110600 | tf_op jit(solution)/shard_map/ppermute | solution.py:178
  51.3 4.9 %collective-permute-start.16 = (bf16[72,256]{1,0:T(8,128)(2,1)S(1)}, bf16[72,256]{1,0:T(8,128)(2,1)S(1)}, u32[]{:S(2)}, u32[]{:S(2)}) collective-permute-start(bf16[72,256]{1,0:T(8,128)(2,1)S(1)} %shard_map.122.refs_0_), channel_id=1, source_target_pairs={{0,8},{1,9},{2,10},{3,11},{4,12},{5,13},{6,14},{7,15},{8,0},{9,1},... | collective-permute-start | bytes 110600 | tf_op jit(solution)/shard_map/ppermute | solution.py:178
  51.3 4.9 %collective-permute-start.15 = (bf16[72,256]{1,0:T(8,128)(2,1)S(1)}, bf16[72,256]{1,0:T(8,128)(2,1)S(1)}, u32[]{:S(2)}, u32[]{:S(2)}) collective-permute-start(bf16[72,256]{1,0:T(8,128)(2,1)S(1)} %shard_map.122.refs_0_), channel_id=1, source_target_pairs={{0,4},{1,5},{2,6},{3,7},{4,0},{5,1},{6,2},{7,3},{8,12},{9,13},{10,... | collective-permute-start | bytes 110600 | tf_op jit(solution)/shard_map/ppermute | solution.py:178
  56.2 4.9 %collective-permute-start.18 = (bf16[4,72,128]{2,1,0:T(8,128)(2,1)S(1)}, bf16[4,72,128]{2,1,0:T(8,128)(2,1)S(1)}, u32[]{:S(2)}, u32[]{:S(2)}) collective-permute-start(bf16[4,72,128]{2,1,0:T(8,128)(2,1)S(1)} %get-tuple-element.46.own_a), channel_id=1, source_target_pairs={{0,1},{1,0},{2,3},{3,2},{4,5},{5,4},{6,7},{7,6},{8,9},{9,8},{10,11... | collective-permute-start | bytes 221192 | tf_op jit(solution)/shard_map/ppermute | solution.py:178
  57.7 4.4 %collective-permute-start.19 = (bf16[4,72,128]{2,1,0:T(8,128)(2,1)S(1)}, bf16[4,72,128]{2,1,0:T(8,128)(2,1)S(1)}, u32[]{:S(2)}, u32[]{:S(2)}) collective-permute-start(bf16[4,72,128]{2,1,0:T(8,128)(2,1)S(1)} %get-tuple-element.47.own_b), channel_id=1, source_target_pairs={{0,2},{1,3},{2,0},{3,1},{4,6},{5,7},{6,4},{7,5},{8,10},{9,11},{10,... | collective-permute-start | bytes 221192 | tf_op jit(solution)/shard_map/ppermute | solution.py:178
  62.1 5.2 %collective-permute-start.20 = (bf16[2,4,72,128]{3,2,1,0:T(8,128)(2,1)S(1)}, bf16[2,4,72,128]{3,2,1,0:T(8,128)(2,1)S(1)}, u32[]{:S(2)}, u32[]{:S(2)}) collective-permute-start(bf16[2,4,72,128]{3,2,1,0:T(8,128)(2,1)S(1)} %get-tuple-element.48.refs_0_), channel_id=1, source_target_pairs={{0,2},{1,3},{2,0},{3,1},{4,6},{5,7},{6,4},{7,5},{8,10},{9,11},{10,... | collective-permute-start | bytes 442376 | tf_op jit(solution)/shard_map/ppermute | solution.py:178
  63.7 5.1 %collective-permute-start.21 = (bf16[2,4,72,128]{3,2,1,0:T(8,128)(2,1)S(1)}, bf16[2,4,72,128]{3,2,1,0:T(8,128)(2,1)S(1)}, u32[]{:S(2)}, u32[]{:S(2)}) collective-permute-start(bf16[2,4,72,128]{3,2,1,0:T(8,128)(2,1)S(1)} %get-tuple-element.49.refs_2_), channel_id=1, source_target_pairs={{0,1},{1,0},{2,3},{3,2},{4,5},{5,4},{6,7},{7,6},{8,9},{9,8},{10,11... | collective-permute-start | bytes 442376 | tf_op jit(solution)/shard_map/ppermute | solution.py:178
  64.2 5.2 %collective-permute-start.22 = (bf16[2,4,72,128]{3,2,1,0:T(8,128)(2,1)S(1)}, bf16[2,4,72,128]{3,2,1,0:T(8,128)(2,1)S(1)}, u32[]{:S(2)}, u32[]{:S(2)}) collective-permute-start(bf16[2,4,72,128]{3,2,1,0:T(8,128)(2,1)S(1)} %get-tuple-element.48.refs_0_), channel_id=1, source_target_pairs={{0,16},{1,17},{2,18},{3,19},{4,20},{5,21},{6,22},{7,23},{8,24},{9,... | collective-permute-start | bytes 442376 | tf_op jit(solution)/shard_map/ppermute | solution.py:178
  64.2 5.2 %collective-permute-start.24 = (bf16[2,4,72,128]{3,2,1,0:T(8,128)(2,1)S(1)}, bf16[2,4,72,128]{3,2,1,0:T(8,128)(2,1)S(1)}, u32[]{:S(2)}, u32[]{:S(2)}) collective-permute-start(bf16[2,4,72,128]{3,2,1,0:T(8,128)(2,1)S(1)} %get-tuple-element.49.refs_2_), channel_id=1, source_target_pairs={{0,16},{1,17},{2,18},{3,19},{4,20},{5,21},{6,22},{7,23},{8,24},{9,... | collective-permute-start | bytes 442376 | tf_op jit(solution)/shard_map/ppermute | solution.py:178
  67.3 2.2 %collective-permute-start.23 = (bf16[2,4,72,128]{3,2,1,0:T(8,128)(2,1)S(1)}, bf16[2,4,72,128]{3,2,1,0:T(8,128)(2,1)S(1)}, u32[]{:S(2)}, u32[]{:S(2)}) collective-permute-start(bf16[2,4,72,128]{3,2,1,0:T(8,128)(2,1)S(1)} %collective-permute-done.20.refs_1_), channel_id=1, source_target_pairs={{0,16},{1,17},{2,18},{3,19},{4,20},{5,21},{6,22},{7,23},{8,24},{9,... | collective-permute-start | bytes 442376 | tf_op jit(solution)/shard_map/ppermute | solution.py:178
  68.8 1.4 %collective-permute-start.25 = (bf16[2,4,72,128]{3,2,1,0:T(8,128)(2,1)S(1)}, bf16[2,4,72,128]{3,2,1,0:T(8,128)(2,1)S(1)}, u32[]{:S(2)}, u32[]{:S(2)}) collective-permute-start(bf16[2,4,72,128]{3,2,1,0:T(8,128)(2,1)S(1)} %collective-permute-done.21.refs_3_), channel_id=1, source_target_pairs={{0,16},{1,17},{2,18},{3,19},{4,20},{5,21},{6,22},{7,23},{8,24},{9,... | collective-permute-start | bytes 442376 | tf_op jit(solution)/shard_map/ppermute | solution.py:178
  (4 other events, 66.7 us)

commit v4 on v3

--- a/solution.py
+++ b/solution.py
@@ -148,61 +148,67 @@
     )(*operands)
 
 
-class Places:
-    def __init__(self):
-        self.sections, side_row, self.side_x = (lax.axis_size(name) for name in names)
-        self.side_y = 2 if side_row % 2 == 0 else 1
-        self.depth = side_row // self.side_y
-        self.sizes = (self.sections, self.depth, self.side_y, self.side_x)
-
-    def row(self):
-        return lax.axis_index("row")
-
-    def pair(self, sec, deep, y, x):
-        at_sec = lax.axis_index("sec") ^ sec
-        at_row = lax.axis_index("row") ^ (deep * self.side_y + y)
-        at_col = lax.axis_index("col") ^ x
-        return (at_sec * (self.depth * self.side_y) + at_row) * self.side_x + at_col
-
-    def move(self, array, sec=0, deep=0, y=0, x=0):
-        shift = (sec, deep, y, x)
-        pairs = []
-        for source in np.ndindex(*self.sizes):
-            target = tuple(at ^ by for at, by in zip(source, shift))
-            pairs.append(
-                (
-                    int(np.ravel_multi_index(source, self.sizes)),
-                    int(np.ravel_multi_index(target, self.sizes)),
-                )
-            )
-        return lax.ppermute(array, names, pairs)
-
-
-def cut_kernel(places, legendre_ref, *refs):
-    outs, turned = refs[:-1], refs[-1]
+def routes(sec, u, v, a, b):
+    return (a + 2 * b, v, u) if sec == 0 else (2 * a + b, u, v)
+
+
+relative = tuple(np.ndindex(2, 2, 2, 2))
+
+
+def place(sec, u, v, a, b):
+    at_sec = lax.axis_index("sec") ^ sec
+    options = []
+    for core in range(2):
+        z, y, x = routes(core, u, v, a, b)
+        options.append((z * 2 + y, x))
+    row = lax.axis_index("row") ^ jnp.where(at_sec == 0, options[0][0], options[1][0])
+    col = lax.axis_index("col") ^ jnp.where(at_sec == 0, options[0][1], options[1][1])
+    return at_sec, row, col
+
+
+def pair_at(sec, where):
+    at_sec, row, col = place(sec, *where)
+    return (at_sec * lax.axis_size("row") + row) * lax.axis_size("col") + col
+
+
+def exchange(array, axis):
+    sizes = tuple(lax.axis_size(name) for name in names)
+    pairs = []
+    for source in np.ndindex(*sizes):
+        sec, row, col = source
+        if axis == "sec":
+            target = (sec ^ 1, row, col)
+        else:
+            z, y, x = routes(sec, *(int(axis == name) for name in "uvab"))
+            target = (sec, row ^ (z * 2 + y), col ^ x)
+        pairs.append(
+            (int(np.ravel_multi_index(source, sizes)), int(np.ravel_multi_index(target, sizes)))
+        )
+    return lax.ppermute(array, names, pairs)
+
+
+def cut_kernel(legendre_ref, keep_ref, send_ref, turned):
     parts, lat_rows, rows = turned.shape
-    plane = parts // len(outs)
     whole = jnp.pad(
         legendre_ref[0].astype(jnp.float32), ((0, rows - legendre_ref.shape[1]), (0, 0))
     ).T.astype(jnp.bfloat16)
     for at in range(parts):
         turned[at] = whole[at * lat_rows : (at + 1) * lat_rows]
-    for deep, out in enumerate(outs):
-        begin = (places.row() ^ (deep * places.side_y)) // places.side_y * plane
-        out[...] = turned[pl.ds(begin, plane)]
-
-
-def turn_kernel(places, *refs):
-    takes, outs = refs[: places.depth], refs[places.depth :]
-    own = places.row() % places.side_y * places.side_x + lax.axis_index("col")
-    for at, out in enumerate(outs):
-        for deep, take in enumerate(takes):
-            out[deep] = take[own ^ at]
-
-
-def stack_kernel(*refs):
-    for at, take in enumerate(refs[:-1]):
-        refs[-1][at] = take[...]
+    for where in relative:
+        _, row, col = place(0, *where)
+        (send_ref if where[0] else keep_ref)[where[1:]] = turned[row * lax.axis_size("col") + col]
+
+
+def pass_kernel(keep_ref, take_ref, keep_out, send_out):
+    for i, j in np.ndindex(2, 2):
+        for source, ref in enumerate((keep_ref, take_ref)):
+            keep_out[i, j, source] = ref[0, i, j]
+            send_out[i, j, source] = ref[1, i, j]
+
+
+def stack_kernel(keep_ref, take_ref, out_ref):
+    out_ref[0] = keep_ref[...]
+    out_ref[1] = take_ref[...]
 
 
 def forward_kernel(table_ref, grid_ref, out_ref, held):
@@ -257,61 +263,32 @@
     return jnp.where(leading, weights, zero), jnp.where(leading, zero, weights)
 
 
-def degrees_kernel(places, sec, degrees, orders_ref, legendre_ref, fourier_ref, out_ref):
-    side_x, side_y = places.side_x, places.side_y
+def degrees_kernel(sec, degrees, orders_ref, legendre_ref, fourier_ref, out_ref):
     contract = (((0,), (0,)), ((), ()))
-    for deep, y, x in np.ndindex(places.depth, side_y, side_x):
-        pair = places.pair(sec, int(deep), int(y), int(x))
-        order = orders_ref[pair]
-        lower, upper = masked(legendre_ref[2 * y + x, deep], order, degrees)
+    for where in relative:
+        order = orders_ref[pair_at(sec, where)]
+        lower, upper = masked(legendre_ref[where[3:] + where[:3]], order, degrees)
         total = lax.dot_general(
             lower, fourier_ref[2 * order], contract, preferred_element_type=jnp.float32
         ) + lax.dot_general(
             upper, fourier_ref[2 * order + 1], contract, preferred_element_type=jnp.float32
         )
-        out_ref[y, x, deep] = total.astype(out_ref.dtype)
-
-
-def plane_kernel(kept_ref, taken_ref, keep_a, send_a, keep_b, send_b):
-    radial = keep_a.shape[-1]
-    for y in range(2):
-        for x in range(2):
-            total = kept_ref[y, x] + taken_ref[y, x].astype(jnp.float32)
-            part_a, part_b = total[..., :radial], total[..., radial:]
-            if x == 0:
-                keep_a[y] = part_a
-            else:
-                send_a[y] = part_a.astype(jnp.bfloat16)
-            if y == 0:
-                keep_b[x] = part_b
-            else:
-                send_b[x] = part_b.astype(jnp.bfloat16)
-
-
-def cross_kernel(keep_a, take_a, keep_b, take_b, keep_a2, send_a2, keep_b2, send_b2):
-    keep_a2[...] = keep_a[0] + take_a[0].astype(jnp.float32)
-    send_a2[...] = (keep_a[1] + take_a[1].astype(jnp.float32)).astype(jnp.bfloat16)
-    keep_b2[...] = keep_b[0] + take_b[0].astype(jnp.float32)
-    send_b2[...] = (keep_b[1] + take_b[1].astype(jnp.float32)).astype(jnp.bfloat16)
-
-
-def depth_kernel(keep_a, take_a, keep_b, take_b, *outs):
-    radial = keep_a.shape[-1]
-    for deep, out in enumerate(outs):
-        out[:, :radial] = (keep_a[deep] + take_a[deep].astype(jnp.float32)).astype(out.dtype)
-        out[:, radial:] = (keep_b[deep] + take_b[deep].astype(jnp.float32)).astype(out.dtype)
-
-
-def solve_kernel(places, orders_ref, *refs):
-    takes = refs[: places.depth]
-    state_ref, kappa_ref, damping_ref, right_ref, left_ref, sent_ref = refs[places.depth :]
+        out_ref[where] = total.astype(out_ref.dtype)
+
+
+def halve_kernel(keep_ref, take_ref, keep_out, send_out):
+    keep_out[...] = keep_ref[0] + take_ref[0].astype(jnp.float32)
+    send_out[...] = (keep_ref[1] + take_ref[1].astype(jnp.float32)).astype(jnp.bfloat16)
+
+
+def solve_kernel(
+    orders_ref, keep_ref, take_ref, state_ref, kappa_ref, damping_ref, right_ref, left_ref, sent_ref
+):
     rows = state_ref.shape[1]
     radial = right_ref.shape[0]
     degrees = rows - 1
-    order = orders_ref[places.pair(0, 0, 0, 0)]
-    coefficient = takes[0][...].astype(jnp.float32)
-    for other in takes[1:]:
-        coefficient += other[...].astype(jnp.float32)
+    order = orders_ref[pair_at(0, (0, 0, 0, 0))]
+    coefficient = keep_ref[...] + take_ref[...].astype(jnp.float32)
     right_side = state_ref[0].astype(jnp.float32) + time_step * coefficient[:rows]
     right_side = right_side.astype(jnp.bfloat16)
     row_index = lax.broadcasted_iota(jnp.int32, (rows, radial), 0)
@@ -334,36 +311,15 @@
         sent_ref[pl.ds(0, rows), columns] = field
 
 
-def spread_kernel(*refs):
-    fields, (out_a, out_b) = refs[:-2], refs[-2:]
-    radial = out_a.shape[-1]
-    for deep, field in enumerate(fields):
-        out_a[deep] = field[:, :radial]
-        out_b[deep] = field[:, radial:]
-
-
-def join_kernel(own_a, take_a, own_b, take_b, out_a, out_b):
-    out_a[0] = own_a[...]
-    out_a[1] = take_a[...]
-    out_b[0] = own_b[...]
-    out_b[1] = take_b[...]
-
-
-def inverse_kernel(places, degrees, orders_ref, here_ref, there_ref, table_ref, *refs):
+def inverse_kernel(degrees, orders_ref, here_ref, there_ref, table_ref, *refs):
     fields, (out_ref, buffer, held, sems) = refs[:-4], refs[-4:]
     blocks, slot_rows, lat_block, radial = held.shape
     slots = slot_rows // 2
-    per_section = len(fields) // places.sections
-
-    for sec in range(places.sections):
-        own_a, far_a, own_b, far_b = fields[sec * per_section : (sec + 1) * per_section]
-        for deep, y, x in np.ndindex(places.depth, places.side_y, places.side_x):
-            deep, y, x = int(deep), int(y), int(x)
-            pair = places.pair(sec, deep, y, x)
-            order = orders_ref[pair]
-            weights = masked((there_ref if sec else here_ref)[2 * y + x, deep], order, degrees)
-            both = ((far_a if y else own_a)[x, deep], (far_b if x else own_b)[y, deep])
-            field = jnp.concatenate(both, axis=1)
+    for sec in range(2):
+        for where in relative:
+            order = orders_ref[pair_at(sec, where)]
+            weights = masked((there_ref if sec else here_ref)[where[3:] + where[:3]], order, degrees)
+            field = fields[2 * sec + where[0]][where[1:]]
             for half in range(2):
                 rebuilt = jnp.dot(weights[half], field, preferred_element_type=jnp.float32)
                 for part in range(2):
@@ -399,13 +355,13 @@
         chunk(at).wait()
 
 
-def inverse_values(places, degrees, pair_orders, legendre, table, fields, lat_rows, lat_block):
+def inverse_values(degrees, pair_orders, legendre, table, fields, lat_rows, lat_block):
     _, phi_count, slot_rows = table.shape
-    radial = fields[0].shape[-1]
+    radial = fields[0].shape[-1] // 2
     blocks = lat_rows // lat_block
     out = jax.ShapeDtypeStruct((lat_rows, phi_count, radial), jnp.float32)
     return pl.pallas_call(
-        functools.partial(inverse_kernel, places, degrees),
+        functools.partial(inverse_kernel, degrees),
         in_specs=[smem()] + [vmem()] * (1 + len(legendre) + len(fields)),
         out_specs=anywhere(),
         out_shape=out,
@@ -430,89 +386,69 @@
     padded = -(-rows // 8) * 8
     columns = 2 * radial
     pair_total = pair_orders.shape[0]
-    places = Places()
-    depth = places.depth
     lat_block = 8
-    table = natural_table(pair_total, places.sections, phi_count)
+    table = natural_table(pair_total, lax.axis_size("sec"), phi_count)
     forward_table = jnp.asarray(table, jnp.bfloat16)
     inverse_table = jnp.asarray(table.transpose(0, 2, 1), jnp.bfloat16)
 
     def shape(*sizes, dtype=jnp.bfloat16):
         return jax.ShapeDtypeStruct(sizes, dtype)
 
-    part = shape(places.side_y * places.side_x, lat_rows, padded)
-    cuts = call(
-        functools.partial(cut_kernel, places),
+    part = shape(2, 2, 2, lat_rows, padded)
+    keep, send = call(
+        cut_kernel,
         [legendre],
-        [part] * depth,
-        scratch=[pltpu.VMEM((depth * part.shape[0], lat_rows, padded), jnp.bfloat16)],
+        [part, part],
+        scratch=[pltpu.VMEM((2 * part.shape[0] * 4, lat_rows, padded), jnp.bfloat16)],
         cost=pl.CostEstimate(flops=int(1.3e10), bytes_accessed=0, transcendentals=0),
     )
-    cuts = [cuts[0]] + [places.move(cuts[deep], deep=deep) for deep in range(1, depth)]
-    part = shape(depth, lat_rows, padded)
-    cuts = call(functools.partial(turn_kernel, places), cuts, [part] * 4)
-    cuts = [cuts[0]] + [places.move(cuts[at], y=at // 2, x=at % 2) for at in range(1, 4)]
-    legendre_here = call(stack_kernel, cuts, shape(4, depth, lat_rows, padded))
-    legendre_there = places.move(legendre_here, sec=1)
-    legendres = (legendre_here, legendre_there)
+    for axis in "uva":
+        keep, send = call(pass_kernel, [keep, exchange(send, axis)], [part, part])
+    here = call(stack_kernel, [keep, exchange(send, "b")], shape(2, 2, 2, 2, lat_rows, padded))
+    legendres = (here, exchange(here, "sec"))
 
     fourier = forward_sums(forward_table, grid_terms, lat_block)
 
     def partial_sums(sec, dtype):
         return call(
-            functools.partial(degrees_kernel, places, sec, degrees),
+            functools.partial(degrees_kernel, sec, degrees),
             [pair_orders, legendres[sec], fourier],
-            shape(2, 2, depth, padded, columns, dtype=dtype),
+            shape(2, 2, 2, 2, padded, columns, dtype=dtype),
             mib=24,
             scalars=1,
             cost=pl.CostEstimate(
-                flops=4 * pair_total * rows * lat_rows * columns // places.sections,
+                flops=2 * pair_total * rows * lat_rows * columns,
                 bytes_accessed=fourier.size * 2,
                 transcendentals=0,
             ),
         )
 
-    taken = places.move(partial_sums(1, jnp.bfloat16), sec=1)
-    kept = partial_sums(0, jnp.float32)
-    wide = shape(2, depth, padded, radial, dtype=jnp.float32)
-    half = shape(2, depth, padded, radial)
-    keep_a, send_a, keep_b, send_b = call(plane_kernel, [kept, taken], [wide, half, wide, half])
-    take_a, take_b = places.move(send_a, x=1), places.move(send_b, y=1)
-    wide = shape(depth, padded, radial, dtype=jnp.float32)
-    half = shape(depth, padded, radial)
-    keep_a, send_a, keep_b, send_b = call(
-        cross_kernel, [keep_a, take_a, keep_b, take_b], [wide, half, wide, half]
-    )
-    take_a, take_b = places.move(send_a, y=1), places.move(send_b, x=1)
-    lines = call(
-        depth_kernel,
-        [keep_a, take_a, keep_b, take_b],
-        [shape(padded, columns, dtype=jnp.float32)] + [shape(padded, columns)] * (depth - 1),
-    )
-    parts = [lines[0]] + [places.move(lines[deep], deep=deep) for deep in range(1, depth)]
+    take = exchange(partial_sums(1, jnp.bfloat16), "sec")
+    keep = partial_sums(0, jnp.float32)
+    rest = (2, 2, 2, padded, columns)
+    for axis in "uvab":
+        keep, send = call(
+            halve_kernel, [keep, take], [shape(*rest, dtype=jnp.float32), shape(*rest)]
+        )
+        take = exchange(send, axis)
+        rest = rest[1:]
 
     radial_mode = np.arange(radial, dtype=np.float32) / np.float32(radial)
     damping = np.exp(-filter_strength * radial_mode**filter_power).astype(np.float32)
     field = call(
-        functools.partial(solve_kernel, places),
-        [pair_orders, *parts, state, kappa[None, :], jnp.asarray(damping)[None, :], right_op, left_op],
+        solve_kernel,
+        [pair_orders, keep, take, state, kappa[None, :], jnp.asarray(damping)[None, :], right_op, left_op],
         shape(padded, columns),
         scalars=1,
     )
     new_state = field[None, :rows]
 
-    fields = [field] + [places.move(field, deep=deep) for deep in range(1, depth)]
-    own_a, own_b = call(spread_kernel, fields, [half, half])
-    take_a, take_b = places.move(own_a, x=1), places.move(own_b, y=1)
-    both = shape(2, depth, padded, radial)
-    own_a, own_b = call(join_kernel, [own_a, take_a, own_b, take_b], [both, both])
-    far_a, far_b = places.move(own_a, y=1), places.move(own_b, x=1)
-    here = [own_a, far_a, own_b, far_b]
-    there = [places.move(part, sec=1) for part in (own_a, own_b)]
-    there += [places.move(part, sec=1) for part in (far_a, far_b)]
-    gathered = here + [there[0], there[2], there[1], there[3]]
+    for axis in "bav":
+        field = call(stack_kernel, [field, exchange(field, axis)], shape(2, *field.shape))
+    far = exchange(field, "u")
+    fields = (field, far, exchange(field, "sec"), exchange(far, "sec"))
     evolved = inverse_values(
-        places, degrees, pair_orders, legendres, inverse_table, gathered, lat_rows, lat_block
+        degrees, pair_orders, legendres, inverse_table, fields, lat_rows, lat_block
     )
     return (evolved, new_state)
 
@@ -523,7 +459,7 @@
     sections, side_row, side_x = (lax.axis_size(name) for name in names)
     fits = args[2].shape[0] == 1 and lat_rows % 16 == 0 and rows <= 2 * lat_rows
     fits = fits and args[0].size * 4 <= 24 * 1024 * 1024
-    fits = fits and sections == 2 and side_x == 2 and side_row in (2, 4, 8, 16)
+    fits = fits and (sections, side_row, side_x) == (2, 8, 2)
     return on_device_compact(*args) if fits else on_device_wide(*args)
 
 

time: 79.3 us -> 85.6 us (1.079)
  waiting for transfers between devices: 33 us -> 39.1 us
    ppermute x26 -> x16, waiting for transfers between devices: 33 us -> 39.1 us  [exchange(): return lax.ppermute(array, names, pairs)]
    pallas_call x11 -> x15, Pallas kernels: 3.52 us -> 3.59 us  [call(): pl.pallas_call(kernel, in_specs=[smem()] * scalars + [vmem()] * (len(oper...]
    ppermute x26 -> x16, starting transfers between devices: 27.6 us -> 27.7 us  [exchange(): return lax.ppermute(array, names, pairs)]
  transfers between devices with their start and end apart: 26 -> 16, of which waited for: 19 -> 14; matrix products, arithmetic and copies ran while one was open for 1% -> 1% of each run, Pallas kernels for 6% -> 5%
where the time goes in v4:
time: 85.6 us; the launch traced here: 85.4 us
  waiting for transfers between devices  39.1 us (46%)
  starting transfers between devices  27.7 us (32%)
  Pallas kernels  16 us (19%)
  local copies, waits for them, and re-layouts  1.72 us (2%)
  between operations  0.86 us (1%)
    ppermute x16, waiting for transfers between devices, exchange(): return lax.ppermute(array, names, pairs)  39.1 us
    ppermute x16, starting transfers between devices, exchange(): return lax.ppermute(array, names, pairs)  27.7 us
    pallas_call x1, Pallas kernels, inverse_values(): pl.pallas_call(functools.partial(inverse_kernel, degrees), in_specs=[smem...  8.94 us
    pallas_call x15, Pallas kernels, call(): pl.pallas_call(kernel, in_specs=[smem()] * scalars + [vmem()] * (len(oper...  3.59 us
    pallas_call x1, Pallas kernels, forward_sums(): pl.pallas_call(forward_kernel, in_specs=[vmem(), vmem()], out_specs=vmem(...  3.46 us
  transfers between devices with their start and end apart: 16, of which 14 were waited for; matrix products, arithmetic and copies ran while one was open for 1% of the time, Pallas kernels for 5%

profile of v4, /device:TPU:0, one launch (start us, length us, event | category | flops | bytes accessed | tf_op | source)
XLA Modules:
  0.0 85.4 jit_solution(4239234832370290269)
XLA Ops:
  0.7 1.0 %copy-done.9 = bf16[1,65,768]{2,1,0:T(8,128)(2,1)S(1)} copy-done((bf16[1,65,768]{2,1,0:T(8,128)(2,1)S(1)}, bf16[1,65,768]{2,1,0:T(8,128)(2,1)}, u32[]{:S(2)}) %copy-start.9) | copy-done | bytes 99864
  2.0 3.0 %collective-permute-start = (bf16[2,2,2,48,72]{4,3,2,1,0:T(8,128)(2,1)S(1)}, bf16[2,2,2,48,72]{4,3,2,1,0:T(8,128)(2,1)S(1)}, u32[]{:S(2)}, u32[]{:S(2)}) collective-permute-start(bf16[2,2,2,48,72]{4,3,2,1,0:T(8,128)(2,1)S(1)} %get-tuple-element.19), channel_id=1, source_target_pairs={{0,1},{1,0},{2,3},{3,2},{4,5},{5,4},{6,7},{7,6},{8,9},{9,8},{10,11... | collective-permute-start | bytes 165896 | tf_op jit(solution)/shard_map/ppermute | solution.py:187
  5.0 2.6 %collective-permute-done.take_ref = bf16[2,2,2,48,72]{4,3,2,1,0:T(8,128)(2,1)S(1)} collective-permute-done((bf16[2,2,2,48,72]{4,3,2,1,0:T(8,128)(2,1)S(1)}, bf16[2,2,2,48,72]{4,3,2,1,0:T(8,128)(2,1)S(1)}, u32[]{:S(2)}, u32[]{:S(2)}) %collective-permute-start) | collective-permute-done | bytes 55328 | tf_op jit(solution)/shard_map/ppermute | solution.py:187
  7.6 2.1 %collective-permute-start.1 = (bf16[2,2,2,48,72]{4,3,2,1,0:T(8,128)(2,1)S(1)}, bf16[2,2,2,48,72]{4,3,2,1,0:T(8,128)(2,1)S(1)}, u32[]{:S(2)}, u32[]{:S(2)}) collective-permute-start(bf16[2,2,2,48,72]{4,3,2,1,0:T(8,128)(2,1)S(1)} %get-tuple-element.21), channel_id=1, source_target_pairs={{0,2},{1,3},{2,0},{3,1},{4,6},{5,7},{6,4},{7,5},{8,10},{9,11},{10,... | collective-permute-start | bytes 165896 | tf_op jit(solution)/shard_map/ppermute | solution.py:187
  9.7 2.6 %collective-permute-done.1.take_ref = bf16[2,2,2,48,72]{4,3,2,1,0:T(8,128)(2,1)S(1)} collective-permute-done((bf16[2,2,2,48,72]{4,3,2,1,0:T(8,128)(2,1)S(1)}, bf16[2,2,2,48,72]{4,3,2,1,0:T(8,128)(2,1)S(1)}, u32[]{:S(2)}, u32[]{:S(2)}) %collective-permute-start.1) | collective-permute-done | bytes 55328 | tf_op jit(solution)/shard_map/ppermute | solution.py:187
  12.4 2.1 %collective-permute-start.2 = (bf16[2,2,2,48,72]{4,3,2,1,0:T(8,128)(2,1)S(1)}, bf16[2,2,2,48,72]{4,3,2,1,0:T(8,128)(2,1)S(1)}, u32[]{:S(2)}, u32[]{:S(2)}) collective-permute-start(bf16[2,2,2,48,72]{4,3,2,1,0:T(8,128)(2,1)S(1)} %get-tuple-element.23), channel_id=1, source_target_pairs={{0,4},{1,5},{2,6},{3,7},{4,0},{5,1},{6,2},{7,3},{8,12},{9,13},{10,... | collective-permute-start | bytes 165896 | tf_op jit(solution)/shard_map/ppermute | solution.py:187
  14.5 2.6 %collective-permute-done.2.take_ref = bf16[2,2,2,48,72]{4,3,2,1,0:T(8,128)(2,1)S(1)} collective-permute-done((bf16[2,2,2,48,72]{4,3,2,1,0:T(8,128)(2,1)S(1)}, bf16[2,2,2,48,72]{4,3,2,1,0:T(8,128)(2,1)S(1)}, u32[]{:S(2)}, u32[]{:S(2)}) %collective-permute-start.2) | collective-permute-done | bytes 55328 | tf_op jit(solution)/shard_map/ppermute | solution.py:187
  17.1 3.1 %collective-permute-start.3 = (bf16[2,2,2,48,72]{4,3,2,1,0:T(8,128)(2,1)S(1)}, bf16[2,2,2,48,72]{4,3,2,1,0:T(8,128)(2,1)S(1)}, u32[]{:S(2)}, u32[]{:S(2)}) collective-permute-start(bf16[2,2,2,48,72]{4,3,2,1,0:T(8,128)(2,1)S(1)} %get-tuple-element.25), channel_id=1, source_target_pairs={{0,8},{1,9},{2,10},{3,11},{4,12},{5,13},{6,14},{7,15},{8,0},{9,1},... | collective-permute-start | bytes 165896 | tf_op jit(solution)/shard_map/ppermute | solution.py:187
  20.2 2.6 %collective-permute-done.3.take_ref = bf16[2,2,2,48,72]{4,3,2,1,0:T(8,128)(2,1)S(1)} collective-permute-done((bf16[2,2,2,48,72]{4,3,2,1,0:T(8,128)(2,1)S(1)}, bf16[2,2,2,48,72]{4,3,2,1,0:T(8,128)(2,1)S(1)}, u32[]{:S(2)}, u32[]{:S(2)}) %collective-permute-start.3) | collective-permute-done | bytes 55328 | tf_op jit(solution)/shard_map/ppermute | solution.py:187
  23.0 3.5 %shard_map.118.fourier_ref = bf16[64,48,256]{2,1,0:T(8,128)(2,1)S(1)} custom-call(bf16[2,128,768]{2,1,0:T(8,128)(2,1)S(1)} %copy-done.2, f32[48,768,128]{2,1,0:T(8,128)S(1)} %copy-done), custom_call_target="tpu_custom_call" | custom-call | flops 1207959552 | bytes 18874368 | tf_op jit(solution)/shard_map/pallas_call | solution.py:244
  26.5 1.1 %shard_map.120 = bf16[2,2,2,2,72,256]{5,4,3,2,1,0:T(8,128)(2,1)S(1)} custom-call(s32[32]{0:T(128)S(1)} %copy-done.6, bf16[2,2,2,2,48,72]{5,4,3,2,1,0:T(8,128)(2,1)S(1)} %collective-permute-done.4.legendre_ref.there_ref, bf16[64,48,256]{2,1,0:T(8,128)(2,1)S(1)} %shard_map.118.fourier_ref), custom_call_target="tpu_custom_call" | custom-call | flops 51118080 | bytes 1572864 | tf_op jit(solution)/shard_map/pallas_call | solution.py:140
  28.1 1.1 %shard_map.119.keep_ref = f32[2,2,2,2,72,256]{5,4,3,2,1,0:T(8,128)S(1)} custom-call(s32[32]{0:T(128)S(1)} %copy-done.6, bf16[2,2,2,2,48,72]{5,4,3,2,1,0:T(8,128)(2,1)S(1)} %shard_map.117.legendre_ref.here_ref, bf16[64,48,256]{2,1,0:T(8,128)(2,1)S(1)} %shard_map.118.fourier_ref), custom_call_target="tpu_custom_call" | custom-call | flops 51118080 | bytes 1572864 | tf_op jit(solution)/shard_map/pallas_call | solution.py:140
  29.8 1.9 %collective-permute-start.6 = (bf16[2,2,2,72,256]{4,3,2,1,0:T(8,128)(2,1)S(1)}, bf16[2,2,2,72,256]{4,3,2,1,0:T(8,128)(2,1)S(1)}, u32[]{:S(2)}, u32[]{:S(2)}) collective-permute-start(bf16[2,2,2,72,256]{4,3,2,1,0:T(8,128)(2,1)S(1)} %get-tuple-element.27), channel_id=1, source_target_pairs={{0,1},{1,0},{2,3},{3,2},{4,5},{5,4},{6,7},{7,6},{8,9},{9,8},{10,11... | collective-permute-start | bytes 884744 | tf_op jit(solution)/shard_map/ppermute | solution.py:187
  31.7 4.9 %collective-permute-done.6.take_ref = bf16[2,2,2,72,256]{4,3,2,1,0:T(8,128)(2,1)S(1)} collective-permute-done((bf16[2,2,2,72,256]{4,3,2,1,0:T(8,128)(2,1)S(1)}, bf16[2,2,2,72,256]{4,3,2,1,0:T(8,128)(2,1)S(1)}, u32[]{:S(2)}, u32[]{:S(2)}) %collective-permute-start.6) | collective-permute-done | bytes 294944 | tf_op jit(solution)/shard_map/ppermute | solution.py:187
  36.7 1.9 %collective-permute-start.7 = (bf16[2,2,72,256]{3,2,1,0:T(8,128)(2,1)S(1)}, bf16[2,2,72,256]{3,2,1,0:T(8,128)(2,1)S(1)}, u32[]{:S(2)}, u32[]{:S(2)}) collective-permute-start(bf16[2,2,72,256]{3,2,1,0:T(8,128)(2,1)S(1)} %get-tuple-element.29), channel_id=1, source_target_pairs={{0,2},{1,3},{2,0},{3,1},{4,6},{5,7},{6,4},{7,5},{8,10},{9,11},{10,... | collective-permute-start | bytes 442376 | tf_op jit(solution)/shard_map/ppermute | solution.py:187
  38.6 3.3 %collective-permute-done.7.take_ref = bf16[2,2,72,256]{3,2,1,0:T(8,128)(2,1)S(1)} collective-permute-done((bf16[2,2,72,256]{3,2,1,0:T(8,128)(2,1)S(1)}, bf16[2,2,72,256]{3,2,1,0:T(8,128)(2,1)S(1)}, u32[]{:S(2)}, u32[]{:S(2)}) %collective-permute-start.7) | collective-permute-done | bytes 147488 | tf_op jit(solution)/shard_map/ppermute | solution.py:187
  41.9 2.1 %collective-permute-start.8 = (bf16[2,72,256]{2,1,0:T(8,128)(2,1)S(1)}, bf16[2,72,256]{2,1,0:T(8,128)(2,1)S(1)}, u32[]{:S(2)}, u32[]{:S(2)}) collective-permute-start(bf16[2,72,256]{2,1,0:T(8,128)(2,1)S(1)} %get-tuple-element.31), channel_id=1, source_target_pairs={{0,4},{1,5},{2,6},{3,7},{4,0},{5,1},{6,2},{7,3},{8,12},{9,13},{10,... | collective-permute-start | bytes 221192 | tf_op jit(solution)/shard_map/ppermute | solution.py:187
  44.1 2.3 %collective-permute-done.8.take_ref = bf16[2,72,256]{2,1,0:T(8,128)(2,1)S(1)} collective-permute-done((bf16[2,72,256]{2,1,0:T(8,128)(2,1)S(1)}, bf16[2,72,256]{2,1,0:T(8,128)(2,1)S(1)}, u32[]{:S(2)}, u32[]{:S(2)}) %collective-permute-start.8) | collective-permute-done | bytes 73760 | tf_op jit(solution)/shard_map/ppermute | solution.py:187
  46.4 3.5 %collective-permute-start.9 = (bf16[72,256]{1,0:T(8,128)(2,1)S(1)}, bf16[72,256]{1,0:T(8,128)(2,1)S(1)}, u32[]{:S(2)}, u32[]{:S(2)}) collective-permute-start(bf16[72,256]{1,0:T(8,128)(2,1)S(1)} %get-tuple-element.33), channel_id=1, source_target_pairs={{0,8},{1,9},{2,10},{3,11},{4,12},{5,13},{6,14},{7,15},{8,0},{9,1},... | collective-permute-start | bytes 110600 | tf_op jit(solution)/shard_map/ppermute | solution.py:187
  49.9 1.9 %collective-permute-done.9.take_ref = bf16[72,256]{1,0:T(8,128)(2,1)S(1)} collective-permute-done((bf16[72,256]{1,0:T(8,128)(2,1)S(1)}, bf16[72,256]{1,0:T(8,128)(2,1)S(1)}, u32[]{:S(2)}, u32[]{:S(2)}) %collective-permute-start.9) | collective-permute-done | bytes 36896 | tf_op jit(solution)/shard_map/ppermute | solution.py:187
  51.8 0.8 shard_map.125.keep_ref
  52.7 3.0 %collective-permute-start.10 = (bf16[72,256]{1,0:T(8,128)(2,1)S(1)}, bf16[72,256]{1,0:T(8,128)(2,1)S(1)}, u32[]{:S(2)}, u32[]{:S(2)}) collective-permute-start(bf16[72,256]{1,0:T(8,128)(2,1)S(1)} %shard_map.125.keep_ref), channel_id=1, source_target_pairs={{0,8},{1,9},{2,10},{3,11},{4,12},{5,13},{6,14},{7,15},{8,0},{9,1},... | collective-permute-start | bytes 110600 | tf_op jit(solution)/shard_map/ppermute | solution.py:187
  55.7 2.7 %collective-permute-done.10.take_ref = bf16[72,256]{1,0:T(8,128)(2,1)S(1)} collective-permute-done((bf16[72,256]{1,0:T(8,128)(2,1)S(1)}, bf16[72,256]{1,0:T(8,128)(2,1)S(1)}, u32[]{:S(2)}, u32[]{:S(2)}) %collective-permute-start.10) | collective-permute-done | bytes 36896 | tf_op jit(solution)/shard_map/ppermute | solution.py:187
  58.4 1.2 %collective-permute-start.11 = (bf16[2,72,256]{2,1,0:T(8,128)(2,1)S(1)}, bf16[2,72,256]{2,1,0:T(8,128)(2,1)S(1)}, u32[]{:S(2)}, u32[]{:S(2)}) collective-permute-start(bf16[2,72,256]{2,1,0:T(8,128)(2,1)S(1)} %shard_map.126.keep_ref), channel_id=1, source_target_pairs={{0,4},{1,5},{2,6},{3,7},{4,0},{5,1},{6,2},{7,3},{8,12},{9,13},{10,... | collective-permute-start | bytes 221192 | tf_op jit(solution)/shard_map/ppermute | solution.py:187
  59.6 3.1 %collective-permute-done.11.take_ref = bf16[2,72,256]{2,1,0:T(8,128)(2,1)S(1)} collective-permute-done((bf16[2,72,256]{2,1,0:T(8,128)(2,1)S(1)}, bf16[2,72,256]{2,1,0:T(8,128)(2,1)S(1)}, u32[]{:S(2)}, u32[]{:S(2)}) %collective-permute-start.11) | collective-permute-done | bytes 73760 | tf_op jit(solution)/shard_map/ppermute | solution.py:187
  62.8 1.6 %collective-permute-start.12 = (bf16[2,2,72,256]{3,2,1,0:T(8,128)(2,1)S(1)}, bf16[2,2,72,256]{3,2,1,0:T(8,128)(2,1)S(1)}, u32[]{:S(2)}, u32[]{:S(2)}) collective-permute-start(bf16[2,2,72,256]{3,2,1,0:T(8,128)(2,1)S(1)} %shard_map.127.keep_ref), channel_id=1, source_target_pairs={{0,2},{1,3},{2,0},{3,1},{4,6},{5,7},{6,4},{7,5},{8,10},{9,11},{10,... | collective-permute-start | bytes 442376 | tf_op jit(solution)/shard_map/ppermute | solution.py:187
  64.3 3.7 %collective-permute-done.12.take_ref = bf16[2,2,72,256]{3,2,1,0:T(8,128)(2,1)S(1)} collective-permute-done((bf16[2,2,72,256]{3,2,1,0:T(8,128)(2,1)S(1)}, bf16[2,2,72,256]{3,2,1,0:T(8,128)(2,1)S(1)}, u32[]{:S(2)}, u32[]{:S(2)}) %collective-permute-start.12) | collective-permute-done | bytes 147488 | tf_op jit(solution)/shard_map/ppermute | solution.py:187
  68.1 1.6 %collective-permute-start.13 = (bf16[2,2,2,72,256]{4,3,2,1,0:T(8,128)(2,1)S(1)}, bf16[2,2,2,72,256]{4,3,2,1,0:T(8,128)(2,1)S(1)}, u32[]{:S(2)}, u32[]{:S(2)}) collective-permute-start(bf16[2,2,2,72,256]{4,3,2,1,0:T(8,128)(2,1)S(1)} %shard_map.128.refs_0_), channel_id=1, source_target_pairs={{0,1},{1,0},{2,3},{3,2},{4,5},{5,4},{6,7},{7,6},{8,9},{9,8},{10,11... | collective-permute-start | bytes 884744 | tf_op jit(solution)/shard_map/ppermute | solution.py:187
  69.7 5.2 %collective-permute-done.13.refs_1_ = bf16[2,2,2,72,256]{4,3,2,1,0:T(8,128)(2,1)S(1)} collective-permute-done((bf16[2,2,2,72,256]{4,3,2,1,0:T(8,128)(2,1)S(1)}, bf16[2,2,2,72,256]{4,3,2,1,0:T(8,128)(2,1)S(1)}, u32[]{:S(2)}, u32[]{:S(2)}) %collective-permute-start.13) | collective-permute-done | bytes 294944 | tf_op jit(solution)/shard_map/ppermute | solution.py:187
  74.9 0.6 slice_bitcast_fusion
  75.5 1.0 %collective-permute-done.15.refs_3_ = bf16[2,2,2,72,256]{4,3,2,1,0:T(8,128)(2,1)S(1)} collective-permute-done((bf16[2,2,2,72,256]{4,3,2,1,0:T(8,128)(2,1)S(1)}, bf16[2,2,2,72,256]{4,3,2,1,0:T(8,128)(2,1)S(1)}, u32[]{:S(2)}, u32[]{:S(2)}) %collective-permute-start.15) | collective-permute-done | bytes 294944 | tf_op jit(solution)/shard_map/ppermute | solution.py:187
  76.5 8.9 %shard_map.129 = f32[48,768,128]{2,1,0:T(8,128)} custom-call(s32[32]{0:T(128)S(1)} %copy-done.6, bf16[2,2,2,2,48,72]{5,4,3,2,1,0:T(8,128)(2,1)S(1)} %shard_map.117.legendre_ref.here_ref, bf16[2,2,2,2,48,72]{5,4,3,2,1,0:T(8,128)(2,1)S(1)} %collective-permute-done.4.legendre_ref.there_ref, bf16[2,768,128]{2,1,0:T(8,128)(2,1)S(1)} %copy-done.1, ...), custom_call_target="tpu_custom_call" | custom-call | flops 1207959552 | bytes 18874368 | tf_op jit(solution)/shard_map/pallas_call | solution.py:363
  (38 shorter events, 1.8 us)
Async XLA Ops:
  0.6 22.3 %copy-start.2 = (bf16[2,128,768]{2,1,0:T(8,128)(2,1)S(1)}, bf16[2,128,768]{2,1,0:T(8,128)(2,1)}, u32[]{:S(2)}) copy-start(bf16[2,128,768]{2,1,0:T(8,128)(2,1)} %constant.6.clone.table_ref) | copy-start | bytes 1179652
  0.6 22.3 %copy-start = (f32[48,768,128]{2,1,0:T(8,128)S(1)}, f32[48,768,128]{2,1,0:T(8,128)}, u32[]{:S(2)}) copy-start(f32[48,768,128]{2,1,0:T(8,128)} %grid_ref.1) | copy-start | bytes 56623108
  0.7 1.0 %copy-start.9 = (bf16[1,65,768]{2,1,0:T(8,128)(2,1)S(1)}, bf16[1,65,768]{2,1,0:T(8,128)(2,1)}, u32[]{:S(2)}) copy-start(bf16[1,65,768]{2,1,0:T(8,128)(2,1)} %legendre_ref.1) | copy-start | bytes 299524
  1.9 24.6 %copy-start.6 = (s32[32]{0:T(128)S(1)}, s32[32]{0:T(128)}, u32[]{:S(2)}) copy-start(s32[32]{0:T(128)} %orders_ref.7) | copy-start | bytes 388
  1.9 49.9 %copy-start.3 = (bf16[1,65,256]{2,1,0:T(8,128)(2,1)S(1)}, bf16[1,65,256]{2,1,0:T(8,128)(2,1)}, u32[]{:S(2)}) copy-start(bf16[1,65,256]{2,1,0:T(8,128)(2,1)} %state_ref.1) | copy-start | bytes 99844
  1.9 49.9 %copy-start.4 = (bf16[128,128]{1,0:T(8,128)(2,1)S(1)}, bf16[128,128]{1,0:T(8,128)(2,1)}, u32[]{:S(2)}) copy-start(bf16[128,128]{1,0:T(8,128)(2,1)} %right_ref.1) | copy-start | bytes 98308
  1.9 49.9 %copy-start.5 = (bf16[128,128]{1,0:T(8,128)(2,1)S(1)}, bf16[128,128]{1,0:T(8,128)(2,1)}, u32[]{:S(2)}) copy-start(bf16[128,128]{1,0:T(8,128)(2,1)} %left_ref.1) | copy-start | bytes 98308
  1.9 49.9 %copy-start.7 = (f32[128]{0:T(128)S(1)}, f32[128]{0:T(128)}, u32[]{:S(2)}) copy-start(f32[128]{0:T(128)} %param.14) | copy-start | bytes 1540
  1.9 49.9 %copy-start.8 = (f32[1,128]{1,0:T(1,128)S(1)}, f32[1,128]{1,0:T(1,128)}, u32[]{:S(2)}) copy-start(f32[1,128]{1,0:T(1,128)} %constant.11.damping_ref) | copy-start | bytes 1540
  1.9 74.5 %copy-start.1 = (bf16[2,768,128]{2,1,0:T(8,128)(2,1)S(1)}, bf16[2,768,128]{2,1,0:T(8,128)(2,1)}, u32[]{:S(2)}) copy-start(bf16[2,768,128]{2,1,0:T(8,128)(2,1)} %constant.7.clone.table_ref) | copy-start | bytes 1179652
  2.0 5.6 %collective-permute-start = (bf16[2,2,2,48,72]{4,3,2,1,0:T(8,128)(2,1)S(1)}, bf16[2,2,2,48,72]{4,3,2,1,0:T(8,128)(2,1)S(1)}, u32[]{:S(2)}, u32[]{:S(2)}) collective-permute-start(bf16[2,2,2,48,72]{4,3,2,1,0:T(8,128)(2,1)S(1)} %get-tuple-element.19), channel_id=1, source_target_pairs={{0,1},{1,0},{2,3},{3,2},{4,5},{5,4},{6,7},{7,6},{8,9},{9,8},{10,11... | collective-permute-start | bytes 165896 | tf_op jit(solution)/shard_map/ppermute | solution.py:187
  7.6 4.7 %collective-permute-start.1 = (bf16[2,2,2,48,72]{4,3,2,1,0:T(8,128)(2,1)S(1)}, bf16[2,2,2,48,72]{4,3,2,1,0:T(8,128)(2,1)S(1)}, u32[]{:S(2)}, u32[]{:S(2)}) collective-permute-start(bf16[2,2,2,48,72]{4,3,2,1,0:T(8,128)(2,1)S(1)} %get-tuple-element.21), channel_id=1, source_target_pairs={{0,2},{1,3},{2,0},{3,1},{4,6},{5,7},{6,4},{7,5},{8,10},{9,11},{10,... | collective-permute-start | bytes 165896 | tf_op jit(solution)/shard_map/ppermute | solution.py:187
  12.4 4.8 %collective-permute-start.2 = (bf16[2,2,2,48,72]{4,3,2,1,0:T(8,128)(2,1)S(1)}, bf16[2,2,2,48,72]{4,3,2,1,0:T(8,128)(2,1)S(1)}, u32[]{:S(2)}, u32[]{:S(2)}) collective-permute-start(bf16[2,2,2,48,72]{4,3,2,1,0:T(8,128)(2,1)S(1)} %get-tuple-element.23), channel_id=1, source_target_pairs={{0,4},{1,5},{2,6},{3,7},{4,0},{5,1},{6,2},{7,3},{8,12},{9,13},{10,... | collective-permute-start | bytes 165896 | tf_op jit(solution)/shard_map/ppermute | solution.py:187
  17.1 5.7 %collective-permute-start.3 = (bf16[2,2,2,48,72]{4,3,2,1,0:T(8,128)(2,1)S(1)}, bf16[2,2,2,48,72]{4,3,2,1,0:T(8,128)(2,1)S(1)}, u32[]{:S(2)}, u32[]{:S(2)}) collective-permute-start(bf16[2,2,2,48,72]{4,3,2,1,0:T(8,128)(2,1)S(1)} %get-tuple-element.25), channel_id=1, source_target_pairs={{0,8},{1,9},{2,10},{3,11},{4,12},{5,13},{6,14},{7,15},{8,0},{9,1},... | collective-permute-start | bytes 165896 | tf_op jit(solution)/shard_map/ppermute | solution.py:187
  22.9 3.6 %collective-permute-start.4 = (bf16[2,2,2,2,48,72]{5,4,3,2,1,0:T(8,128)(2,1)S(1)}, bf16[2,2,2,2,48,72]{5,4,3,2,1,0:T(8,128)(2,1)S(1)}, u32[]{:S(2)}, u32[]{:S(2)}) collective-permute-start(bf16[2,2,2,2,48,72]{5,4,3,2,1,0:T(8,128)(2,1)S(1)} %shard_map.117.legendre_ref.here_ref), channel_id=1, source_target_pairs={{0,16},{1,17},{2,18},{3,19},{4,20},{5,21},{6,22},{7,23},{8,24},{9,... | collective-permute-start | bytes 331784 | tf_op jit(solution)/shard_map/ppermute | solution.py:187
  27.6 2.2 %collective-permute-start.5 = (bf16[2,2,2,2,72,256]{5,4,3,2,1,0:T(8,128)(2,1)S(1)}, bf16[2,2,2,2,72,256]{5,4,3,2,1,0:T(8,128)(2,1)S(1)}, u32[]{:S(2)}, u32[]{:S(2)}) collective-permute-start(bf16[2,2,2,2,72,256]{5,4,3,2,1,0:T(8,128)(2,1)S(1)} %shard_map.120), channel_id=1, source_target_pairs={{0,16},{1,17},{2,18},{3,19},{4,20},{5,21},{6,22},{7,23},{8,24},{9,... | collective-permute-start | bytes 1769480 | tf_op jit(solution)/shard_map/ppermute | solution.py:187
  29.8 6.8 %collective-permute-start.6 = (bf16[2,2,2,72,256]{4,3,2,1,0:T(8,128)(2,1)S(1)}, bf16[2,2,2,72,256]{4,3,2,1,0:T(8,128)(2,1)S(1)}, u32[]{:S(2)}, u32[]{:S(2)}) collective-permute-start(bf16[2,2,2,72,256]{4,3,2,1,0:T(8,128)(2,1)S(1)} %get-tuple-element.27), channel_id=1, source_target_pairs={{0,1},{1,0},{2,3},{3,2},{4,5},{5,4},{6,7},{7,6},{8,9},{9,8},{10,11... | collective-permute-start | bytes 884744 | tf_op jit(solution)/shard_map/ppermute | solution.py:187
  36.7 5.2 %collective-permute-start.7 = (bf16[2,2,72,256]{3,2,1,0:T(8,128)(2,1)S(1)}, bf16[2,2,72,256]{3,2,1,0:T(8,128)(2,1)S(1)}, u32[]{:S(2)}, u32[]{:S(2)}) collective-permute-start(bf16[2,2,72,256]{3,2,1,0:T(8,128)(2,1)S(1)} %get-tuple-element.29), channel_id=1, source_target_pairs={{0,2},{1,3},{2,0},{3,1},{4,6},{5,7},{6,4},{7,5},{8,10},{9,11},{10,... | collective-permute-start | bytes 442376 | tf_op jit(solution)/shard_map/ppermute | solution.py:187
  41.9 4.5 %collective-permute-start.8 = (bf16[2,72,256]{2,1,0:T(8,128)(2,1)S(1)}, bf16[2,72,256]{2,1,0:T(8,128)(2,1)S(1)}, u32[]{:S(2)}, u32[]{:S(2)}) collective-permute-start(bf16[2,72,256]{2,1,0:T(8,128)(2,1)S(1)} %get-tuple-element.31), channel_id=1, source_target_pairs={{0,4},{1,5},{2,6},{3,7},{4,0},{5,1},{6,2},{7,3},{8,12},{9,13},{10,... | collective-permute-start | bytes 221192 | tf_op jit(solution)/shard_map/ppermute | solution.py:187
  46.4 5.4 %collective-permute-start.9 = (bf16[72,256]{1,0:T(8,128)(2,1)S(1)}, bf16[72,256]{1,0:T(8,128)(2,1)S(1)}, u32[]{:S(2)}, u32[]{:S(2)}) collective-permute-start(bf16[72,256]{1,0:T(8,128)(2,1)S(1)} %get-tuple-element.33), channel_id=1, source_target_pairs={{0,8},{1,9},{2,10},{3,11},{4,12},{5,13},{6,14},{7,15},{8,0},{9,1},... | collective-permute-start | bytes 110600 | tf_op jit(solution)/shard_map/ppermute | solution.py:187
  52.7 5.7 %collective-permute-start.10 = (bf16[72,256]{1,0:T(8,128)(2,1)S(1)}, bf16[72,256]{1,0:T(8,128)(2,1)S(1)}, u32[]{:S(2)}, u32[]{:S(2)}) collective-permute-start(bf16[72,256]{1,0:T(8,128)(2,1)S(1)} %shard_map.125.keep_ref), channel_id=1, source_target_pairs={{0,8},{1,9},{2,10},{3,11},{4,12},{5,13},{6,14},{7,15},{8,0},{9,1},... | collective-permute-start | bytes 110600 | tf_op jit(solution)/shard_map/ppermute | solution.py:187
  58.4 4.4 %collective-permute-start.11 = (bf16[2,72,256]{2,1,0:T(8,128)(2,1)S(1)}, bf16[2,72,256]{2,1,0:T(8,128)(2,1)S(1)}, u32[]{:S(2)}, u32[]{:S(2)}) collective-permute-start(bf16[2,72,256]{2,1,0:T(8,128)(2,1)S(1)} %shard_map.126.keep_ref), channel_id=1, source_target_pairs={{0,4},{1,5},{2,6},{3,7},{4,0},{5,1},{6,2},{7,3},{8,12},{9,13},{10,... | collective-permute-start | bytes 221192 | tf_op jit(solution)/shard_map/ppermute | solution.py:187
  62.8 5.3 %collective-permute-start.12 = (bf16[2,2,72,256]{3,2,1,0:T(8,128)(2,1)S(1)}, bf16[2,2,72,256]{3,2,1,0:T(8,128)(2,1)S(1)}, u32[]{:S(2)}, u32[]{:S(2)}) collective-permute-start(bf16[2,2,72,256]{3,2,1,0:T(8,128)(2,1)S(1)} %shard_map.127.keep_ref), channel_id=1, source_target_pairs={{0,2},{1,3},{2,0},{3,1},{4,6},{5,7},{6,4},{7,5},{8,10},{9,11},{10,... | collective-permute-start | bytes 442376 | tf_op jit(solution)/shard_map/ppermute | solution.py:187
  68.1 6.8 %collective-permute-start.13 = (bf16[2,2,2,72,256]{4,3,2,1,0:T(8,128)(2,1)S(1)}, bf16[2,2,2,72,256]{4,3,2,1,0:T(8,128)(2,1)S(1)}, u32[]{:S(2)}, u32[]{:S(2)}) collective-permute-start(bf16[2,2,2,72,256]{4,3,2,1,0:T(8,128)(2,1)S(1)} %shard_map.128.refs_0_), channel_id=1, source_target_pairs={{0,1},{1,0},{2,3},{3,2},{4,5},{5,4},{6,7},{7,6},{8,9},{9,8},{10,11... | collective-permute-start | bytes 884744 | tf_op jit(solution)/shard_map/ppermute | solution.py:187
  69.7 5.9 %collective-permute-start.14 = (bf16[2,2,2,72,256]{4,3,2,1,0:T(8,128)(2,1)S(1)}, bf16[2,2,2,72,256]{4,3,2,1,0:T(8,128)(2,1)S(1)}, u32[]{:S(2)}, u32[]{:S(2)}) collective-permute-start(bf16[2,2,2,72,256]{4,3,2,1,0:T(8,128)(2,1)S(1)} %shard_map.128.refs_0_), channel_id=1, source_target_pairs={{0,16},{1,17},{2,18},{3,19},{4,20},{5,21},{6,22},{7,23},{8,24},{9,... | collective-permute-start | bytes 884744 | tf_op jit(solution)/shard_map/ppermute | solution.py:187
  74.9 1.6 %collective-permute-start.15 = (bf16[2,2,2,72,256]{4,3,2,1,0:T(8,128)(2,1)S(1)}, bf16[2,2,2,72,256]{4,3,2,1,0:T(8,128)(2,1)S(1)}, u32[]{:S(2)}, u32[]{:S(2)}) collective-permute-start(bf16[2,2,2,72,256]{4,3,2,1,0:T(8,128)(2,1)S(1)} %collective-permute-done.13.refs_1_), channel_id=1, source_target_pairs={{0,16},{1,17},{2,18},{3,19},{4,20},{5,21},{6,22},{7,23},{8,24},{9,... | collective-permute-start | bytes 884744 | tf_op jit(solution)/shard_map/ppermute | solution.py:187

commit v5 on v4

--- a/solution.py
+++ b/solution.py
@@ -148,147 +148,174 @@
     )(*operands)
 
 
-def routes(sec, u, v, a, b):
-    return (a + 2 * b, v, u) if sec == 0 else (2 * a + b, u, v)
-
-
-relative = tuple(np.ndindex(2, 2, 2, 2))
-
-
-def place(sec, u, v, a, b):
+four = range(4)
+
+
+def plane_index():
+    return lax.axis_index("row") % 2 * 2 + lax.axis_index("col")
+
+
+def depth_index():
+    return lax.axis_index("row") // 2
+
+
+def pair_at(sec, deep, flat):
+    row = lax.axis_index("row") ^ (2 * deep + flat // 2)
+    col = lax.axis_index("col") ^ (flat % 2)
     at_sec = lax.axis_index("sec") ^ sec
-    options = []
-    for core in range(2):
-        z, y, x = routes(core, u, v, a, b)
-        options.append((z * 2 + y, x))
-    row = lax.axis_index("row") ^ jnp.where(at_sec == 0, options[0][0], options[1][0])
-    col = lax.axis_index("col") ^ jnp.where(at_sec == 0, options[0][1], options[1][1])
-    return at_sec, row, col
-
-
-def pair_at(sec, where):
-    at_sec, row, col = place(sec, *where)
     return (at_sec * lax.axis_size("row") + row) * lax.axis_size("col") + col
 
 
-def exchange(array, axis):
+def exchange(array, sec=0, deep=0, flat=0):
     sizes = tuple(lax.axis_size(name) for name in names)
     pairs = []
     for source in np.ndindex(*sizes):
-        sec, row, col = source
-        if axis == "sec":
-            target = (sec ^ 1, row, col)
-        else:
-            z, y, x = routes(sec, *(int(axis == name) for name in "uvab"))
-            target = (sec, row ^ (z * 2 + y), col ^ x)
+        target = (source[0] ^ sec, source[1] ^ (2 * deep + flat // 2), source[2] ^ (flat % 2))
         pairs.append(
             (int(np.ravel_multi_index(source, sizes)), int(np.ravel_multi_index(target, sizes)))
         )
     return lax.ppermute(array, names, pairs)
 
 
-def cut_kernel(legendre_ref, keep_ref, send_ref, turned):
-    parts, lat_rows, rows = turned.shape
-    whole = jnp.pad(
-        legendre_ref[0].astype(jnp.float32), ((0, rows - legendre_ref.shape[1]), (0, 0))
-    ).T.astype(jnp.bfloat16)
-    for at in range(parts):
-        turned[at] = whole[at * lat_rows : (at + 1) * lat_rows]
-    for where in relative:
-        _, row, col = place(0, *where)
-        (send_ref if where[0] else keep_ref)[where[1:]] = turned[row * lax.axis_size("col") + col]
-
-
-def pass_kernel(keep_ref, take_ref, keep_out, send_out):
-    for i, j in np.ndindex(2, 2):
-        for source, ref in enumerate((keep_ref, take_ref)):
-            keep_out[i, j, source] = ref[0, i, j]
-            send_out[i, j, source] = ref[1, i, j]
-
-
-def stack_kernel(keep_ref, take_ref, out_ref):
-    out_ref[0] = keep_ref[...]
-    out_ref[1] = take_ref[...]
-
-
-def forward_kernel(table_ref, grid_ref, out_ref, held):
+def cut_kernel(legendre_ref, *refs):
+    outs, slabs = refs[:-1], refs[-1]
+    count, rows, lats = slabs.shape
+    given = legendre_ref.shape[1]
+    slabs[...] = jnp.zeros_like(slabs)
+    for at in range(count):
+        slabs[at, :given] = legendre_ref[0, :, at * lats : (at + 1) * lats]
+    for deep, out in enumerate(outs):
+        out[...] = slabs[depth_index() ^ deep]
+
+
+def forward_kernel(
+    orders_ref, table_ref, grid_ref, keep_ref, send_ref, table, buffer, held, sems, table_sem
+):
     blocks, rows, lat_block, radial = held.shape
     slots = rows // 2
-    table = table_ref[lax.axis_index("sec")]
+
+    def chunk(at):
+        return pltpu.make_async_copy(
+            grid_ref.at[pl.ds(2 * at, 2)], buffer.at[pl.ds(2 * at, 2)], sems.at[at]
+        )
+
+    first = pltpu.make_async_copy(table_ref.at[lax.axis_index("sec")], table, table_sem)
+    first.start()
+    for at in range(sems.shape[0]):
+        chunk(at).start()
+    first.wait()
 
     def one_block(block, carry):
         for at in range(0, lat_block, 2):
             lat = block * lat_block + at
+            chunk(lat // 2).wait()
             two = jnp.concatenate(
-                [grid_ref[lat].astype(jnp.bfloat16), grid_ref[lat + 1].astype(jnp.bfloat16)], axis=1
+                [buffer[lat].astype(jnp.bfloat16), buffer[lat + 1].astype(jnp.bfloat16)], axis=1
             )
-            sums = jnp.dot(table, two, preferred_element_type=jnp.float32)
+            sums = jnp.dot(table[...], two, preferred_element_type=jnp.float32)
             held[block, :, at, :] = sums[:, :radial]
             held[block, :, at + 1, :] = sums[:, radial:]
         return carry
 
     lax.fori_loop(0, blocks, one_block, 0)
-    for block in range(0, blocks, 2):
-        for part in range(2):
-            rows_of = pl.ds(part * slots, slots)
-            both = jnp.concatenate([held[block, rows_of], held[block + 1, rows_of]], axis=1)
-            out_ref[:, pl.ds(block * lat_block, 2 * lat_block), pl.ds(part * radial, radial)] = (
-                both.astype(jnp.bfloat16)
-            )
-
-
-def forward_sums(table, grid_terms, lat_block):
+    for sec, out in ((1, send_ref), (0, keep_ref)):
+        for flat, deep in np.ndindex(4, 4):
+            order = orders_ref[pair_at(sec, deep, flat)]
+            for half, part in np.ndindex(2, 2):
+                values = held[:, part * slots + 2 * order + half]
+                out[flat, deep, half, :, pl.ds(part * radial, radial)] = values.reshape(
+                    blocks * lat_block, radial
+                ).astype(out.dtype)
+
+
+def forward_sums(pair_orders, table, grid_terms, lat_block):
     sections, rows, phi_count = table.shape
     lat_rows, _, radial = grid_terms.shape
     blocks = lat_rows // lat_block
+    sizes = (4, 4, 2, lat_rows, 2 * radial)
+    in_memory = pl.BlockSpec(memory_space=pltpu.HBM)
     return pl.pallas_call(
         forward_kernel,
-        in_specs=[vmem(), vmem()],
-        out_specs=vmem(),
-        out_shape=jax.ShapeDtypeStruct((rows // 2, lat_rows, 2 * radial), jnp.bfloat16),
-        scratch_shapes=[pltpu.VMEM((blocks, rows, lat_block, radial), jnp.float32)],
-        compiler_params=params(8),
+        in_specs=[smem(), in_memory, in_memory],
+        out_specs=[vmem(), vmem()],
+        out_shape=[
+            jax.ShapeDtypeStruct(sizes, jnp.float32),
+            jax.ShapeDtypeStruct(sizes, jnp.bfloat16),
+        ],
+        scratch_shapes=[
+            pltpu.VMEM((rows, phi_count), table.dtype),
+            pltpu.VMEM(grid_terms.shape, jnp.float32),
+            pltpu.VMEM((blocks, rows, lat_block, radial), jnp.float32),
+            pltpu.SemaphoreType.DMA((lat_rows // 2,)),
+            pltpu.SemaphoreType.DMA,
+        ],
+        compiler_params=params(36),
         cost_estimate=pl.CostEstimate(
             flops=2 * rows * phi_count * lat_rows * radial,
             bytes_accessed=4 * lat_rows * phi_count * radial,
             transcendentals=0,
         ),
-    )(table, pltpu.with_memory_space_constraint(grid_terms, pltpu.VMEM))
+    )(pair_orders, table, grid_terms)
+
+
+def add_kernel(keep_ref, take_ref, *outs):
+    for flat, out in enumerate(outs):
+        out[...] = (keep_ref[flat] + take_ref[flat].astype(jnp.float32)).astype(out.dtype)
 
 
 def masked(weights, order, degrees):
-    row_index = lax.broadcasted_iota(jnp.int32, weights.shape, 1)
+    row_index = lax.broadcasted_iota(jnp.int32, weights.shape, 0)
     leading = row_index < degrees - order
     zero = jnp.zeros_like(weights)
     return jnp.where(leading, weights, zero), jnp.where(leading, zero, weights)
 
 
-def degrees_kernel(sec, degrees, orders_ref, legendre_ref, fourier_ref, out_ref):
+def degrees_kernel(degrees, orders_ref, *refs):
+    weights, takes, outs, gathered = refs[:4], refs[4:8], refs[8:12], refs[12]
+    _, _, _, lat_rows, columns = gathered.shape
+    own = plane_index()
+    for flat in four:
+        for deep, half in np.ndindex(4, 2):
+            gathered[deep, half, own ^ flat] = takes[flat][deep, half]
+    for deep in four:
+        chosen = masked(weights[deep][...], orders_ref[pair_at(0, deep, 0)], degrees)
+        total = 0.0
+        for half in range(2):
+            total += jnp.dot(
+                chosen[half],
+                gathered[deep, half].reshape(4 * lat_rows, columns),
+                preferred_element_type=jnp.float32,
+            )
+        outs[deep][...] = total.astype(outs[deep].dtype)
+
+
+def synthesis_kernel(degrees, orders_ref, *refs):
+    weights, fields, outs, spread = refs[:4], refs[4:8], refs[8:12], refs[12]
+    _, _, _, lat_rows, columns = spread.shape
     contract = (((0,), (0,)), ((), ()))
-    for where in relative:
-        order = orders_ref[pair_at(sec, where)]
-        lower, upper = masked(legendre_ref[where[3:] + where[:3]], order, degrees)
-        total = lax.dot_general(
-            lower, fourier_ref[2 * order], contract, preferred_element_type=jnp.float32
-        ) + lax.dot_general(
-            upper, fourier_ref[2 * order + 1], contract, preferred_element_type=jnp.float32
-        )
-        out_ref[where] = total.astype(out_ref.dtype)
-
-
-def halve_kernel(keep_ref, take_ref, keep_out, send_out):
-    keep_out[...] = keep_ref[0] + take_ref[0].astype(jnp.float32)
-    send_out[...] = (keep_ref[1] + take_ref[1].astype(jnp.float32)).astype(jnp.bfloat16)
+    own = plane_index()
+    for deep in four:
+        chosen = masked(weights[deep][...], orders_ref[pair_at(0, deep, 0)], degrees)
+        for half in range(2):
+            values = lax.dot_general(
+                chosen[half], fields[deep][...], contract, preferred_element_type=jnp.float32
+            )
+            spread[deep, half] = values.astype(spread.dtype).reshape(4, lat_rows, columns)
+    for flat in (3, 1, 2, 0):
+        for deep, half in np.ndindex(4, 2):
+            outs[flat][deep, half] = spread[deep, half, own ^ flat]
 
 
 def solve_kernel(
-    orders_ref, keep_ref, take_ref, state_ref, kappa_ref, damping_ref, right_ref, left_ref, sent_ref
+    orders_ref, one, two, three, last, state_ref, kappa_ref, damping_ref, right_ref, left_ref, sent_ref
 ):
     rows = state_ref.shape[1]
     radial = right_ref.shape[0]
     degrees = rows - 1
-    order = orders_ref[pair_at(0, (0, 0, 0, 0))]
-    coefficient = keep_ref[...] + take_ref[...].astype(jnp.float32)
+    order = orders_ref[pair_at(0, 0, 0)]
+    coefficient = one[...]
+    for other in (two, three, last):
+        coefficient += other[...].astype(jnp.float32)
     right_side = state_ref[0].astype(jnp.float32) + time_step * coefficient[:rows]
     right_side = right_side.astype(jnp.bfloat16)
     row_index = lax.broadcasted_iota(jnp.int32, (rows, radial), 0)
@@ -311,21 +338,18 @@
         sent_ref[pl.ds(0, rows), columns] = field
 
 
-def inverse_kernel(degrees, orders_ref, here_ref, there_ref, table_ref, *refs):
-    fields, (out_ref, buffer, held, sems) = refs[:-4], refs[-4:]
+def inverse_kernel(orders_ref, table_ref, *refs):
+    takes, (out_ref, buffer, held, sems) = refs[:-4], refs[-4:]
     blocks, slot_rows, lat_block, radial = held.shape
     slots = slot_rows // 2
-    for sec in range(2):
-        for where in relative:
-            order = orders_ref[pair_at(sec, where)]
-            weights = masked((there_ref if sec else here_ref)[where[3:] + where[:3]], order, degrees)
-            field = fields[2 * sec + where[0]][where[1:]]
-            for half in range(2):
-                rebuilt = jnp.dot(weights[half], field, preferred_element_type=jnp.float32)
-                for part in range(2):
-                    held[:, part * slots + 2 * order + half] = rebuilt[
-                        :, part * radial : (part + 1) * radial
-                    ].reshape(blocks, lat_block, radial)
+
+    for sec, flat, deep in np.ndindex(2, 4, 4):
+        order = orders_ref[pair_at(sec, deep, flat)]
+        for half, part in np.ndindex(2, 2):
+            values = takes[4 * sec + flat][deep, half, :, pl.ds(part * radial, radial)]
+            held[:, part * slots + 2 * order + half] = values.astype(jnp.float32).reshape(
+                blocks, lat_block, radial
+            )
 
     table = table_ref[lax.axis_index("sec")]
 
@@ -355,14 +379,14 @@
         chunk(at).wait()
 
 
-def inverse_values(degrees, pair_orders, legendre, table, fields, lat_rows, lat_block):
+def inverse_values(pair_orders, table, takes, lat_block):
     _, phi_count, slot_rows = table.shape
-    radial = fields[0].shape[-1] // 2
+    lat_rows, radial = takes[0].shape[2], takes[0].shape[3] // 2
     blocks = lat_rows // lat_block
     out = jax.ShapeDtypeStruct((lat_rows, phi_count, radial), jnp.float32)
     return pl.pallas_call(
-        functools.partial(inverse_kernel, degrees),
-        in_specs=[smem()] + [vmem()] * (1 + len(legendre) + len(fields)),
+        inverse_kernel,
+        in_specs=[smem()] + [vmem()] * (1 + len(takes)),
         out_specs=anywhere(),
         out_shape=out,
         scratch_shapes=[
@@ -376,7 +400,7 @@
             bytes_accessed=4 * lat_rows * phi_count * radial,
             transcendentals=0,
         ),
-    )(pair_orders, *legendre, table, *fields)
+    )(pair_orders, table, *takes)
 
 
 def on_device_compact(grid_terms, pair_orders, legendre, state, kappa, right_op, left_op):
@@ -394,62 +418,51 @@
     def shape(*sizes, dtype=jnp.bfloat16):
         return jax.ShapeDtypeStruct(sizes, dtype)
 
-    part = shape(2, 2, 2, lat_rows, padded)
-    keep, send = call(
+    slab = shape(padded, 4 * lat_rows)
+    cuts = call(
         cut_kernel,
         [legendre],
-        [part, part],
-        scratch=[pltpu.VMEM((2 * part.shape[0] * 4, lat_rows, padded), jnp.bfloat16)],
-        cost=pl.CostEstimate(flops=int(1.3e10), bytes_accessed=0, transcendentals=0),
-    )
-    for axis in "uva":
-        keep, send = call(pass_kernel, [keep, exchange(send, axis)], [part, part])
-    here = call(stack_kernel, [keep, exchange(send, "b")], shape(2, 2, 2, 2, lat_rows, padded))
-    legendres = (here, exchange(here, "sec"))
-
-    fourier = forward_sums(forward_table, grid_terms, lat_block)
-
-    def partial_sums(sec, dtype):
-        return call(
-            functools.partial(degrees_kernel, sec, degrees),
-            [pair_orders, legendres[sec], fourier],
-            shape(2, 2, 2, 2, padded, columns, dtype=dtype),
-            mib=24,
-            scalars=1,
-            cost=pl.CostEstimate(
-                flops=2 * pair_total * rows * lat_rows * columns,
-                bytes_accessed=fourier.size * 2,
-                transcendentals=0,
-            ),
-        )
-
-    take = exchange(partial_sums(1, jnp.bfloat16), "sec")
-    keep = partial_sums(0, jnp.float32)
-    rest = (2, 2, 2, padded, columns)
-    for axis in "uvab":
-        keep, send = call(
-            halve_kernel, [keep, take], [shape(*rest, dtype=jnp.float32), shape(*rest)]
-        )
-        take = exchange(send, axis)
-        rest = rest[1:]
+        [slab] * 4,
+        scratch=[pltpu.VMEM((4, padded, 4 * lat_rows), jnp.bfloat16)],
+    )
+    weights = [cuts[0]] + [exchange(cuts[deep], deep=deep) for deep in (1, 2, 3)]
+
+    keep, send = forward_sums(pair_orders, forward_table, grid_terms, lat_block)
+    block = shape(4, 2, lat_rows, columns)
+    blocks = call(add_kernel, [keep, exchange(send, sec=1)], [block] * 4, mib=24)
+    takes = [blocks[0]] + [exchange(blocks[flat], flat=flat) for flat in (1, 2, 3)]
+
+    gathered = pltpu.VMEM((4, 2, 4, lat_rows, columns), jnp.bfloat16)
+    sums = call(
+        functools.partial(degrees_kernel, degrees),
+        [pair_orders, *weights, *takes],
+        [shape(padded, columns, dtype=jnp.float32)] + [shape(padded, columns)] * 3,
+        scalars=1,
+        scratch=[gathered],
+    )
+    sums = [sums[0]] + [exchange(sums[deep], deep=deep) for deep in (1, 2, 3)]
 
     radial_mode = np.arange(radial, dtype=np.float32) / np.float32(radial)
     damping = np.exp(-filter_strength * radial_mode**filter_power).astype(np.float32)
     field = call(
         solve_kernel,
-        [pair_orders, keep, take, state, kappa[None, :], jnp.asarray(damping)[None, :], right_op, left_op],
+        [pair_orders, *sums, state, kappa[None, :], jnp.asarray(damping)[None, :], right_op, left_op],
         shape(padded, columns),
         scalars=1,
     )
     new_state = field[None, :rows]
 
-    for axis in "bav":
-        field = call(stack_kernel, [field, exchange(field, axis)], shape(2, *field.shape))
-    far = exchange(field, "u")
-    fields = (field, far, exchange(field, "sec"), exchange(far, "sec"))
-    evolved = inverse_values(
-        degrees, pair_orders, legendres, inverse_table, fields, lat_rows, lat_block
-    )
+    fields = [field] + [exchange(field, deep=deep) for deep in (1, 2, 3)]
+    blocks = call(
+        functools.partial(synthesis_kernel, degrees),
+        [pair_orders, *weights, *fields],
+        [block] * 4,
+        scalars=1,
+        scratch=[gathered],
+    )
+    takes = [blocks[0]] + [exchange(blocks[flat], flat=flat) for flat in (1, 2, 3)]
+    takes += [exchange(take, sec=1) for take in takes]
+    evolved = inverse_values(pair_orders, inverse_table, takes, lat_block)
     return (evolved, new_state)
 
 

time: 85.6 us -> 68.4 us (0.80)
  waiting for transfers between devices: 39.1 us -> 18.4 us
  Pallas kernels: 16 us -> 21.2 us
  starting transfers between devices: 27.7 us -> 25.5 us
    ppermute x16 -> x20, waiting for transfers between devices: 39.1 us -> 18.4 us  [exchange(): return lax.ppermute(array, names, pairs)]
    pallas_call x2, Pallas kernels: 12.4 us -> 18.2 us  [the longest x1 9.51 us: forward_sums(): pl.pallas_call(forward_kernel, in_specs=[smem(), in_memory, in_memory], o...]
    ppermute x16 -> x20, starting transfers between devices: 27.7 us -> 25.5 us  [exchange(): return lax.ppermute(array, names, pairs)]
    unnamed x20 -> x18, local copies, waits for them, and re-layouts: 1.1 us -> 1.73 us
    pallas_call x15 -> x5, Pallas kernels: 3.59 us -> 2.97 us  [call(): pl.pallas_call(kernel, in_specs=[smem()] * scalars + [vmem()] * (len(oper...]
  transfers between devices with their start and end apart: 16 -> 20, of which waited for: 14 -> 10; matrix products, arithmetic and copies ran while one was open for 1% -> 1% of each run, Pallas kernels for 5% -> 0%
where the time goes in v5:
time: 68.4 us; the launch traced here: 68.3 us
  starting transfers between devices  25.5 us (37%)
  Pallas kernels  21.2 us (31%)
  waiting for transfers between devices  18.4 us (27%)
  local copies, waits for them, and re-layouts  2.35 us (3%)
  between operations  0.76 us (1%)
    ppermute x20, starting transfers between devices, exchange(): return lax.ppermute(array, names, pairs)  25.5 us
    ppermute x20, waiting for transfers between devices, exchange(): return lax.ppermute(array, names, pairs)  18.4 us
    pallas_call x1, Pallas kernels, forward_sums(): pl.pallas_call(forward_kernel, in_specs=[smem(), in_memory, in_memory], o...  9.51 us
    pallas_call x1, Pallas kernels, inverse_values(): pl.pallas_call(inverse_kernel, in_specs=[smem()] + [vmem()] * (1 + len(ta...  8.72 us
    pallas_call x5, Pallas kernels, call(): pl.pallas_call(kernel, in_specs=[smem()] * scalars + [vmem()] * (len(oper...  2.97 us
    unnamed x18, local copies, waits for them, and re-layouts  1.73 us
  transfers between devices with their start and end apart: 20, of which 10 were waited for; matrix products, arithmetic and copies ran while one was open for 1% of the time, Pallas kernels for 0%

profile of v5, /device:TPU:0, one launch (start us, length us, event | category | flops | bytes accessed | tf_op | source)
XLA Modules:
  0.0 68.3 jit_solution(8308951703082093287)
XLA Ops:
  0.7 1.0 %copy-done.1 = bf16[2,128,768]{2,1,0:T(8,128)(2,1)S(1)} copy-done((bf16[2,128,768]{2,1,0:T(8,128)(2,1)S(1)}, bf16[2,128,768]{2,1,0:T(8,128)(2,1)}, u32[]{:S(2)}) %copy-start.1) | copy-done | bytes 393240
  1.7 0.7 copy-done.6
  2.4 9.5 %shard_map.114 = (f32[4,4,2,48,256]{4,3,2,1,0:T(8,128)S(1)}, bf16[4,4,2,48,256]{4,3,2,1,0:T(8,128)(2,1)S(1)}) custom-call(s32[32]{0:T(128)S(1)} %copy-done.6, bf16[2,128,768]{2,1,0:T(8,128)(2,1)S(1)} %copy-done.1, f32[48,768,128]{2,1,0:T(8,128)} %grid_ref.1), custom_call_target="tpu_custom_call" | custom-call | flops 1207959552 | bytes 18874368 | tf_op jit(solution)/shard_map/pallas_call | solution.py:237
  11.9 0.5 collective-permute-start.3
  12.4 1.9 %collective-permute-done.3.take_ref = bf16[4,4,2,48,256]{4,3,2,1,0:T(8,128)(2,1)S(1)} collective-permute-done((bf16[4,4,2,48,256]{4,3,2,1,0:T(8,128)(2,1)S(1)}, bf16[4,4,2,48,256]{4,3,2,1,0:T(8,128)(2,1)S(1)}, u32[]{:S(2)}, u32[]{:S(2)}) %collective-permute-start.3) | collective-permute-done | bytes 786464 | tf_op jit(solution)/shard_map/ppermute | solution.py:177
  14.5 2.9 %collective-permute-start.4 = (bf16[4,2,48,256]{3,2,1,0:T(8,128)(2,1)S(1)}, bf16[4,2,48,256]{3,2,1,0:T(8,128)(2,1)S(1)}, u32[]{:S(2)}, u32[]{:S(2)}) collective-permute-start(bf16[4,2,48,256]{3,2,1,0:T(8,128)(2,1)S(1)} %get-tuple-element.27), channel_id=1, source_target_pairs={{0,1},{1,0},{2,3},{3,2},{4,5},{5,4},{6,7},{7,6},{8,9},{9,8},{10,11... | collective-permute-start | bytes 589832 | tf_op jit(solution)/shard_map/ppermute | solution.py:177
  17.4 1.5 %collective-permute-start.5 = (bf16[4,2,48,256]{3,2,1,0:T(8,128)(2,1)S(1)}, bf16[4,2,48,256]{3,2,1,0:T(8,128)(2,1)S(1)}, u32[]{:S(2)}, u32[]{:S(2)}) collective-permute-start(bf16[4,2,48,256]{3,2,1,0:T(8,128)(2,1)S(1)} %get-tuple-element.28), channel_id=1, source_target_pairs={{0,2},{1,3},{2,0},{3,1},{4,6},{5,7},{6,4},{7,5},{8,10},{9,11},{10,... | collective-permute-start | bytes 589832 | tf_op jit(solution)/shard_map/ppermute | solution.py:177
  19.1 2.1 %collective-permute-start = (bf16[72,192]{1,0:T(8,128)(2,1)S(1)}, bf16[72,192]{1,0:T(8,128)(2,1)S(1)}, u32[]{:S(2)}, u32[]{:S(2)}) collective-permute-start(bf16[72,192]{1,0:T(8,128)(2,1)S(1)} %get-tuple-element.21), channel_id=1, source_target_pairs={{0,4},{1,5},{2,6},{3,7},{4,0},{5,1},{6,2},{7,3},{8,12},{9,13},{10,... | collective-permute-start | bytes 82952 | tf_op jit(solution)/shard_map/ppermute | solution.py:177
  21.2 2.6 %collective-permute-start.1 = (bf16[72,192]{1,0:T(8,128)(2,1)S(1)}, bf16[72,192]{1,0:T(8,128)(2,1)S(1)}, u32[]{:S(2)}, u32[]{:S(2)}) collective-permute-start(bf16[72,192]{1,0:T(8,128)(2,1)S(1)} %get-tuple-element.22), channel_id=1, source_target_pairs={{0,8},{1,9},{2,10},{3,11},{4,12},{5,13},{6,14},{7,15},{8,0},{9,1},... | collective-permute-start | bytes 82952 | tf_op jit(solution)/shard_map/ppermute | solution.py:177
  23.8 3.4 %collective-permute-start.2 = (bf16[72,192]{1,0:T(8,128)(2,1)S(1)}, bf16[72,192]{1,0:T(8,128)(2,1)S(1)}, u32[]{:S(2)}, u32[]{:S(2)}) collective-permute-start(bf16[72,192]{1,0:T(8,128)(2,1)S(1)} %get-tuple-element.23), channel_id=1, source_target_pairs={{0,12},{1,13},{2,14},{3,15},{4,8},{5,9},{6,10},{7,11},{8,4},{9,5},... | collective-permute-start | bytes 82952 | tf_op jit(solution)/shard_map/ppermute | solution.py:177
  27.2 2.4 %collective-permute-done.2.refs_3_ = bf16[72,192]{1,0:T(8,128)(2,1)S(1)} collective-permute-done((bf16[72,192]{1,0:T(8,128)(2,1)S(1)}, bf16[72,192]{1,0:T(8,128)(2,1)S(1)}, u32[]{:S(2)}, u32[]{:S(2)}) %collective-permute-start.2) | collective-permute-done | bytes 27680 | tf_op jit(solution)/shard_map/ppermute | solution.py:177
  29.5 0.9 %shard_map.116 = (f32[72,256]{1,0:T(8,128)S(1)}, bf16[72,256]{1,0:T(8,128)(2,1)S(1)}, bf16[72,256]{1,0:T(8,128)(2,1)S(1)}, bf16[72,256]{1,0:T(8,128)(2,1)S(1)}) custom-call(s32[32]{0:T(128)S(1)} %copy-done.6, bf16[72,192]{1,0:T(8,128)(2,1)S(1)} %get-tuple-element.20.refs_0_, bf16[72,192]{1,0:T(8,128)(2,1)S(1)} %collective-permute-done.refs_1_, ...), custom_call_target="tpu_custom_call" | custom-call | tf_op jit(solution)/shard_map/pallas_call | solution.py:140
  30.4 0.4 collective-permute-start.7
  30.8 3.6 %collective-permute-start.8 = (bf16[72,256]{1,0:T(8,128)(2,1)S(1)}, bf16[72,256]{1,0:T(8,128)(2,1)S(1)}, u32[]{:S(2)}, u32[]{:S(2)}) collective-permute-start(bf16[72,256]{1,0:T(8,128)(2,1)S(1)} %get-tuple-element.32), channel_id=1, source_target_pairs={{0,8},{1,9},{2,10},{3,11},{4,12},{5,13},{6,14},{7,15},{8,0},{9,1},... | collective-permute-start | bytes 110600 | tf_op jit(solution)/shard_map/ppermute | solution.py:177
  34.4 0.4 collective-permute-start.9
  34.9 1.5 %collective-permute-done.8.three = bf16[72,256]{1,0:T(8,128)(2,1)S(1)} collective-permute-done((bf16[72,256]{1,0:T(8,128)(2,1)S(1)}, bf16[72,256]{1,0:T(8,128)(2,1)S(1)}, u32[]{:S(2)}, u32[]{:S(2)}) %collective-permute-start.8) | collective-permute-done | bytes 36896 | tf_op jit(solution)/shard_map/ppermute | solution.py:177
  36.4 3.8 %collective-permute-done.9.last = bf16[72,256]{1,0:T(8,128)(2,1)S(1)} collective-permute-done((bf16[72,256]{1,0:T(8,128)(2,1)S(1)}, bf16[72,256]{1,0:T(8,128)(2,1)S(1)}, u32[]{:S(2)}, u32[]{:S(2)}) %collective-permute-start.9) | collective-permute-done | bytes 36896 | tf_op jit(solution)/shard_map/ppermute | solution.py:177
  40.2 0.8 %shard_map.117.refs_4_ = bf16[72,256]{1,0:T(8,128)(2,1)S(1)} custom-call(s32[32]{0:T(128)S(1)} %copy-done.6, f32[72,256]{1,0:T(8,128)S(1)} %get-tuple-element.30.one, bf16[72,256]{1,0:T(8,128)(2,1)S(1)} %collective-permute-done.7.two, bf16[72,256]{1,0:T(8,128)(2,1)S(1)} %collective-permute-done.8.three, bf16[72,256]{1,0:T(8,128)(2,1)S(1)} %collective-permute-done.9.last, ...), custom_call_target="tpu_custom_call" | custom-call | tf_op jit(solution)/shard_map/pallas_call | solution.py:140
  41.1 0.5 collective-permute-start.12
  41.6 3.9 %collective-permute-start.10 = (bf16[72,256]{1,0:T(8,128)(2,1)S(1)}, bf16[72,256]{1,0:T(8,128)(2,1)S(1)}, u32[]{:S(2)}, u32[]{:S(2)}) collective-permute-start(bf16[72,256]{1,0:T(8,128)(2,1)S(1)} %shard_map.117.refs_4_), channel_id=1, source_target_pairs={{0,4},{1,5},{2,6},{3,7},{4,0},{5,1},{6,2},{7,3},{8,12},{9,13},{10,... | collective-permute-start | bytes 110600 | tf_op jit(solution)/shard_map/ppermute | solution.py:177
  45.5 1.4 %collective-permute-done.12.refs_7_ = bf16[72,256]{1,0:T(8,128)(2,1)S(1)} collective-permute-done((bf16[72,256]{1,0:T(8,128)(2,1)S(1)}, bf16[72,256]{1,0:T(8,128)(2,1)S(1)}, u32[]{:S(2)}, u32[]{:S(2)}) %collective-permute-start.12) | collective-permute-done | bytes 36896 | tf_op jit(solution)/shard_map/ppermute | solution.py:177
  46.9 0.6 collective-permute-done.10.refs_5_
  47.4 1.0 %shard_map.118 = (bf16[4,2,48,256]{3,2,1,0:T(8,128)(2,1)S(1)}, bf16[4,2,48,256]{3,2,1,0:T(8,128)(2,1)S(1)}, bf16[4,2,48,256]{3,2,1,0:T(8,128)(2,1)S(1)}, bf16[4,2,48,256]{3,2,1,0:T(8,128)(2,1)S(1)}) custom-call(s32[32]{0:T(128)S(1)} %copy-done.6, bf16[72,192]{1,0:T(8,128)(2,1)S(1)} %get-tuple-element.20.refs_0_, ...), custom_call_target="tpu_custom_call" | custom-call | tf_op jit(solution)/shard_map/pallas_call | solution.py:140
  48.5 1.6 %collective-permute-start.13 = (bf16[4,2,48,256]{3,2,1,0:T(8,128)(2,1)S(1)}, bf16[4,2,48,256]{3,2,1,0:T(8,128)(2,1)S(1)}, u32[]{:S(2)}, u32[]{:S(2)}) collective-permute-start(bf16[4,2,48,256]{3,2,1,0:T(8,128)(2,1)S(1)} %get-tuple-element.35), channel_id=1, source_target_pairs={{0,1},{1,0},{2,3},{3,2},{4,5},{5,4},{6,7},{7,6},{8,9},{9,8},{10,11... | collective-permute-start | bytes 589832 | tf_op jit(solution)/shard_map/ppermute | solution.py:177
  50.0 1.5 %collective-permute-start.14 = (bf16[4,2,48,256]{3,2,1,0:T(8,128)(2,1)S(1)}, bf16[4,2,48,256]{3,2,1,0:T(8,128)(2,1)S(1)}, u32[]{:S(2)}, u32[]{:S(2)}) collective-permute-start(bf16[4,2,48,256]{3,2,1,0:T(8,128)(2,1)S(1)} %get-tuple-element.36), channel_id=1, source_target_pairs={{0,2},{1,3},{2,0},{3,1},{4,6},{5,7},{6,4},{7,5},{8,10},{9,11},{10,... | collective-permute-start | bytes 589832 | tf_op jit(solution)/shard_map/ppermute | solution.py:177
  51.5 0.5 collective-permute-start.15
  52.0 2.2 %collective-permute-done.13.refs_1_ = bf16[4,2,48,256]{3,2,1,0:T(8,128)(2,1)S(1)} collective-permute-done((bf16[4,2,48,256]{3,2,1,0:T(8,128)(2,1)S(1)}, bf16[4,2,48,256]{3,2,1,0:T(8,128)(2,1)S(1)}, u32[]{:S(2)}, u32[]{:S(2)}) %collective-permute-start.13) | collective-permute-done | bytes 196640 | tf_op jit(solution)/shard_map/ppermute | solution.py:177
  54.2 2.7 %collective-permute-done.14.refs_2_ = bf16[4,2,48,256]{3,2,1,0:T(8,128)(2,1)S(1)} collective-permute-done((bf16[4,2,48,256]{3,2,1,0:T(8,128)(2,1)S(1)}, bf16[4,2,48,256]{3,2,1,0:T(8,128)(2,1)S(1)}, u32[]{:S(2)}, u32[]{:S(2)}) %collective-permute-start.14) | collective-permute-done | bytes 196640 | tf_op jit(solution)/shard_map/ppermute | solution.py:177
  56.9 1.2 %collective-permute-done.15.refs_3_ = bf16[4,2,48,256]{3,2,1,0:T(8,128)(2,1)S(1)} collective-permute-done((bf16[4,2,48,256]{3,2,1,0:T(8,128)(2,1)S(1)}, bf16[4,2,48,256]{3,2,1,0:T(8,128)(2,1)S(1)}, u32[]{:S(2)}, u32[]{:S(2)}) %collective-permute-start.15) | collective-permute-done | bytes 196640 | tf_op jit(solution)/shard_map/ppermute | solution.py:177
  58.1 0.6 slice_bitcast_fusion
  58.7 0.8 %collective-permute-done.19.refs_7_ = bf16[4,2,48,256]{3,2,1,0:T(8,128)(2,1)S(1)} collective-permute-done((bf16[4,2,48,256]{3,2,1,0:T(8,128)(2,1)S(1)}, bf16[4,2,48,256]{3,2,1,0:T(8,128)(2,1)S(1)}, u32[]{:S(2)}, u32[]{:S(2)}) %collective-permute-start.19) | collective-permute-done | bytes 196640 | tf_op jit(solution)/shard_map/ppermute | solution.py:177
  59.6 8.7 %shard_map.119 = f32[48,768,128]{2,1,0:T(8,128)} custom-call(s32[32]{0:T(128)S(1)} %copy-done.6, bf16[2,768,128]{2,1,0:T(8,128)(2,1)S(1)} %copy-done, bf16[4,2,48,256]{3,2,1,0:T(8,128)(2,1)S(1)} %get-tuple-element.34.refs_0_, bf16[4,2,48,256]{3,2,1,0:T(8,128)(2,1)S(1)} %collective-permute-done.13.refs_1_, ...), custom_call_target="tpu_custom_call" | custom-call | flops 1207959552 | bytes 18874368 | tf_op jit(solution)/shard_map/pallas_call | solution.py:387
  (34 shorter events, 0.4 us)
Async XLA Ops:
  0.6 39.6 %copy-start.8 = (f32[1,128]{1,0:T(1,128)S(1)}, f32[1,128]{1,0:T(1,128)}, u32[]{:S(2)}) copy-start(f32[1,128]{1,0:T(1,128)} %constant.11.damping_ref) | copy-start | bytes 1540
  0.6 58.9 %copy-start = (bf16[2,768,128]{2,1,0:T(8,128)(2,1)S(1)}, bf16[2,768,128]{2,1,0:T(8,128)(2,1)}, u32[]{:S(2)}) copy-start(bf16[2,768,128]{2,1,0:T(8,128)(2,1)} %constant.7.clone.table_ref) | copy-start | bytes 1179652
  0.7 1.0 %copy-start.1 = (bf16[2,128,768]{2,1,0:T(8,128)(2,1)S(1)}, bf16[2,128,768]{2,1,0:T(8,128)(2,1)}, u32[]{:S(2)}) copy-start(bf16[2,128,768]{2,1,0:T(8,128)(2,1)} %constant.6.clone.table_ref) | copy-start | bytes 1179652
  1.7 0.7 copy-start.6
  2.4 16.6 %copy-start.2 = (bf16[1,65,768]{2,1,0:T(8,128)(2,1)S(1)}, bf16[1,65,768]{2,1,0:T(8,128)(2,1)}, u32[]{:S(2)}) copy-start(bf16[1,65,768]{2,1,0:T(8,128)(2,1)} %legendre_ref.1) | copy-start | bytes 299524
  2.4 37.8 %copy-start.3 = (bf16[1,65,256]{2,1,0:T(8,128)(2,1)S(1)}, bf16[1,65,256]{2,1,0:T(8,128)(2,1)}, u32[]{:S(2)}) copy-start(bf16[1,65,256]{2,1,0:T(8,128)(2,1)} %state_ref.1) | copy-start | bytes 99844
  2.4 37.8 %copy-start.4 = (bf16[128,128]{1,0:T(8,128)(2,1)S(1)}, bf16[128,128]{1,0:T(8,128)(2,1)}, u32[]{:S(2)}) copy-start(bf16[128,128]{1,0:T(8,128)(2,1)} %right_ref.1) | copy-start | bytes 98308
  2.4 37.8 %copy-start.5 = (bf16[128,128]{1,0:T(8,128)(2,1)S(1)}, bf16[128,128]{1,0:T(8,128)(2,1)}, u32[]{:S(2)}) copy-start(bf16[128,128]{1,0:T(8,128)(2,1)} %left_ref.1) | copy-start | bytes 98308
  2.4 37.8 %copy-start.7 = (f32[128]{0:T(128)S(1)}, f32[128]{0:T(128)}, u32[]{:S(2)}) copy-start(f32[128]{0:T(128)} %param.14) | copy-start | bytes 1540
  11.9 2.4 %collective-permute-start.3 = (bf16[4,4,2,48,256]{4,3,2,1,0:T(8,128)(2,1)S(1)}, bf16[4,4,2,48,256]{4,3,2,1,0:T(8,128)(2,1)S(1)}, u32[]{:S(2)}, u32[]{:S(2)}) collective-permute-start(bf16[4,4,2,48,256]{4,3,2,1,0:T(8,128)(2,1)S(1)} %get-tuple-element.25), channel_id=1, source_target_pairs={{0,16},{1,17},{2,18},{3,19},{4,20},{5,21},{6,22},{7,23},{8,24},{9,... | collective-permute-start | bytes 2359304 | tf_op jit(solution)/shard_map/ppermute | solution.py:177
  14.5 15.0 %collective-permute-start.4 = (bf16[4,2,48,256]{3,2,1,0:T(8,128)(2,1)S(1)}, bf16[4,2,48,256]{3,2,1,0:T(8,128)(2,1)S(1)}, u32[]{:S(2)}, u32[]{:S(2)}) collective-permute-start(bf16[4,2,48,256]{3,2,1,0:T(8,128)(2,1)S(1)} %get-tuple-element.27), channel_id=1, source_target_pairs={{0,1},{1,0},{2,3},{3,2},{4,5},{5,4},{6,7},{7,6},{8,9},{9,8},{10,11... | collective-permute-start | bytes 589832 | tf_op jit(solution)/shard_map/ppermute | solution.py:177
  17.4 12.1 %collective-permute-start.5 = (bf16[4,2,48,256]{3,2,1,0:T(8,128)(2,1)S(1)}, bf16[4,2,48,256]{3,2,1,0:T(8,128)(2,1)S(1)}, u32[]{:S(2)}, u32[]{:S(2)}) collective-permute-start(bf16[4,2,48,256]{3,2,1,0:T(8,128)(2,1)S(1)} %get-tuple-element.28), channel_id=1, source_target_pairs={{0,2},{1,3},{2,0},{3,1},{4,6},{5,7},{6,4},{7,5},{8,10},{9,11},{10,... | collective-permute-start | bytes 589832 | tf_op jit(solution)/shard_map/ppermute | solution.py:177
  18.9 10.6 %collective-permute-start.6 = (bf16[4,2,48,256]{3,2,1,0:T(8,128)(2,1)S(1)}, bf16[4,2,48,256]{3,2,1,0:T(8,128)(2,1)S(1)}, u32[]{:S(2)}, u32[]{:S(2)}) collective-permute-start(bf16[4,2,48,256]{3,2,1,0:T(8,128)(2,1)S(1)} %get-tuple-element.29), channel_id=1, source_target_pairs={{0,3},{1,2},{2,1},{3,0},{4,7},{5,6},{6,5},{7,4},{8,11},{9,10},{10,... | collective-permute-start | bytes 589832 | tf_op jit(solution)/shard_map/ppermute | solution.py:177
  19.1 4.7 %collective-permute-start = (bf16[72,192]{1,0:T(8,128)(2,1)S(1)}, bf16[72,192]{1,0:T(8,128)(2,1)S(1)}, u32[]{:S(2)}, u32[]{:S(2)}) collective-permute-start(bf16[72,192]{1,0:T(8,128)(2,1)S(1)} %get-tuple-element.21), channel_id=1, source_target_pairs={{0,4},{1,5},{2,6},{3,7},{4,0},{5,1},{6,2},{7,3},{8,12},{9,13},{10,... | collective-permute-start | bytes 82952 | tf_op jit(solution)/shard_map/ppermute | solution.py:177
  21.2 6.0 %collective-permute-start.1 = (bf16[72,192]{1,0:T(8,128)(2,1)S(1)}, bf16[72,192]{1,0:T(8,128)(2,1)S(1)}, u32[]{:S(2)}, u32[]{:S(2)}) collective-permute-start(bf16[72,192]{1,0:T(8,128)(2,1)S(1)} %get-tuple-element.22), channel_id=1, source_target_pairs={{0,8},{1,9},{2,10},{3,11},{4,12},{5,13},{6,14},{7,15},{8,0},{9,1},... | collective-permute-start | bytes 82952 | tf_op jit(solution)/shard_map/ppermute | solution.py:177
  23.8 5.8 %collective-permute-start.2 = (bf16[72,192]{1,0:T(8,128)(2,1)S(1)}, bf16[72,192]{1,0:T(8,128)(2,1)S(1)}, u32[]{:S(2)}, u32[]{:S(2)}) collective-permute-start(bf16[72,192]{1,0:T(8,128)(2,1)S(1)} %get-tuple-element.23), channel_id=1, source_target_pairs={{0,12},{1,13},{2,14},{3,15},{4,8},{5,9},{6,10},{7,11},{8,4},{9,5},... | collective-permute-start | bytes 82952 | tf_op jit(solution)/shard_map/ppermute | solution.py:177
  30.4 4.5 %collective-permute-start.7 = (bf16[72,256]{1,0:T(8,128)(2,1)S(1)}, bf16[72,256]{1,0:T(8,128)(2,1)S(1)}, u32[]{:S(2)}, u32[]{:S(2)}) collective-permute-start(bf16[72,256]{1,0:T(8,128)(2,1)S(1)} %get-tuple-element.31), channel_id=1, source_target_pairs={{0,4},{1,5},{2,6},{3,7},{4,0},{5,1},{6,2},{7,3},{8,12},{9,13},{10,... | collective-permute-start | bytes 110600 | tf_op jit(solution)/shard_map/ppermute | solution.py:177
  30.8 5.6 %collective-permute-start.8 = (bf16[72,256]{1,0:T(8,128)(2,1)S(1)}, bf16[72,256]{1,0:T(8,128)(2,1)S(1)}, u32[]{:S(2)}, u32[]{:S(2)}) collective-permute-start(bf16[72,256]{1,0:T(8,128)(2,1)S(1)} %get-tuple-element.32), channel_id=1, source_target_pairs={{0,8},{1,9},{2,10},{3,11},{4,12},{5,13},{6,14},{7,15},{8,0},{9,1},... | collective-permute-start | bytes 110600 | tf_op jit(solution)/shard_map/ppermute | solution.py:177
  34.4 5.8 %collective-permute-start.9 = (bf16[72,256]{1,0:T(8,128)(2,1)S(1)}, bf16[72,256]{1,0:T(8,128)(2,1)S(1)}, u32[]{:S(2)}, u32[]{:S(2)}) collective-permute-start(bf16[72,256]{1,0:T(8,128)(2,1)S(1)} %get-tuple-element.33), channel_id=1, source_target_pairs={{0,12},{1,13},{2,14},{3,15},{4,8},{5,9},{6,10},{7,11},{8,4},{9,5},... | collective-permute-start | bytes 110600 | tf_op jit(solution)/shard_map/ppermute | solution.py:177
  41.1 5.8 %collective-permute-start.12 = (bf16[72,256]{1,0:T(8,128)(2,1)S(1)}, bf16[72,256]{1,0:T(8,128)(2,1)S(1)}, u32[]{:S(2)}, u32[]{:S(2)}) collective-permute-start(bf16[72,256]{1,0:T(8,128)(2,1)S(1)} %shard_map.117.refs_4_), channel_id=1, source_target_pairs={{0,12},{1,13},{2,14},{3,15},{4,8},{5,9},{6,10},{7,11},{8,4},{9,5},... | collective-permute-start | bytes 110600 | tf_op jit(solution)/shard_map/ppermute | solution.py:177
  41.6 5.3 %collective-permute-start.11 = (bf16[72,256]{1,0:T(8,128)(2,1)S(1)}, bf16[72,256]{1,0:T(8,128)(2,1)S(1)}, u32[]{:S(2)}, u32[]{:S(2)}) collective-permute-start(bf16[72,256]{1,0:T(8,128)(2,1)S(1)} %shard_map.117.refs_4_), channel_id=1, source_target_pairs={{0,8},{1,9},{2,10},{3,11},{4,12},{5,13},{6,14},{7,15},{8,0},{9,1},... | collective-permute-start | bytes 110600 | tf_op jit(solution)/shard_map/ppermute | solution.py:177
  41.6 5.9 %collective-permute-start.10 = (bf16[72,256]{1,0:T(8,128)(2,1)S(1)}, bf16[72,256]{1,0:T(8,128)(2,1)S(1)}, u32[]{:S(2)}, u32[]{:S(2)}) collective-permute-start(bf16[72,256]{1,0:T(8,128)(2,1)S(1)} %shard_map.117.refs_4_), channel_id=1, source_target_pairs={{0,4},{1,5},{2,6},{3,7},{4,0},{5,1},{6,2},{7,3},{8,12},{9,13},{10,... | collective-permute-start | bytes 110600 | tf_op jit(solution)/shard_map/ppermute | solution.py:177
  48.5 5.7 %collective-permute-start.13 = (bf16[4,2,48,256]{3,2,1,0:T(8,128)(2,1)S(1)}, bf16[4,2,48,256]{3,2,1,0:T(8,128)(2,1)S(1)}, u32[]{:S(2)}, u32[]{:S(2)}) collective-permute-start(bf16[4,2,48,256]{3,2,1,0:T(8,128)(2,1)S(1)} %get-tuple-element.35), channel_id=1, source_target_pairs={{0,1},{1,0},{2,3},{3,2},{4,5},{5,4},{6,7},{7,6},{8,9},{9,8},{10,11... | collective-permute-start | bytes 589832 | tf_op jit(solution)/shard_map/ppermute | solution.py:177
  50.0 6.8 %collective-permute-start.14 = (bf16[4,2,48,256]{3,2,1,0:T(8,128)(2,1)S(1)}, bf16[4,2,48,256]{3,2,1,0:T(8,128)(2,1)S(1)}, u32[]{:S(2)}, u32[]{:S(2)}) collective-permute-start(bf16[4,2,48,256]{3,2,1,0:T(8,128)(2,1)S(1)} %get-tuple-element.36), channel_id=1, source_target_pairs={{0,2},{1,3},{2,0},{3,1},{4,6},{5,7},{6,4},{7,5},{8,10},{9,11},{10,... | collective-permute-start | bytes 589832 | tf_op jit(solution)/shard_map/ppermute | solution.py:177
  51.5 6.6 %collective-permute-start.15 = (bf16[4,2,48,256]{3,2,1,0:T(8,128)(2,1)S(1)}, bf16[4,2,48,256]{3,2,1,0:T(8,128)(2,1)S(1)}, u32[]{:S(2)}, u32[]{:S(2)}) collective-permute-start(bf16[4,2,48,256]{3,2,1,0:T(8,128)(2,1)S(1)} %get-tuple-element.37), channel_id=1, source_target_pairs={{0,3},{1,2},{2,1},{3,0},{4,7},{5,6},{6,5},{7,4},{8,11},{9,10},{10,... | collective-permute-start | bytes 589832 | tf_op jit(solution)/shard_map/ppermute | solution.py:177
  52.0 6.7 %collective-permute-start.16 = (bf16[4,2,48,256]{3,2,1,0:T(8,128)(2,1)S(1)}, bf16[4,2,48,256]{3,2,1,0:T(8,128)(2,1)S(1)}, u32[]{:S(2)}, u32[]{:S(2)}) collective-permute-start(bf16[4,2,48,256]{3,2,1,0:T(8,128)(2,1)S(1)} %get-tuple-element.34.refs_0_), channel_id=1, source_target_pairs={{0,16},{1,17},{2,18},{3,19},{4,20},{5,21},{6,22},{7,23},{8,24},{9,... | collective-permute-start | bytes 589832 | tf_op jit(solution)/shard_map/ppermute | solution.py:177
  54.2 4.5 %collective-permute-start.17 = (bf16[4,2,48,256]{3,2,1,0:T(8,128)(2,1)S(1)}, bf16[4,2,48,256]{3,2,1,0:T(8,128)(2,1)S(1)}, u32[]{:S(2)}, u32[]{:S(2)}) collective-permute-start(bf16[4,2,48,256]{3,2,1,0:T(8,128)(2,1)S(1)} %collective-permute-done.13.refs_1_), channel_id=1, source_target_pairs={{0,16},{1,17},{2,18},{3,19},{4,20},{5,21},{6,22},{7,23},{8,24},{9,... | collective-permute-start | bytes 589832 | tf_op jit(solution)/shard_map/ppermute | solution.py:177
  56.9 1.9 %collective-permute-start.18 = (bf16[4,2,48,256]{3,2,1,0:T(8,128)(2,1)S(1)}, bf16[4,2,48,256]{3,2,1,0:T(8,128)(2,1)S(1)}, u32[]{:S(2)}, u32[]{:S(2)}) collective-permute-start(bf16[4,2,48,256]{3,2,1,0:T(8,128)(2,1)S(1)} %collective-permute-done.14.refs_2_), channel_id=1, source_target_pairs={{0,16},{1,17},{2,18},{3,19},{4,20},{5,21},{6,22},{7,23},{8,24},{9,... | collective-permute-start | bytes 589832 | tf_op jit(solution)/shard_map/ppermute | solution.py:177
  58.1 1.4 %collective-permute-start.19 = (bf16[4,2,48,256]{3,2,1,0:T(8,128)(2,1)S(1)}, bf16[4,2,48,256]{3,2,1,0:T(8,128)(2,1)S(1)}, u32[]{:S(2)}, u32[]{:S(2)}) collective-permute-start(bf16[4,2,48,256]{3,2,1,0:T(8,128)(2,1)S(1)} %collective-permute-done.15.refs_3_), channel_id=1, source_target_pairs={{0,16},{1,17},{2,18},{3,19},{4,20},{5,21},{6,22},{7,23},{8,24},{9,... | collective-permute-start | bytes 589832 | tf_op jit(solution)/shard_map/ppermute | solution.py:177

commit v6 on v5

--- a/solution.py
+++ b/solution.py
@@ -189,9 +189,9 @@
 
 
 def forward_kernel(
-    orders_ref, table_ref, grid_ref, keep_ref, send_ref, table, buffer, held, sems, table_sem
+    orders_from, table_ref, grid_ref, keep_ref, send_ref, orders_ref, table, buffer, held, sems, more
 ):
-    blocks, rows, lat_block, radial = held.shape
+    rows, lat_block, radial = held.shape
     slots = rows // 2
 
     def chunk(at):
@@ -199,55 +199,59 @@
             grid_ref.at[pl.ds(2 * at, 2)], buffer.at[pl.ds(2 * at, 2)], sems.at[at]
         )
 
-    first = pltpu.make_async_copy(table_ref.at[lax.axis_index("sec")], table, table_sem)
-    first.start()
+    table_copy = pltpu.make_async_copy(table_ref.at[lax.axis_index("sec")], table, more.at[0])
+    orders_copy = pltpu.make_async_copy(orders_from, orders_ref, more.at[1])
+    table_copy.start()
+    orders_copy.start()
     for at in range(sems.shape[0]):
         chunk(at).start()
-    first.wait()
+    table_copy.wait()
+    orders_copy.wait()
 
     def one_block(block, carry):
+        begin = pl.multiple_of(block * lat_block, lat_block)
         for at in range(0, lat_block, 2):
-            lat = block * lat_block + at
+            lat = begin + at
             chunk(lat // 2).wait()
             two = jnp.concatenate(
                 [buffer[lat].astype(jnp.bfloat16), buffer[lat + 1].astype(jnp.bfloat16)], axis=1
             )
             sums = jnp.dot(table[...], two, preferred_element_type=jnp.float32)
-            held[block, :, at, :] = sums[:, :radial]
-            held[block, :, at + 1, :] = sums[:, radial:]
+            held[:, at, :] = sums[:, :radial]
+            held[:, at + 1, :] = sums[:, radial:]
+        for sec, out in ((1, send_ref), (0, keep_ref)):
+            for flat, deep in np.ndindex(4, 4):
+                order = orders_ref[pair_at(sec, deep, flat)]
+                for half, part in np.ndindex(2, 2):
+                    values = held[part * slots + 2 * order + half]
+                    out[flat, deep, half, pl.ds(begin, lat_block), pl.ds(part * radial, radial)] = (
+                        values.astype(out.dtype)
+                    )
         return carry
 
-    lax.fori_loop(0, blocks, one_block, 0)
-    for sec, out in ((1, send_ref), (0, keep_ref)):
-        for flat, deep in np.ndindex(4, 4):
-            order = orders_ref[pair_at(sec, deep, flat)]
-            for half, part in np.ndindex(2, 2):
-                values = held[:, part * slots + 2 * order + half]
-                out[flat, deep, half, :, pl.ds(part * radial, radial)] = values.reshape(
-                    blocks * lat_block, radial
-                ).astype(out.dtype)
+    lax.fori_loop(0, buffer.shape[0] // lat_block, one_block, 0)
 
 
 def forward_sums(pair_orders, table, grid_terms, lat_block):
     sections, rows, phi_count = table.shape
     lat_rows, _, radial = grid_terms.shape
-    blocks = lat_rows // lat_block
     sizes = (4, 4, 2, lat_rows, 2 * radial)
-    in_memory = pl.BlockSpec(memory_space=pltpu.HBM)
+    in_memory = [pltpu.with_memory_space_constraint(x, pltpu.HBM) for x in (pair_orders, table)]
     return pl.pallas_call(
         forward_kernel,
-        in_specs=[smem(), in_memory, in_memory],
+        in_specs=[pl.BlockSpec(memory_space=pltpu.HBM)] * 2 + [anywhere()],
         out_specs=[vmem(), vmem()],
         out_shape=[
             jax.ShapeDtypeStruct(sizes, jnp.float32),
             jax.ShapeDtypeStruct(sizes, jnp.bfloat16),
         ],
         scratch_shapes=[
+            pltpu.SMEM(pair_orders.shape, jnp.int32),
             pltpu.VMEM((rows, phi_count), table.dtype),
             pltpu.VMEM(grid_terms.shape, jnp.float32),
-            pltpu.VMEM((blocks, rows, lat_block, radial), jnp.float32),
+            pltpu.VMEM((rows, lat_block, radial), jnp.float32),
             pltpu.SemaphoreType.DMA((lat_rows // 2,)),
-            pltpu.SemaphoreType.DMA,
+            pltpu.SemaphoreType.DMA((2,)),
         ],
         compiler_params=params(36),
         cost_estimate=pl.CostEstimate(
@@ -255,7 +259,7 @@
             bytes_accessed=4 * lat_rows * phi_count * radial,
             transcendentals=0,
         ),
-    )(pair_orders, table, grid_terms)
+    )(*in_memory, grid_terms)
 
 
 def add_kernel(keep_ref, take_ref, *outs):
@@ -340,17 +344,8 @@
 
 def inverse_kernel(orders_ref, table_ref, *refs):
     takes, (out_ref, buffer, held, sems) = refs[:-4], refs[-4:]
-    blocks, slot_rows, lat_block, radial = held.shape
+    slot_rows, lat_block, radial = held.shape
     slots = slot_rows // 2
-
-    for sec, flat, deep in np.ndindex(2, 4, 4):
-        order = orders_ref[pair_at(sec, deep, flat)]
-        for half, part in np.ndindex(2, 2):
-            values = takes[4 * sec + flat][deep, half, :, pl.ds(part * radial, radial)]
-            held[:, part * slots + 2 * order + half] = values.astype(jnp.float32).reshape(
-                blocks, lat_block, radial
-            )
-
     table = table_ref[lax.axis_index("sec")]
 
     def chunk(at):
@@ -359,22 +354,27 @@
         )
 
     def one_block(block, carry):
+        begin = pl.multiple_of(block * lat_block, lat_block)
+        for sec, flat, deep in np.ndindex(2, 4, 4):
+            order = orders_ref[pair_at(sec, deep, flat)]
+            for half, part in np.ndindex(2, 2):
+                values = takes[4 * sec + flat][
+                    deep, half, pl.ds(begin, lat_block), pl.ds(part * radial, radial)
+                ]
+                held[part * slots + 2 * order + half] = values.astype(jnp.float32)
         for at in range(0, lat_block, 2):
             two = jnp.concatenate(
-                [
-                    held[block, :, at, :].astype(jnp.bfloat16),
-                    held[block, :, at + 1, :].astype(jnp.bfloat16),
-                ],
+                [held[:, at, :].astype(jnp.bfloat16), held[:, at + 1, :].astype(jnp.bfloat16)],
                 axis=1,
             )
             values = jnp.dot(table, two, preferred_element_type=jnp.float32)
-            lat = block * lat_block + at
+            lat = begin + at
             buffer[lat] = values[:, :radial]
             buffer[lat + 1] = values[:, radial:]
             chunk(lat // 2).start()
         return carry
 
-    lax.fori_loop(0, blocks, one_block, 0)
+    lax.fori_loop(0, buffer.shape[0] // lat_block, one_block, 0)
     for at in range(sems.shape[0]):
         chunk(at).wait()
 
@@ -382,7 +382,6 @@
 def inverse_values(pair_orders, table, takes, lat_block):
     _, phi_count, slot_rows = table.shape
     lat_rows, radial = takes[0].shape[2], takes[0].shape[3] // 2
-    blocks = lat_rows // lat_block
     out = jax.ShapeDtypeStruct((lat_rows, phi_count, radial), jnp.float32)
     return pl.pallas_call(
         inverse_kernel,
@@ -391,7 +390,7 @@
         out_shape=out,
         scratch_shapes=[
             pltpu.VMEM(out.shape, jnp.float32),
-            pltpu.VMEM((blocks, slot_rows, lat_block, radial), jnp.float32),
+            pltpu.VMEM((slot_rows, lat_block, radial), jnp.float32),
             pltpu.SemaphoreType.DMA((lat_rows // 2,)),
         ],
         compiler_params=params(36),
@@ -410,7 +409,7 @@
     padded = -(-rows // 8) * 8
     columns = 2 * radial
     pair_total = pair_orders.shape[0]
-    lat_block = 8
+    lat_block = 16
     table = natural_table(pair_total, lax.axis_size("sec"), phi_count)
     forward_table = jnp.asarray(table, jnp.bfloat16)
     inverse_table = jnp.asarray(table.transpose(0, 2, 1), jnp.bfloat16)
@@ -440,7 +439,7 @@
         scalars=1,
         scratch=[gathered],
     )
-    sums = [sums[0]] + [exchange(sums[deep], deep=deep) for deep in (1, 2, 3)]
+    sums = [sums[0]] + [exchange(sums[deep], deep=deep) for deep in (3, 2, 1)]
 
     radial_mode = np.arange(radial, dtype=np.float32) / np.float32(radial)
     damping = np.exp(-filter_strength * radial_mode**filter_power).astype(np.float32)

time: 68.4 us -> 69.7 us (1.019)
  Pallas kernels: 21.2 us -> 25 us
  local copies, waits for them, and re-layouts: 2.35 us -> 0.66 us
  waiting for transfers between devices: 18.4 us -> 17.5 us
    pallas_call x1, Pallas kernels: 9.51 us -> 14 us  [forward_sums(): pl.pallas_call(forward_kernel, in_specs=[pl.BlockSpec(memory_space=pltpu....]
    unnamed x18 -> x16, local copies, waits for them, and re-layouts: 1.73 us -> 0.04 us
    ppermute x20, waiting for transfers between devices: 18.4 us -> 17.5 us  [exchange(): return lax.ppermute(array, names, pairs)]
  transfers between devices with their start and end apart: 20 -> 20, of which waited for: 10 -> 11; matrix products, arithmetic and copies ran while one was open for 1% -> 1% of each run, Pallas kernels for 0% -> 0%
where the time goes in v6:
time: 69.7 us; the launch traced here: 69.5 us
  starting transfers between devices  25.5 us (37%)
  Pallas kernels  25 us (36%)
  waiting for transfers between devices  17.5 us (25%)
  between operations  0.8 us (1%)
    ppermute x20, starting transfers between devices, exchange(): return lax.ppermute(array, names, pairs)  25.5 us
    ppermute x20, waiting for transfers between devices, exchange(): return lax.ppermute(array, names, pairs)  17.5 us
    pallas_call x1, Pallas kernels, forward_sums(): pl.pallas_call(forward_kernel, in_specs=[pl.BlockSpec(memory_space=pltpu....  14 us
    pallas_call x1, Pallas kernels, inverse_values(): pl.pallas_call(inverse_kernel, in_specs=[smem()] + [vmem()] * (1 + len(ta...  8.06 us
    pallas_call x5, Pallas kernels, call(): pl.pallas_call(kernel, in_specs=[smem()] * scalars + [vmem()] * (len(oper...  2.94 us
  transfers between devices with their start and end apart: 20, of which 11 were waited for; matrix products, arithmetic and copies ran while one was open for 1% of the time, Pallas kernels for 0%

profile of v6, /device:TPU:0, one launch (start us, length us, event | category | flops | bytes accessed | tf_op | source)
XLA Modules:
  0.0 69.5 jit_solution(14246140508515608613)
XLA Ops:
  0.7 14.0 %shard_map.114 = (f32[4,4,2,48,256]{4,3,2,1,0:T(8,128)S(1)}, bf16[4,4,2,48,256]{4,3,2,1,0:T(8,128)(2,1)S(1)}) custom-call(s32[32]{0:T(128)} %orders_ref.7, bf16[2,128,768]{2,1,0:T(8,128)(2,1)} %constant.6.clone.table_ref, f32[48,768,128]{2,1,0:T(8,128)} %grid_ref.1), custom_call_target="tpu_custom_call" | custom-call | flops 1207959552 | bytes 18874368 | tf_op jit(solution)/shard_map/pallas_call | solution.py:240
  14.8 0.5 collective-permute-start.3
  15.3 1.9 %collective-permute-done.3.take_ref = bf16[4,4,2,48,256]{4,3,2,1,0:T(8,128)(2,1)S(1)} collective-permute-done((bf16[4,4,2,48,256]{4,3,2,1,0:T(8,128)(2,1)S(1)}, bf16[4,4,2,48,256]{4,3,2,1,0:T(8,128)(2,1)S(1)}, u32[]{:S(2)}, u32[]{:S(2)}) %collective-permute-start.3) | collective-permute-done | bytes 786464 | tf_op jit(solution)/shard_map/ppermute | solution.py:177
  17.2 0.1 shard_map.115
  17.3 2.9 %collective-permute-start.4 = (bf16[4,2,48,256]{3,2,1,0:T(8,128)(2,1)S(1)}, bf16[4,2,48,256]{3,2,1,0:T(8,128)(2,1)S(1)}, u32[]{:S(2)}, u32[]{:S(2)}) collective-permute-start(bf16[4,2,48,256]{3,2,1,0:T(8,128)(2,1)S(1)} %get-tuple-element.27), channel_id=1, source_target_pairs={{0,1},{1,0},{2,3},{3,2},{4,5},{5,4},{6,7},{7,6},{8,9},{9,8},{10,11... | collective-permute-start | bytes 589832 | tf_op jit(solution)/shard_map/ppermute | solution.py:177
  20.2 1.5 %collective-permute-start.5 = (bf16[4,2,48,256]{3,2,1,0:T(8,128)(2,1)S(1)}, bf16[4,2,48,256]{3,2,1,0:T(8,128)(2,1)S(1)}, u32[]{:S(2)}, u32[]{:S(2)}) collective-permute-start(bf16[4,2,48,256]{3,2,1,0:T(8,128)(2,1)S(1)} %get-tuple-element.28), channel_id=1, source_target_pairs={{0,2},{1,3},{2,0},{3,1},{4,6},{5,7},{6,4},{7,5},{8,10},{9,11},{10,... | collective-permute-start | bytes 589832 | tf_op jit(solution)/shard_map/ppermute | solution.py:177
  21.9 2.1 %collective-permute-start = (bf16[72,192]{1,0:T(8,128)(2,1)S(1)}, bf16[72,192]{1,0:T(8,128)(2,1)S(1)}, u32[]{:S(2)}, u32[]{:S(2)}) collective-permute-start(bf16[72,192]{1,0:T(8,128)(2,1)S(1)} %get-tuple-element.21), channel_id=1, source_target_pairs={{0,4},{1,5},{2,6},{3,7},{4,0},{5,1},{6,2},{7,3},{8,12},{9,13},{10,... | collective-permute-start | bytes 82952 | tf_op jit(solution)/shard_map/ppermute | solution.py:177
  24.0 2.6 %collective-permute-start.1 = (bf16[72,192]{1,0:T(8,128)(2,1)S(1)}, bf16[72,192]{1,0:T(8,128)(2,1)S(1)}, u32[]{:S(2)}, u32[]{:S(2)}) collective-permute-start(bf16[72,192]{1,0:T(8,128)(2,1)S(1)} %get-tuple-element.22), channel_id=1, source_target_pairs={{0,8},{1,9},{2,10},{3,11},{4,12},{5,13},{6,14},{7,15},{8,0},{9,1},... | collective-permute-start | bytes 82952 | tf_op jit(solution)/shard_map/ppermute | solution.py:177
  26.6 3.4 %collective-permute-start.2 = (bf16[72,192]{1,0:T(8,128)(2,1)S(1)}, bf16[72,192]{1,0:T(8,128)(2,1)S(1)}, u32[]{:S(2)}, u32[]{:S(2)}) collective-permute-start(bf16[72,192]{1,0:T(8,128)(2,1)S(1)} %get-tuple-element.23), channel_id=1, source_target_pairs={{0,12},{1,13},{2,14},{3,15},{4,8},{5,9},{6,10},{7,11},{8,4},{9,5},... | collective-permute-start | bytes 82952 | tf_op jit(solution)/shard_map/ppermute | solution.py:177
  30.0 2.4 %collective-permute-done.2.refs_3_ = bf16[72,192]{1,0:T(8,128)(2,1)S(1)} collective-permute-done((bf16[72,192]{1,0:T(8,128)(2,1)S(1)}, bf16[72,192]{1,0:T(8,128)(2,1)S(1)}, u32[]{:S(2)}, u32[]{:S(2)}) %collective-permute-start.2) | collective-permute-done | bytes 27680 | tf_op jit(solution)/shard_map/ppermute | solution.py:177
  32.4 0.9 %shard_map.116 = (f32[72,256]{1,0:T(8,128)S(1)}, bf16[72,256]{1,0:T(8,128)(2,1)S(1)}, bf16[72,256]{1,0:T(8,128)(2,1)S(1)}, bf16[72,256]{1,0:T(8,128)(2,1)S(1)}) custom-call(s32[32]{0:T(128)S(1)} %copy-done.5, bf16[72,192]{1,0:T(8,128)(2,1)S(1)} %get-tuple-element.20.refs_0_, bf16[72,192]{1,0:T(8,128)(2,1)S(1)} %collective-permute-done.refs_1_, ...), custom_call_target="tpu_custom_call" | custom-call | tf_op jit(solution)/shard_map/pallas_call | solution.py:140
  33.2 3.5 %collective-permute-start.7 = (bf16[72,256]{1,0:T(8,128)(2,1)S(1)}, bf16[72,256]{1,0:T(8,128)(2,1)S(1)}, u32[]{:S(2)}, u32[]{:S(2)}) collective-permute-start(bf16[72,256]{1,0:T(8,128)(2,1)S(1)} %get-tuple-element.31), channel_id=1, source_target_pairs={{0,12},{1,13},{2,14},{3,15},{4,8},{5,9},{6,10},{7,11},{8,4},{9,5},... | collective-permute-start | bytes 110600 | tf_op jit(solution)/shard_map/ppermute | solution.py:177
  36.7 1.0 %collective-permute-start.9 = (bf16[72,256]{1,0:T(8,128)(2,1)S(1)}, bf16[72,256]{1,0:T(8,128)(2,1)S(1)}, u32[]{:S(2)}, u32[]{:S(2)}) collective-permute-start(bf16[72,256]{1,0:T(8,128)(2,1)S(1)} %get-tuple-element.33), channel_id=1, source_target_pairs={{0,4},{1,5},{2,6},{3,7},{4,0},{5,1},{6,2},{7,3},{8,12},{9,13},{10,... | collective-permute-start | bytes 110600 | tf_op jit(solution)/shard_map/ppermute | solution.py:177
  37.7 1.4 %collective-permute-done.7.two = bf16[72,256]{1,0:T(8,128)(2,1)S(1)} collective-permute-done((bf16[72,256]{1,0:T(8,128)(2,1)S(1)}, bf16[72,256]{1,0:T(8,128)(2,1)S(1)}, u32[]{:S(2)}, u32[]{:S(2)}) %collective-permute-start.7) | collective-permute-done | bytes 36896 | tf_op jit(solution)/shard_map/ppermute | solution.py:177
  39.1 2.5 %collective-permute-done.8.three = bf16[72,256]{1,0:T(8,128)(2,1)S(1)} collective-permute-done((bf16[72,256]{1,0:T(8,128)(2,1)S(1)}, bf16[72,256]{1,0:T(8,128)(2,1)S(1)}, u32[]{:S(2)}, u32[]{:S(2)}) %collective-permute-start.8) | collective-permute-done | bytes 36896 | tf_op jit(solution)/shard_map/ppermute | solution.py:177
  41.6 0.8 %shard_map.117.refs_4_ = bf16[72,256]{1,0:T(8,128)(2,1)S(1)} custom-call(s32[32]{0:T(128)S(1)} %copy-done.5, f32[72,256]{1,0:T(8,128)S(1)} %get-tuple-element.30.one, bf16[72,256]{1,0:T(8,128)(2,1)S(1)} %collective-permute-done.7.two, bf16[72,256]{1,0:T(8,128)(2,1)S(1)} %collective-permute-done.8.three, bf16[72,256]{1,0:T(8,128)(2,1)S(1)} %collective-permute-done.9.last, ...), custom_call_target="tpu_custom_call" | custom-call | tf_op jit(solution)/shard_map/pallas_call | solution.py:140
  42.4 1.5 %collective-permute-start.12 = (bf16[72,256]{1,0:T(8,128)(2,1)S(1)}, bf16[72,256]{1,0:T(8,128)(2,1)S(1)}, u32[]{:S(2)}, u32[]{:S(2)}) collective-permute-start(bf16[72,256]{1,0:T(8,128)(2,1)S(1)} %shard_map.117.refs_4_), channel_id=1, source_target_pairs={{0,12},{1,13},{2,14},{3,15},{4,8},{5,9},{6,10},{7,11},{8,4},{9,5},... | collective-permute-start | bytes 110600 | tf_op jit(solution)/shard_map/ppermute | solution.py:177
  44.0 0.6 collective-permute-start.11
  44.6 2.3 %collective-permute-start.10 = (bf16[72,256]{1,0:T(8,128)(2,1)S(1)}, bf16[72,256]{1,0:T(8,128)(2,1)S(1)}, u32[]{:S(2)}, u32[]{:S(2)}) collective-permute-start(bf16[72,256]{1,0:T(8,128)(2,1)S(1)} %shard_map.117.refs_4_), channel_id=1, source_target_pairs={{0,4},{1,5},{2,6},{3,7},{4,0},{5,1},{6,2},{7,3},{8,12},{9,13},{10,... | collective-permute-start | bytes 110600 | tf_op jit(solution)/shard_map/ppermute | solution.py:177
  46.9 1.4 %collective-permute-done.12.refs_7_ = bf16[72,256]{1,0:T(8,128)(2,1)S(1)} collective-permute-done((bf16[72,256]{1,0:T(8,128)(2,1)S(1)}, bf16[72,256]{1,0:T(8,128)(2,1)S(1)}, u32[]{:S(2)}, u32[]{:S(2)}) %collective-permute-start.12) | collective-permute-done | bytes 36896 | tf_op jit(solution)/shard_map/ppermute | solution.py:177
  48.3 0.6 collective-permute-done.11.refs_6_
  48.9 0.4 collective-permute-done.10.refs_5_
  49.2 1.0 %shard_map.118 = (bf16[4,2,48,256]{3,2,1,0:T(8,128)(2,1)S(1)}, bf16[4,2,48,256]{3,2,1,0:T(8,128)(2,1)S(1)}, bf16[4,2,48,256]{3,2,1,0:T(8,128)(2,1)S(1)}, bf16[4,2,48,256]{3,2,1,0:T(8,128)(2,1)S(1)}) custom-call(s32[32]{0:T(128)S(1)} %copy-done.5, bf16[72,192]{1,0:T(8,128)(2,1)S(1)} %get-tuple-element.20.refs_0_, ...), custom_call_target="tpu_custom_call" | custom-call | tf_op jit(solution)/shard_map/pallas_call | solution.py:140
  50.2 1.6 %collective-permute-start.13 = (bf16[4,2,48,256]{3,2,1,0:T(8,128)(2,1)S(1)}, bf16[4,2,48,256]{3,2,1,0:T(8,128)(2,1)S(1)}, u32[]{:S(2)}, u32[]{:S(2)}) collective-permute-start(bf16[4,2,48,256]{3,2,1,0:T(8,128)(2,1)S(1)} %get-tuple-element.35), channel_id=1, source_target_pairs={{0,1},{1,0},{2,3},{3,2},{4,5},{5,4},{6,7},{7,6},{8,9},{9,8},{10,11... | collective-permute-start | bytes 589832 | tf_op jit(solution)/shard_map/ppermute | solution.py:177
  51.8 1.7 %collective-permute-start.14 = (bf16[4,2,48,256]{3,2,1,0:T(8,128)(2,1)S(1)}, bf16[4,2,48,256]{3,2,1,0:T(8,128)(2,1)S(1)}, u32[]{:S(2)}, u32[]{:S(2)}) collective-permute-start(bf16[4,2,48,256]{3,2,1,0:T(8,128)(2,1)S(1)} %get-tuple-element.36), channel_id=1, source_target_pairs={{0,2},{1,3},{2,0},{3,1},{4,6},{5,7},{6,4},{7,5},{8,10},{9,11},{10,... | collective-permute-start | bytes 589832 | tf_op jit(solution)/shard_map/ppermute | solution.py:177
  53.4 0.3 collective-permute-start.15
  53.8 2.2 %collective-permute-done.13.refs_1_ = bf16[4,2,48,256]{3,2,1,0:T(8,128)(2,1)S(1)} collective-permute-done((bf16[4,2,48,256]{3,2,1,0:T(8,128)(2,1)S(1)}, bf16[4,2,48,256]{3,2,1,0:T(8,128)(2,1)S(1)}, u32[]{:S(2)}, u32[]{:S(2)}) %collective-permute-start.13) | collective-permute-done | bytes 196640 | tf_op jit(solution)/shard_map/ppermute | solution.py:177
  56.0 2.8 %collective-permute-done.14.refs_2_ = bf16[4,2,48,256]{3,2,1,0:T(8,128)(2,1)S(1)} collective-permute-done((bf16[4,2,48,256]{3,2,1,0:T(8,128)(2,1)S(1)}, bf16[4,2,48,256]{3,2,1,0:T(8,128)(2,1)S(1)}, u32[]{:S(2)}, u32[]{:S(2)}) %collective-permute-start.14) | collective-permute-done | bytes 196640 | tf_op jit(solution)/shard_map/ppermute | solution.py:177
  58.7 1.3 %collective-permute-done.15.refs_3_ = bf16[4,2,48,256]{3,2,1,0:T(8,128)(2,1)S(1)} collective-permute-done((bf16[4,2,48,256]{3,2,1,0:T(8,128)(2,1)S(1)}, bf16[4,2,48,256]{3,2,1,0:T(8,128)(2,1)S(1)}, u32[]{:S(2)}, u32[]{:S(2)}) %collective-permute-start.15) | collective-permute-done | bytes 196640 | tf_op jit(solution)/shard_map/ppermute | solution.py:177
  60.0 0.6 slice_bitcast_fusion
  60.6 0.8 %collective-permute-done.19.refs_7_ = bf16[4,2,48,256]{3,2,1,0:T(8,128)(2,1)S(1)} collective-permute-done((bf16[4,2,48,256]{3,2,1,0:T(8,128)(2,1)S(1)}, bf16[4,2,48,256]{3,2,1,0:T(8,128)(2,1)S(1)}, u32[]{:S(2)}, u32[]{:S(2)}) %collective-permute-start.19) | collective-permute-done | bytes 196640 | tf_op jit(solution)/shard_map/ppermute | solution.py:177
  61.5 8.1 %shard_map.119 = f32[48,768,128]{2,1,0:T(8,128)} custom-call(s32[32]{0:T(128)S(1)} %copy-done.5, bf16[2,768,128]{2,1,0:T(8,128)(2,1)S(1)} %copy-done, bf16[4,2,48,256]{3,2,1,0:T(8,128)(2,1)S(1)} %get-tuple-element.34.refs_0_, bf16[4,2,48,256]{3,2,1,0:T(8,128)(2,1)S(1)} %collective-permute-done.13.refs_1_, ...), custom_call_target="tpu_custom_call" | custom-call | flops 1207959552 | bytes 18874368 | tf_op jit(solution)/shard_map/pallas_call | solution.py:386
  (32 shorter events, 0.2 us)
Async XLA Ops:
  0.6 40.9 %copy-start.7 = (f32[1,128]{1,0:T(1,128)S(1)}, f32[1,128]{1,0:T(1,128)}, u32[]{:S(2)}) copy-start(f32[1,128]{1,0:T(1,128)} %constant.11.damping_ref) | copy-start | bytes 1540
  0.6 60.8 %copy-start = (bf16[2,768,128]{2,1,0:T(8,128)(2,1)S(1)}, bf16[2,768,128]{2,1,0:T(8,128)(2,1)}, u32[]{:S(2)}) copy-start(bf16[2,768,128]{2,1,0:T(8,128)(2,1)} %constant.7.clone.table_ref) | copy-start | bytes 1179652
  0.7 31.7 %copy-start.5 = (s32[32]{0:T(128)S(1)}, s32[32]{0:T(128)}, u32[]{:S(2)}) copy-start(s32[32]{0:T(128)} %orders_ref.7) | copy-start | bytes 388
  0.7 21.1 %copy-start.1 = (bf16[1,65,768]{2,1,0:T(8,128)(2,1)S(1)}, bf16[1,65,768]{2,1,0:T(8,128)(2,1)}, u32[]{:S(2)}) copy-start(bf16[1,65,768]{2,1,0:T(8,128)(2,1)} %legendre_ref.1) | copy-start | bytes 299524
  0.7 40.9 %copy-start.4 = (bf16[128,128]{1,0:T(8,128)(2,1)S(1)}, bf16[128,128]{1,0:T(8,128)(2,1)}, u32[]{:S(2)}) copy-start(bf16[128,128]{1,0:T(8,128)(2,1)} %left_ref.1) | copy-start | bytes 98308
  0.7 40.9 %copy-start.3 = (bf16[128,128]{1,0:T(8,128)(2,1)S(1)}, bf16[128,128]{1,0:T(8,128)(2,1)}, u32[]{:S(2)}) copy-start(bf16[128,128]{1,0:T(8,128)(2,1)} %right_ref.1) | copy-start | bytes 98308
  0.7 40.9 %copy-start.6 = (f32[128]{0:T(128)S(1)}, f32[128]{0:T(128)}, u32[]{:S(2)}) copy-start(f32[128]{0:T(128)} %param.14) | copy-start | bytes 1540
  0.7 40.9 %copy-start.2 = (bf16[1,65,256]{2,1,0:T(8,128)(2,1)S(1)}, bf16[1,65,256]{2,1,0:T(8,128)(2,1)}, u32[]{:S(2)}) copy-start(bf16[1,65,256]{2,1,0:T(8,128)(2,1)} %state_ref.1) | copy-start | bytes 99844
  14.8 2.4 %collective-permute-start.3 = (bf16[4,4,2,48,256]{4,3,2,1,0:T(8,128)(2,1)S(1)}, bf16[4,4,2,48,256]{4,3,2,1,0:T(8,128)(2,1)S(1)}, u32[]{:S(2)}, u32[]{:S(2)}) collective-permute-start(bf16[4,4,2,48,256]{4,3,2,1,0:T(8,128)(2,1)S(1)} %get-tuple-element.25), channel_id=1, source_target_pairs={{0,16},{1,17},{2,18},{3,19},{4,20},{5,21},{6,22},{7,23},{8,24},{9,... | collective-permute-start | bytes 2359304 | tf_op jit(solution)/shard_map/ppermute | solution.py:177
  17.3 15.0 %collective-permute-start.4 = (bf16[4,2,48,256]{3,2,1,0:T(8,128)(2,1)S(1)}, bf16[4,2,48,256]{3,2,1,0:T(8,128)(2,1)S(1)}, u32[]{:S(2)}, u32[]{:S(2)}) collective-permute-start(bf16[4,2,48,256]{3,2,1,0:T(8,128)(2,1)S(1)} %get-tuple-element.27), channel_id=1, source_target_pairs={{0,1},{1,0},{2,3},{3,2},{4,5},{5,4},{6,7},{7,6},{8,9},{9,8},{10,11... | collective-permute-start | bytes 589832 | tf_op jit(solution)/shard_map/ppermute | solution.py:177
  20.2 12.1 %collective-permute-start.5 = (bf16[4,2,48,256]{3,2,1,0:T(8,128)(2,1)S(1)}, bf16[4,2,48,256]{3,2,1,0:T(8,128)(2,1)S(1)}, u32[]{:S(2)}, u32[]{:S(2)}) collective-permute-start(bf16[4,2,48,256]{3,2,1,0:T(8,128)(2,1)S(1)} %get-tuple-element.28), channel_id=1, source_target_pairs={{0,2},{1,3},{2,0},{3,1},{4,6},{5,7},{6,4},{7,5},{8,10},{9,11},{10,... | collective-permute-start | bytes 589832 | tf_op jit(solution)/shard_map/ppermute | solution.py:177
  21.8 10.6 %collective-permute-start.6 = (bf16[4,2,48,256]{3,2,1,0:T(8,128)(2,1)S(1)}, bf16[4,2,48,256]{3,2,1,0:T(8,128)(2,1)S(1)}, u32[]{:S(2)}, u32[]{:S(2)}) collective-permute-start(bf16[4,2,48,256]{3,2,1,0:T(8,128)(2,1)S(1)} %get-tuple-element.29), channel_id=1, source_target_pairs={{0,3},{1,2},{2,1},{3,0},{4,7},{5,6},{6,5},{7,4},{8,11},{9,10},{10,... | collective-permute-start | bytes 589832 | tf_op jit(solution)/shard_map/ppermute | solution.py:177
  21.9 4.7 %collective-permute-start = (bf16[72,192]{1,0:T(8,128)(2,1)S(1)}, bf16[72,192]{1,0:T(8,128)(2,1)S(1)}, u32[]{:S(2)}, u32[]{:S(2)}) collective-permute-start(bf16[72,192]{1,0:T(8,128)(2,1)S(1)} %get-tuple-element.21), channel_id=1, source_target_pairs={{0,4},{1,5},{2,6},{3,7},{4,0},{5,1},{6,2},{7,3},{8,12},{9,13},{10,... | collective-permute-start | bytes 82952 | tf_op jit(solution)/shard_map/ppermute | solution.py:177
  24.0 6.0 %collective-permute-start.1 = (bf16[72,192]{1,0:T(8,128)(2,1)S(1)}, bf16[72,192]{1,0:T(8,128)(2,1)S(1)}, u32[]{:S(2)}, u32[]{:S(2)}) collective-permute-start(bf16[72,192]{1,0:T(8,128)(2,1)S(1)} %get-tuple-element.22), channel_id=1, source_target_pairs={{0,8},{1,9},{2,10},{3,11},{4,12},{5,13},{6,14},{7,15},{8,0},{9,1},... | collective-permute-start | bytes 82952 | tf_op jit(solution)/shard_map/ppermute | solution.py:177
  26.6 5.8 %collective-permute-start.2 = (bf16[72,192]{1,0:T(8,128)(2,1)S(1)}, bf16[72,192]{1,0:T(8,128)(2,1)S(1)}, u32[]{:S(2)}, u32[]{:S(2)}) collective-permute-start(bf16[72,192]{1,0:T(8,128)(2,1)S(1)} %get-tuple-element.23), channel_id=1, source_target_pairs={{0,12},{1,13},{2,14},{3,15},{4,8},{5,9},{6,10},{7,11},{8,4},{9,5},... | collective-permute-start | bytes 82952 | tf_op jit(solution)/shard_map/ppermute | solution.py:177
  33.2 5.8 %collective-permute-start.7 = (bf16[72,256]{1,0:T(8,128)(2,1)S(1)}, bf16[72,256]{1,0:T(8,128)(2,1)S(1)}, u32[]{:S(2)}, u32[]{:S(2)}) collective-permute-start(bf16[72,256]{1,0:T(8,128)(2,1)S(1)} %get-tuple-element.31), channel_id=1, source_target_pairs={{0,12},{1,13},{2,14},{3,15},{4,8},{5,9},{6,10},{7,11},{8,4},{9,5},... | collective-permute-start | bytes 110600 | tf_op jit(solution)/shard_map/ppermute | solution.py:177
  36.7 4.9 %collective-permute-start.8 = (bf16[72,256]{1,0:T(8,128)(2,1)S(1)}, bf16[72,256]{1,0:T(8,128)(2,1)S(1)}, u32[]{:S(2)}, u32[]{:S(2)}) collective-permute-start(bf16[72,256]{1,0:T(8,128)(2,1)S(1)} %get-tuple-element.32), channel_id=1, source_target_pairs={{0,8},{1,9},{2,10},{3,11},{4,12},{5,13},{6,14},{7,15},{8,0},{9,1},... | collective-permute-start | bytes 110600 | tf_op jit(solution)/shard_map/ppermute | solution.py:177
  36.7 4.9 %collective-permute-start.9 = (bf16[72,256]{1,0:T(8,128)(2,1)S(1)}, bf16[72,256]{1,0:T(8,128)(2,1)S(1)}, u32[]{:S(2)}, u32[]{:S(2)}) collective-permute-start(bf16[72,256]{1,0:T(8,128)(2,1)S(1)} %get-tuple-element.33), channel_id=1, source_target_pairs={{0,4},{1,5},{2,6},{3,7},{4,0},{5,1},{6,2},{7,3},{8,12},{9,13},{10,... | collective-permute-start | bytes 110600 | tf_op jit(solution)/shard_map/ppermute | solution.py:177
  42.4 5.8 %collective-permute-start.12 = (bf16[72,256]{1,0:T(8,128)(2,1)S(1)}, bf16[72,256]{1,0:T(8,128)(2,1)S(1)}, u32[]{:S(2)}, u32[]{:S(2)}) collective-permute-start(bf16[72,256]{1,0:T(8,128)(2,1)S(1)} %shard_map.117.refs_4_), channel_id=1, source_target_pairs={{0,12},{1,13},{2,14},{3,15},{4,8},{5,9},{6,10},{7,11},{8,4},{9,5},... | collective-permute-start | bytes 110600 | tf_op jit(solution)/shard_map/ppermute | solution.py:177
  44.0 4.9 %collective-permute-start.11 = (bf16[72,256]{1,0:T(8,128)(2,1)S(1)}, bf16[72,256]{1,0:T(8,128)(2,1)S(1)}, u32[]{:S(2)}, u32[]{:S(2)}) collective-permute-start(bf16[72,256]{1,0:T(8,128)(2,1)S(1)} %shard_map.117.refs_4_), channel_id=1, source_target_pairs={{0,8},{1,9},{2,10},{3,11},{4,12},{5,13},{6,14},{7,15},{8,0},{9,1},... | collective-permute-start | bytes 110600 | tf_op jit(solution)/shard_map/ppermute | solution.py:177
  44.6 4.6 %collective-permute-start.10 = (bf16[72,256]{1,0:T(8,128)(2,1)S(1)}, bf16[72,256]{1,0:T(8,128)(2,1)S(1)}, u32[]{:S(2)}, u32[]{:S(2)}) collective-permute-start(bf16[72,256]{1,0:T(8,128)(2,1)S(1)} %shard_map.117.refs_4_), channel_id=1, source_target_pairs={{0,4},{1,5},{2,6},{3,7},{4,0},{5,1},{6,2},{7,3},{8,12},{9,13},{10,... | collective-permute-start | bytes 110600 | tf_op jit(solution)/shard_map/ppermute | solution.py:177
  50.2 5.7 %collective-permute-start.13 = (bf16[4,2,48,256]{3,2,1,0:T(8,128)(2,1)S(1)}, bf16[4,2,48,256]{3,2,1,0:T(8,128)(2,1)S(1)}, u32[]{:S(2)}, u32[]{:S(2)}) collective-permute-start(bf16[4,2,48,256]{3,2,1,0:T(8,128)(2,1)S(1)} %get-tuple-element.35), channel_id=1, source_target_pairs={{0,1},{1,0},{2,3},{3,2},{4,5},{5,4},{6,7},{7,6},{8,9},{9,8},{10,11... | collective-permute-start | bytes 589832 | tf_op jit(solution)/shard_map/ppermute | solution.py:177
  51.8 7.0 %collective-permute-start.14 = (bf16[4,2,48,256]{3,2,1,0:T(8,128)(2,1)S(1)}, bf16[4,2,48,256]{3,2,1,0:T(8,128)(2,1)S(1)}, u32[]{:S(2)}, u32[]{:S(2)}) collective-permute-start(bf16[4,2,48,256]{3,2,1,0:T(8,128)(2,1)S(1)} %get-tuple-element.36), channel_id=1, source_target_pairs={{0,2},{1,3},{2,0},{3,1},{4,6},{5,7},{6,4},{7,5},{8,10},{9,11},{10,... | collective-permute-start | bytes 589832 | tf_op jit(solution)/shard_map/ppermute | solution.py:177
  53.4 6.6 %collective-permute-start.15 = (bf16[4,2,48,256]{3,2,1,0:T(8,128)(2,1)S(1)}, bf16[4,2,48,256]{3,2,1,0:T(8,128)(2,1)S(1)}, u32[]{:S(2)}, u32[]{:S(2)}) collective-permute-start(bf16[4,2,48,256]{3,2,1,0:T(8,128)(2,1)S(1)} %get-tuple-element.37), channel_id=1, source_target_pairs={{0,3},{1,2},{2,1},{3,0},{4,7},{5,6},{6,5},{7,4},{8,11},{9,10},{10,... | collective-permute-start | bytes 589832 | tf_op jit(solution)/shard_map/ppermute | solution.py:177
  53.8 6.9 %collective-permute-start.16 = (bf16[4,2,48,256]{3,2,1,0:T(8,128)(2,1)S(1)}, bf16[4,2,48,256]{3,2,1,0:T(8,128)(2,1)S(1)}, u32[]{:S(2)}, u32[]{:S(2)}) collective-permute-start(bf16[4,2,48,256]{3,2,1,0:T(8,128)(2,1)S(1)} %get-tuple-element.34.refs_0_), channel_id=1, source_target_pairs={{0,16},{1,17},{2,18},{3,19},{4,20},{5,21},{6,22},{7,23},{8,24},{9,... | collective-permute-start | bytes 589832 | tf_op jit(solution)/shard_map/ppermute | solution.py:177
  56.0 4.7 %collective-permute-start.17 = (bf16[4,2,48,256]{3,2,1,0:T(8,128)(2,1)S(1)}, bf16[4,2,48,256]{3,2,1,0:T(8,128)(2,1)S(1)}, u32[]{:S(2)}, u32[]{:S(2)}) collective-permute-start(bf16[4,2,48,256]{3,2,1,0:T(8,128)(2,1)S(1)} %collective-permute-done.13.refs_1_), channel_id=1, source_target_pairs={{0,16},{1,17},{2,18},{3,19},{4,20},{5,21},{6,22},{7,23},{8,24},{9,... | collective-permute-start | bytes 589832 | tf_op jit(solution)/shard_map/ppermute | solution.py:177
  58.7 1.9 %collective-permute-start.18 = (bf16[4,2,48,256]{3,2,1,0:T(8,128)(2,1)S(1)}, bf16[4,2,48,256]{3,2,1,0:T(8,128)(2,1)S(1)}, u32[]{:S(2)}, u32[]{:S(2)}) collective-permute-start(bf16[4,2,48,256]{3,2,1,0:T(8,128)(2,1)S(1)} %collective-permute-done.14.refs_2_), channel_id=1, source_target_pairs={{0,16},{1,17},{2,18},{3,19},{4,20},{5,21},{6,22},{7,23},{8,24},{9,... | collective-permute-start | bytes 589832 | tf_op jit(solution)/shard_map/ppermute | solution.py:177
  60.0 1.4 %collective-permute-start.19 = (bf16[4,2,48,256]{3,2,1,0:T(8,128)(2,1)S(1)}, bf16[4,2,48,256]{3,2,1,0:T(8,128)(2,1)S(1)}, u32[]{:S(2)}, u32[]{:S(2)}) collective-permute-start(bf16[4,2,48,256]{3,2,1,0:T(8,128)(2,1)S(1)} %collective-permute-done.15.refs_3_), channel_id=1, source_target_pairs={{0,16},{1,17},{2,18},{3,19},{4,20},{5,21},{6,22},{7,23},{8,24},{9,... | collective-permute-start | bytes 589832 | tf_op jit(solution)/shard_map/ppermute | solution.py:177

commit v7 on v6

--- a/solution.py
+++ b/solution.py
@@ -178,20 +178,21 @@
 
 
 def cut_kernel(legendre_ref, *refs):
-    outs, slabs = refs[:-1], refs[-1]
-    count, rows, lats = slabs.shape
+    outs, parts = refs[:-1], refs[-1]
+    count, rows, lats = parts.shape
     given = legendre_ref.shape[1]
-    slabs[...] = jnp.zeros_like(slabs)
+    parts[...] = jnp.zeros_like(parts)
     for at in range(count):
-        slabs[at, :given] = legendre_ref[0, :, at * lats : (at + 1) * lats]
+        parts[at, :given] = legendre_ref[0, :, at * lats : (at + 1) * lats]
     for deep, out in enumerate(outs):
-        out[...] = slabs[depth_index() ^ deep]
+        first = (depth_index() ^ deep) * 4
+        out[...] = jnp.concatenate([parts[first + (plane_index() ^ flat)] for flat in four], axis=1)
 
 
 def forward_kernel(
     orders_from, table_ref, grid_ref, keep_ref, send_ref, orders_ref, table, buffer, held, sems, more
 ):
-    rows, lat_block, radial = held.shape
+    blocks, rows, lat_block, radial = held.shape
     slots = rows // 2
 
     def chunk(at):
@@ -209,27 +210,27 @@
     orders_copy.wait()
 
     def one_block(block, carry):
-        begin = pl.multiple_of(block * lat_block, lat_block)
         for at in range(0, lat_block, 2):
-            lat = begin + at
+            lat = block * lat_block + at
             chunk(lat // 2).wait()
             two = jnp.concatenate(
                 [buffer[lat].astype(jnp.bfloat16), buffer[lat + 1].astype(jnp.bfloat16)], axis=1
             )
             sums = jnp.dot(table[...], two, preferred_element_type=jnp.float32)
-            held[:, at, :] = sums[:, :radial]
-            held[:, at + 1, :] = sums[:, radial:]
-        for sec, out in ((1, send_ref), (0, keep_ref)):
-            for flat, deep in np.ndindex(4, 4):
-                order = orders_ref[pair_at(sec, deep, flat)]
-                for half, part in np.ndindex(2, 2):
-                    values = held[part * slots + 2 * order + half]
-                    out[flat, deep, half, pl.ds(begin, lat_block), pl.ds(part * radial, radial)] = (
-                        values.astype(out.dtype)
-                    )
+            held[block, :, at, :] = sums[:, :radial]
+            held[block, :, at + 1, :] = sums[:, radial:]
         return carry
 
-    lax.fori_loop(0, buffer.shape[0] // lat_block, one_block, 0)
+    lax.fori_loop(0, blocks, one_block, 0)
+    for sec, out in ((1, send_ref), (0, keep_ref)):
+        for flat, deep in np.ndindex(4, 4):
+            order = orders_ref[pair_at(sec, deep, flat)]
+            for part in range(2):
+                values = held[:, pl.ds(part * slots + 2 * order, 2)].astype(out.dtype)
+                for half in range(2):
+                    out[flat, deep, half, :, pl.ds(part * radial, radial)] = values[
+                        :, half
+                    ].reshape(blocks * lat_block, radial)
 
 
 def forward_sums(pair_orders, table, grid_terms, lat_block):
@@ -249,7 +250,7 @@
             pltpu.SMEM(pair_orders.shape, jnp.int32),
             pltpu.VMEM((rows, phi_count), table.dtype),
             pltpu.VMEM(grid_terms.shape, jnp.float32),
-            pltpu.VMEM((rows, lat_block, radial), jnp.float32),
+            pltpu.VMEM((lat_rows // lat_block, rows, lat_block, radial), jnp.float32),
             pltpu.SemaphoreType.DMA((lat_rows // 2,)),
             pltpu.SemaphoreType.DMA((2,)),
         ],
@@ -275,59 +276,48 @@
 
 
 def degrees_kernel(degrees, orders_ref, *refs):
-    weights, takes, outs, gathered = refs[:4], refs[4:8], refs[8:12], refs[12]
-    _, _, _, lat_rows, columns = gathered.shape
-    own = plane_index()
-    for flat in four:
-        for deep, half in np.ndindex(4, 2):
-            gathered[deep, half, own ^ flat] = takes[flat][deep, half]
+    weights, takes, outs = refs[:4], refs[4:8], refs[8:]
     for deep in four:
         chosen = masked(weights[deep][...], orders_ref[pair_at(0, deep, 0)], degrees)
         total = 0.0
         for half in range(2):
-            total += jnp.dot(
-                chosen[half],
-                gathered[deep, half].reshape(4 * lat_rows, columns),
-                preferred_element_type=jnp.float32,
-            )
+            rows = jnp.concatenate([take[deep, half] for take in takes], axis=0)
+            total += jnp.dot(chosen[half], rows, preferred_element_type=jnp.float32)
         outs[deep][...] = total.astype(outs[deep].dtype)
 
 
 def synthesis_kernel(degrees, orders_ref, *refs):
-    weights, fields, outs, spread = refs[:4], refs[4:8], refs[8:12], refs[12]
-    _, _, _, lat_rows, columns = spread.shape
+    weights, fields, outs = refs[:4], refs[4:8], refs[8:]
+    lat_rows = outs[0].shape[2]
     contract = (((0,), (0,)), ((), ()))
-    own = plane_index()
     for deep in four:
         chosen = masked(weights[deep][...], orders_ref[pair_at(0, deep, 0)], degrees)
         for half in range(2):
             values = lax.dot_general(
                 chosen[half], fields[deep][...], contract, preferred_element_type=jnp.float32
-            )
-            spread[deep, half] = values.astype(spread.dtype).reshape(4, lat_rows, columns)
-    for flat in (3, 1, 2, 0):
-        for deep, half in np.ndindex(4, 2):
-            outs[flat][deep, half] = spread[deep, half, own ^ flat]
-
-
-def solve_kernel(
-    orders_ref, one, two, three, last, state_ref, kappa_ref, damping_ref, right_ref, left_ref, sent_ref
-):
+            ).astype(jnp.bfloat16)
+            for flat, out in enumerate(outs):
+                out[deep, half] = values[flat * lat_rows : (flat + 1) * lat_rows]
+
+
+def factor_kernel(degrees, orders_ref, kappa_ref, damping_ref, factor_ref):
+    order = orders_ref[pair_at(0, 0, 0)]
+    row_index = lax.broadcasted_iota(jnp.int32, factor_ref.shape, 0)
+    degree = jnp.where(row_index < degrees - order, order + row_index, row_index - 1)
+    degree = degree.astype(jnp.float32)
+    factor_ref[...] = damping_ref[...] / (
+        1.0 + kappa_ref[...] + degree * (degree + 1.0) / (degrees * degrees)
+    )
+
+
+def solve_kernel(one, two, three, last, state_ref, factor_ref, right_ref, left_ref, sent_ref):
     rows = state_ref.shape[1]
     radial = right_ref.shape[0]
-    degrees = rows - 1
-    order = orders_ref[pair_at(0, 0, 0)]
     coefficient = one[...]
     for other in (two, three, last):
         coefficient += other[...].astype(jnp.float32)
     right_side = state_ref[0].astype(jnp.float32) + time_step * coefficient[:rows]
     right_side = right_side.astype(jnp.bfloat16)
-    row_index = lax.broadcasted_iota(jnp.int32, (rows, radial), 0)
-    degree = jnp.where(row_index < degrees - order, order + row_index, row_index - 1)
-    degree = degree.astype(jnp.float32)
-    factor = damping_ref[...] / (
-        1.0 + kappa_ref[...] + degree * (degree + 1.0) / (degrees * degrees)
-    )
     sent_ref[...] = jnp.zeros_like(sent_ref)
     for part in range(2):
         columns = pl.ds(part * radial, radial)
@@ -336,10 +326,9 @@
             right_ref[...],
             preferred_element_type=jnp.float32,
         )
-        scaled = (eigen * factor).astype(jnp.bfloat16)
+        scaled = (eigen * factor_ref[...]).astype(jnp.bfloat16)
         field = jnp.dot(scaled, left_ref[...], preferred_element_type=jnp.float32)
-        field = field.astype(jnp.bfloat16)
-        sent_ref[pl.ds(0, rows), columns] = field
+        sent_ref[pl.ds(0, rows), columns] = field.astype(jnp.bfloat16)
 
 
 def inverse_kernel(orders_ref, table_ref, *refs):
@@ -409,7 +398,6 @@
     padded = -(-rows // 8) * 8
     columns = 2 * radial
     pair_total = pair_orders.shape[0]
-    lat_block = 16
     table = natural_table(pair_total, lax.axis_size("sec"), phi_count)
     forward_table = jnp.asarray(table, jnp.bfloat16)
     inverse_table = jnp.asarray(table.transpose(0, 2, 1), jnp.bfloat16)
@@ -422,32 +410,33 @@
         cut_kernel,
         [legendre],
         [slab] * 4,
-        scratch=[pltpu.VMEM((4, padded, 4 * lat_rows), jnp.bfloat16)],
+        scratch=[pltpu.VMEM((16, padded, lat_rows), jnp.bfloat16)],
     )
     weights = [cuts[0]] + [exchange(cuts[deep], deep=deep) for deep in (1, 2, 3)]
 
-    keep, send = forward_sums(pair_orders, forward_table, grid_terms, lat_block)
+    keep, send = forward_sums(pair_orders, forward_table, grid_terms, 8)
     block = shape(4, 2, lat_rows, columns)
     blocks = call(add_kernel, [keep, exchange(send, sec=1)], [block] * 4, mib=24)
     takes = [blocks[0]] + [exchange(blocks[flat], flat=flat) for flat in (1, 2, 3)]
 
-    gathered = pltpu.VMEM((4, 2, 4, lat_rows, columns), jnp.bfloat16)
     sums = call(
         functools.partial(degrees_kernel, degrees),
         [pair_orders, *weights, *takes],
         [shape(padded, columns, dtype=jnp.float32)] + [shape(padded, columns)] * 3,
         scalars=1,
-        scratch=[gathered],
     )
     sums = [sums[0]] + [exchange(sums[deep], deep=deep) for deep in (3, 2, 1)]
 
     radial_mode = np.arange(radial, dtype=np.float32) / np.float32(radial)
     damping = np.exp(-filter_strength * radial_mode**filter_power).astype(np.float32)
+    factor = call(
+        functools.partial(factor_kernel, degrees),
+        [pair_orders, kappa[None, :], jnp.asarray(damping)[None, :]],
+        shape(rows, radial, dtype=jnp.float32),
+        scalars=1,
+    )
     field = call(
-        solve_kernel,
-        [pair_orders, *sums, state, kappa[None, :], jnp.asarray(damping)[None, :], right_op, left_op],
-        shape(padded, columns),
-        scalars=1,
+        solve_kernel, [*sums, state, factor, right_op, left_op], shape(padded, columns)
     )
     new_state = field[None, :rows]
 
@@ -457,11 +446,10 @@
         [pair_orders, *weights, *fields],
         [block] * 4,
         scalars=1,
-        scratch=[gathered],
     )
     takes = [blocks[0]] + [exchange(blocks[flat], flat=flat) for flat in (1, 2, 3)]
     takes += [exchange(take, sec=1) for take in takes]
-    evolved = inverse_values(pair_orders, inverse_table, takes, lat_block)
+    evolved = inverse_values(pair_orders, inverse_table, takes, 16)
     return (evolved, new_state)
 
 

time: 69.7 us -> 69.1 us (level)
  waiting for transfers between devices: 17.5 us -> 16.8 us
    ppermute x20, waiting for transfers between devices: 17.5 us -> 16.8 us  [exchange(): return lax.ppermute(array, names, pairs)]
    pallas_call x5 -> x6, Pallas kernels: 2.94 us -> 3.09 us  [call(): pl.pallas_call(kernel, in_specs=[smem()] * scalars + [vmem()] * (len(oper...]
  transfers between devices with their start and end apart: 20 -> 20, of which waited for: 11 -> 11; matrix products, arithmetic and copies ran while one was open for 1% -> 1% of each run, Pallas kernels for 0% -> 1%
where the time goes in v7:
time: 69.1 us; the launch traced here: 69 us
  starting transfers between devices  25.5 us (37%)
  Pallas kernels  25.2 us (36%)
  waiting for transfers between devices  16.8 us (24%)
  between operations  0.79 us (1%)
    ppermute x20, starting transfers between devices, exchange(): return lax.ppermute(array, names, pairs)  25.5 us
    ppermute x20, waiting for transfers between devices, exchange(): return lax.ppermute(array, names, pairs)  16.8 us
    pallas_call x1, Pallas kernels, forward_sums(): pl.pallas_call(forward_kernel, in_specs=[pl.BlockSpec(memory_space=pltpu....  14.1 us
    pallas_call x1, Pallas kernels, inverse_values(): pl.pallas_call(inverse_kernel, in_specs=[smem()] + [vmem()] * (1 + len(ta...  8.06 us
    pallas_call x6, Pallas kernels, call(): pl.pallas_call(kernel, in_specs=[smem()] * scalars + [vmem()] * (len(oper...  3.09 us
  transfers between devices with their start and end apart: 20, of which 11 were waited for; matrix products, arithmetic and copies ran while one was open for 1% of the time, Pallas kernels for 1%

profile of v7, /device:TPU:0, one launch (start us, length us, event | category | flops | bytes accessed | tf_op | source)
XLA Modules:
  0.0 69.0 jit_solution(6119499348391461369)
XLA Ops:
  0.7 14.1 %shard_map.114 = (f32[4,4,2,48,256]{4,3,2,1,0:T(8,128)S(1)}, bf16[4,4,2,48,256]{4,3,2,1,0:T(8,128)(2,1)S(1)}) custom-call(s32[32]{0:T(128)} %orders_ref.7, bf16[2,128,768]{2,1,0:T(8,128)(2,1)} %constant.6.clone.table_ref, f32[48,768,128]{2,1,0:T(8,128)} %grid_ref.1), custom_call_target="tpu_custom_call" | custom-call | flops 1207959552 | bytes 18874368 | tf_op jit(solution)/shard_map/pallas_call | solution.py:241
  14.8 0.5 collective-permute-start.3
  15.3 1.9 %collective-permute-done.3.take_ref = bf16[4,4,2,48,256]{4,3,2,1,0:T(8,128)(2,1)S(1)} collective-permute-done((bf16[4,4,2,48,256]{4,3,2,1,0:T(8,128)(2,1)S(1)}, bf16[4,4,2,48,256]{4,3,2,1,0:T(8,128)(2,1)S(1)}, u32[]{:S(2)}, u32[]{:S(2)}) %collective-permute-start.3) | collective-permute-done | bytes 786464 | tf_op jit(solution)/shard_map/ppermute | solution.py:177
  17.4 2.9 %collective-permute-start.4 = (bf16[4,2,48,256]{3,2,1,0:T(8,128)(2,1)S(1)}, bf16[4,2,48,256]{3,2,1,0:T(8,128)(2,1)S(1)}, u32[]{:S(2)}, u32[]{:S(2)}) collective-permute-start(bf16[4,2,48,256]{3,2,1,0:T(8,128)(2,1)S(1)} %get-tuple-element.27), channel_id=1, source_target_pairs={{0,1},{1,0},{2,3},{3,2},{4,5},{5,4},{6,7},{7,6},{8,9},{9,8},{10,11... | collective-permute-start | bytes 589832 | tf_op jit(solution)/shard_map/ppermute | solution.py:177
  20.3 1.5 %collective-permute-start.5 = (bf16[4,2,48,256]{3,2,1,0:T(8,128)(2,1)S(1)}, bf16[4,2,48,256]{3,2,1,0:T(8,128)(2,1)S(1)}, u32[]{:S(2)}, u32[]{:S(2)}) collective-permute-start(bf16[4,2,48,256]{3,2,1,0:T(8,128)(2,1)S(1)} %get-tuple-element.28), channel_id=1, source_target_pairs={{0,2},{1,3},{2,0},{3,1},{4,6},{5,7},{6,4},{7,5},{8,10},{9,11},{10,... | collective-permute-start | bytes 589832 | tf_op jit(solution)/shard_map/ppermute | solution.py:177
  21.8 0.3 shard_map.113
  22.2 2.1 %collective-permute-start = (bf16[72,192]{1,0:T(8,128)(2,1)S(1)}, bf16[72,192]{1,0:T(8,128)(2,1)S(1)}, u32[]{:S(2)}, u32[]{:S(2)}) collective-permute-start(bf16[72,192]{1,0:T(8,128)(2,1)S(1)} %get-tuple-element.21), channel_id=1, source_target_pairs={{0,4},{1,5},{2,6},{3,7},{4,0},{5,1},{6,2},{7,3},{8,12},{9,13},{10,... | collective-permute-start | bytes 82952 | tf_op jit(solution)/shard_map/ppermute | solution.py:177
  24.3 2.6 %collective-permute-start.1 = (bf16[72,192]{1,0:T(8,128)(2,1)S(1)}, bf16[72,192]{1,0:T(8,128)(2,1)S(1)}, u32[]{:S(2)}, u32[]{:S(2)}) collective-permute-start(bf16[72,192]{1,0:T(8,128)(2,1)S(1)} %get-tuple-element.22), channel_id=1, source_target_pairs={{0,8},{1,9},{2,10},{3,11},{4,12},{5,13},{6,14},{7,15},{8,0},{9,1},... | collective-permute-start | bytes 82952 | tf_op jit(solution)/shard_map/ppermute | solution.py:177
  26.9 3.4 %collective-permute-start.2 = (bf16[72,192]{1,0:T(8,128)(2,1)S(1)}, bf16[72,192]{1,0:T(8,128)(2,1)S(1)}, u32[]{:S(2)}, u32[]{:S(2)}) collective-permute-start(bf16[72,192]{1,0:T(8,128)(2,1)S(1)} %get-tuple-element.23), channel_id=1, source_target_pairs={{0,12},{1,13},{2,14},{3,15},{4,8},{5,9},{6,10},{7,11},{8,4},{9,5},... | collective-permute-start | bytes 82952 | tf_op jit(solution)/shard_map/ppermute | solution.py:177
  30.3 2.4 %collective-permute-done.2.refs_3_ = bf16[72,192]{1,0:T(8,128)(2,1)S(1)} collective-permute-done((bf16[72,192]{1,0:T(8,128)(2,1)S(1)}, bf16[72,192]{1,0:T(8,128)(2,1)S(1)}, u32[]{:S(2)}, u32[]{:S(2)}) %collective-permute-start.2) | collective-permute-done | bytes 27680 | tf_op jit(solution)/shard_map/ppermute | solution.py:177
  32.6 0.8 %shard_map.116 = (f32[72,256]{1,0:T(8,128)S(1)}, bf16[72,256]{1,0:T(8,128)(2,1)S(1)}, bf16[72,256]{1,0:T(8,128)(2,1)S(1)}, bf16[72,256]{1,0:T(8,128)(2,1)S(1)}) custom-call(s32[32]{0:T(128)S(1)} %copy-done.5, bf16[72,192]{1,0:T(8,128)(2,1)S(1)} %get-tuple-element.20.refs_0_, bf16[72,192]{1,0:T(8,128)(2,1)S(1)} %collective-permute-done.refs_1_, ...), custom_call_target="tpu_custom_call" | custom-call | tf_op jit(solution)/shard_map/pallas_call | solution.py:140
  33.4 3.5 %collective-permute-start.7 = (bf16[72,256]{1,0:T(8,128)(2,1)S(1)}, bf16[72,256]{1,0:T(8,128)(2,1)S(1)}, u32[]{:S(2)}, u32[]{:S(2)}) collective-permute-start(bf16[72,256]{1,0:T(8,128)(2,1)S(1)} %get-tuple-element.31), channel_id=1, source_target_pairs={{0,12},{1,13},{2,14},{3,15},{4,8},{5,9},{6,10},{7,11},{8,4},{9,5},... | collective-permute-start | bytes 110600 | tf_op jit(solution)/shard_map/ppermute | solution.py:177
  36.9 1.0 %collective-permute-start.9 = (bf16[72,256]{1,0:T(8,128)(2,1)S(1)}, bf16[72,256]{1,0:T(8,128)(2,1)S(1)}, u32[]{:S(2)}, u32[]{:S(2)}) collective-permute-start(bf16[72,256]{1,0:T(8,128)(2,1)S(1)} %get-tuple-element.33), channel_id=1, source_target_pairs={{0,4},{1,5},{2,6},{3,7},{4,0},{5,1},{6,2},{7,3},{8,12},{9,13},{10,... | collective-permute-start | bytes 110600 | tf_op jit(solution)/shard_map/ppermute | solution.py:177
  37.9 0.6 shard_map.117.factor_ref
  38.5 0.9 %collective-permute-done.7.two = bf16[72,256]{1,0:T(8,128)(2,1)S(1)} collective-permute-done((bf16[72,256]{1,0:T(8,128)(2,1)S(1)}, bf16[72,256]{1,0:T(8,128)(2,1)S(1)}, u32[]{:S(2)}, u32[]{:S(2)}) %collective-permute-start.7) | collective-permute-done | bytes 36896 | tf_op jit(solution)/shard_map/ppermute | solution.py:177
  39.4 2.6 %collective-permute-done.8.three = bf16[72,256]{1,0:T(8,128)(2,1)S(1)} collective-permute-done((bf16[72,256]{1,0:T(8,128)(2,1)S(1)}, bf16[72,256]{1,0:T(8,128)(2,1)S(1)}, u32[]{:S(2)}, u32[]{:S(2)}) %collective-permute-start.8) | collective-permute-done | bytes 36896 | tf_op jit(solution)/shard_map/ppermute | solution.py:177
  42.3 1.3 %collective-permute-start.12 = (bf16[72,256]{1,0:T(8,128)(2,1)S(1)}, bf16[72,256]{1,0:T(8,128)(2,1)S(1)}, u32[]{:S(2)}, u32[]{:S(2)}) collective-permute-start(bf16[72,256]{1,0:T(8,128)(2,1)S(1)} %shard_map.118.refs_4_), channel_id=1, source_target_pairs={{0,12},{1,13},{2,14},{3,15},{4,8},{5,9},{6,10},{7,11},{8,4},{9,5},... | collective-permute-start | bytes 110600 | tf_op jit(solution)/shard_map/ppermute | solution.py:177
  43.6 0.9 %collective-permute-start.11 = (bf16[72,256]{1,0:T(8,128)(2,1)S(1)}, bf16[72,256]{1,0:T(8,128)(2,1)S(1)}, u32[]{:S(2)}, u32[]{:S(2)}) collective-permute-start(bf16[72,256]{1,0:T(8,128)(2,1)S(1)} %shard_map.118.refs_4_), channel_id=1, source_target_pairs={{0,8},{1,9},{2,10},{3,11},{4,12},{5,13},{6,14},{7,15},{8,0},{9,1},... | collective-permute-start | bytes 110600 | tf_op jit(solution)/shard_map/ppermute | solution.py:177
  44.5 2.2 %collective-permute-start.10 = (bf16[72,256]{1,0:T(8,128)(2,1)S(1)}, bf16[72,256]{1,0:T(8,128)(2,1)S(1)}, u32[]{:S(2)}, u32[]{:S(2)}) collective-permute-start(bf16[72,256]{1,0:T(8,128)(2,1)S(1)} %shard_map.118.refs_4_), channel_id=1, source_target_pairs={{0,4},{1,5},{2,6},{3,7},{4,0},{5,1},{6,2},{7,3},{8,12},{9,13},{10,... | collective-permute-start | bytes 110600 | tf_op jit(solution)/shard_map/ppermute | solution.py:177
  46.8 1.4 %collective-permute-done.12.refs_7_ = bf16[72,256]{1,0:T(8,128)(2,1)S(1)} collective-permute-done((bf16[72,256]{1,0:T(8,128)(2,1)S(1)}, bf16[72,256]{1,0:T(8,128)(2,1)S(1)}, u32[]{:S(2)}, u32[]{:S(2)}) %collective-permute-start.12) | collective-permute-done | bytes 36896 | tf_op jit(solution)/shard_map/ppermute | solution.py:177
  48.1 0.4 collective-permute-done.11.refs_6_
  48.5 0.4 collective-permute-done.10.refs_5_
  48.9 1.0 %shard_map.119 = (bf16[4,2,48,256]{3,2,1,0:T(8,128)(2,1)S(1)}, bf16[4,2,48,256]{3,2,1,0:T(8,128)(2,1)S(1)}, bf16[4,2,48,256]{3,2,1,0:T(8,128)(2,1)S(1)}, bf16[4,2,48,256]{3,2,1,0:T(8,128)(2,1)S(1)}) custom-call(s32[32]{0:T(128)S(1)} %copy-done.5, bf16[72,192]{1,0:T(8,128)(2,1)S(1)} %get-tuple-element.20.refs_0_, ...), custom_call_target="tpu_custom_call" | custom-call | tf_op jit(solution)/shard_map/pallas_call | solution.py:140
  49.9 1.6 %collective-permute-start.13 = (bf16[4,2,48,256]{3,2,1,0:T(8,128)(2,1)S(1)}, bf16[4,2,48,256]{3,2,1,0:T(8,128)(2,1)S(1)}, u32[]{:S(2)}, u32[]{:S(2)}) collective-permute-start(bf16[4,2,48,256]{3,2,1,0:T(8,128)(2,1)S(1)} %get-tuple-element.35), channel_id=1, source_target_pairs={{0,1},{1,0},{2,3},{3,2},{4,5},{5,4},{6,7},{7,6},{8,9},{9,8},{10,11... | collective-permute-start | bytes 589832 | tf_op jit(solution)/shard_map/ppermute | solution.py:177
  51.5 1.4 %collective-permute-start.14 = (bf16[4,2,48,256]{3,2,1,0:T(8,128)(2,1)S(1)}, bf16[4,2,48,256]{3,2,1,0:T(8,128)(2,1)S(1)}, u32[]{:S(2)}, u32[]{:S(2)}) collective-permute-start(bf16[4,2,48,256]{3,2,1,0:T(8,128)(2,1)S(1)} %get-tuple-element.36), channel_id=1, source_target_pairs={{0,2},{1,3},{2,0},{3,1},{4,6},{5,7},{6,4},{7,5},{8,10},{9,11},{10,... | collective-permute-start | bytes 589832 | tf_op jit(solution)/shard_map/ppermute | solution.py:177
  52.9 0.6 collective-permute-start.15
  53.4 2.2 %collective-permute-done.13.refs_1_ = bf16[4,2,48,256]{3,2,1,0:T(8,128)(2,1)S(1)} collective-permute-done((bf16[4,2,48,256]{3,2,1,0:T(8,128)(2,1)S(1)}, bf16[4,2,48,256]{3,2,1,0:T(8,128)(2,1)S(1)}, u32[]{:S(2)}, u32[]{:S(2)}) %collective-permute-start.13) | collective-permute-done | bytes 196640 | tf_op jit(solution)/shard_map/ppermute | solution.py:177
  55.6 2.6 %collective-permute-done.14.refs_2_ = bf16[4,2,48,256]{3,2,1,0:T(8,128)(2,1)S(1)} collective-permute-done((bf16[4,2,48,256]{3,2,1,0:T(8,128)(2,1)S(1)}, bf16[4,2,48,256]{3,2,1,0:T(8,128)(2,1)S(1)}, u32[]{:S(2)}, u32[]{:S(2)}) %collective-permute-start.14) | collective-permute-done | bytes 196640 | tf_op jit(solution)/shard_map/ppermute | solution.py:177
  58.2 1.2 %collective-permute-done.15.refs_3_ = bf16[4,2,48,256]{3,2,1,0:T(8,128)(2,1)S(1)} collective-permute-done((bf16[4,2,48,256]{3,2,1,0:T(8,128)(2,1)S(1)}, bf16[4,2,48,256]{3,2,1,0:T(8,128)(2,1)S(1)}, u32[]{:S(2)}, u32[]{:S(2)}) %collective-permute-start.15) | collective-permute-done | bytes 196640 | tf_op jit(solution)/shard_map/ppermute | solution.py:177
  59.5 0.6 slice_bitcast_fusion
  60.1 0.8 %collective-permute-done.19.refs_7_ = bf16[4,2,48,256]{3,2,1,0:T(8,128)(2,1)S(1)} collective-permute-done((bf16[4,2,48,256]{3,2,1,0:T(8,128)(2,1)S(1)}, bf16[4,2,48,256]{3,2,1,0:T(8,128)(2,1)S(1)}, u32[]{:S(2)}, u32[]{:S(2)}) %collective-permute-start.19) | collective-permute-done | bytes 196640 | tf_op jit(solution)/shard_map/ppermute | solution.py:177
  60.9 8.1 %shard_map.120 = f32[48,768,128]{2,1,0:T(8,128)} custom-call(s32[32]{0:T(128)S(1)} %copy-done.5, bf16[2,768,128]{2,1,0:T(8,128)(2,1)S(1)} %copy-done, bf16[4,2,48,256]{3,2,1,0:T(8,128)(2,1)S(1)} %get-tuple-element.34.refs_0_, bf16[4,2,48,256]{3,2,1,0:T(8,128)(2,1)S(1)} %collective-permute-done.13.refs_1_, ...), custom_call_target="tpu_custom_call" | custom-call | flops 1207959552 | bytes 18874368 | tf_op jit(solution)/shard_map/pallas_call | solution.py:375
  (33 shorter events, 0.5 us)
Async XLA Ops:
  0.6 37.3 %copy-start.7 = (f32[1,128]{1,0:T(1,128)S(1)}, f32[1,128]{1,0:T(1,128)}, u32[]{:S(2)}) copy-start(f32[1,128]{1,0:T(1,128)} %constant.11.damping_ref) | copy-start | bytes 1540
  0.6 60.3 %copy-start = (bf16[2,768,128]{2,1,0:T(8,128)(2,1)S(1)}, bf16[2,768,128]{2,1,0:T(8,128)(2,1)}, u32[]{:S(2)}) copy-start(bf16[2,768,128]{2,1,0:T(8,128)(2,1)} %constant.7.clone.table_ref) | copy-start | bytes 1179652
  0.7 32.0 %copy-start.5 = (s32[32]{0:T(128)S(1)}, s32[32]{0:T(128)}, u32[]{:S(2)}) copy-start(s32[32]{0:T(128)} %orders_ref.7) | copy-start | bytes 388
  0.7 21.2 %copy-start.1 = (bf16[1,65,768]{2,1,0:T(8,128)(2,1)S(1)}, bf16[1,65,768]{2,1,0:T(8,128)(2,1)}, u32[]{:S(2)}) copy-start(bf16[1,65,768]{2,1,0:T(8,128)(2,1)} %legendre_ref.1) | copy-start | bytes 299524
  0.7 37.2 %copy-start.6 = (f32[128]{0:T(128)S(1)}, f32[128]{0:T(128)}, u32[]{:S(2)}) copy-start(f32[128]{0:T(128)} %param.14) | copy-start | bytes 1540
  0.7 41.3 %copy-start.4 = (bf16[128,128]{1,0:T(8,128)(2,1)S(1)}, bf16[128,128]{1,0:T(8,128)(2,1)}, u32[]{:S(2)}) copy-start(bf16[128,128]{1,0:T(8,128)(2,1)} %left_ref.1) | copy-start | bytes 98308
  0.7 41.3 %copy-start.3 = (bf16[128,128]{1,0:T(8,128)(2,1)S(1)}, bf16[128,128]{1,0:T(8,128)(2,1)}, u32[]{:S(2)}) copy-start(bf16[128,128]{1,0:T(8,128)(2,1)} %right_ref.1) | copy-start | bytes 98308
  0.7 41.3 %copy-start.2 = (bf16[1,65,256]{2,1,0:T(8,128)(2,1)S(1)}, bf16[1,65,256]{2,1,0:T(8,128)(2,1)}, u32[]{:S(2)}) copy-start(bf16[1,65,256]{2,1,0:T(8,128)(2,1)} %state_ref.1) | copy-start | bytes 99844
  14.8 2.4 %collective-permute-start.3 = (bf16[4,4,2,48,256]{4,3,2,1,0:T(8,128)(2,1)S(1)}, bf16[4,4,2,48,256]{4,3,2,1,0:T(8,128)(2,1)S(1)}, u32[]{:S(2)}, u32[]{:S(2)}) collective-permute-start(bf16[4,4,2,48,256]{4,3,2,1,0:T(8,128)(2,1)S(1)} %get-tuple-element.25), channel_id=1, source_target_pairs={{0,16},{1,17},{2,18},{3,19},{4,20},{5,21},{6,22},{7,23},{8,24},{9,... | collective-permute-start | bytes 2359304 | tf_op jit(solution)/shard_map/ppermute | solution.py:177
  17.4 15.3 %collective-permute-start.4 = (bf16[4,2,48,256]{3,2,1,0:T(8,128)(2,1)S(1)}, bf16[4,2,48,256]{3,2,1,0:T(8,128)(2,1)S(1)}, u32[]{:S(2)}, u32[]{:S(2)}) collective-permute-start(bf16[4,2,48,256]{3,2,1,0:T(8,128)(2,1)S(1)} %get-tuple-element.27), channel_id=1, source_target_pairs={{0,1},{1,0},{2,3},{3,2},{4,5},{5,4},{6,7},{7,6},{8,9},{9,8},{10,11... | collective-permute-start | bytes 589832 | tf_op jit(solution)/shard_map/ppermute | solution.py:177
  20.3 12.3 %collective-permute-start.5 = (bf16[4,2,48,256]{3,2,1,0:T(8,128)(2,1)S(1)}, bf16[4,2,48,256]{3,2,1,0:T(8,128)(2,1)S(1)}, u32[]{:S(2)}, u32[]{:S(2)}) collective-permute-start(bf16[4,2,48,256]{3,2,1,0:T(8,128)(2,1)S(1)} %get-tuple-element.28), channel_id=1, source_target_pairs={{0,2},{1,3},{2,0},{3,1},{4,6},{5,7},{6,4},{7,5},{8,10},{9,11},{10,... | collective-permute-start | bytes 589832 | tf_op jit(solution)/shard_map/ppermute | solution.py:177
  21.8 10.8 %collective-permute-start.6 = (bf16[4,2,48,256]{3,2,1,0:T(8,128)(2,1)S(1)}, bf16[4,2,48,256]{3,2,1,0:T(8,128)(2,1)S(1)}, u32[]{:S(2)}, u32[]{:S(2)}) collective-permute-start(bf16[4,2,48,256]{3,2,1,0:T(8,128)(2,1)S(1)} %get-tuple-element.29), channel_id=1, source_target_pairs={{0,3},{1,2},{2,1},{3,0},{4,7},{5,6},{6,5},{7,4},{8,11},{9,10},{10,... | collective-permute-start | bytes 589832 | tf_op jit(solution)/shard_map/ppermute | solution.py:177
  22.2 4.7 %collective-permute-start = (bf16[72,192]{1,0:T(8,128)(2,1)S(1)}, bf16[72,192]{1,0:T(8,128)(2,1)S(1)}, u32[]{:S(2)}, u32[]{:S(2)}) collective-permute-start(bf16[72,192]{1,0:T(8,128)(2,1)S(1)} %get-tuple-element.21), channel_id=1, source_target_pairs={{0,4},{1,5},{2,6},{3,7},{4,0},{5,1},{6,2},{7,3},{8,12},{9,13},{10,... | collective-permute-start | bytes 82952 | tf_op jit(solution)/shard_map/ppermute | solution.py:177
  24.3 6.0 %collective-permute-start.1 = (bf16[72,192]{1,0:T(8,128)(2,1)S(1)}, bf16[72,192]{1,0:T(8,128)(2,1)S(1)}, u32[]{:S(2)}, u32[]{:S(2)}) collective-permute-start(bf16[72,192]{1,0:T(8,128)(2,1)S(1)} %get-tuple-element.22), channel_id=1, source_target_pairs={{0,8},{1,9},{2,10},{3,11},{4,12},{5,13},{6,14},{7,15},{8,0},{9,1},... | collective-permute-start | bytes 82952 | tf_op jit(solution)/shard_map/ppermute | solution.py:177
  26.9 5.8 %collective-permute-start.2 = (bf16[72,192]{1,0:T(8,128)(2,1)S(1)}, bf16[72,192]{1,0:T(8,128)(2,1)S(1)}, u32[]{:S(2)}, u32[]{:S(2)}) collective-permute-start(bf16[72,192]{1,0:T(8,128)(2,1)S(1)} %get-tuple-element.23), channel_id=1, source_target_pairs={{0,12},{1,13},{2,14},{3,15},{4,8},{5,9},{6,10},{7,11},{8,4},{9,5},... | collective-permute-start | bytes 82952 | tf_op jit(solution)/shard_map/ppermute | solution.py:177
  33.4 6.0 %collective-permute-start.7 = (bf16[72,256]{1,0:T(8,128)(2,1)S(1)}, bf16[72,256]{1,0:T(8,128)(2,1)S(1)}, u32[]{:S(2)}, u32[]{:S(2)}) collective-permute-start(bf16[72,256]{1,0:T(8,128)(2,1)S(1)} %get-tuple-element.31), channel_id=1, source_target_pairs={{0,12},{1,13},{2,14},{3,15},{4,8},{5,9},{6,10},{7,11},{8,4},{9,5},... | collective-permute-start | bytes 110600 | tf_op jit(solution)/shard_map/ppermute | solution.py:177
  36.9 5.1 %collective-permute-start.8 = (bf16[72,256]{1,0:T(8,128)(2,1)S(1)}, bf16[72,256]{1,0:T(8,128)(2,1)S(1)}, u32[]{:S(2)}, u32[]{:S(2)}) collective-permute-start(bf16[72,256]{1,0:T(8,128)(2,1)S(1)} %get-tuple-element.32), channel_id=1, source_target_pairs={{0,8},{1,9},{2,10},{3,11},{4,12},{5,13},{6,14},{7,15},{8,0},{9,1},... | collective-permute-start | bytes 110600 | tf_op jit(solution)/shard_map/ppermute | solution.py:177
  36.9 5.1 %collective-permute-start.9 = (bf16[72,256]{1,0:T(8,128)(2,1)S(1)}, bf16[72,256]{1,0:T(8,128)(2,1)S(1)}, u32[]{:S(2)}, u32[]{:S(2)}) collective-permute-start(bf16[72,256]{1,0:T(8,128)(2,1)S(1)} %get-tuple-element.33), channel_id=1, source_target_pairs={{0,4},{1,5},{2,6},{3,7},{4,0},{5,1},{6,2},{7,3},{8,12},{9,13},{10,... | collective-permute-start | bytes 110600 | tf_op jit(solution)/shard_map/ppermute | solution.py:177
  42.3 5.8 %collective-permute-start.12 = (bf16[72,256]{1,0:T(8,128)(2,1)S(1)}, bf16[72,256]{1,0:T(8,128)(2,1)S(1)}, u32[]{:S(2)}, u32[]{:S(2)}) collective-permute-start(bf16[72,256]{1,0:T(8,128)(2,1)S(1)} %shard_map.118.refs_4_), channel_id=1, source_target_pairs={{0,12},{1,13},{2,14},{3,15},{4,8},{5,9},{6,10},{7,11},{8,4},{9,5},... | collective-permute-start | bytes 110600 | tf_op jit(solution)/shard_map/ppermute | solution.py:177
  43.6 4.9 %collective-permute-start.11 = (bf16[72,256]{1,0:T(8,128)(2,1)S(1)}, bf16[72,256]{1,0:T(8,128)(2,1)S(1)}, u32[]{:S(2)}, u32[]{:S(2)}) collective-permute-start(bf16[72,256]{1,0:T(8,128)(2,1)S(1)} %shard_map.118.refs_4_), channel_id=1, source_target_pairs={{0,8},{1,9},{2,10},{3,11},{4,12},{5,13},{6,14},{7,15},{8,0},{9,1},... | collective-permute-start | bytes 110600 | tf_op jit(solution)/shard_map/ppermute | solution.py:177
  44.5 4.4 %collective-permute-start.10 = (bf16[72,256]{1,0:T(8,128)(2,1)S(1)}, bf16[72,256]{1,0:T(8,128)(2,1)S(1)}, u32[]{:S(2)}, u32[]{:S(2)}) collective-permute-start(bf16[72,256]{1,0:T(8,128)(2,1)S(1)} %shard_map.118.refs_4_), channel_id=1, source_target_pairs={{0,4},{1,5},{2,6},{3,7},{4,0},{5,1},{6,2},{7,3},{8,12},{9,13},{10,... | collective-permute-start | bytes 110600 | tf_op jit(solution)/shard_map/ppermute | solution.py:177
  49.9 5.7 %collective-permute-start.13 = (bf16[4,2,48,256]{3,2,1,0:T(8,128)(2,1)S(1)}, bf16[4,2,48,256]{3,2,1,0:T(8,128)(2,1)S(1)}, u32[]{:S(2)}, u32[]{:S(2)}) collective-permute-start(bf16[4,2,48,256]{3,2,1,0:T(8,128)(2,1)S(1)} %get-tuple-element.35), channel_id=1, source_target_pairs={{0,1},{1,0},{2,3},{3,2},{4,5},{5,4},{6,7},{7,6},{8,9},{9,8},{10,11... | collective-permute-start | bytes 589832 | tf_op jit(solution)/shard_map/ppermute | solution.py:177
  51.5 6.7 %collective-permute-start.14 = (bf16[4,2,48,256]{3,2,1,0:T(8,128)(2,1)S(1)}, bf16[4,2,48,256]{3,2,1,0:T(8,128)(2,1)S(1)}, u32[]{:S(2)}, u32[]{:S(2)}) collective-permute-start(bf16[4,2,48,256]{3,2,1,0:T(8,128)(2,1)S(1)} %get-tuple-element.36), channel_id=1, source_target_pairs={{0,2},{1,3},{2,0},{3,1},{4,6},{5,7},{6,4},{7,5},{8,10},{9,11},{10,... | collective-permute-start | bytes 589832 | tf_op jit(solution)/shard_map/ppermute | solution.py:177
  52.9 6.6 %collective-permute-start.15 = (bf16[4,2,48,256]{3,2,1,0:T(8,128)(2,1)S(1)}, bf16[4,2,48,256]{3,2,1,0:T(8,128)(2,1)S(1)}, u32[]{:S(2)}, u32[]{:S(2)}) collective-permute-start(bf16[4,2,48,256]{3,2,1,0:T(8,128)(2,1)S(1)} %get-tuple-element.37), channel_id=1, source_target_pairs={{0,3},{1,2},{2,1},{3,0},{4,7},{5,6},{6,5},{7,4},{8,11},{9,10},{10,... | collective-permute-start | bytes 589832 | tf_op jit(solution)/shard_map/ppermute | solution.py:177
  53.4 6.6 %collective-permute-start.16 = (bf16[4,2,48,256]{3,2,1,0:T(8,128)(2,1)S(1)}, bf16[4,2,48,256]{3,2,1,0:T(8,128)(2,1)S(1)}, u32[]{:S(2)}, u32[]{:S(2)}) collective-permute-start(bf16[4,2,48,256]{3,2,1,0:T(8,128)(2,1)S(1)} %get-tuple-element.34.refs_0_), channel_id=1, source_target_pairs={{0,16},{1,17},{2,18},{3,19},{4,20},{5,21},{6,22},{7,23},{8,24},{9,... | collective-permute-start | bytes 589832 | tf_op jit(solution)/shard_map/ppermute | solution.py:177
  55.6 4.5 %collective-permute-start.17 = (bf16[4,2,48,256]{3,2,1,0:T(8,128)(2,1)S(1)}, bf16[4,2,48,256]{3,2,1,0:T(8,128)(2,1)S(1)}, u32[]{:S(2)}, u32[]{:S(2)}) collective-permute-start(bf16[4,2,48,256]{3,2,1,0:T(8,128)(2,1)S(1)} %collective-permute-done.13.refs_1_), channel_id=1, source_target_pairs={{0,16},{1,17},{2,18},{3,19},{4,20},{5,21},{6,22},{7,23},{8,24},{9,... | collective-permute-start | bytes 589832 | tf_op jit(solution)/shard_map/ppermute | solution.py:177
  58.2 1.9 %collective-permute-start.18 = (bf16[4,2,48,256]{3,2,1,0:T(8,128)(2,1)S(1)}, bf16[4,2,48,256]{3,2,1,0:T(8,128)(2,1)S(1)}, u32[]{:S(2)}, u32[]{:S(2)}) collective-permute-start(bf16[4,2,48,256]{3,2,1,0:T(8,128)(2,1)S(1)} %collective-permute-done.14.refs_2_), channel_id=1, source_target_pairs={{0,16},{1,17},{2,18},{3,19},{4,20},{5,21},{6,22},{7,23},{8,24},{9,... | collective-permute-start | bytes 589832 | tf_op jit(solution)/shard_map/ppermute | solution.py:177
  59.5 1.4 %collective-permute-start.19 = (bf16[4,2,48,256]{3,2,1,0:T(8,128)(2,1)S(1)}, bf16[4,2,48,256]{3,2,1,0:T(8,128)(2,1)S(1)}, u32[]{:S(2)}, u32[]{:S(2)}) collective-permute-start(bf16[4,2,48,256]{3,2,1,0:T(8,128)(2,1)S(1)} %collective-permute-done.15.refs_3_), channel_id=1, source_target_pairs={{0,16},{1,17},{2,18},{3,19},{4,20},{5,21},{6,22},{7,23},{8,24},{9,... | collective-permute-start | bytes 589832 | tf_op jit(solution)/shard_map/ppermute | solution.py:177

commit v8 on v7

--- a/solution.py
+++ b/solution.py
@@ -207,7 +207,6 @@
     for at in range(sems.shape[0]):
         chunk(at).start()
     table_copy.wait()
-    orders_copy.wait()
 
     def one_block(block, carry):
         for at in range(0, lat_block, 2):
@@ -222,6 +221,7 @@
         return carry
 
     lax.fori_loop(0, blocks, one_block, 0)
+    orders_copy.wait()
     for sec, out in ((1, send_ref), (0, keep_ref)):
         for flat, deep in np.ndindex(4, 4):
             order = orders_ref[pair_at(sec, deep, flat)]
@@ -412,11 +412,13 @@
         [slab] * 4,
         scratch=[pltpu.VMEM((16, padded, lat_rows), jnp.bfloat16)],
     )
-    weights = [cuts[0]] + [exchange(cuts[deep], deep=deep) for deep in (1, 2, 3)]
+    near = exchange(cuts[1], deep=1)
 
     keep, send = forward_sums(pair_orders, forward_table, grid_terms, 8)
     block = shape(4, 2, lat_rows, columns)
-    blocks = call(add_kernel, [keep, exchange(send, sec=1)], [block] * 4, mib=24)
+    taken, near = lax.optimization_barrier((exchange(send, sec=1), near))
+    blocks = call(add_kernel, [keep, taken], [block] * 4, mib=24)
+    weights = [cuts[0], near] + [exchange(cuts[deep], deep=deep) for deep in (2, 3)]
     takes = [blocks[0]] + [exchange(blocks[flat], flat=flat) for flat in (1, 2, 3)]
 
     sums = call(

time: 69.1 us -> 69 us (level)
  starting transfers between devices: 25.5 us -> 23.9 us
  waiting for transfers between devices: 16.8 us -> 18.3 us
    ppermute x20, starting transfers between devices: 25.5 us -> 23.9 us  [exchange(): return lax.ppermute(array, names, pairs)]
    ppermute x20, waiting for transfers between devices: 16.8 us -> 18.3 us  [exchange(): return lax.ppermute(array, names, pairs)]
  transfers between devices with their start and end apart: 20 -> 20, of which waited for: 11 -> 12; matrix products, arithmetic and copies ran while one was open for 1% -> 1% of each run, Pallas kernels for 1% -> 1%
where the time goes in v8:
time: 69 us; the launch traced here: 68.9 us
  Pallas kernels  25.2 us (37%)
  starting transfers between devices  23.9 us (35%)
  waiting for transfers between devices  18.3 us (27%)
  between operations  0.79 us (1%)
    ppermute x20, starting transfers between devices, exchange(): return lax.ppermute(array, names, pairs)  23.9 us
    ppermute x20, waiting for transfers between devices, exchange(): return lax.ppermute(array, names, pairs)  18.3 us
    pallas_call x1, Pallas kernels, forward_sums(): pl.pallas_call(forward_kernel, in_specs=[pl.BlockSpec(memory_space=pltpu....  14.1 us
    pallas_call x1, Pallas kernels, inverse_values(): pl.pallas_call(inverse_kernel, in_specs=[smem()] + [vmem()] * (1 + len(ta...  8.06 us
    pallas_call x6, Pallas kernels, call(): pl.pallas_call(kernel, in_specs=[smem()] * scalars + [vmem()] * (len(oper...  3.09 us
  transfers between devices with their start and end apart: 20, of which 12 were waited for; matrix products, arithmetic and copies ran while one was open for 1% of the time, Pallas kernels for 1%

profile of v8, /device:TPU:0, one launch (start us, length us, event | category | flops | bytes accessed | tf_op | source)
XLA Modules:
  0.0 68.9 jit_solution(3145400839808590319)
XLA Ops:
  0.7 14.1 %shard_map.114 = (f32[4,4,2,48,256]{4,3,2,1,0:T(8,128)S(1)}, bf16[4,4,2,48,256]{4,3,2,1,0:T(8,128)(2,1)S(1)}) custom-call(s32[32]{0:T(128)} %orders_ref.7, bf16[2,128,768]{2,1,0:T(8,128)(2,1)} %constant.6.clone.table_ref, f32[48,768,128]{2,1,0:T(8,128)} %grid_ref.1), custom_call_target="tpu_custom_call" | custom-call | flops 1207959552 | bytes 18874368 | tf_op jit(solution)/shard_map/pallas_call | solution.py:241
  14.8 0.5 collective-permute-start
  15.3 0.3 shard_map.113
  15.6 2.7 %collective-permute-start.1 = (bf16[72,192]{1,0:T(8,128)(2,1)S(1)}, bf16[72,192]{1,0:T(8,128)(2,1)S(1)}, u32[]{:S(2)}, u32[]{:S(2)}) collective-permute-start(bf16[72,192]{1,0:T(8,128)(2,1)S(1)} %get-tuple-element.24), channel_id=1, source_target_pairs={{0,4},{1,5},{2,6},{3,7},{4,0},{5,1},{6,2},{7,3},{8,12},{9,13},{10,... | collective-permute-start | bytes 82952 | tf_op jit(solution)/shard_map/ppermute | solution.py:177
  18.3 2.1 %collective-permute-done.1.refs_1_ = bf16[72,192]{1,0:T(8,128)(2,1)S(1)} collective-permute-done((bf16[72,192]{1,0:T(8,128)(2,1)S(1)}, bf16[72,192]{1,0:T(8,128)(2,1)S(1)}, u32[]{:S(2)}, u32[]{:S(2)}) %collective-permute-start.1) | collective-permute-done | bytes 27680 | tf_op jit(solution)/shard_map/ppermute | solution.py:177
  20.6 1.8 %collective-permute-start.4 = (bf16[4,2,48,256]{3,2,1,0:T(8,128)(2,1)S(1)}, bf16[4,2,48,256]{3,2,1,0:T(8,128)(2,1)S(1)}, u32[]{:S(2)}, u32[]{:S(2)}) collective-permute-start(bf16[4,2,48,256]{3,2,1,0:T(8,128)(2,1)S(1)} %get-tuple-element.31), channel_id=1, source_target_pairs={{0,1},{1,0},{2,3},{3,2},{4,5},{5,4},{6,7},{7,6},{8,9},{9,8},{10,11... | collective-permute-start | bytes 589832 | tf_op jit(solution)/shard_map/ppermute | solution.py:177
  22.4 1.5 %collective-permute-start.5 = (bf16[4,2,48,256]{3,2,1,0:T(8,128)(2,1)S(1)}, bf16[4,2,48,256]{3,2,1,0:T(8,128)(2,1)S(1)}, u32[]{:S(2)}, u32[]{:S(2)}) collective-permute-start(bf16[4,2,48,256]{3,2,1,0:T(8,128)(2,1)S(1)} %get-tuple-element.32), channel_id=1, source_target_pairs={{0,2},{1,3},{2,0},{3,1},{4,6},{5,7},{6,4},{7,5},{8,10},{9,11},{10,... | collective-permute-start | bytes 589832 | tf_op jit(solution)/shard_map/ppermute | solution.py:177
  24.1 2.8 %collective-permute-start.2 = (bf16[72,192]{1,0:T(8,128)(2,1)S(1)}, bf16[72,192]{1,0:T(8,128)(2,1)S(1)}, u32[]{:S(2)}, u32[]{:S(2)}) collective-permute-start(bf16[72,192]{1,0:T(8,128)(2,1)S(1)} %get-tuple-element.26), channel_id=1, source_target_pairs={{0,8},{1,9},{2,10},{3,11},{4,12},{5,13},{6,14},{7,15},{8,0},{9,1},... | collective-permute-start | bytes 82952 | tf_op jit(solution)/shard_map/ppermute | solution.py:177
  27.0 1.3 %collective-permute-start.3 = (bf16[72,192]{1,0:T(8,128)(2,1)S(1)}, bf16[72,192]{1,0:T(8,128)(2,1)S(1)}, u32[]{:S(2)}, u32[]{:S(2)}) collective-permute-start(bf16[72,192]{1,0:T(8,128)(2,1)S(1)} %get-tuple-element.27), channel_id=1, source_target_pairs={{0,12},{1,13},{2,14},{3,15},{4,8},{5,9},{6,10},{7,11},{8,4},{9,5},... | collective-permute-start | bytes 82952 | tf_op jit(solution)/shard_map/ppermute | solution.py:177
  28.3 0.8 %collective-permute-done.2.refs_2_ = bf16[72,192]{1,0:T(8,128)(2,1)S(1)} collective-permute-done((bf16[72,192]{1,0:T(8,128)(2,1)S(1)}, bf16[72,192]{1,0:T(8,128)(2,1)S(1)}, u32[]{:S(2)}, u32[]{:S(2)}) %collective-permute-start.2) | collective-permute-done | bytes 27680 | tf_op jit(solution)/shard_map/ppermute | solution.py:177
  29.2 3.6 %collective-permute-done.3.refs_3_ = bf16[72,192]{1,0:T(8,128)(2,1)S(1)} collective-permute-done((bf16[72,192]{1,0:T(8,128)(2,1)S(1)}, bf16[72,192]{1,0:T(8,128)(2,1)S(1)}, u32[]{:S(2)}, u32[]{:S(2)}) %collective-permute-start.3) | collective-permute-done | bytes 27680 | tf_op jit(solution)/shard_map/ppermute | solution.py:177
  32.7 0.8 %shard_map.116 = (f32[72,256]{1,0:T(8,128)S(1)}, bf16[72,256]{1,0:T(8,128)(2,1)S(1)}, bf16[72,256]{1,0:T(8,128)(2,1)S(1)}, bf16[72,256]{1,0:T(8,128)(2,1)S(1)}) custom-call(s32[32]{0:T(128)S(1)} %copy-done.5, bf16[72,192]{1,0:T(8,128)(2,1)S(1)} %get-tuple-element.22.refs_0_, bf16[72,192]{1,0:T(8,128)(2,1)S(1)} %collective-permute-done.1.refs_1_, ...), custom_call_target="tpu_custom_call" | custom-call | tf_op jit(solution)/shard_map/pallas_call | solution.py:140
  33.6 3.4 %collective-permute-start.7 = (bf16[72,256]{1,0:T(8,128)(2,1)S(1)}, bf16[72,256]{1,0:T(8,128)(2,1)S(1)}, u32[]{:S(2)}, u32[]{:S(2)}) collective-permute-start(bf16[72,256]{1,0:T(8,128)(2,1)S(1)} %get-tuple-element.35), channel_id=1, source_target_pairs={{0,12},{1,13},{2,14},{3,15},{4,8},{5,9},{6,10},{7,11},{8,4},{9,5},... | collective-permute-start | bytes 110600 | tf_op jit(solution)/shard_map/ppermute | solution.py:177
  36.9 1.1 %collective-permute-start.9 = (bf16[72,256]{1,0:T(8,128)(2,1)S(1)}, bf16[72,256]{1,0:T(8,128)(2,1)S(1)}, u32[]{:S(2)}, u32[]{:S(2)}) collective-permute-start(bf16[72,256]{1,0:T(8,128)(2,1)S(1)} %get-tuple-element.37), channel_id=1, source_target_pairs={{0,4},{1,5},{2,6},{3,7},{4,0},{5,1},{6,2},{7,3},{8,12},{9,13},{10,... | collective-permute-start | bytes 110600 | tf_op jit(solution)/shard_map/ppermute | solution.py:177
  38.0 0.6 shard_map.117.factor_ref
  38.6 0.8 %collective-permute-done.7.two = bf16[72,256]{1,0:T(8,128)(2,1)S(1)} collective-permute-done((bf16[72,256]{1,0:T(8,128)(2,1)S(1)}, bf16[72,256]{1,0:T(8,128)(2,1)S(1)}, u32[]{:S(2)}, u32[]{:S(2)}) %collective-permute-start.7) | collective-permute-done | bytes 36896 | tf_op jit(solution)/shard_map/ppermute | solution.py:177
  39.4 2.7 %collective-permute-done.8.three = bf16[72,256]{1,0:T(8,128)(2,1)S(1)} collective-permute-done((bf16[72,256]{1,0:T(8,128)(2,1)S(1)}, bf16[72,256]{1,0:T(8,128)(2,1)S(1)}, u32[]{:S(2)}, u32[]{:S(2)}) %collective-permute-start.8) | collective-permute-done | bytes 36896 | tf_op jit(solution)/shard_map/ppermute | solution.py:177
  42.4 1.2 %collective-permute-start.12 = (bf16[72,256]{1,0:T(8,128)(2,1)S(1)}, bf16[72,256]{1,0:T(8,128)(2,1)S(1)}, u32[]{:S(2)}, u32[]{:S(2)}) collective-permute-start(bf16[72,256]{1,0:T(8,128)(2,1)S(1)} %shard_map.118.refs_4_), channel_id=1, source_target_pairs={{0,12},{1,13},{2,14},{3,15},{4,8},{5,9},{6,10},{7,11},{8,4},{9,5},... | collective-permute-start | bytes 110600 | tf_op jit(solution)/shard_map/ppermute | solution.py:177
  43.6 0.6 collective-permute-start.11
  44.3 2.6 %collective-permute-start.10 = (bf16[72,256]{1,0:T(8,128)(2,1)S(1)}, bf16[72,256]{1,0:T(8,128)(2,1)S(1)}, u32[]{:S(2)}, u32[]{:S(2)}) collective-permute-start(bf16[72,256]{1,0:T(8,128)(2,1)S(1)} %shard_map.118.refs_4_), channel_id=1, source_target_pairs={{0,4},{1,5},{2,6},{3,7},{4,0},{5,1},{6,2},{7,3},{8,12},{9,13},{10,... | collective-permute-start | bytes 110600 | tf_op jit(solution)/shard_map/ppermute | solution.py:177
  46.9 1.4 %collective-permute-done.12.refs_7_ = bf16[72,256]{1,0:T(8,128)(2,1)S(1)} collective-permute-done((bf16[72,256]{1,0:T(8,128)(2,1)S(1)}, bf16[72,256]{1,0:T(8,128)(2,1)S(1)}, u32[]{:S(2)}, u32[]{:S(2)}) %collective-permute-start.12) | collective-permute-done | bytes 36896 | tf_op jit(solution)/shard_map/ppermute | solution.py:177
  48.2 0.4 collective-permute-done.11.refs_6_
  48.6 0.4 collective-permute-done.10.refs_5_
  49.0 1.0 %shard_map.119 = (bf16[4,2,48,256]{3,2,1,0:T(8,128)(2,1)S(1)}, bf16[4,2,48,256]{3,2,1,0:T(8,128)(2,1)S(1)}, bf16[4,2,48,256]{3,2,1,0:T(8,128)(2,1)S(1)}, bf16[4,2,48,256]{3,2,1,0:T(8,128)(2,1)S(1)}) custom-call(s32[32]{0:T(128)S(1)} %copy-done.5, bf16[72,192]{1,0:T(8,128)(2,1)S(1)} %get-tuple-element.22.refs_0_, ...), custom_call_target="tpu_custom_call" | custom-call | tf_op jit(solution)/shard_map/pallas_call | solution.py:140
  50.0 1.3 %collective-permute-start.13 = (bf16[4,2,48,256]{3,2,1,0:T(8,128)(2,1)S(1)}, bf16[4,2,48,256]{3,2,1,0:T(8,128)(2,1)S(1)}, u32[]{:S(2)}, u32[]{:S(2)}) collective-permute-start(bf16[4,2,48,256]{3,2,1,0:T(8,128)(2,1)S(1)} %get-tuple-element.39), channel_id=1, source_target_pairs={{0,1},{1,0},{2,3},{3,2},{4,5},{5,4},{6,7},{7,6},{8,9},{9,8},{10,11... | collective-permute-start | bytes 589832 | tf_op jit(solution)/shard_map/ppermute | solution.py:177
  51.3 1.1 %collective-permute-start.14 = (bf16[4,2,48,256]{3,2,1,0:T(8,128)(2,1)S(1)}, bf16[4,2,48,256]{3,2,1,0:T(8,128)(2,1)S(1)}, u32[]{:S(2)}, u32[]{:S(2)}) collective-permute-start(bf16[4,2,48,256]{3,2,1,0:T(8,128)(2,1)S(1)} %get-tuple-element.40), channel_id=1, source_target_pairs={{0,2},{1,3},{2,0},{3,1},{4,6},{5,7},{6,4},{7,5},{8,10},{9,11},{10,... | collective-permute-start | bytes 589832 | tf_op jit(solution)/shard_map/ppermute | solution.py:177
  52.4 1.2 %collective-permute-start.15 = (bf16[4,2,48,256]{3,2,1,0:T(8,128)(2,1)S(1)}, bf16[4,2,48,256]{3,2,1,0:T(8,128)(2,1)S(1)}, u32[]{:S(2)}, u32[]{:S(2)}) collective-permute-start(bf16[4,2,48,256]{3,2,1,0:T(8,128)(2,1)S(1)} %get-tuple-element.41), channel_id=1, source_target_pairs={{0,3},{1,2},{2,1},{3,0},{4,7},{5,6},{6,5},{7,4},{8,11},{9,10},{10,... | collective-permute-start | bytes 589832 | tf_op jit(solution)/shard_map/ppermute | solution.py:177
  53.5 2.2 %collective-permute-done.13.refs_1_ = bf16[4,2,48,256]{3,2,1,0:T(8,128)(2,1)S(1)} collective-permute-done((bf16[4,2,48,256]{3,2,1,0:T(8,128)(2,1)S(1)}, bf16[4,2,48,256]{3,2,1,0:T(8,128)(2,1)S(1)}, u32[]{:S(2)}, u32[]{:S(2)}) %collective-permute-start.13) | collective-permute-done | bytes 196640 | tf_op jit(solution)/shard_map/ppermute | solution.py:177
  55.7 3.4 %collective-permute-done.14.refs_2_ = bf16[4,2,48,256]{3,2,1,0:T(8,128)(2,1)S(1)} collective-permute-done((bf16[4,2,48,256]{3,2,1,0:T(8,128)(2,1)S(1)}, bf16[4,2,48,256]{3,2,1,0:T(8,128)(2,1)S(1)}, u32[]{:S(2)}, u32[]{:S(2)}) %collective-permute-start.14) | collective-permute-done | bytes 196640 | tf_op jit(solution)/shard_map/ppermute | solution.py:177
  59.1 0.5 collective-permute-start.19
  59.6 0.6 slice_bitcast_fusion
  60.8 8.1 %shard_map.120 = f32[48,768,128]{2,1,0:T(8,128)} custom-call(s32[32]{0:T(128)S(1)} %copy-done.5, bf16[2,768,128]{2,1,0:T(8,128)(2,1)S(1)} %copy-done, bf16[4,2,48,256]{3,2,1,0:T(8,128)(2,1)S(1)} %get-tuple-element.38.refs_0_, bf16[4,2,48,256]{3,2,1,0:T(8,128)(2,1)S(1)} %collective-permute-done.13.refs_1_, ...), custom_call_target="tpu_custom_call" | custom-call | flops 1207959552 | bytes 18874368 | tf_op jit(solution)/shard_map/pallas_call | solution.py:375
  (33 shorter events, 1.3 us)
Async XLA Ops:
  0.6 37.4 %copy-start.7 = (f32[1,128]{1,0:T(1,128)S(1)}, f32[1,128]{1,0:T(1,128)}, u32[]{:S(2)}) copy-start(f32[1,128]{1,0:T(1,128)} %constant.11.damping_ref) | copy-start | bytes 1540
  0.6 60.1 %copy-start = (bf16[2,768,128]{2,1,0:T(8,128)(2,1)S(1)}, bf16[2,768,128]{2,1,0:T(8,128)(2,1)}, u32[]{:S(2)}) copy-start(bf16[2,768,128]{2,1,0:T(8,128)(2,1)} %constant.7.clone.table_ref) | copy-start | bytes 1179652
  0.7 32.1 %copy-start.5 = (s32[32]{0:T(128)S(1)}, s32[32]{0:T(128)}, u32[]{:S(2)}) copy-start(s32[32]{0:T(128)} %orders_ref.7) | copy-start | bytes 388
  0.7 14.6 %copy-start.1 = (bf16[1,65,768]{2,1,0:T(8,128)(2,1)S(1)}, bf16[1,65,768]{2,1,0:T(8,128)(2,1)}, u32[]{:S(2)}) copy-start(bf16[1,65,768]{2,1,0:T(8,128)(2,1)} %legendre_ref.1) | copy-start | bytes 299524
  0.7 37.3 %copy-start.6 = (f32[128]{0:T(128)S(1)}, f32[128]{0:T(128)}, u32[]{:S(2)}) copy-start(f32[128]{0:T(128)} %param.14) | copy-start | bytes 1540
  0.7 41.4 %copy-start.4 = (bf16[128,128]{1,0:T(8,128)(2,1)S(1)}, bf16[128,128]{1,0:T(8,128)(2,1)}, u32[]{:S(2)}) copy-start(bf16[128,128]{1,0:T(8,128)(2,1)} %left_ref.1) | copy-start | bytes 98308
  0.7 41.4 %copy-start.3 = (bf16[128,128]{1,0:T(8,128)(2,1)S(1)}, bf16[128,128]{1,0:T(8,128)(2,1)}, u32[]{:S(2)}) copy-start(bf16[128,128]{1,0:T(8,128)(2,1)} %right_ref.1) | copy-start | bytes 98308
  0.7 41.4 %copy-start.2 = (bf16[1,65,256]{2,1,0:T(8,128)(2,1)S(1)}, bf16[1,65,256]{2,1,0:T(8,128)(2,1)}, u32[]{:S(2)}) copy-start(bf16[1,65,256]{2,1,0:T(8,128)(2,1)} %state_ref.1) | copy-start | bytes 99844
  14.8 5.6 %collective-permute-start = (bf16[4,4,2,48,256]{4,3,2,1,0:T(8,128)(2,1)S(1)}, bf16[4,4,2,48,256]{4,3,2,1,0:T(8,128)(2,1)S(1)}, u32[]{:S(2)}, u32[]{:S(2)}) collective-permute-start(bf16[4,4,2,48,256]{4,3,2,1,0:T(8,128)(2,1)S(1)} %get-tuple-element.23), channel_id=1, source_target_pairs={{0,16},{1,17},{2,18},{3,19},{4,20},{5,21},{6,22},{7,23},{8,24},{9,... | collective-permute-start | bytes 2359304 | tf_op jit(solution)/shard_map/ppermute | solution.py:177
  15.6 4.8 %collective-permute-start.1 = (bf16[72,192]{1,0:T(8,128)(2,1)S(1)}, bf16[72,192]{1,0:T(8,128)(2,1)S(1)}, u32[]{:S(2)}, u32[]{:S(2)}) collective-permute-start(bf16[72,192]{1,0:T(8,128)(2,1)S(1)} %get-tuple-element.24), channel_id=1, source_target_pairs={{0,4},{1,5},{2,6},{3,7},{4,0},{5,1},{6,2},{7,3},{8,12},{9,13},{10,... | collective-permute-start | bytes 82952 | tf_op jit(solution)/shard_map/ppermute | solution.py:177
  20.6 12.2 %collective-permute-start.4 = (bf16[4,2,48,256]{3,2,1,0:T(8,128)(2,1)S(1)}, bf16[4,2,48,256]{3,2,1,0:T(8,128)(2,1)S(1)}, u32[]{:S(2)}, u32[]{:S(2)}) collective-permute-start(bf16[4,2,48,256]{3,2,1,0:T(8,128)(2,1)S(1)} %get-tuple-element.31), channel_id=1, source_target_pairs={{0,1},{1,0},{2,3},{3,2},{4,5},{5,4},{6,7},{7,6},{8,9},{9,8},{10,11... | collective-permute-start | bytes 589832 | tf_op jit(solution)/shard_map/ppermute | solution.py:177
  22.4 10.3 %collective-permute-start.5 = (bf16[4,2,48,256]{3,2,1,0:T(8,128)(2,1)S(1)}, bf16[4,2,48,256]{3,2,1,0:T(8,128)(2,1)S(1)}, u32[]{:S(2)}, u32[]{:S(2)}) collective-permute-start(bf16[4,2,48,256]{3,2,1,0:T(8,128)(2,1)S(1)} %get-tuple-element.32), channel_id=1, source_target_pairs={{0,2},{1,3},{2,0},{3,1},{4,6},{5,7},{6,4},{7,5},{8,10},{9,11},{10,... | collective-permute-start | bytes 589832 | tf_op jit(solution)/shard_map/ppermute | solution.py:177
  23.9 8.8 %collective-permute-start.6 = (bf16[4,2,48,256]{3,2,1,0:T(8,128)(2,1)S(1)}, bf16[4,2,48,256]{3,2,1,0:T(8,128)(2,1)S(1)}, u32[]{:S(2)}, u32[]{:S(2)}) collective-permute-start(bf16[4,2,48,256]{3,2,1,0:T(8,128)(2,1)S(1)} %get-tuple-element.33), channel_id=1, source_target_pairs={{0,3},{1,2},{2,1},{3,0},{4,7},{5,6},{6,5},{7,4},{8,11},{9,10},{10,... | collective-permute-start | bytes 589832 | tf_op jit(solution)/shard_map/ppermute | solution.py:177
  24.1 5.0 %collective-permute-start.2 = (bf16[72,192]{1,0:T(8,128)(2,1)S(1)}, bf16[72,192]{1,0:T(8,128)(2,1)S(1)}, u32[]{:S(2)}, u32[]{:S(2)}) collective-permute-start(bf16[72,192]{1,0:T(8,128)(2,1)S(1)} %get-tuple-element.26), channel_id=1, source_target_pairs={{0,8},{1,9},{2,10},{3,11},{4,12},{5,13},{6,14},{7,15},{8,0},{9,1},... | collective-permute-start | bytes 82952 | tf_op jit(solution)/shard_map/ppermute | solution.py:177
  27.0 5.8 %collective-permute-start.3 = (bf16[72,192]{1,0:T(8,128)(2,1)S(1)}, bf16[72,192]{1,0:T(8,128)(2,1)S(1)}, u32[]{:S(2)}, u32[]{:S(2)}) collective-permute-start(bf16[72,192]{1,0:T(8,128)(2,1)S(1)} %get-tuple-element.27), channel_id=1, source_target_pairs={{0,12},{1,13},{2,14},{3,15},{4,8},{5,9},{6,10},{7,11},{8,4},{9,5},... | collective-permute-start | bytes 82952 | tf_op jit(solution)/shard_map/ppermute | solution.py:177
  33.6 5.8 %collective-permute-start.7 = (bf16[72,256]{1,0:T(8,128)(2,1)S(1)}, bf16[72,256]{1,0:T(8,128)(2,1)S(1)}, u32[]{:S(2)}, u32[]{:S(2)}) collective-permute-start(bf16[72,256]{1,0:T(8,128)(2,1)S(1)} %get-tuple-element.35), channel_id=1, source_target_pairs={{0,12},{1,13},{2,14},{3,15},{4,8},{5,9},{6,10},{7,11},{8,4},{9,5},... | collective-permute-start | bytes 110600 | tf_op jit(solution)/shard_map/ppermute | solution.py:177
  36.9 5.1 %collective-permute-start.8 = (bf16[72,256]{1,0:T(8,128)(2,1)S(1)}, bf16[72,256]{1,0:T(8,128)(2,1)S(1)}, u32[]{:S(2)}, u32[]{:S(2)}) collective-permute-start(bf16[72,256]{1,0:T(8,128)(2,1)S(1)} %get-tuple-element.36), channel_id=1, source_target_pairs={{0,8},{1,9},{2,10},{3,11},{4,12},{5,13},{6,14},{7,15},{8,0},{9,1},... | collective-permute-start | bytes 110600 | tf_op jit(solution)/shard_map/ppermute | solution.py:177
  36.9 5.1 %collective-permute-start.9 = (bf16[72,256]{1,0:T(8,128)(2,1)S(1)}, bf16[72,256]{1,0:T(8,128)(2,1)S(1)}, u32[]{:S(2)}, u32[]{:S(2)}) collective-permute-start(bf16[72,256]{1,0:T(8,128)(2,1)S(1)} %get-tuple-element.37), channel_id=1, source_target_pairs={{0,4},{1,5},{2,6},{3,7},{4,0},{5,1},{6,2},{7,3},{8,12},{9,13},{10,... | collective-permute-start | bytes 110600 | tf_op jit(solution)/shard_map/ppermute | solution.py:177
  42.4 5.8 %collective-permute-start.12 = (bf16[72,256]{1,0:T(8,128)(2,1)S(1)}, bf16[72,256]{1,0:T(8,128)(2,1)S(1)}, u32[]{:S(2)}, u32[]{:S(2)}) collective-permute-start(bf16[72,256]{1,0:T(8,128)(2,1)S(1)} %shard_map.118.refs_4_), channel_id=1, source_target_pairs={{0,12},{1,13},{2,14},{3,15},{4,8},{5,9},{6,10},{7,11},{8,4},{9,5},... | collective-permute-start | bytes 110600 | tf_op jit(solution)/shard_map/ppermute | solution.py:177
  43.6 5.0 %collective-permute-start.11 = (bf16[72,256]{1,0:T(8,128)(2,1)S(1)}, bf16[72,256]{1,0:T(8,128)(2,1)S(1)}, u32[]{:S(2)}, u32[]{:S(2)}) collective-permute-start(bf16[72,256]{1,0:T(8,128)(2,1)S(1)} %shard_map.118.refs_4_), channel_id=1, source_target_pairs={{0,8},{1,9},{2,10},{3,11},{4,12},{5,13},{6,14},{7,15},{8,0},{9,1},... | collective-permute-start | bytes 110600 | tf_op jit(solution)/shard_map/ppermute | solution.py:177
  44.3 4.7 %collective-permute-start.10 = (bf16[72,256]{1,0:T(8,128)(2,1)S(1)}, bf16[72,256]{1,0:T(8,128)(2,1)S(1)}, u32[]{:S(2)}, u32[]{:S(2)}) collective-permute-start(bf16[72,256]{1,0:T(8,128)(2,1)S(1)} %shard_map.118.refs_4_), channel_id=1, source_target_pairs={{0,4},{1,5},{2,6},{3,7},{4,0},{5,1},{6,2},{7,3},{8,12},{9,13},{10,... | collective-permute-start | bytes 110600 | tf_op jit(solution)/shard_map/ppermute | solution.py:177
  50.0 5.7 %collective-permute-start.13 = (bf16[4,2,48,256]{3,2,1,0:T(8,128)(2,1)S(1)}, bf16[4,2,48,256]{3,2,1,0:T(8,128)(2,1)S(1)}, u32[]{:S(2)}, u32[]{:S(2)}) collective-permute-start(bf16[4,2,48,256]{3,2,1,0:T(8,128)(2,1)S(1)} %get-tuple-element.39), channel_id=1, source_target_pairs={{0,1},{1,0},{2,3},{3,2},{4,5},{5,4},{6,7},{7,6},{8,9},{9,8},{10,11... | collective-permute-start | bytes 589832 | tf_op jit(solution)/shard_map/ppermute | solution.py:177
  51.3 7.8 %collective-permute-start.14 = (bf16[4,2,48,256]{3,2,1,0:T(8,128)(2,1)S(1)}, bf16[4,2,48,256]{3,2,1,0:T(8,128)(2,1)S(1)}, u32[]{:S(2)}, u32[]{:S(2)}) collective-permute-start(bf16[4,2,48,256]{3,2,1,0:T(8,128)(2,1)S(1)} %get-tuple-element.40), channel_id=1, source_target_pairs={{0,2},{1,3},{2,0},{3,1},{4,6},{5,7},{6,4},{7,5},{8,10},{9,11},{10,... | collective-permute-start | bytes 589832 | tf_op jit(solution)/shard_map/ppermute | solution.py:177
  52.4 6.7 %collective-permute-start.15 = (bf16[4,2,48,256]{3,2,1,0:T(8,128)(2,1)S(1)}, bf16[4,2,48,256]{3,2,1,0:T(8,128)(2,1)S(1)}, u32[]{:S(2)}, u32[]{:S(2)}) collective-permute-start(bf16[4,2,48,256]{3,2,1,0:T(8,128)(2,1)S(1)} %get-tuple-element.41), channel_id=1, source_target_pairs={{0,3},{1,2},{2,1},{3,0},{4,7},{5,6},{6,5},{7,4},{8,11},{9,10},{10,... | collective-permute-start | bytes 589832 | tf_op jit(solution)/shard_map/ppermute | solution.py:177
  53.5 6.7 %collective-permute-start.16 = (bf16[4,2,48,256]{3,2,1,0:T(8,128)(2,1)S(1)}, bf16[4,2,48,256]{3,2,1,0:T(8,128)(2,1)S(1)}, u32[]{:S(2)}, u32[]{:S(2)}) collective-permute-start(bf16[4,2,48,256]{3,2,1,0:T(8,128)(2,1)S(1)} %get-tuple-element.38.refs_0_), channel_id=1, source_target_pairs={{0,16},{1,17},{2,18},{3,19},{4,20},{5,21},{6,22},{7,23},{8,24},{9,... | collective-permute-start | bytes 589832 | tf_op jit(solution)/shard_map/ppermute | solution.py:177
  55.7 4.5 %collective-permute-start.17 = (bf16[4,2,48,256]{3,2,1,0:T(8,128)(2,1)S(1)}, bf16[4,2,48,256]{3,2,1,0:T(8,128)(2,1)S(1)}, u32[]{:S(2)}, u32[]{:S(2)}) collective-permute-start(bf16[4,2,48,256]{3,2,1,0:T(8,128)(2,1)S(1)} %collective-permute-done.13.refs_1_), channel_id=1, source_target_pairs={{0,16},{1,17},{2,18},{3,19},{4,20},{5,21},{6,22},{7,23},{8,24},{9,... | collective-permute-start | bytes 589832 | tf_op jit(solution)/shard_map/ppermute | solution.py:177
  59.1 1.4 %collective-permute-start.18 = (bf16[4,2,48,256]{3,2,1,0:T(8,128)(2,1)S(1)}, bf16[4,2,48,256]{3,2,1,0:T(8,128)(2,1)S(1)}, u32[]{:S(2)}, u32[]{:S(2)}) collective-permute-start(bf16[4,2,48,256]{3,2,1,0:T(8,128)(2,1)S(1)} %collective-permute-done.14.refs_2_), channel_id=1, source_target_pairs={{0,16},{1,17},{2,18},{3,19},{4,20},{5,21},{6,22},{7,23},{8,24},{9,... | collective-permute-start | bytes 589832 | tf_op jit(solution)/shard_map/ppermute | solution.py:177
  59.1 1.7 %collective-permute-start.19 = (bf16[4,2,48,256]{3,2,1,0:T(8,128)(2,1)S(1)}, bf16[4,2,48,256]{3,2,1,0:T(8,128)(2,1)S(1)}, u32[]{:S(2)}, u32[]{:S(2)}) collective-permute-start(bf16[4,2,48,256]{3,2,1,0:T(8,128)(2,1)S(1)} %collective-permute-done.15.refs_3_), channel_id=1, source_target_pairs={{0,16},{1,17},{2,18},{3,19},{4,20},{5,21},{6,22},{7,23},{8,24},{9,... | collective-permute-start | bytes 589832 | tf_op jit(solution)/shard_map/ppermute | solution.py:177

commit v9 on v8

--- a/solution.py
+++ b/solution.py
@@ -189,24 +189,37 @@
         out[...] = jnp.concatenate([parts[first + (plane_index() ^ flat)] for flat in four], axis=1)
 
 
+def arrange_kernel(sec, orders_ref, held, out_ref):
+    blocks, rows, lat_block, radial = held.shape
+    slots = rows // 2
+    for flat, deep in np.ndindex(4, 4):
+        order = orders_ref[pair_at(sec, deep, flat)]
+        for part in range(2):
+            values = held[:, pl.ds(part * slots + 2 * order, 2)].astype(out_ref.dtype)
+            for half in range(2):
+                out_ref[flat, deep, half, :, pl.ds(part * radial, radial)] = values[
+                    :, half
+                ].reshape(blocks * lat_block, radial)
+
+
 def forward_kernel(
-    orders_from, table_ref, grid_ref, keep_ref, send_ref, orders_ref, table, buffer, held, sems, more
+    orders_from, table_ref, grid_ref, held, send_ref, orders_ref, wide, table, buffer, sems, more
 ):
     blocks, rows, lat_block, radial = held.shape
-    slots = rows // 2
 
     def chunk(at):
         return pltpu.make_async_copy(
             grid_ref.at[pl.ds(2 * at, 2)], buffer.at[pl.ds(2 * at, 2)], sems.at[at]
         )
 
-    table_copy = pltpu.make_async_copy(table_ref.at[lax.axis_index("sec")], table, more.at[0])
+    table_copy = pltpu.make_async_copy(table_ref.at[lax.axis_index("sec")], wide, more.at[0])
     orders_copy = pltpu.make_async_copy(orders_from, orders_ref, more.at[1])
     table_copy.start()
     orders_copy.start()
     for at in range(sems.shape[0]):
         chunk(at).start()
     table_copy.wait()
+    table[...] = wide[...].astype(table.dtype)
 
     def one_block(block, carry):
         for at in range(0, lat_block, 2):
@@ -222,15 +235,7 @@
 
     lax.fori_loop(0, blocks, one_block, 0)
     orders_copy.wait()
-    for sec, out in ((1, send_ref), (0, keep_ref)):
-        for flat, deep in np.ndindex(4, 4):
-            order = orders_ref[pair_at(sec, deep, flat)]
-            for part in range(2):
-                values = held[:, pl.ds(part * slots + 2 * order, 2)].astype(out.dtype)
-                for half in range(2):
-                    out[flat, deep, half, :, pl.ds(part * radial, radial)] = values[
-                        :, half
-                    ].reshape(blocks * lat_block, radial)
+    arrange_kernel(1, orders_ref, held, send_ref)
 
 
 def forward_sums(pair_orders, table, grid_terms, lat_block):
@@ -243,14 +248,14 @@
         in_specs=[pl.BlockSpec(memory_space=pltpu.HBM)] * 2 + [anywhere()],
         out_specs=[vmem(), vmem()],
         out_shape=[
-            jax.ShapeDtypeStruct(sizes, jnp.float32),
+            jax.ShapeDtypeStruct((lat_rows // lat_block, rows, lat_block, radial), jnp.float32),
             jax.ShapeDtypeStruct(sizes, jnp.bfloat16),
         ],
         scratch_shapes=[
             pltpu.SMEM(pair_orders.shape, jnp.int32),
-            pltpu.VMEM((rows, phi_count), table.dtype),
+            pltpu.VMEM((rows, phi_count), jnp.float32),
+            pltpu.VMEM((rows, phi_count), jnp.bfloat16),
             pltpu.VMEM(grid_terms.shape, jnp.float32),
-            pltpu.VMEM((lat_rows // lat_block, rows, lat_block, radial), jnp.float32),
             pltpu.SemaphoreType.DMA((lat_rows // 2,)),
             pltpu.SemaphoreType.DMA((2,)),
         ],
@@ -399,7 +404,7 @@
     columns = 2 * radial
     pair_total = pair_orders.shape[0]
     table = natural_table(pair_total, lax.axis_size("sec"), phi_count)
-    forward_table = jnp.asarray(table, jnp.bfloat16)
+    forward_table = jnp.asarray(table)
     inverse_table = jnp.asarray(table.transpose(0, 2, 1), jnp.bfloat16)
 
     def shape(*sizes, dtype=jnp.bfloat16):
@@ -412,13 +417,20 @@
         [slab] * 4,
         scratch=[pltpu.VMEM((16, padded, lat_rows), jnp.bfloat16)],
     )
-    near = exchange(cuts[1], deep=1)
-
-    keep, send = forward_sums(pair_orders, forward_table, grid_terms, 8)
+    weights = [cuts[0]] + [exchange(cuts[deep], deep=deep) for deep in (1, 2, 3)]
+
+    held, send = forward_sums(pair_orders, forward_table, grid_terms, 8)
     block = shape(4, 2, lat_rows, columns)
-    taken, near = lax.optimization_barrier((exchange(send, sec=1), near))
+    taken = exchange(send, sec=1)
+    sizes = (4, 4, 2, lat_rows, columns)
+    keep = call(
+        functools.partial(arrange_kernel, 0),
+        [pair_orders, held],
+        shape(*sizes, dtype=jnp.float32),
+        mib=24,
+        scalars=1,
+    )
     blocks = call(add_kernel, [keep, taken], [block] * 4, mib=24)
-    weights = [cuts[0], near] + [exchange(cuts[deep], deep=deep) for deep in (2, 3)]
     takes = [blocks[0]] + [exchange(blocks[flat], flat=flat) for flat in (1, 2, 3)]
 
     sums = call(
@@ -442,7 +454,8 @@
     )
     new_state = field[None, :rows]
 
-    fields = [field] + [exchange(field, deep=deep) for deep in (1, 2, 3)]
+    moved, new_state = lax.optimization_barrier((exchange(field, deep=1), new_state))
+    fields = [field, moved] + [exchange(field, deep=deep) for deep in (2, 3)]
     blocks = call(
         functools.partial(synthesis_kernel, degrees),
         [pair_orders, *weights, *fields],

time: 69 us -> 69.1 us (level)
  waiting for transfers between devices: 18.3 us -> 16.1 us
  starting transfers between devices: 23.9 us -> 25.5 us
  Pallas kernels: 25.2 us -> 25.9 us
    ppermute x20, waiting for transfers between devices: 18.3 us -> 16.1 us  [exchange(): return lax.ppermute(array, names, pairs)]
    ppermute x20, starting transfers between devices: 23.9 us -> 25.5 us  [exchange(): return lax.ppermute(array, names, pairs)]
    pallas_call x6 -> x7, Pallas kernels: 3.09 us -> 3.76 us  [call(): pl.pallas_call(kernel, in_specs=[smem()] * scalars + [vmem()] * (len(oper...]
  transfers between devices with their start and end apart: 20 -> 20, of which waited for: 12 -> 10; matrix products, arithmetic and copies ran while one was open for 1% -> 1% of each run, Pallas kernels for 1% -> 2%
where the time goes in v9:
time: 69.1 us; the launch traced here: 68.9 us
  Pallas kernels  25.9 us (37%)
  starting transfers between devices  25.5 us (37%)
  waiting for transfers between devices  16.1 us (23%)
  between operations  0.79 us (1%)
    ppermute x20, starting transfers between devices, exchange(): return lax.ppermute(array, names, pairs)  25.5 us
    ppermute x20, waiting for transfers between devices, exchange(): return lax.ppermute(array, names, pairs)  16.1 us
    pallas_call x1, Pallas kernels, forward_sums(): pl.pallas_call(forward_kernel, in_specs=[pl.BlockSpec(memory_space=pltpu....  14.1 us
    pallas_call x1, Pallas kernels, inverse_values(): pl.pallas_call(inverse_kernel, in_specs=[smem()] + [vmem()] * (1 + len(ta...  8.06 us
    pallas_call x7, Pallas kernels, call(): pl.pallas_call(kernel, in_specs=[smem()] * scalars + [vmem()] * (len(oper...  3.76 us
  transfers between devices with their start and end apart: 20, of which 10 were waited for; matrix products, arithmetic and copies ran while one was open for 1% of the time, Pallas kernels for 2%

profile of v9, /device:TPU:0, one launch (start us, length us, event | category | flops | bytes accessed | tf_op | source)
XLA Modules:
  0.0 68.9 jit_solution(7124101130886636640)
XLA Ops:
  0.7 14.1 %shard_map.114 = (f32[6,128,8,128]{3,2,1,0:T(8,128)S(1)}, bf16[4,4,2,48,256]{4,3,2,1,0:T(8,128)(2,1)S(1)}) custom-call(s32[32]{0:T(128)} %orders_ref.9, f32[2,128,768]{2,1,0:T(8,128)} %constant.6.clone.table_ref, f32[48,768,128]{2,1,0:T(8,128)} %grid_ref.1), custom_call_target="tpu_custom_call" | custom-call | flops 1207959552 | bytes 18874368 | tf_op jit(solution)/shard_map/pallas_call | solution.py:246
  14.8 0.5 collective-permute-start.3
  15.3 0.7 shard_map.115.keep_ref
  16.0 1.2 %collective-permute-done.3.take_ref = bf16[4,4,2,48,256]{4,3,2,1,0:T(8,128)(2,1)S(1)} collective-permute-done((bf16[4,4,2,48,256]{4,3,2,1,0:T(8,128)(2,1)S(1)}, bf16[4,4,2,48,256]{4,3,2,1,0:T(8,128)(2,1)S(1)}, u32[]{:S(2)}, u32[]{:S(2)}) %collective-permute-start.3) | collective-permute-done | bytes 786464 | tf_op jit(solution)/shard_map/ppermute | solution.py:177
  17.4 2.9 %collective-permute-start.4 = (bf16[4,2,48,256]{3,2,1,0:T(8,128)(2,1)S(1)}, bf16[4,2,48,256]{3,2,1,0:T(8,128)(2,1)S(1)}, u32[]{:S(2)}, u32[]{:S(2)}) collective-permute-start(bf16[4,2,48,256]{3,2,1,0:T(8,128)(2,1)S(1)} %get-tuple-element.29), channel_id=1, source_target_pairs={{0,1},{1,0},{2,3},{3,2},{4,5},{5,4},{6,7},{7,6},{8,9},{9,8},{10,11... | collective-permute-start | bytes 589832 | tf_op jit(solution)/shard_map/ppermute | solution.py:177
  20.3 1.5 %collective-permute-start.5 = (bf16[4,2,48,256]{3,2,1,0:T(8,128)(2,1)S(1)}, bf16[4,2,48,256]{3,2,1,0:T(8,128)(2,1)S(1)}, u32[]{:S(2)}, u32[]{:S(2)}) collective-permute-start(bf16[4,2,48,256]{3,2,1,0:T(8,128)(2,1)S(1)} %get-tuple-element.30), channel_id=1, source_target_pairs={{0,2},{1,3},{2,0},{3,1},{4,6},{5,7},{6,4},{7,5},{8,10},{9,11},{10,... | collective-permute-start | bytes 589832 | tf_op jit(solution)/shard_map/ppermute | solution.py:177
  21.8 0.3 shard_map.113
  22.2 2.1 %collective-permute-start = (bf16[72,192]{1,0:T(8,128)(2,1)S(1)}, bf16[72,192]{1,0:T(8,128)(2,1)S(1)}, u32[]{:S(2)}, u32[]{:S(2)}) collective-permute-start(bf16[72,192]{1,0:T(8,128)(2,1)S(1)} %get-tuple-element.23), channel_id=1, source_target_pairs={{0,4},{1,5},{2,6},{3,7},{4,0},{5,1},{6,2},{7,3},{8,12},{9,13},{10,... | collective-permute-start | bytes 82952 | tf_op jit(solution)/shard_map/ppermute | solution.py:177
  24.3 2.6 %collective-permute-start.1 = (bf16[72,192]{1,0:T(8,128)(2,1)S(1)}, bf16[72,192]{1,0:T(8,128)(2,1)S(1)}, u32[]{:S(2)}, u32[]{:S(2)}) collective-permute-start(bf16[72,192]{1,0:T(8,128)(2,1)S(1)} %get-tuple-element.24), channel_id=1, source_target_pairs={{0,8},{1,9},{2,10},{3,11},{4,12},{5,13},{6,14},{7,15},{8,0},{9,1},... | collective-permute-start | bytes 82952 | tf_op jit(solution)/shard_map/ppermute | solution.py:177
  26.8 3.4 %collective-permute-start.2 = (bf16[72,192]{1,0:T(8,128)(2,1)S(1)}, bf16[72,192]{1,0:T(8,128)(2,1)S(1)}, u32[]{:S(2)}, u32[]{:S(2)}) collective-permute-start(bf16[72,192]{1,0:T(8,128)(2,1)S(1)} %get-tuple-element.25), channel_id=1, source_target_pairs={{0,12},{1,13},{2,14},{3,15},{4,8},{5,9},{6,10},{7,11},{8,4},{9,5},... | collective-permute-start | bytes 82952 | tf_op jit(solution)/shard_map/ppermute | solution.py:177
  30.2 2.4 %collective-permute-done.2.refs_3_ = bf16[72,192]{1,0:T(8,128)(2,1)S(1)} collective-permute-done((bf16[72,192]{1,0:T(8,128)(2,1)S(1)}, bf16[72,192]{1,0:T(8,128)(2,1)S(1)}, u32[]{:S(2)}, u32[]{:S(2)}) %collective-permute-start.2) | collective-permute-done | bytes 27680 | tf_op jit(solution)/shard_map/ppermute | solution.py:177
  32.6 0.8 %shard_map.117 = (f32[72,256]{1,0:T(8,128)S(1)}, bf16[72,256]{1,0:T(8,128)(2,1)S(1)}, bf16[72,256]{1,0:T(8,128)(2,1)S(1)}, bf16[72,256]{1,0:T(8,128)(2,1)S(1)}) custom-call(s32[32]{0:T(128)S(1)} %copy-done.5, bf16[72,192]{1,0:T(8,128)(2,1)S(1)} %get-tuple-element.22.refs_0_, bf16[72,192]{1,0:T(8,128)(2,1)S(1)} %collective-permute-done.refs_1_, ...), custom_call_target="tpu_custom_call" | custom-call | tf_op jit(solution)/shard_map/pallas_call | solution.py:140
  33.4 3.5 %collective-permute-start.7 = (bf16[72,256]{1,0:T(8,128)(2,1)S(1)}, bf16[72,256]{1,0:T(8,128)(2,1)S(1)}, u32[]{:S(2)}, u32[]{:S(2)}) collective-permute-start(bf16[72,256]{1,0:T(8,128)(2,1)S(1)} %get-tuple-element.33), channel_id=1, source_target_pairs={{0,12},{1,13},{2,14},{3,15},{4,8},{5,9},{6,10},{7,11},{8,4},{9,5},... | collective-permute-start | bytes 110600 | tf_op jit(solution)/shard_map/ppermute | solution.py:177
  36.9 1.0 %collective-permute-start.9 = (bf16[72,256]{1,0:T(8,128)(2,1)S(1)}, bf16[72,256]{1,0:T(8,128)(2,1)S(1)}, u32[]{:S(2)}, u32[]{:S(2)}) collective-permute-start(bf16[72,256]{1,0:T(8,128)(2,1)S(1)} %get-tuple-element.35), channel_id=1, source_target_pairs={{0,4},{1,5},{2,6},{3,7},{4,0},{5,1},{6,2},{7,3},{8,12},{9,13},{10,... | collective-permute-start | bytes 110600 | tf_op jit(solution)/shard_map/ppermute | solution.py:177
  37.9 0.6 shard_map.118.factor_ref
  38.5 0.9 %collective-permute-done.7.two = bf16[72,256]{1,0:T(8,128)(2,1)S(1)} collective-permute-done((bf16[72,256]{1,0:T(8,128)(2,1)S(1)}, bf16[72,256]{1,0:T(8,128)(2,1)S(1)}, u32[]{:S(2)}, u32[]{:S(2)}) %collective-permute-start.7) | collective-permute-done | bytes 36896 | tf_op jit(solution)/shard_map/ppermute | solution.py:177
  39.4 2.6 %collective-permute-done.8.three = bf16[72,256]{1,0:T(8,128)(2,1)S(1)} collective-permute-done((bf16[72,256]{1,0:T(8,128)(2,1)S(1)}, bf16[72,256]{1,0:T(8,128)(2,1)S(1)}, u32[]{:S(2)}, u32[]{:S(2)}) %collective-permute-start.8) | collective-permute-done | bytes 36896 | tf_op jit(solution)/shard_map/ppermute | solution.py:177
  42.0 0.3 shard_map.119.refs_4_
  42.3 1.3 %collective-permute-start.12 = (bf16[72,256]{1,0:T(8,128)(2,1)S(1)}, bf16[72,256]{1,0:T(8,128)(2,1)S(1)}, u32[]{:S(2)}, u32[]{:S(2)}) collective-permute-start(bf16[72,256]{1,0:T(8,128)(2,1)S(1)} %shard_map.119.refs_4_), channel_id=1, source_target_pairs={{0,12},{1,13},{2,14},{3,15},{4,8},{5,9},{6,10},{7,11},{8,4},{9,5},... | collective-permute-start | bytes 110600 | tf_op jit(solution)/shard_map/ppermute | solution.py:177
  43.6 0.9 %collective-permute-start.11 = (bf16[72,256]{1,0:T(8,128)(2,1)S(1)}, bf16[72,256]{1,0:T(8,128)(2,1)S(1)}, u32[]{:S(2)}, u32[]{:S(2)}) collective-permute-start(bf16[72,256]{1,0:T(8,128)(2,1)S(1)} %shard_map.119.refs_4_), channel_id=1, source_target_pairs={{0,8},{1,9},{2,10},{3,11},{4,12},{5,13},{6,14},{7,15},{8,0},{9,1},... | collective-permute-start | bytes 110600 | tf_op jit(solution)/shard_map/ppermute | solution.py:177
  44.5 2.2 %collective-permute-start.10 = (bf16[72,256]{1,0:T(8,128)(2,1)S(1)}, bf16[72,256]{1,0:T(8,128)(2,1)S(1)}, u32[]{:S(2)}, u32[]{:S(2)}) collective-permute-start(bf16[72,256]{1,0:T(8,128)(2,1)S(1)} %shard_map.119.refs_4_), channel_id=1, source_target_pairs={{0,4},{1,5},{2,6},{3,7},{4,0},{5,1},{6,2},{7,3},{8,12},{9,13},{10,... | collective-permute-start | bytes 110600 | tf_op jit(solution)/shard_map/ppermute | solution.py:177
  46.7 0.6 slice_bitcast_fusion
  47.4 1.5 %collective-permute-done.10.refs_5_ = bf16[72,256]{1,0:T(8,128)(2,1)S(1)} collective-permute-done((bf16[72,256]{1,0:T(8,128)(2,1)S(1)}, bf16[72,256]{1,0:T(8,128)(2,1)S(1)}, u32[]{:S(2)}, u32[]{:S(2)}) %collective-permute-start.10) | collective-permute-done | bytes 36896 | tf_op jit(solution)/shard_map/ppermute | solution.py:177
  48.9 1.0 %shard_map.120 = (bf16[4,2,48,256]{3,2,1,0:T(8,128)(2,1)S(1)}, bf16[4,2,48,256]{3,2,1,0:T(8,128)(2,1)S(1)}, bf16[4,2,48,256]{3,2,1,0:T(8,128)(2,1)S(1)}, bf16[4,2,48,256]{3,2,1,0:T(8,128)(2,1)S(1)}) custom-call(s32[32]{0:T(128)S(1)} %copy-done.5, bf16[72,192]{1,0:T(8,128)(2,1)S(1)} %get-tuple-element.22.refs_0_, ...), custom_call_target="tpu_custom_call" | custom-call | tf_op jit(solution)/shard_map/pallas_call | solution.py:140
  49.9 1.6 %collective-permute-start.13 = (bf16[4,2,48,256]{3,2,1,0:T(8,128)(2,1)S(1)}, bf16[4,2,48,256]{3,2,1,0:T(8,128)(2,1)S(1)}, u32[]{:S(2)}, u32[]{:S(2)}) collective-permute-start(bf16[4,2,48,256]{3,2,1,0:T(8,128)(2,1)S(1)} %get-tuple-element.38), channel_id=1, source_target_pairs={{0,1},{1,0},{2,3},{3,2},{4,5},{5,4},{6,7},{7,6},{8,9},{9,8},{10,11... | collective-permute-start | bytes 589832 | tf_op jit(solution)/shard_map/ppermute | solution.py:177
  51.5 1.4 %collective-permute-start.14 = (bf16[4,2,48,256]{3,2,1,0:T(8,128)(2,1)S(1)}, bf16[4,2,48,256]{3,2,1,0:T(8,128)(2,1)S(1)}, u32[]{:S(2)}, u32[]{:S(2)}) collective-permute-start(bf16[4,2,48,256]{3,2,1,0:T(8,128)(2,1)S(1)} %get-tuple-element.39), channel_id=1, source_target_pairs={{0,2},{1,3},{2,0},{3,1},{4,6},{5,7},{6,4},{7,5},{8,10},{9,11},{10,... | collective-permute-start | bytes 589832 | tf_op jit(solution)/shard_map/ppermute | solution.py:177
  52.9 0.5 collective-permute-start.15
  53.4 2.2 %collective-permute-done.13.refs_1_ = bf16[4,2,48,256]{3,2,1,0:T(8,128)(2,1)S(1)} collective-permute-done((bf16[4,2,48,256]{3,2,1,0:T(8,128)(2,1)S(1)}, bf16[4,2,48,256]{3,2,1,0:T(8,128)(2,1)S(1)}, u32[]{:S(2)}, u32[]{:S(2)}) %collective-permute-start.13) | collective-permute-done | bytes 196640 | tf_op jit(solution)/shard_map/ppermute | solution.py:177
  55.6 2.6 %collective-permute-done.14.refs_2_ = bf16[4,2,48,256]{3,2,1,0:T(8,128)(2,1)S(1)} collective-permute-done((bf16[4,2,48,256]{3,2,1,0:T(8,128)(2,1)S(1)}, bf16[4,2,48,256]{3,2,1,0:T(8,128)(2,1)S(1)}, u32[]{:S(2)}, u32[]{:S(2)}) %collective-permute-start.14) | collective-permute-done | bytes 196640 | tf_op jit(solution)/shard_map/ppermute | solution.py:177
  58.2 1.2 %collective-permute-done.15.refs_3_ = bf16[4,2,48,256]{3,2,1,0:T(8,128)(2,1)S(1)} collective-permute-done((bf16[4,2,48,256]{3,2,1,0:T(8,128)(2,1)S(1)}, bf16[4,2,48,256]{3,2,1,0:T(8,128)(2,1)S(1)}, u32[]{:S(2)}, u32[]{:S(2)}) %collective-permute-start.15) | collective-permute-done | bytes 196640 | tf_op jit(solution)/shard_map/ppermute | solution.py:177
  59.6 1.2 %collective-permute-done.19.refs_7_ = bf16[4,2,48,256]{3,2,1,0:T(8,128)(2,1)S(1)} collective-permute-done((bf16[4,2,48,256]{3,2,1,0:T(8,128)(2,1)S(1)}, bf16[4,2,48,256]{3,2,1,0:T(8,128)(2,1)S(1)}, u32[]{:S(2)}, u32[]{:S(2)}) %collective-permute-start.19) | collective-permute-done | bytes 196640 | tf_op jit(solution)/shard_map/ppermute | solution.py:177
  60.9 8.1 %shard_map.121 = f32[48,768,128]{2,1,0:T(8,128)} custom-call(s32[32]{0:T(128)S(1)} %copy-done.5, bf16[2,768,128]{2,1,0:T(8,128)(2,1)S(1)} %copy-done, bf16[4,2,48,256]{3,2,1,0:T(8,128)(2,1)S(1)} %get-tuple-element.37.refs_0_, bf16[4,2,48,256]{3,2,1,0:T(8,128)(2,1)S(1)} %collective-permute-done.13.refs_1_, ...), custom_call_target="tpu_custom_call" | custom-call | flops 1207959552 | bytes 18874368 | tf_op jit(solution)/shard_map/pallas_call | solution.py:380
  (34 shorter events, 0.4 us)
Async XLA Ops:
  0.6 37.3 %copy-start.7 = (f32[1,128]{1,0:T(1,128)S(1)}, f32[1,128]{1,0:T(1,128)}, u32[]{:S(2)}) copy-start(f32[1,128]{1,0:T(1,128)} %constant.11.damping_ref) | copy-start | bytes 1540
  0.6 60.2 %copy-start = (bf16[2,768,128]{2,1,0:T(8,128)(2,1)S(1)}, bf16[2,768,128]{2,1,0:T(8,128)(2,1)}, u32[]{:S(2)}) copy-start(bf16[2,768,128]{2,1,0:T(8,128)(2,1)} %constant.7.clone.table_ref) | copy-start | bytes 1179652
  0.7 14.6 %copy-start.5 = (s32[32]{0:T(128)S(1)}, s32[32]{0:T(128)}, u32[]{:S(2)}) copy-start(s32[32]{0:T(128)} %orders_ref.9) | copy-start | bytes 388
  0.7 21.2 %copy-start.1 = (bf16[1,65,768]{2,1,0:T(8,128)(2,1)S(1)}, bf16[1,65,768]{2,1,0:T(8,128)(2,1)}, u32[]{:S(2)}) copy-start(bf16[1,65,768]{2,1,0:T(8,128)(2,1)} %legendre_ref.1) | copy-start | bytes 299524
  0.7 37.2 %copy-start.6 = (f32[128]{0:T(128)S(1)}, f32[128]{0:T(128)}, u32[]{:S(2)}) copy-start(f32[128]{0:T(128)} %param.14) | copy-start | bytes 1540
  0.7 41.3 %copy-start.4 = (bf16[128,128]{1,0:T(8,128)(2,1)S(1)}, bf16[128,128]{1,0:T(8,128)(2,1)}, u32[]{:S(2)}) copy-start(bf16[128,128]{1,0:T(8,128)(2,1)} %left_ref.1) | copy-start | bytes 98308
  0.7 41.3 %copy-start.3 = (bf16[128,128]{1,0:T(8,128)(2,1)S(1)}, bf16[128,128]{1,0:T(8,128)(2,1)}, u32[]{:S(2)}) copy-start(bf16[128,128]{1,0:T(8,128)(2,1)} %right_ref.1) | copy-start | bytes 98308
  0.7 41.3 %copy-start.2 = (bf16[1,65,256]{2,1,0:T(8,128)(2,1)S(1)}, bf16[1,65,256]{2,1,0:T(8,128)(2,1)}, u32[]{:S(2)}) copy-start(bf16[1,65,256]{2,1,0:T(8,128)(2,1)} %state_ref.1) | copy-start | bytes 99844
  14.8 2.4 %collective-permute-start.3 = (bf16[4,4,2,48,256]{4,3,2,1,0:T(8,128)(2,1)S(1)}, bf16[4,4,2,48,256]{4,3,2,1,0:T(8,128)(2,1)S(1)}, u32[]{:S(2)}, u32[]{:S(2)}) collective-permute-start(bf16[4,4,2,48,256]{4,3,2,1,0:T(8,128)(2,1)S(1)} %get-tuple-element.27), channel_id=1, source_target_pairs={{0,16},{1,17},{2,18},{3,19},{4,20},{5,21},{6,22},{7,23},{8,24},{9,... | collective-permute-start | bytes 2359304 | tf_op jit(solution)/shard_map/ppermute | solution.py:177
  17.4 15.3 %collective-permute-start.4 = (bf16[4,2,48,256]{3,2,1,0:T(8,128)(2,1)S(1)}, bf16[4,2,48,256]{3,2,1,0:T(8,128)(2,1)S(1)}, u32[]{:S(2)}, u32[]{:S(2)}) collective-permute-start(bf16[4,2,48,256]{3,2,1,0:T(8,128)(2,1)S(1)} %get-tuple-element.29), channel_id=1, source_target_pairs={{0,1},{1,0},{2,3},{3,2},{4,5},{5,4},{6,7},{7,6},{8,9},{9,8},{10,11... | collective-permute-start | bytes 589832 | tf_op jit(solution)/shard_map/ppermute | solution.py:177
  20.3 12.3 %collective-permute-start.5 = (bf16[4,2,48,256]{3,2,1,0:T(8,128)(2,1)S(1)}, bf16[4,2,48,256]{3,2,1,0:T(8,128)(2,1)S(1)}, u32[]{:S(2)}, u32[]{:S(2)}) collective-permute-start(bf16[4,2,48,256]{3,2,1,0:T(8,128)(2,1)S(1)} %get-tuple-element.30), channel_id=1, source_target_pairs={{0,2},{1,3},{2,0},{3,1},{4,6},{5,7},{6,4},{7,5},{8,10},{9,11},{10,... | collective-permute-start | bytes 589832 | tf_op jit(solution)/shard_map/ppermute | solution.py:177
  21.8 10.8 %collective-permute-start.6 = (bf16[4,2,48,256]{3,2,1,0:T(8,128)(2,1)S(1)}, bf16[4,2,48,256]{3,2,1,0:T(8,128)(2,1)S(1)}, u32[]{:S(2)}, u32[]{:S(2)}) collective-permute-start(bf16[4,2,48,256]{3,2,1,0:T(8,128)(2,1)S(1)} %get-tuple-element.31), channel_id=1, source_target_pairs={{0,3},{1,2},{2,1},{3,0},{4,7},{5,6},{6,5},{7,4},{8,11},{9,10},{10,... | collective-permute-start | bytes 589832 | tf_op jit(solution)/shard_map/ppermute | solution.py:177
  22.2 4.7 %collective-permute-start = (bf16[72,192]{1,0:T(8,128)(2,1)S(1)}, bf16[72,192]{1,0:T(8,128)(2,1)S(1)}, u32[]{:S(2)}, u32[]{:S(2)}) collective-permute-start(bf16[72,192]{1,0:T(8,128)(2,1)S(1)} %get-tuple-element.23), channel_id=1, source_target_pairs={{0,4},{1,5},{2,6},{3,7},{4,0},{5,1},{6,2},{7,3},{8,12},{9,13},{10,... | collective-permute-start | bytes 82952 | tf_op jit(solution)/shard_map/ppermute | solution.py:177
  24.3 6.0 %collective-permute-start.1 = (bf16[72,192]{1,0:T(8,128)(2,1)S(1)}, bf16[72,192]{1,0:T(8,128)(2,1)S(1)}, u32[]{:S(2)}, u32[]{:S(2)}) collective-permute-start(bf16[72,192]{1,0:T(8,128)(2,1)S(1)} %get-tuple-element.24), channel_id=1, source_target_pairs={{0,8},{1,9},{2,10},{3,11},{4,12},{5,13},{6,14},{7,15},{8,0},{9,1},... | collective-permute-start | bytes 82952 | tf_op jit(solution)/shard_map/ppermute | solution.py:177
  26.8 5.8 %collective-permute-start.2 = (bf16[72,192]{1,0:T(8,128)(2,1)S(1)}, bf16[72,192]{1,0:T(8,128)(2,1)S(1)}, u32[]{:S(2)}, u32[]{:S(2)}) collective-permute-start(bf16[72,192]{1,0:T(8,128)(2,1)S(1)} %get-tuple-element.25), channel_id=1, source_target_pairs={{0,12},{1,13},{2,14},{3,15},{4,8},{5,9},{6,10},{7,11},{8,4},{9,5},... | collective-permute-start | bytes 82952 | tf_op jit(solution)/shard_map/ppermute | solution.py:177
  33.4 6.0 %collective-permute-start.7 = (bf16[72,256]{1,0:T(8,128)(2,1)S(1)}, bf16[72,256]{1,0:T(8,128)(2,1)S(1)}, u32[]{:S(2)}, u32[]{:S(2)}) collective-permute-start(bf16[72,256]{1,0:T(8,128)(2,1)S(1)} %get-tuple-element.33), channel_id=1, source_target_pairs={{0,12},{1,13},{2,14},{3,15},{4,8},{5,9},{6,10},{7,11},{8,4},{9,5},... | collective-permute-start | bytes 110600 | tf_op jit(solution)/shard_map/ppermute | solution.py:177
  36.9 5.1 %collective-permute-start.8 = (bf16[72,256]{1,0:T(8,128)(2,1)S(1)}, bf16[72,256]{1,0:T(8,128)(2,1)S(1)}, u32[]{:S(2)}, u32[]{:S(2)}) collective-permute-start(bf16[72,256]{1,0:T(8,128)(2,1)S(1)} %get-tuple-element.34), channel_id=1, source_target_pairs={{0,8},{1,9},{2,10},{3,11},{4,12},{5,13},{6,14},{7,15},{8,0},{9,1},... | collective-permute-start | bytes 110600 | tf_op jit(solution)/shard_map/ppermute | solution.py:177
  36.9 5.1 %collective-permute-start.9 = (bf16[72,256]{1,0:T(8,128)(2,1)S(1)}, bf16[72,256]{1,0:T(8,128)(2,1)S(1)}, u32[]{:S(2)}, u32[]{:S(2)}) collective-permute-start(bf16[72,256]{1,0:T(8,128)(2,1)S(1)} %get-tuple-element.35), channel_id=1, source_target_pairs={{0,4},{1,5},{2,6},{3,7},{4,0},{5,1},{6,2},{7,3},{8,12},{9,13},{10,... | collective-permute-start | bytes 110600 | tf_op jit(solution)/shard_map/ppermute | solution.py:177
  42.3 6.6 %collective-permute-start.12 = (bf16[72,256]{1,0:T(8,128)(2,1)S(1)}, bf16[72,256]{1,0:T(8,128)(2,1)S(1)}, u32[]{:S(2)}, u32[]{:S(2)}) collective-permute-start(bf16[72,256]{1,0:T(8,128)(2,1)S(1)} %shard_map.119.refs_4_), channel_id=1, source_target_pairs={{0,12},{1,13},{2,14},{3,15},{4,8},{5,9},{6,10},{7,11},{8,4},{9,5},... | collective-permute-start | bytes 110600 | tf_op jit(solution)/shard_map/ppermute | solution.py:177
  43.6 5.3 %collective-permute-start.11 = (bf16[72,256]{1,0:T(8,128)(2,1)S(1)}, bf16[72,256]{1,0:T(8,128)(2,1)S(1)}, u32[]{:S(2)}, u32[]{:S(2)}) collective-permute-start(bf16[72,256]{1,0:T(8,128)(2,1)S(1)} %shard_map.119.refs_4_), channel_id=1, source_target_pairs={{0,8},{1,9},{2,10},{3,11},{4,12},{5,13},{6,14},{7,15},{8,0},{9,1},... | collective-permute-start | bytes 110600 | tf_op jit(solution)/shard_map/ppermute | solution.py:177
  44.5 4.4 %collective-permute-start.10 = (bf16[72,256]{1,0:T(8,128)(2,1)S(1)}, bf16[72,256]{1,0:T(8,128)(2,1)S(1)}, u32[]{:S(2)}, u32[]{:S(2)}) collective-permute-start(bf16[72,256]{1,0:T(8,128)(2,1)S(1)} %shard_map.119.refs_4_), channel_id=1, source_target_pairs={{0,4},{1,5},{2,6},{3,7},{4,0},{5,1},{6,2},{7,3},{8,12},{9,13},{10,... | collective-permute-start | bytes 110600 | tf_op jit(solution)/shard_map/ppermute | solution.py:177
  49.9 5.7 %collective-permute-start.13 = (bf16[4,2,48,256]{3,2,1,0:T(8,128)(2,1)S(1)}, bf16[4,2,48,256]{3,2,1,0:T(8,128)(2,1)S(1)}, u32[]{:S(2)}, u32[]{:S(2)}) collective-permute-start(bf16[4,2,48,256]{3,2,1,0:T(8,128)(2,1)S(1)} %get-tuple-element.38), channel_id=1, source_target_pairs={{0,1},{1,0},{2,3},{3,2},{4,5},{5,4},{6,7},{7,6},{8,9},{9,8},{10,11... | collective-permute-start | bytes 589832 | tf_op jit(solution)/shard_map/ppermute | solution.py:177
  51.5 6.7 %collective-permute-start.14 = (bf16[4,2,48,256]{3,2,1,0:T(8,128)(2,1)S(1)}, bf16[4,2,48,256]{3,2,1,0:T(8,128)(2,1)S(1)}, u32[]{:S(2)}, u32[]{:S(2)}) collective-permute-start(bf16[4,2,48,256]{3,2,1,0:T(8,128)(2,1)S(1)} %get-tuple-element.39), channel_id=1, source_target_pairs={{0,2},{1,3},{2,0},{3,1},{4,6},{5,7},{6,4},{7,5},{8,10},{9,11},{10,... | collective-permute-start | bytes 589832 | tf_op jit(solution)/shard_map/ppermute | solution.py:177
  52.9 6.6 %collective-permute-start.15 = (bf16[4,2,48,256]{3,2,1,0:T(8,128)(2,1)S(1)}, bf16[4,2,48,256]{3,2,1,0:T(8,128)(2,1)S(1)}, u32[]{:S(2)}, u32[]{:S(2)}) collective-permute-start(bf16[4,2,48,256]{3,2,1,0:T(8,128)(2,1)S(1)} %get-tuple-element.40), channel_id=1, source_target_pairs={{0,3},{1,2},{2,1},{3,0},{4,7},{5,6},{6,5},{7,4},{8,11},{9,10},{10,... | collective-permute-start | bytes 589832 | tf_op jit(solution)/shard_map/ppermute | solution.py:177
  53.4 6.0 %collective-permute-start.16 = (bf16[4,2,48,256]{3,2,1,0:T(8,128)(2,1)S(1)}, bf16[4,2,48,256]{3,2,1,0:T(8,128)(2,1)S(1)}, u32[]{:S(2)}, u32[]{:S(2)}) collective-permute-start(bf16[4,2,48,256]{3,2,1,0:T(8,128)(2,1)S(1)} %get-tuple-element.37.refs_0_), channel_id=1, source_target_pairs={{0,16},{1,17},{2,18},{3,19},{4,20},{5,21},{6,22},{7,23},{8,24},{9,... | collective-permute-start | bytes 589832 | tf_op jit(solution)/shard_map/ppermute | solution.py:177
  55.6 3.9 %collective-permute-start.17 = (bf16[4,2,48,256]{3,2,1,0:T(8,128)(2,1)S(1)}, bf16[4,2,48,256]{3,2,1,0:T(8,128)(2,1)S(1)}, u32[]{:S(2)}, u32[]{:S(2)}) collective-permute-start(bf16[4,2,48,256]{3,2,1,0:T(8,128)(2,1)S(1)} %collective-permute-done.13.refs_1_), channel_id=1, source_target_pairs={{0,16},{1,17},{2,18},{3,19},{4,20},{5,21},{6,22},{7,23},{8,24},{9,... | collective-permute-start | bytes 589832 | tf_op jit(solution)/shard_map/ppermute | solution.py:177
  58.2 1.4 %collective-permute-start.18 = (bf16[4,2,48,256]{3,2,1,0:T(8,128)(2,1)S(1)}, bf16[4,2,48,256]{3,2,1,0:T(8,128)(2,1)S(1)}, u32[]{:S(2)}, u32[]{:S(2)}) collective-permute-start(bf16[4,2,48,256]{3,2,1,0:T(8,128)(2,1)S(1)} %collective-permute-done.14.refs_2_), channel_id=1, source_target_pairs={{0,16},{1,17},{2,18},{3,19},{4,20},{5,21},{6,22},{7,23},{8,24},{9,... | collective-permute-start | bytes 589832 | tf_op jit(solution)/shard_map/ppermute | solution.py:177
  59.4 1.4 %collective-permute-start.19 = (bf16[4,2,48,256]{3,2,1,0:T(8,128)(2,1)S(1)}, bf16[4,2,48,256]{3,2,1,0:T(8,128)(2,1)S(1)}, u32[]{:S(2)}, u32[]{:S(2)}) collective-permute-start(bf16[4,2,48,256]{3,2,1,0:T(8,128)(2,1)S(1)} %collective-permute-done.15.refs_3_), channel_id=1, source_target_pairs={{0,16},{1,17},{2,18},{3,19},{4,20},{5,21},{6,22},{7,23},{8,24},{9,... | collective-permute-start | bytes 589832 | tf_op jit(solution)/shard_map/ppermute | solution.py:177

commit v10 on v9

--- a/solution.py
+++ b/solution.py
@@ -202,9 +202,7 @@
                 ].reshape(blocks * lat_block, radial)
 
 
-def forward_kernel(
-    orders_from, table_ref, grid_ref, held, send_ref, orders_ref, wide, table, buffer, sems, more
-):
+def forward_kernel(table_ref, grid_ref, held, buffer, sems):
     blocks, rows, lat_block, radial = held.shape
 
     def chunk(at):
@@ -212,14 +210,9 @@
             grid_ref.at[pl.ds(2 * at, 2)], buffer.at[pl.ds(2 * at, 2)], sems.at[at]
         )
 
-    table_copy = pltpu.make_async_copy(table_ref.at[lax.axis_index("sec")], wide, more.at[0])
-    orders_copy = pltpu.make_async_copy(orders_from, orders_ref, more.at[1])
-    table_copy.start()
-    orders_copy.start()
     for at in range(sems.shape[0]):
         chunk(at).start()
-    table_copy.wait()
-    table[...] = wide[...].astype(table.dtype)
+    table = table_ref[lax.axis_index("sec")]
 
     def one_block(block, carry):
         for at in range(0, lat_block, 2):
@@ -228,36 +221,25 @@
             two = jnp.concatenate(
                 [buffer[lat].astype(jnp.bfloat16), buffer[lat + 1].astype(jnp.bfloat16)], axis=1
             )
-            sums = jnp.dot(table[...], two, preferred_element_type=jnp.float32)
+            sums = jnp.dot(table, two, preferred_element_type=jnp.float32)
             held[block, :, at, :] = sums[:, :radial]
             held[block, :, at + 1, :] = sums[:, radial:]
         return carry
 
     lax.fori_loop(0, blocks, one_block, 0)
-    orders_copy.wait()
-    arrange_kernel(1, orders_ref, held, send_ref)
-
-
-def forward_sums(pair_orders, table, grid_terms, lat_block):
+
+
+def forward_sums(table, grid_terms, lat_block):
     sections, rows, phi_count = table.shape
     lat_rows, _, radial = grid_terms.shape
-    sizes = (4, 4, 2, lat_rows, 2 * radial)
-    in_memory = [pltpu.with_memory_space_constraint(x, pltpu.HBM) for x in (pair_orders, table)]
     return pl.pallas_call(
         forward_kernel,
-        in_specs=[pl.BlockSpec(memory_space=pltpu.HBM)] * 2 + [anywhere()],
-        out_specs=[vmem(), vmem()],
-        out_shape=[
-            jax.ShapeDtypeStruct((lat_rows // lat_block, rows, lat_block, radial), jnp.float32),
-            jax.ShapeDtypeStruct(sizes, jnp.bfloat16),
-        ],
+        in_specs=[vmem(), anywhere()],
+        out_specs=vmem(),
+        out_shape=jax.ShapeDtypeStruct((lat_rows // lat_block, rows, lat_block, radial), jnp.float32),
         scratch_shapes=[
-            pltpu.SMEM(pair_orders.shape, jnp.int32),
-            pltpu.VMEM((rows, phi_count), jnp.float32),
-            pltpu.VMEM((rows, phi_count), jnp.bfloat16),
             pltpu.VMEM(grid_terms.shape, jnp.float32),
             pltpu.SemaphoreType.DMA((lat_rows // 2,)),
-            pltpu.SemaphoreType.DMA((2,)),
         ],
         compiler_params=params(36),
         cost_estimate=pl.CostEstimate(
@@ -265,7 +247,7 @@
             bytes_accessed=4 * lat_rows * phi_count * radial,
             transcendentals=0,
         ),
-    )(*in_memory, grid_terms)
+    )(table, grid_terms)
 
 
 def add_kernel(keep_ref, take_ref, *outs):
@@ -404,7 +386,7 @@
     columns = 2 * radial
     pair_total = pair_orders.shape[0]
     table = natural_table(pair_total, lax.axis_size("sec"), phi_count)
-    forward_table = jnp.asarray(table)
+    forward_table = jnp.asarray(table, jnp.bfloat16)
     inverse_table = jnp.asarray(table.transpose(0, 2, 1), jnp.bfloat16)
 
     def shape(*sizes, dtype=jnp.bfloat16):
@@ -419,17 +401,20 @@
     )
     weights = [cuts[0]] + [exchange(cuts[deep], deep=deep) for deep in (1, 2, 3)]
 
-    held, send = forward_sums(pair_orders, forward_table, grid_terms, 8)
+    held = forward_sums(forward_table, grid_terms, 8)
     block = shape(4, 2, lat_rows, columns)
-    taken = exchange(send, sec=1)
-    sizes = (4, 4, 2, lat_rows, columns)
-    keep = call(
-        functools.partial(arrange_kernel, 0),
-        [pair_orders, held],
-        shape(*sizes, dtype=jnp.float32),
-        mib=24,
-        scalars=1,
-    )
+
+    def arranged(sec, dtype):
+        return call(
+            functools.partial(arrange_kernel, sec),
+            [pair_orders, held],
+            shape(4, 4, 2, lat_rows, columns, dtype=dtype),
+            mib=24,
+            scalars=1,
+        )
+
+    taken = exchange(arranged(1, jnp.bfloat16), sec=1)
+    keep = arranged(0, jnp.float32)
     blocks = call(add_kernel, [keep, taken], [block] * 4, mib=24)
     takes = [blocks[0]] + [exchange(blocks[flat], flat=flat) for flat in (1, 2, 3)]
 

time: 69.1 us -> 65.4 us (0.946)
  Pallas kernels: 25.9 us -> 21.1 us
  local copies, waits for them, and re-layouts: 0.66 us -> 1.7 us
    pallas_call x1, Pallas kernels: 14.1 us -> 8.58 us  [forward_sums(): pl.pallas_call(forward_kernel, in_specs=[vmem(), anywhere()], out_specs=v...]
    unnamed x16 -> x18, local copies, waits for them, and re-layouts: 0.04 us -> 1.08 us
    pallas_call x7 -> x8, Pallas kernels: 3.76 us -> 4.51 us  [call(): pl.pallas_call(kernel, in_specs=[smem()] * scalars + [vmem()] * (len(oper...]
where the time goes in v10:
time: 65.4 us; the launch traced here: 65.3 us
  starting transfers between devices  25.5 us (39%)
  Pallas kernels  21.1 us (32%)
  waiting for transfers between devices  16.1 us (25%)
  local copies, waits for them, and re-layouts  1.7 us (3%)
  between operations  0.79 us (1%)
    ppermute x20, starting transfers between devices, exchange(): return lax.ppermute(array, names, pairs)  25.5 us
    ppermute x20, waiting for transfers between devices, exchange(): return lax.ppermute(array, names, pairs)  16.1 us
    pallas_call x1, Pallas kernels, forward_sums(): pl.pallas_call(forward_kernel, in_specs=[vmem(), anywhere()], out_specs=v...  8.58 us
    pallas_call x1, Pallas kernels, inverse_values(): pl.pallas_call(inverse_kernel, in_specs=[smem()] + [vmem()] * (1 + len(ta...  8.06 us
    pallas_call x8, Pallas kernels, call(): pl.pallas_call(kernel, in_specs=[smem()] * scalars + [vmem()] * (len(oper...  4.51 us
  transfers between devices with their start and end apart: 20, of which 10 were waited for; matrix products, arithmetic and copies ran while one was open for 1% of the time, Pallas kernels for 2%

profile of v10, /device:TPU:0, one launch (start us, length us, event | category | flops | bytes accessed | tf_op | source)
XLA Modules:
  0.0 65.3 jit_solution(12435191075667907019)
XLA Ops:
  0.7 1.0 %copy-done.1 = bf16[2,128,768]{2,1,0:T(8,128)(2,1)S(1)} copy-done((bf16[2,128,768]{2,1,0:T(8,128)(2,1)S(1)}, bf16[2,128,768]{2,1,0:T(8,128)(2,1)}, u32[]{:S(2)}) %copy-start.1) | copy-done | bytes 393240
  1.7 8.6 %shard_map.114.held = f32[6,128,8,128]{3,2,1,0:T(8,128)S(1)} custom-call(bf16[2,128,768]{2,1,0:T(8,128)(2,1)S(1)} %copy-done.1, f32[48,768,128]{2,1,0:T(8,128)} %grid_ref.1), custom_call_target="tpu_custom_call" | custom-call | flops 1207959552 | bytes 18874368 | tf_op jit(solution)/shard_map/pallas_call | solution.py:235
  10.3 0.7 %shard_map.116 = bf16[4,4,2,48,256]{4,3,2,1,0:T(8,128)(2,1)S(1)} custom-call(s32[32]{0:T(128)S(1)} %copy-done.6, f32[6,128,8,128]{3,2,1,0:T(8,128)S(1)} %shard_map.114.held), custom_call_target="tpu_custom_call" | custom-call | tf_op jit(solution)/shard_map/pallas_call | solution.py:140
  11.0 0.5 collective-permute-start.3
  11.5 0.7 %shard_map.115.keep_ref = f32[4,4,2,48,256]{4,3,2,1,0:T(8,128)S(1)} custom-call(s32[32]{0:T(128)S(1)} %copy-done.6, f32[6,128,8,128]{3,2,1,0:T(8,128)S(1)} %shard_map.114.held), custom_call_target="tpu_custom_call" | custom-call | tf_op jit(solution)/shard_map/pallas_call | solution.py:140
  12.2 1.2 %collective-permute-done.3.take_ref = bf16[4,4,2,48,256]{4,3,2,1,0:T(8,128)(2,1)S(1)} collective-permute-done((bf16[4,4,2,48,256]{4,3,2,1,0:T(8,128)(2,1)S(1)}, bf16[4,4,2,48,256]{4,3,2,1,0:T(8,128)(2,1)S(1)}, u32[]{:S(2)}, u32[]{:S(2)}) %collective-permute-start.3) | collective-permute-done | bytes 786464 | tf_op jit(solution)/shard_map/ppermute | solution.py:177
  13.7 2.9 %collective-permute-start.4 = (bf16[4,2,48,256]{3,2,1,0:T(8,128)(2,1)S(1)}, bf16[4,2,48,256]{3,2,1,0:T(8,128)(2,1)S(1)}, u32[]{:S(2)}, u32[]{:S(2)}) collective-permute-start(bf16[4,2,48,256]{3,2,1,0:T(8,128)(2,1)S(1)} %get-tuple-element.25), channel_id=1, source_target_pairs={{0,1},{1,0},{2,3},{3,2},{4,5},{5,4},{6,7},{7,6},{8,9},{9,8},{10,11... | collective-permute-start | bytes 589832 | tf_op jit(solution)/shard_map/ppermute | solution.py:177
  16.6 1.5 %collective-permute-start.5 = (bf16[4,2,48,256]{3,2,1,0:T(8,128)(2,1)S(1)}, bf16[4,2,48,256]{3,2,1,0:T(8,128)(2,1)S(1)}, u32[]{:S(2)}, u32[]{:S(2)}) collective-permute-start(bf16[4,2,48,256]{3,2,1,0:T(8,128)(2,1)S(1)} %get-tuple-element.26), channel_id=1, source_target_pairs={{0,2},{1,3},{2,0},{3,1},{4,6},{5,7},{6,4},{7,5},{8,10},{9,11},{10,... | collective-permute-start | bytes 589832 | tf_op jit(solution)/shard_map/ppermute | solution.py:177
  18.5 2.1 %collective-permute-start = (bf16[72,192]{1,0:T(8,128)(2,1)S(1)}, bf16[72,192]{1,0:T(8,128)(2,1)S(1)}, u32[]{:S(2)}, u32[]{:S(2)}) collective-permute-start(bf16[72,192]{1,0:T(8,128)(2,1)S(1)} %get-tuple-element.21), channel_id=1, source_target_pairs={{0,4},{1,5},{2,6},{3,7},{4,0},{5,1},{6,2},{7,3},{8,12},{9,13},{10,... | collective-permute-start | bytes 82952 | tf_op jit(solution)/shard_map/ppermute | solution.py:177
  20.6 2.6 %collective-permute-start.1 = (bf16[72,192]{1,0:T(8,128)(2,1)S(1)}, bf16[72,192]{1,0:T(8,128)(2,1)S(1)}, u32[]{:S(2)}, u32[]{:S(2)}) collective-permute-start(bf16[72,192]{1,0:T(8,128)(2,1)S(1)} %get-tuple-element.22), channel_id=1, source_target_pairs={{0,8},{1,9},{2,10},{3,11},{4,12},{5,13},{6,14},{7,15},{8,0},{9,1},... | collective-permute-start | bytes 82952 | tf_op jit(solution)/shard_map/ppermute | solution.py:177
  23.2 3.4 %collective-permute-start.2 = (bf16[72,192]{1,0:T(8,128)(2,1)S(1)}, bf16[72,192]{1,0:T(8,128)(2,1)S(1)}, u32[]{:S(2)}, u32[]{:S(2)}) collective-permute-start(bf16[72,192]{1,0:T(8,128)(2,1)S(1)} %get-tuple-element.23), channel_id=1, source_target_pairs={{0,12},{1,13},{2,14},{3,15},{4,8},{5,9},{6,10},{7,11},{8,4},{9,5},... | collective-permute-start | bytes 82952 | tf_op jit(solution)/shard_map/ppermute | solution.py:177
  26.6 2.4 %collective-permute-done.2.refs_3_ = bf16[72,192]{1,0:T(8,128)(2,1)S(1)} collective-permute-done((bf16[72,192]{1,0:T(8,128)(2,1)S(1)}, bf16[72,192]{1,0:T(8,128)(2,1)S(1)}, u32[]{:S(2)}, u32[]{:S(2)}) %collective-permute-start.2) | collective-permute-done | bytes 27680 | tf_op jit(solution)/shard_map/ppermute | solution.py:177
  28.9 0.8 %shard_map.118 = (f32[72,256]{1,0:T(8,128)S(1)}, bf16[72,256]{1,0:T(8,128)(2,1)S(1)}, bf16[72,256]{1,0:T(8,128)(2,1)S(1)}, bf16[72,256]{1,0:T(8,128)(2,1)S(1)}) custom-call(s32[32]{0:T(128)S(1)} %copy-done.6, bf16[72,192]{1,0:T(8,128)(2,1)S(1)} %get-tuple-element.20.refs_0_, bf16[72,192]{1,0:T(8,128)(2,1)S(1)} %collective-permute-done.refs_1_, ...), custom_call_target="tpu_custom_call" | custom-call | tf_op jit(solution)/shard_map/pallas_call | solution.py:140
  29.7 3.5 %collective-permute-start.7 = (bf16[72,256]{1,0:T(8,128)(2,1)S(1)}, bf16[72,256]{1,0:T(8,128)(2,1)S(1)}, u32[]{:S(2)}, u32[]{:S(2)}) collective-permute-start(bf16[72,256]{1,0:T(8,128)(2,1)S(1)} %get-tuple-element.29), channel_id=1, source_target_pairs={{0,12},{1,13},{2,14},{3,15},{4,8},{5,9},{6,10},{7,11},{8,4},{9,5},... | collective-permute-start | bytes 110600 | tf_op jit(solution)/shard_map/ppermute | solution.py:177
  33.2 1.0 %collective-permute-start.9 = (bf16[72,256]{1,0:T(8,128)(2,1)S(1)}, bf16[72,256]{1,0:T(8,128)(2,1)S(1)}, u32[]{:S(2)}, u32[]{:S(2)}) collective-permute-start(bf16[72,256]{1,0:T(8,128)(2,1)S(1)} %get-tuple-element.31), channel_id=1, source_target_pairs={{0,4},{1,5},{2,6},{3,7},{4,0},{5,1},{6,2},{7,3},{8,12},{9,13},{10,... | collective-permute-start | bytes 110600 | tf_op jit(solution)/shard_map/ppermute | solution.py:177
  34.2 0.6 shard_map.119.factor_ref
  34.8 0.9 %collective-permute-done.7.two = bf16[72,256]{1,0:T(8,128)(2,1)S(1)} collective-permute-done((bf16[72,256]{1,0:T(8,128)(2,1)S(1)}, bf16[72,256]{1,0:T(8,128)(2,1)S(1)}, u32[]{:S(2)}, u32[]{:S(2)}) %collective-permute-start.7) | collective-permute-done | bytes 36896 | tf_op jit(solution)/shard_map/ppermute | solution.py:177
  35.7 2.6 %collective-permute-done.8.three = bf16[72,256]{1,0:T(8,128)(2,1)S(1)} collective-permute-done((bf16[72,256]{1,0:T(8,128)(2,1)S(1)}, bf16[72,256]{1,0:T(8,128)(2,1)S(1)}, u32[]{:S(2)}, u32[]{:S(2)}) %collective-permute-start.8) | collective-permute-done | bytes 36896 | tf_op jit(solution)/shard_map/ppermute | solution.py:177
  38.6 1.3 %collective-permute-start.12 = (bf16[72,256]{1,0:T(8,128)(2,1)S(1)}, bf16[72,256]{1,0:T(8,128)(2,1)S(1)}, u32[]{:S(2)}, u32[]{:S(2)}) collective-permute-start(bf16[72,256]{1,0:T(8,128)(2,1)S(1)} %shard_map.120.refs_4_), channel_id=1, source_target_pairs={{0,12},{1,13},{2,14},{3,15},{4,8},{5,9},{6,10},{7,11},{8,4},{9,5},... | collective-permute-start | bytes 110600 | tf_op jit(solution)/shard_map/ppermute | solution.py:177
  39.9 0.9 %collective-permute-start.11 = (bf16[72,256]{1,0:T(8,128)(2,1)S(1)}, bf16[72,256]{1,0:T(8,128)(2,1)S(1)}, u32[]{:S(2)}, u32[]{:S(2)}) collective-permute-start(bf16[72,256]{1,0:T(8,128)(2,1)S(1)} %shard_map.120.refs_4_), channel_id=1, source_target_pairs={{0,8},{1,9},{2,10},{3,11},{4,12},{5,13},{6,14},{7,15},{8,0},{9,1},... | collective-permute-start | bytes 110600 | tf_op jit(solution)/shard_map/ppermute | solution.py:177
  40.8 2.2 %collective-permute-start.10 = (bf16[72,256]{1,0:T(8,128)(2,1)S(1)}, bf16[72,256]{1,0:T(8,128)(2,1)S(1)}, u32[]{:S(2)}, u32[]{:S(2)}) collective-permute-start(bf16[72,256]{1,0:T(8,128)(2,1)S(1)} %shard_map.120.refs_4_), channel_id=1, source_target_pairs={{0,4},{1,5},{2,6},{3,7},{4,0},{5,1},{6,2},{7,3},{8,12},{9,13},{10,... | collective-permute-start | bytes 110600 | tf_op jit(solution)/shard_map/ppermute | solution.py:177
  43.1 0.6 slice_bitcast_fusion
  43.7 1.5 %collective-permute-done.10.refs_5_ = bf16[72,256]{1,0:T(8,128)(2,1)S(1)} collective-permute-done((bf16[72,256]{1,0:T(8,128)(2,1)S(1)}, bf16[72,256]{1,0:T(8,128)(2,1)S(1)}, u32[]{:S(2)}, u32[]{:S(2)}) %collective-permute-start.10) | collective-permute-done | bytes 36896 | tf_op jit(solution)/shard_map/ppermute | solution.py:177
  45.2 1.0 %shard_map.121 = (bf16[4,2,48,256]{3,2,1,0:T(8,128)(2,1)S(1)}, bf16[4,2,48,256]{3,2,1,0:T(8,128)(2,1)S(1)}, bf16[4,2,48,256]{3,2,1,0:T(8,128)(2,1)S(1)}, bf16[4,2,48,256]{3,2,1,0:T(8,128)(2,1)S(1)}) custom-call(s32[32]{0:T(128)S(1)} %copy-done.6, bf16[72,192]{1,0:T(8,128)(2,1)S(1)} %get-tuple-element.20.refs_0_, ...), custom_call_target="tpu_custom_call" | custom-call | tf_op jit(solution)/shard_map/pallas_call | solution.py:140
  46.2 1.6 %collective-permute-start.13 = (bf16[4,2,48,256]{3,2,1,0:T(8,128)(2,1)S(1)}, bf16[4,2,48,256]{3,2,1,0:T(8,128)(2,1)S(1)}, u32[]{:S(2)}, u32[]{:S(2)}) collective-permute-start(bf16[4,2,48,256]{3,2,1,0:T(8,128)(2,1)S(1)} %get-tuple-element.34), channel_id=1, source_target_pairs={{0,1},{1,0},{2,3},{3,2},{4,5},{5,4},{6,7},{7,6},{8,9},{9,8},{10,11... | collective-permute-start | bytes 589832 | tf_op jit(solution)/shard_map/ppermute | solution.py:177
  47.8 1.4 %collective-permute-start.14 = (bf16[4,2,48,256]{3,2,1,0:T(8,128)(2,1)S(1)}, bf16[4,2,48,256]{3,2,1,0:T(8,128)(2,1)S(1)}, u32[]{:S(2)}, u32[]{:S(2)}) collective-permute-start(bf16[4,2,48,256]{3,2,1,0:T(8,128)(2,1)S(1)} %get-tuple-element.35), channel_id=1, source_target_pairs={{0,2},{1,3},{2,0},{3,1},{4,6},{5,7},{6,4},{7,5},{8,10},{9,11},{10,... | collective-permute-start | bytes 589832 | tf_op jit(solution)/shard_map/ppermute | solution.py:177
  49.2 0.5 collective-permute-start.15
  49.7 2.2 %collective-permute-done.13.refs_1_ = bf16[4,2,48,256]{3,2,1,0:T(8,128)(2,1)S(1)} collective-permute-done((bf16[4,2,48,256]{3,2,1,0:T(8,128)(2,1)S(1)}, bf16[4,2,48,256]{3,2,1,0:T(8,128)(2,1)S(1)}, u32[]{:S(2)}, u32[]{:S(2)}) %collective-permute-start.13) | collective-permute-done | bytes 196640 | tf_op jit(solution)/shard_map/ppermute | solution.py:177
  51.9 2.6 %collective-permute-done.14.refs_2_ = bf16[4,2,48,256]{3,2,1,0:T(8,128)(2,1)S(1)} collective-permute-done((bf16[4,2,48,256]{3,2,1,0:T(8,128)(2,1)S(1)}, bf16[4,2,48,256]{3,2,1,0:T(8,128)(2,1)S(1)}, u32[]{:S(2)}, u32[]{:S(2)}) %collective-permute-start.14) | collective-permute-done | bytes 196640 | tf_op jit(solution)/shard_map/ppermute | solution.py:177
  54.5 1.2 %collective-permute-done.15.refs_3_ = bf16[4,2,48,256]{3,2,1,0:T(8,128)(2,1)S(1)} collective-permute-done((bf16[4,2,48,256]{3,2,1,0:T(8,128)(2,1)S(1)}, bf16[4,2,48,256]{3,2,1,0:T(8,128)(2,1)S(1)}, u32[]{:S(2)}, u32[]{:S(2)}) %collective-permute-start.15) | collective-permute-done | bytes 196640 | tf_op jit(solution)/shard_map/ppermute | solution.py:177
  56.0 1.2 %collective-permute-done.19.refs_7_ = bf16[4,2,48,256]{3,2,1,0:T(8,128)(2,1)S(1)} collective-permute-done((bf16[4,2,48,256]{3,2,1,0:T(8,128)(2,1)S(1)}, bf16[4,2,48,256]{3,2,1,0:T(8,128)(2,1)S(1)}, u32[]{:S(2)}, u32[]{:S(2)}) %collective-permute-start.19) | collective-permute-done | bytes 196640 | tf_op jit(solution)/shard_map/ppermute | solution.py:177
  57.2 8.1 %shard_map.122 = f32[48,768,128]{2,1,0:T(8,128)} custom-call(s32[32]{0:T(128)S(1)} %copy-done.6, bf16[2,768,128]{2,1,0:T(8,128)(2,1)S(1)} %copy-done, bf16[4,2,48,256]{3,2,1,0:T(8,128)(2,1)S(1)} %get-tuple-element.33.refs_0_, bf16[4,2,48,256]{3,2,1,0:T(8,128)(2,1)S(1)} %collective-permute-done.13.refs_1_, ...), custom_call_target="tpu_custom_call" | custom-call | flops 1207959552 | bytes 18874368 | tf_op jit(solution)/shard_map/pallas_call | solution.py:362
  (37 shorter events, 1.1 us)
Async XLA Ops:
  0.6 33.6 %copy-start.8 = (f32[1,128]{1,0:T(1,128)S(1)}, f32[1,128]{1,0:T(1,128)}, u32[]{:S(2)}) copy-start(f32[1,128]{1,0:T(1,128)} %constant.11.damping_ref) | copy-start | bytes 1540
  0.6 56.6 %copy-start = (bf16[2,768,128]{2,1,0:T(8,128)(2,1)S(1)}, bf16[2,768,128]{2,1,0:T(8,128)(2,1)}, u32[]{:S(2)}) copy-start(bf16[2,768,128]{2,1,0:T(8,128)(2,1)} %constant.7.clone.table_ref) | copy-start | bytes 1179652
  0.7 1.0 %copy-start.1 = (bf16[2,128,768]{2,1,0:T(8,128)(2,1)S(1)}, bf16[2,128,768]{2,1,0:T(8,128)(2,1)}, u32[]{:S(2)}) copy-start(bf16[2,128,768]{2,1,0:T(8,128)(2,1)} %constant.6.clone.table_ref) | copy-start | bytes 1179652
  1.7 8.6 %copy-start.6 = (s32[32]{0:T(128)S(1)}, s32[32]{0:T(128)}, u32[]{:S(2)}) copy-start(s32[32]{0:T(128)} %orders_ref.11) | copy-start | bytes 388
  1.7 16.4 %copy-start.2 = (bf16[1,65,768]{2,1,0:T(8,128)(2,1)S(1)}, bf16[1,65,768]{2,1,0:T(8,128)(2,1)}, u32[]{:S(2)}) copy-start(bf16[1,65,768]{2,1,0:T(8,128)(2,1)} %legendre_ref.1) | copy-start | bytes 299524
  1.7 32.5 %copy-start.7 = (f32[128]{0:T(128)S(1)}, f32[128]{0:T(128)}, u32[]{:S(2)}) copy-start(f32[128]{0:T(128)} %param.14) | copy-start | bytes 1540
  1.7 36.6 %copy-start.3 = (bf16[1,65,256]{2,1,0:T(8,128)(2,1)S(1)}, bf16[1,65,256]{2,1,0:T(8,128)(2,1)}, u32[]{:S(2)}) copy-start(bf16[1,65,256]{2,1,0:T(8,128)(2,1)} %state_ref.1) | copy-start | bytes 99844
  1.7 36.6 %copy-start.4 = (bf16[128,128]{1,0:T(8,128)(2,1)S(1)}, bf16[128,128]{1,0:T(8,128)(2,1)}, u32[]{:S(2)}) copy-start(bf16[128,128]{1,0:T(8,128)(2,1)} %right_ref.1) | copy-start | bytes 98308
  1.7 36.6 %copy-start.5 = (bf16[128,128]{1,0:T(8,128)(2,1)S(1)}, bf16[128,128]{1,0:T(8,128)(2,1)}, u32[]{:S(2)}) copy-start(bf16[128,128]{1,0:T(8,128)(2,1)} %left_ref.1) | copy-start | bytes 98308
  11.0 2.4 %collective-permute-start.3 = (bf16[4,4,2,48,256]{4,3,2,1,0:T(8,128)(2,1)S(1)}, bf16[4,4,2,48,256]{4,3,2,1,0:T(8,128)(2,1)S(1)}, u32[]{:S(2)}, u32[]{:S(2)}) collective-permute-start(bf16[4,4,2,48,256]{4,3,2,1,0:T(8,128)(2,1)S(1)} %shard_map.116), channel_id=1, source_target_pairs={{0,16},{1,17},{2,18},{3,19},{4,20},{5,21},{6,22},{7,23},{8,24},{9,... | collective-permute-start | bytes 2359304 | tf_op jit(solution)/shard_map/ppermute | solution.py:177
  13.7 15.3 %collective-permute-start.4 = (bf16[4,2,48,256]{3,2,1,0:T(8,128)(2,1)S(1)}, bf16[4,2,48,256]{3,2,1,0:T(8,128)(2,1)S(1)}, u32[]{:S(2)}, u32[]{:S(2)}) collective-permute-start(bf16[4,2,48,256]{3,2,1,0:T(8,128)(2,1)S(1)} %get-tuple-element.25), channel_id=1, source_target_pairs={{0,1},{1,0},{2,3},{3,2},{4,5},{5,4},{6,7},{7,6},{8,9},{9,8},{10,11... | collective-permute-start | bytes 589832 | tf_op jit(solution)/shard_map/ppermute | solution.py:177
  16.6 12.3 %collective-permute-start.5 = (bf16[4,2,48,256]{3,2,1,0:T(8,128)(2,1)S(1)}, bf16[4,2,48,256]{3,2,1,0:T(8,128)(2,1)S(1)}, u32[]{:S(2)}, u32[]{:S(2)}) collective-permute-start(bf16[4,2,48,256]{3,2,1,0:T(8,128)(2,1)S(1)} %get-tuple-element.26), channel_id=1, source_target_pairs={{0,2},{1,3},{2,0},{3,1},{4,6},{5,7},{6,4},{7,5},{8,10},{9,11},{10,... | collective-permute-start | bytes 589832 | tf_op jit(solution)/shard_map/ppermute | solution.py:177
  18.1 10.8 %collective-permute-start.6 = (bf16[4,2,48,256]{3,2,1,0:T(8,128)(2,1)S(1)}, bf16[4,2,48,256]{3,2,1,0:T(8,128)(2,1)S(1)}, u32[]{:S(2)}, u32[]{:S(2)}) collective-permute-start(bf16[4,2,48,256]{3,2,1,0:T(8,128)(2,1)S(1)} %get-tuple-element.27), channel_id=1, source_target_pairs={{0,3},{1,2},{2,1},{3,0},{4,7},{5,6},{6,5},{7,4},{8,11},{9,10},{10,... | collective-permute-start | bytes 589832 | tf_op jit(solution)/shard_map/ppermute | solution.py:177
  18.5 4.7 %collective-permute-start = (bf16[72,192]{1,0:T(8,128)(2,1)S(1)}, bf16[72,192]{1,0:T(8,128)(2,1)S(1)}, u32[]{:S(2)}, u32[]{:S(2)}) collective-permute-start(bf16[72,192]{1,0:T(8,128)(2,1)S(1)} %get-tuple-element.21), channel_id=1, source_target_pairs={{0,4},{1,5},{2,6},{3,7},{4,0},{5,1},{6,2},{7,3},{8,12},{9,13},{10,... | collective-permute-start | bytes 82952 | tf_op jit(solution)/shard_map/ppermute | solution.py:177
  20.6 6.0 %collective-permute-start.1 = (bf16[72,192]{1,0:T(8,128)(2,1)S(1)}, bf16[72,192]{1,0:T(8,128)(2,1)S(1)}, u32[]{:S(2)}, u32[]{:S(2)}) collective-permute-start(bf16[72,192]{1,0:T(8,128)(2,1)S(1)} %get-tuple-element.22), channel_id=1, source_target_pairs={{0,8},{1,9},{2,10},{3,11},{4,12},{5,13},{6,14},{7,15},{8,0},{9,1},... | collective-permute-start | bytes 82952 | tf_op jit(solution)/shard_map/ppermute | solution.py:177
  23.2 5.8 %collective-permute-start.2 = (bf16[72,192]{1,0:T(8,128)(2,1)S(1)}, bf16[72,192]{1,0:T(8,128)(2,1)S(1)}, u32[]{:S(2)}, u32[]{:S(2)}) collective-permute-start(bf16[72,192]{1,0:T(8,128)(2,1)S(1)} %get-tuple-element.23), channel_id=1, source_target_pairs={{0,12},{1,13},{2,14},{3,15},{4,8},{5,9},{6,10},{7,11},{8,4},{9,5},... | collective-permute-start | bytes 82952 | tf_op jit(solution)/shard_map/ppermute | solution.py:177
  29.7 6.0 %collective-permute-start.7 = (bf16[72,256]{1,0:T(8,128)(2,1)S(1)}, bf16[72,256]{1,0:T(8,128)(2,1)S(1)}, u32[]{:S(2)}, u32[]{:S(2)}) collective-permute-start(bf16[72,256]{1,0:T(8,128)(2,1)S(1)} %get-tuple-element.29), channel_id=1, source_target_pairs={{0,12},{1,13},{2,14},{3,15},{4,8},{5,9},{6,10},{7,11},{8,4},{9,5},... | collective-permute-start | bytes 110600 | tf_op jit(solution)/shard_map/ppermute | solution.py:177
  33.2 5.1 %collective-permute-start.8 = (bf16[72,256]{1,0:T(8,128)(2,1)S(1)}, bf16[72,256]{1,0:T(8,128)(2,1)S(1)}, u32[]{:S(2)}, u32[]{:S(2)}) collective-permute-start(bf16[72,256]{1,0:T(8,128)(2,1)S(1)} %get-tuple-element.30), channel_id=1, source_target_pairs={{0,8},{1,9},{2,10},{3,11},{4,12},{5,13},{6,14},{7,15},{8,0},{9,1},... | collective-permute-start | bytes 110600 | tf_op jit(solution)/shard_map/ppermute | solution.py:177
  33.2 5.1 %collective-permute-start.9 = (bf16[72,256]{1,0:T(8,128)(2,1)S(1)}, bf16[72,256]{1,0:T(8,128)(2,1)S(1)}, u32[]{:S(2)}, u32[]{:S(2)}) collective-permute-start(bf16[72,256]{1,0:T(8,128)(2,1)S(1)} %get-tuple-element.31), channel_id=1, source_target_pairs={{0,4},{1,5},{2,6},{3,7},{4,0},{5,1},{6,2},{7,3},{8,12},{9,13},{10,... | collective-permute-start | bytes 110600 | tf_op jit(solution)/shard_map/ppermute | solution.py:177
  38.6 6.6 %collective-permute-start.12 = (bf16[72,256]{1,0:T(8,128)(2,1)S(1)}, bf16[72,256]{1,0:T(8,128)(2,1)S(1)}, u32[]{:S(2)}, u32[]{:S(2)}) collective-permute-start(bf16[72,256]{1,0:T(8,128)(2,1)S(1)} %shard_map.120.refs_4_), channel_id=1, source_target_pairs={{0,12},{1,13},{2,14},{3,15},{4,8},{5,9},{6,10},{7,11},{8,4},{9,5},... | collective-permute-start | bytes 110600 | tf_op jit(solution)/shard_map/ppermute | solution.py:177
  39.9 5.3 %collective-permute-start.11 = (bf16[72,256]{1,0:T(8,128)(2,1)S(1)}, bf16[72,256]{1,0:T(8,128)(2,1)S(1)}, u32[]{:S(2)}, u32[]{:S(2)}) collective-permute-start(bf16[72,256]{1,0:T(8,128)(2,1)S(1)} %shard_map.120.refs_4_), channel_id=1, source_target_pairs={{0,8},{1,9},{2,10},{3,11},{4,12},{5,13},{6,14},{7,15},{8,0},{9,1},... | collective-permute-start | bytes 110600 | tf_op jit(solution)/shard_map/ppermute | solution.py:177
  40.8 4.4 %collective-permute-start.10 = (bf16[72,256]{1,0:T(8,128)(2,1)S(1)}, bf16[72,256]{1,0:T(8,128)(2,1)S(1)}, u32[]{:S(2)}, u32[]{:S(2)}) collective-permute-start(bf16[72,256]{1,0:T(8,128)(2,1)S(1)} %shard_map.120.refs_4_), channel_id=1, source_target_pairs={{0,4},{1,5},{2,6},{3,7},{4,0},{5,1},{6,2},{7,3},{8,12},{9,13},{10,... | collective-permute-start | bytes 110600 | tf_op jit(solution)/shard_map/ppermute | solution.py:177
  46.2 5.7 %collective-permute-start.13 = (bf16[4,2,48,256]{3,2,1,0:T(8,128)(2,1)S(1)}, bf16[4,2,48,256]{3,2,1,0:T(8,128)(2,1)S(1)}, u32[]{:S(2)}, u32[]{:S(2)}) collective-permute-start(bf16[4,2,48,256]{3,2,1,0:T(8,128)(2,1)S(1)} %get-tuple-element.34), channel_id=1, source_target_pairs={{0,1},{1,0},{2,3},{3,2},{4,5},{5,4},{6,7},{7,6},{8,9},{9,8},{10,11... | collective-permute-start | bytes 589832 | tf_op jit(solution)/shard_map/ppermute | solution.py:177
  47.8 6.7 %collective-permute-start.14 = (bf16[4,2,48,256]{3,2,1,0:T(8,128)(2,1)S(1)}, bf16[4,2,48,256]{3,2,1,0:T(8,128)(2,1)S(1)}, u32[]{:S(2)}, u32[]{:S(2)}) collective-permute-start(bf16[4,2,48,256]{3,2,1,0:T(8,128)(2,1)S(1)} %get-tuple-element.35), channel_id=1, source_target_pairs={{0,2},{1,3},{2,0},{3,1},{4,6},{5,7},{6,4},{7,5},{8,10},{9,11},{10,... | collective-permute-start | bytes 589832 | tf_op jit(solution)/shard_map/ppermute | solution.py:177
  49.2 6.6 %collective-permute-start.15 = (bf16[4,2,48,256]{3,2,1,0:T(8,128)(2,1)S(1)}, bf16[4,2,48,256]{3,2,1,0:T(8,128)(2,1)S(1)}, u32[]{:S(2)}, u32[]{:S(2)}) collective-permute-start(bf16[4,2,48,256]{3,2,1,0:T(8,128)(2,1)S(1)} %get-tuple-element.36), channel_id=1, source_target_pairs={{0,3},{1,2},{2,1},{3,0},{4,7},{5,6},{6,5},{7,4},{8,11},{9,10},{10,... | collective-permute-start | bytes 589832 | tf_op jit(solution)/shard_map/ppermute | solution.py:177
  49.7 6.0 %collective-permute-start.16 = (bf16[4,2,48,256]{3,2,1,0:T(8,128)(2,1)S(1)}, bf16[4,2,48,256]{3,2,1,0:T(8,128)(2,1)S(1)}, u32[]{:S(2)}, u32[]{:S(2)}) collective-permute-start(bf16[4,2,48,256]{3,2,1,0:T(8,128)(2,1)S(1)} %get-tuple-element.33.refs_0_), channel_id=1, source_target_pairs={{0,16},{1,17},{2,18},{3,19},{4,20},{5,21},{6,22},{7,23},{8,24},{9,... | collective-permute-start | bytes 589832 | tf_op jit(solution)/shard_map/ppermute | solution.py:177
  51.9 3.9 %collective-permute-start.17 = (bf16[4,2,48,256]{3,2,1,0:T(8,128)(2,1)S(1)}, bf16[4,2,48,256]{3,2,1,0:T(8,128)(2,1)S(1)}, u32[]{:S(2)}, u32[]{:S(2)}) collective-permute-start(bf16[4,2,48,256]{3,2,1,0:T(8,128)(2,1)S(1)} %collective-permute-done.13.refs_1_), channel_id=1, source_target_pairs={{0,16},{1,17},{2,18},{3,19},{4,20},{5,21},{6,22},{7,23},{8,24},{9,... | collective-permute-start | bytes 589832 | tf_op jit(solution)/shard_map/ppermute | solution.py:177
  54.5 1.4 %collective-permute-start.18 = (bf16[4,2,48,256]{3,2,1,0:T(8,128)(2,1)S(1)}, bf16[4,2,48,256]{3,2,1,0:T(8,128)(2,1)S(1)}, u32[]{:S(2)}, u32[]{:S(2)}) collective-permute-start(bf16[4,2,48,256]{3,2,1,0:T(8,128)(2,1)S(1)} %collective-permute-done.14.refs_2_), channel_id=1, source_target_pairs={{0,16},{1,17},{2,18},{3,19},{4,20},{5,21},{6,22},{7,23},{8,24},{9,... | collective-permute-start | bytes 589832 | tf_op jit(solution)/shard_map/ppermute | solution.py:177
  55.8 1.4 %collective-permute-start.19 = (bf16[4,2,48,256]{3,2,1,0:T(8,128)(2,1)S(1)}, bf16[4,2,48,256]{3,2,1,0:T(8,128)(2,1)S(1)}, u32[]{:S(2)}, u32[]{:S(2)}) collective-permute-start(bf16[4,2,48,256]{3,2,1,0:T(8,128)(2,1)S(1)} %collective-permute-done.15.refs_3_), channel_id=1, source_target_pairs={{0,16},{1,17},{2,18},{3,19},{4,20},{5,21},{6,22},{7,23},{8,24},{9,... | collective-permute-start | bytes 589832 | tf_op jit(solution)/shard_map/ppermute | solution.py:177

commit v11 on v10

--- a/solution.py
+++ b/solution.py
@@ -202,7 +202,7 @@
                 ].reshape(blocks * lat_block, radial)
 
 
-def forward_kernel(table_ref, grid_ref, held, buffer, sems):
+def forward_kernel(table_ref, grid_ref, held, wide, table_held, buffer, sems, table_sem):
     blocks, rows, lat_block, radial = held.shape
 
     def chunk(at):
@@ -210,9 +210,13 @@
             grid_ref.at[pl.ds(2 * at, 2)], buffer.at[pl.ds(2 * at, 2)], sems.at[at]
         )
 
+    table_copy = pltpu.make_async_copy(table_ref.at[lax.axis_index("sec")], wide, table_sem)
+    table_copy.start()
     for at in range(sems.shape[0]):
         chunk(at).start()
-    table = table_ref[lax.axis_index("sec")]
+    table_copy.wait()
+    table_held[...] = wide[...].astype(table_held.dtype)
+    table = table_held[...]
 
     def one_block(block, carry):
         for at in range(0, lat_block, 2):
@@ -234,12 +238,15 @@
     lat_rows, _, radial = grid_terms.shape
     return pl.pallas_call(
         forward_kernel,
-        in_specs=[vmem(), anywhere()],
+        in_specs=[pl.BlockSpec(memory_space=pltpu.HBM), anywhere()],
         out_specs=vmem(),
         out_shape=jax.ShapeDtypeStruct((lat_rows // lat_block, rows, lat_block, radial), jnp.float32),
         scratch_shapes=[
+            pltpu.VMEM((rows, phi_count), jnp.float32),
+            pltpu.VMEM((rows, phi_count), jnp.bfloat16),
             pltpu.VMEM(grid_terms.shape, jnp.float32),
             pltpu.SemaphoreType.DMA((lat_rows // 2,)),
+            pltpu.SemaphoreType.DMA,
         ],
         compiler_params=params(36),
         cost_estimate=pl.CostEstimate(
@@ -247,7 +254,7 @@
             bytes_accessed=4 * lat_rows * phi_count * radial,
             transcendentals=0,
         ),
-    )(table, grid_terms)
+    )(pltpu.with_memory_space_constraint(table, pltpu.HBM), grid_terms)
 
 
 def add_kernel(keep_ref, take_ref, *outs):
@@ -386,7 +393,7 @@
     columns = 2 * radial
     pair_total = pair_orders.shape[0]
     table = natural_table(pair_total, lax.axis_size("sec"), phi_count)
-    forward_table = jnp.asarray(table, jnp.bfloat16)
+    forward_table = jnp.asarray(table)
     inverse_table = jnp.asarray(table.transpose(0, 2, 1), jnp.bfloat16)
 
     def shape(*sizes, dtype=jnp.bfloat16):

time: 65.4 us -> 69.8 us (1.067)
  Pallas kernels: 21.1 us -> 26.5 us
  local copies, waits for them, and re-layouts: 1.7 us -> 0.66 us
    pallas_call x1, Pallas kernels: 8.58 us -> 14 us  [forward_sums(): pl.pallas_call(forward_kernel, in_specs=[pl.BlockSpec(memory_space=pltpu....]
    unnamed x18 -> x16, local copies, waits for them, and re-layouts: 1.08 us -> 0.04 us
where the time goes in v11:
time: 69.8 us; the launch traced here: 69.6 us
  Pallas kernels  26.5 us (38%)
  starting transfers between devices  25.5 us (37%)
  waiting for transfers between devices  16.1 us (23%)
  between operations  0.81 us (1%)
    ppermute x20, starting transfers between devices, exchange(): return lax.ppermute(array, names, pairs)  25.5 us
    ppermute x20, waiting for transfers between devices, exchange(): return lax.ppermute(array, names, pairs)  16.1 us
    pallas_call x1, Pallas kernels, forward_sums(): pl.pallas_call(forward_kernel, in_specs=[pl.BlockSpec(memory_space=pltpu....  14 us
    pallas_call x1, Pallas kernels, inverse_values(): pl.pallas_call(inverse_kernel, in_specs=[smem()] + [vmem()] * (1 + len(ta...  8.06 us
    pallas_call x8, Pallas kernels, call(): pl.pallas_call(kernel, in_specs=[smem()] * scalars + [vmem()] * (len(oper...  4.51 us
  transfers between devices with their start and end apart: 20, of which 10 were waited for; matrix products, arithmetic and copies ran while one was open for 1% of the time, Pallas kernels for 2%

profile of v11, /device:TPU:0, one launch (start us, length us, event | category | flops | bytes accessed | tf_op | source)
XLA Modules:
  0.0 69.6 jit_solution(10911928972720834044)
XLA Ops:
  0.7 14.0 %shard_map.114.held = f32[6,128,8,128]{3,2,1,0:T(8,128)S(1)} custom-call(f32[2,128,768]{2,1,0:T(8,128)} %constant.6.clone.table_ref, f32[48,768,128]{2,1,0:T(8,128)} %grid_ref.1), custom_call_target="tpu_custom_call" | custom-call | flops 1207959552 | bytes 18874368 | tf_op jit(solution)/shard_map/pallas_call | solution.py:239
  14.7 0.7 shard_map.116
  15.4 0.5 collective-permute-start.3
  15.9 0.7 shard_map.115.keep_ref
  16.6 1.2 %collective-permute-done.3.take_ref = bf16[4,4,2,48,256]{4,3,2,1,0:T(8,128)(2,1)S(1)} collective-permute-done((bf16[4,4,2,48,256]{4,3,2,1,0:T(8,128)(2,1)S(1)}, bf16[4,4,2,48,256]{4,3,2,1,0:T(8,128)(2,1)S(1)}, u32[]{:S(2)}, u32[]{:S(2)}) %collective-permute-start.3) | collective-permute-done | bytes 786464 | tf_op jit(solution)/shard_map/ppermute | solution.py:177
  18.0 2.9 %collective-permute-start.4 = (bf16[4,2,48,256]{3,2,1,0:T(8,128)(2,1)S(1)}, bf16[4,2,48,256]{3,2,1,0:T(8,128)(2,1)S(1)}, u32[]{:S(2)}, u32[]{:S(2)}) collective-permute-start(bf16[4,2,48,256]{3,2,1,0:T(8,128)(2,1)S(1)} %get-tuple-element.25), channel_id=1, source_target_pairs={{0,1},{1,0},{2,3},{3,2},{4,5},{5,4},{6,7},{7,6},{8,9},{9,8},{10,11... | collective-permute-start | bytes 589832 | tf_op jit(solution)/shard_map/ppermute | solution.py:177
  20.9 1.5 %collective-permute-start.5 = (bf16[4,2,48,256]{3,2,1,0:T(8,128)(2,1)S(1)}, bf16[4,2,48,256]{3,2,1,0:T(8,128)(2,1)S(1)}, u32[]{:S(2)}, u32[]{:S(2)}) collective-permute-start(bf16[4,2,48,256]{3,2,1,0:T(8,128)(2,1)S(1)} %get-tuple-element.26), channel_id=1, source_target_pairs={{0,2},{1,3},{2,0},{3,1},{4,6},{5,7},{6,4},{7,5},{8,10},{9,11},{10,... | collective-permute-start | bytes 589832 | tf_op jit(solution)/shard_map/ppermute | solution.py:177
  22.5 0.3 shard_map.113
  22.8 2.1 %collective-permute-start = (bf16[72,192]{1,0:T(8,128)(2,1)S(1)}, bf16[72,192]{1,0:T(8,128)(2,1)S(1)}, u32[]{:S(2)}, u32[]{:S(2)}) collective-permute-start(bf16[72,192]{1,0:T(8,128)(2,1)S(1)} %get-tuple-element.21), channel_id=1, source_target_pairs={{0,4},{1,5},{2,6},{3,7},{4,0},{5,1},{6,2},{7,3},{8,12},{9,13},{10,... | collective-permute-start | bytes 82952 | tf_op jit(solution)/shard_map/ppermute | solution.py:177
  24.9 2.6 %collective-permute-start.1 = (bf16[72,192]{1,0:T(8,128)(2,1)S(1)}, bf16[72,192]{1,0:T(8,128)(2,1)S(1)}, u32[]{:S(2)}, u32[]{:S(2)}) collective-permute-start(bf16[72,192]{1,0:T(8,128)(2,1)S(1)} %get-tuple-element.22), channel_id=1, source_target_pairs={{0,8},{1,9},{2,10},{3,11},{4,12},{5,13},{6,14},{7,15},{8,0},{9,1},... | collective-permute-start | bytes 82952 | tf_op jit(solution)/shard_map/ppermute | solution.py:177
  27.5 3.4 %collective-permute-start.2 = (bf16[72,192]{1,0:T(8,128)(2,1)S(1)}, bf16[72,192]{1,0:T(8,128)(2,1)S(1)}, u32[]{:S(2)}, u32[]{:S(2)}) collective-permute-start(bf16[72,192]{1,0:T(8,128)(2,1)S(1)} %get-tuple-element.23), channel_id=1, source_target_pairs={{0,12},{1,13},{2,14},{3,15},{4,8},{5,9},{6,10},{7,11},{8,4},{9,5},... | collective-permute-start | bytes 82952 | tf_op jit(solution)/shard_map/ppermute | solution.py:177
  30.9 2.4 %collective-permute-done.2.refs_3_ = bf16[72,192]{1,0:T(8,128)(2,1)S(1)} collective-permute-done((bf16[72,192]{1,0:T(8,128)(2,1)S(1)}, bf16[72,192]{1,0:T(8,128)(2,1)S(1)}, u32[]{:S(2)}, u32[]{:S(2)}) %collective-permute-start.2) | collective-permute-done | bytes 27680 | tf_op jit(solution)/shard_map/ppermute | solution.py:177
  33.3 0.8 %shard_map.118 = (f32[72,256]{1,0:T(8,128)S(1)}, bf16[72,256]{1,0:T(8,128)(2,1)S(1)}, bf16[72,256]{1,0:T(8,128)(2,1)S(1)}, bf16[72,256]{1,0:T(8,128)(2,1)S(1)}) custom-call(s32[32]{0:T(128)S(1)} %copy-done.5, bf16[72,192]{1,0:T(8,128)(2,1)S(1)} %get-tuple-element.20.refs_0_, bf16[72,192]{1,0:T(8,128)(2,1)S(1)} %collective-permute-done.refs_1_, ...), custom_call_target="tpu_custom_call" | custom-call | tf_op jit(solution)/shard_map/pallas_call | solution.py:140
  34.1 3.5 %collective-permute-start.7 = (bf16[72,256]{1,0:T(8,128)(2,1)S(1)}, bf16[72,256]{1,0:T(8,128)(2,1)S(1)}, u32[]{:S(2)}, u32[]{:S(2)}) collective-permute-start(bf16[72,256]{1,0:T(8,128)(2,1)S(1)} %get-tuple-element.29), channel_id=1, source_target_pairs={{0,12},{1,13},{2,14},{3,15},{4,8},{5,9},{6,10},{7,11},{8,4},{9,5},... | collective-permute-start | bytes 110600 | tf_op jit(solution)/shard_map/ppermute | solution.py:177
  37.6 1.0 %collective-permute-start.9 = (bf16[72,256]{1,0:T(8,128)(2,1)S(1)}, bf16[72,256]{1,0:T(8,128)(2,1)S(1)}, u32[]{:S(2)}, u32[]{:S(2)}) collective-permute-start(bf16[72,256]{1,0:T(8,128)(2,1)S(1)} %get-tuple-element.31), channel_id=1, source_target_pairs={{0,4},{1,5},{2,6},{3,7},{4,0},{5,1},{6,2},{7,3},{8,12},{9,13},{10,... | collective-permute-start | bytes 110600 | tf_op jit(solution)/shard_map/ppermute | solution.py:177
  38.6 0.6 shard_map.119.factor_ref
  39.1 0.9 %collective-permute-done.7.two = bf16[72,256]{1,0:T(8,128)(2,1)S(1)} collective-permute-done((bf16[72,256]{1,0:T(8,128)(2,1)S(1)}, bf16[72,256]{1,0:T(8,128)(2,1)S(1)}, u32[]{:S(2)}, u32[]{:S(2)}) %collective-permute-start.7) | collective-permute-done | bytes 36896 | tf_op jit(solution)/shard_map/ppermute | solution.py:177
  40.0 2.6 %collective-permute-done.8.three = bf16[72,256]{1,0:T(8,128)(2,1)S(1)} collective-permute-done((bf16[72,256]{1,0:T(8,128)(2,1)S(1)}, bf16[72,256]{1,0:T(8,128)(2,1)S(1)}, u32[]{:S(2)}, u32[]{:S(2)}) %collective-permute-start.8) | collective-permute-done | bytes 36896 | tf_op jit(solution)/shard_map/ppermute | solution.py:177
  43.0 1.3 %collective-permute-start.12 = (bf16[72,256]{1,0:T(8,128)(2,1)S(1)}, bf16[72,256]{1,0:T(8,128)(2,1)S(1)}, u32[]{:S(2)}, u32[]{:S(2)}) collective-permute-start(bf16[72,256]{1,0:T(8,128)(2,1)S(1)} %shard_map.120.refs_4_), channel_id=1, source_target_pairs={{0,12},{1,13},{2,14},{3,15},{4,8},{5,9},{6,10},{7,11},{8,4},{9,5},... | collective-permute-start | bytes 110600 | tf_op jit(solution)/shard_map/ppermute | solution.py:177
  44.3 0.9 %collective-permute-start.11 = (bf16[72,256]{1,0:T(8,128)(2,1)S(1)}, bf16[72,256]{1,0:T(8,128)(2,1)S(1)}, u32[]{:S(2)}, u32[]{:S(2)}) collective-permute-start(bf16[72,256]{1,0:T(8,128)(2,1)S(1)} %shard_map.120.refs_4_), channel_id=1, source_target_pairs={{0,8},{1,9},{2,10},{3,11},{4,12},{5,13},{6,14},{7,15},{8,0},{9,1},... | collective-permute-start | bytes 110600 | tf_op jit(solution)/shard_map/ppermute | solution.py:177
  45.2 2.2 %collective-permute-start.10 = (bf16[72,256]{1,0:T(8,128)(2,1)S(1)}, bf16[72,256]{1,0:T(8,128)(2,1)S(1)}, u32[]{:S(2)}, u32[]{:S(2)}) collective-permute-start(bf16[72,256]{1,0:T(8,128)(2,1)S(1)} %shard_map.120.refs_4_), channel_id=1, source_target_pairs={{0,4},{1,5},{2,6},{3,7},{4,0},{5,1},{6,2},{7,3},{8,12},{9,13},{10,... | collective-permute-start | bytes 110600 | tf_op jit(solution)/shard_map/ppermute | solution.py:177
  47.4 0.6 slice_bitcast_fusion
  48.0 1.5 %collective-permute-done.10.refs_5_ = bf16[72,256]{1,0:T(8,128)(2,1)S(1)} collective-permute-done((bf16[72,256]{1,0:T(8,128)(2,1)S(1)}, bf16[72,256]{1,0:T(8,128)(2,1)S(1)}, u32[]{:S(2)}, u32[]{:S(2)}) %collective-permute-start.10) | collective-permute-done | bytes 36896 | tf_op jit(solution)/shard_map/ppermute | solution.py:177
  49.6 1.0 %shard_map.121 = (bf16[4,2,48,256]{3,2,1,0:T(8,128)(2,1)S(1)}, bf16[4,2,48,256]{3,2,1,0:T(8,128)(2,1)S(1)}, bf16[4,2,48,256]{3,2,1,0:T(8,128)(2,1)S(1)}, bf16[4,2,48,256]{3,2,1,0:T(8,128)(2,1)S(1)}) custom-call(s32[32]{0:T(128)S(1)} %copy-done.5, bf16[72,192]{1,0:T(8,128)(2,1)S(1)} %get-tuple-element.20.refs_0_, ...), custom_call_target="tpu_custom_call" | custom-call | tf_op jit(solution)/shard_map/pallas_call | solution.py:140
  50.5 1.6 %collective-permute-start.13 = (bf16[4,2,48,256]{3,2,1,0:T(8,128)(2,1)S(1)}, bf16[4,2,48,256]{3,2,1,0:T(8,128)(2,1)S(1)}, u32[]{:S(2)}, u32[]{:S(2)}) collective-permute-start(bf16[4,2,48,256]{3,2,1,0:T(8,128)(2,1)S(1)} %get-tuple-element.34), channel_id=1, source_target_pairs={{0,1},{1,0},{2,3},{3,2},{4,5},{5,4},{6,7},{7,6},{8,9},{9,8},{10,11... | collective-permute-start | bytes 589832 | tf_op jit(solution)/shard_map/ppermute | solution.py:177
  52.1 1.4 %collective-permute-start.14 = (bf16[4,2,48,256]{3,2,1,0:T(8,128)(2,1)S(1)}, bf16[4,2,48,256]{3,2,1,0:T(8,128)(2,1)S(1)}, u32[]{:S(2)}, u32[]{:S(2)}) collective-permute-start(bf16[4,2,48,256]{3,2,1,0:T(8,128)(2,1)S(1)} %get-tuple-element.35), channel_id=1, source_target_pairs={{0,2},{1,3},{2,0},{3,1},{4,6},{5,7},{6,4},{7,5},{8,10},{9,11},{10,... | collective-permute-start | bytes 589832 | tf_op jit(solution)/shard_map/ppermute | solution.py:177
  53.5 0.5 collective-permute-start.15
  54.1 2.2 %collective-permute-done.13.refs_1_ = bf16[4,2,48,256]{3,2,1,0:T(8,128)(2,1)S(1)} collective-permute-done((bf16[4,2,48,256]{3,2,1,0:T(8,128)(2,1)S(1)}, bf16[4,2,48,256]{3,2,1,0:T(8,128)(2,1)S(1)}, u32[]{:S(2)}, u32[]{:S(2)}) %collective-permute-start.13) | collective-permute-done | bytes 196640 | tf_op jit(solution)/shard_map/ppermute | solution.py:177
  56.3 2.6 %collective-permute-done.14.refs_2_ = bf16[4,2,48,256]{3,2,1,0:T(8,128)(2,1)S(1)} collective-permute-done((bf16[4,2,48,256]{3,2,1,0:T(8,128)(2,1)S(1)}, bf16[4,2,48,256]{3,2,1,0:T(8,128)(2,1)S(1)}, u32[]{:S(2)}, u32[]{:S(2)}) %collective-permute-start.14) | collective-permute-done | bytes 196640 | tf_op jit(solution)/shard_map/ppermute | solution.py:177
  58.9 1.2 %collective-permute-done.15.refs_3_ = bf16[4,2,48,256]{3,2,1,0:T(8,128)(2,1)S(1)} collective-permute-done((bf16[4,2,48,256]{3,2,1,0:T(8,128)(2,1)S(1)}, bf16[4,2,48,256]{3,2,1,0:T(8,128)(2,1)S(1)}, u32[]{:S(2)}, u32[]{:S(2)}) %collective-permute-start.15) | collective-permute-done | bytes 196640 | tf_op jit(solution)/shard_map/ppermute | solution.py:177
  60.3 1.2 %collective-permute-done.19.refs_7_ = bf16[4,2,48,256]{3,2,1,0:T(8,128)(2,1)S(1)} collective-permute-done((bf16[4,2,48,256]{3,2,1,0:T(8,128)(2,1)S(1)}, bf16[4,2,48,256]{3,2,1,0:T(8,128)(2,1)S(1)}, u32[]{:S(2)}, u32[]{:S(2)}) %collective-permute-start.19) | collective-permute-done | bytes 196640 | tf_op jit(solution)/shard_map/ppermute | solution.py:177
  61.6 8.1 %shard_map.122 = f32[48,768,128]{2,1,0:T(8,128)} custom-call(s32[32]{0:T(128)S(1)} %copy-done.5, bf16[2,768,128]{2,1,0:T(8,128)(2,1)S(1)} %copy-done, bf16[4,2,48,256]{3,2,1,0:T(8,128)(2,1)S(1)} %get-tuple-element.33.refs_0_, bf16[4,2,48,256]{3,2,1,0:T(8,128)(2,1)S(1)} %collective-permute-done.13.refs_1_, ...), custom_call_target="tpu_custom_call" | custom-call | flops 1207959552 | bytes 18874368 | tf_op jit(solution)/shard_map/pallas_call | solution.py:369
  (35 shorter events, 0.8 us)
Async XLA Ops:
  0.6 37.9 %copy-start.7 = (f32[1,128]{1,0:T(1,128)S(1)}, f32[1,128]{1,0:T(1,128)}, u32[]{:S(2)}) copy-start(f32[1,128]{1,0:T(1,128)} %constant.11.damping_ref) | copy-start | bytes 1540
  0.6 60.9 %copy-start = (bf16[2,768,128]{2,1,0:T(8,128)(2,1)S(1)}, bf16[2,768,128]{2,1,0:T(8,128)(2,1)}, u32[]{:S(2)}) copy-start(bf16[2,768,128]{2,1,0:T(8,128)(2,1)} %constant.7.clone.table_ref) | copy-start | bytes 1179652
  0.7 14.0 %copy-start.5 = (s32[32]{0:T(128)S(1)}, s32[32]{0:T(128)}, u32[]{:S(2)}) copy-start(s32[32]{0:T(128)} %orders_ref.11) | copy-start | bytes 388
  0.7 21.8 %copy-start.1 = (bf16[1,65,768]{2,1,0:T(8,128)(2,1)S(1)}, bf16[1,65,768]{2,1,0:T(8,128)(2,1)}, u32[]{:S(2)}) copy-start(bf16[1,65,768]{2,1,0:T(8,128)(2,1)} %legendre_ref.1) | copy-start | bytes 299524
  0.7 37.9 %copy-start.6 = (f32[128]{0:T(128)S(1)}, f32[128]{0:T(128)}, u32[]{:S(2)}) copy-start(f32[128]{0:T(128)} %param.14) | copy-start | bytes 1540
  0.7 42.0 %copy-start.4 = (bf16[128,128]{1,0:T(8,128)(2,1)S(1)}, bf16[128,128]{1,0:T(8,128)(2,1)}, u32[]{:S(2)}) copy-start(bf16[128,128]{1,0:T(8,128)(2,1)} %left_ref.1) | copy-start | bytes 98308
  0.7 41.9 %copy-start.3 = (bf16[128,128]{1,0:T(8,128)(2,1)S(1)}, bf16[128,128]{1,0:T(8,128)(2,1)}, u32[]{:S(2)}) copy-start(bf16[128,128]{1,0:T(8,128)(2,1)} %right_ref.1) | copy-start | bytes 98308
  0.7 41.9 %copy-start.2 = (bf16[1,65,256]{2,1,0:T(8,128)(2,1)S(1)}, bf16[1,65,256]{2,1,0:T(8,128)(2,1)}, u32[]{:S(2)}) copy-start(bf16[1,65,256]{2,1,0:T(8,128)(2,1)} %state_ref.1) | copy-start | bytes 99844
  15.4 2.4 %collective-permute-start.3 = (bf16[4,4,2,48,256]{4,3,2,1,0:T(8,128)(2,1)S(1)}, bf16[4,4,2,48,256]{4,3,2,1,0:T(8,128)(2,1)S(1)}, u32[]{:S(2)}, u32[]{:S(2)}) collective-permute-start(bf16[4,4,2,48,256]{4,3,2,1,0:T(8,128)(2,1)S(1)} %shard_map.116), channel_id=1, source_target_pairs={{0,16},{1,17},{2,18},{3,19},{4,20},{5,21},{6,22},{7,23},{8,24},{9,... | collective-permute-start | bytes 2359304 | tf_op jit(solution)/shard_map/ppermute | solution.py:177
  18.0 15.3 %collective-permute-start.4 = (bf16[4,2,48,256]{3,2,1,0:T(8,128)(2,1)S(1)}, bf16[4,2,48,256]{3,2,1,0:T(8,128)(2,1)S(1)}, u32[]{:S(2)}, u32[]{:S(2)}) collective-permute-start(bf16[4,2,48,256]{3,2,1,0:T(8,128)(2,1)S(1)} %get-tuple-element.25), channel_id=1, source_target_pairs={{0,1},{1,0},{2,3},{3,2},{4,5},{5,4},{6,7},{7,6},{8,9},{9,8},{10,11... | collective-permute-start | bytes 589832 | tf_op jit(solution)/shard_map/ppermute | solution.py:177
  20.9 12.3 %collective-permute-start.5 = (bf16[4,2,48,256]{3,2,1,0:T(8,128)(2,1)S(1)}, bf16[4,2,48,256]{3,2,1,0:T(8,128)(2,1)S(1)}, u32[]{:S(2)}, u32[]{:S(2)}) collective-permute-start(bf16[4,2,48,256]{3,2,1,0:T(8,128)(2,1)S(1)} %get-tuple-element.26), channel_id=1, source_target_pairs={{0,2},{1,3},{2,0},{3,1},{4,6},{5,7},{6,4},{7,5},{8,10},{9,11},{10,... | collective-permute-start | bytes 589832 | tf_op jit(solution)/shard_map/ppermute | solution.py:177
  22.5 10.8 %collective-permute-start.6 = (bf16[4,2,48,256]{3,2,1,0:T(8,128)(2,1)S(1)}, bf16[4,2,48,256]{3,2,1,0:T(8,128)(2,1)S(1)}, u32[]{:S(2)}, u32[]{:S(2)}) collective-permute-start(bf16[4,2,48,256]{3,2,1,0:T(8,128)(2,1)S(1)} %get-tuple-element.27), channel_id=1, source_target_pairs={{0,3},{1,2},{2,1},{3,0},{4,7},{5,6},{6,5},{7,4},{8,11},{9,10},{10,... | collective-permute-start | bytes 589832 | tf_op jit(solution)/shard_map/ppermute | solution.py:177
  22.8 4.7 %collective-permute-start = (bf16[72,192]{1,0:T(8,128)(2,1)S(1)}, bf16[72,192]{1,0:T(8,128)(2,1)S(1)}, u32[]{:S(2)}, u32[]{:S(2)}) collective-permute-start(bf16[72,192]{1,0:T(8,128)(2,1)S(1)} %get-tuple-element.21), channel_id=1, source_target_pairs={{0,4},{1,5},{2,6},{3,7},{4,0},{5,1},{6,2},{7,3},{8,12},{9,13},{10,... | collective-permute-start | bytes 82952 | tf_op jit(solution)/shard_map/ppermute | solution.py:177
  24.9 6.0 %collective-permute-start.1 = (bf16[72,192]{1,0:T(8,128)(2,1)S(1)}, bf16[72,192]{1,0:T(8,128)(2,1)S(1)}, u32[]{:S(2)}, u32[]{:S(2)}) collective-permute-start(bf16[72,192]{1,0:T(8,128)(2,1)S(1)} %get-tuple-element.22), channel_id=1, source_target_pairs={{0,8},{1,9},{2,10},{3,11},{4,12},{5,13},{6,14},{7,15},{8,0},{9,1},... | collective-permute-start | bytes 82952 | tf_op jit(solution)/shard_map/ppermute | solution.py:177
  27.5 5.8 %collective-permute-start.2 = (bf16[72,192]{1,0:T(8,128)(2,1)S(1)}, bf16[72,192]{1,0:T(8,128)(2,1)S(1)}, u32[]{:S(2)}, u32[]{:S(2)}) collective-permute-start(bf16[72,192]{1,0:T(8,128)(2,1)S(1)} %get-tuple-element.23), channel_id=1, source_target_pairs={{0,12},{1,13},{2,14},{3,15},{4,8},{5,9},{6,10},{7,11},{8,4},{9,5},... | collective-permute-start | bytes 82952 | tf_op jit(solution)/shard_map/ppermute | solution.py:177
  34.1 6.0 %collective-permute-start.7 = (bf16[72,256]{1,0:T(8,128)(2,1)S(1)}, bf16[72,256]{1,0:T(8,128)(2,1)S(1)}, u32[]{:S(2)}, u32[]{:S(2)}) collective-permute-start(bf16[72,256]{1,0:T(8,128)(2,1)S(1)} %get-tuple-element.29), channel_id=1, source_target_pairs={{0,12},{1,13},{2,14},{3,15},{4,8},{5,9},{6,10},{7,11},{8,4},{9,5},... | collective-permute-start | bytes 110600 | tf_op jit(solution)/shard_map/ppermute | solution.py:177
  37.6 5.1 %collective-permute-start.8 = (bf16[72,256]{1,0:T(8,128)(2,1)S(1)}, bf16[72,256]{1,0:T(8,128)(2,1)S(1)}, u32[]{:S(2)}, u32[]{:S(2)}) collective-permute-start(bf16[72,256]{1,0:T(8,128)(2,1)S(1)} %get-tuple-element.30), channel_id=1, source_target_pairs={{0,8},{1,9},{2,10},{3,11},{4,12},{5,13},{6,14},{7,15},{8,0},{9,1},... | collective-permute-start | bytes 110600 | tf_op jit(solution)/shard_map/ppermute | solution.py:177
  37.6 5.1 %collective-permute-start.9 = (bf16[72,256]{1,0:T(8,128)(2,1)S(1)}, bf16[72,256]{1,0:T(8,128)(2,1)S(1)}, u32[]{:S(2)}, u32[]{:S(2)}) collective-permute-start(bf16[72,256]{1,0:T(8,128)(2,1)S(1)} %get-tuple-element.31), channel_id=1, source_target_pairs={{0,4},{1,5},{2,6},{3,7},{4,0},{5,1},{6,2},{7,3},{8,12},{9,13},{10,... | collective-permute-start | bytes 110600 | tf_op jit(solution)/shard_map/ppermute | solution.py:177
  43.0 6.6 %collective-permute-start.12 = (bf16[72,256]{1,0:T(8,128)(2,1)S(1)}, bf16[72,256]{1,0:T(8,128)(2,1)S(1)}, u32[]{:S(2)}, u32[]{:S(2)}) collective-permute-start(bf16[72,256]{1,0:T(8,128)(2,1)S(1)} %shard_map.120.refs_4_), channel_id=1, source_target_pairs={{0,12},{1,13},{2,14},{3,15},{4,8},{5,9},{6,10},{7,11},{8,4},{9,5},... | collective-permute-start | bytes 110600 | tf_op jit(solution)/shard_map/ppermute | solution.py:177
  44.3 5.3 %collective-permute-start.11 = (bf16[72,256]{1,0:T(8,128)(2,1)S(1)}, bf16[72,256]{1,0:T(8,128)(2,1)S(1)}, u32[]{:S(2)}, u32[]{:S(2)}) collective-permute-start(bf16[72,256]{1,0:T(8,128)(2,1)S(1)} %shard_map.120.refs_4_), channel_id=1, source_target_pairs={{0,8},{1,9},{2,10},{3,11},{4,12},{5,13},{6,14},{7,15},{8,0},{9,1},... | collective-permute-start | bytes 110600 | tf_op jit(solution)/shard_map/ppermute | solution.py:177
  45.2 4.4 %collective-permute-start.10 = (bf16[72,256]{1,0:T(8,128)(2,1)S(1)}, bf16[72,256]{1,0:T(8,128)(2,1)S(1)}, u32[]{:S(2)}, u32[]{:S(2)}) collective-permute-start(bf16[72,256]{1,0:T(8,128)(2,1)S(1)} %shard_map.120.refs_4_), channel_id=1, source_target_pairs={{0,4},{1,5},{2,6},{3,7},{4,0},{5,1},{6,2},{7,3},{8,12},{9,13},{10,... | collective-permute-start | bytes 110600 | tf_op jit(solution)/shard_map/ppermute | solution.py:177
  50.5 5.7 %collective-permute-start.13 = (bf16[4,2,48,256]{3,2,1,0:T(8,128)(2,1)S(1)}, bf16[4,2,48,256]{3,2,1,0:T(8,128)(2,1)S(1)}, u32[]{:S(2)}, u32[]{:S(2)}) collective-permute-start(bf16[4,2,48,256]{3,2,1,0:T(8,128)(2,1)S(1)} %get-tuple-element.34), channel_id=1, source_target_pairs={{0,1},{1,0},{2,3},{3,2},{4,5},{5,4},{6,7},{7,6},{8,9},{9,8},{10,11... | collective-permute-start | bytes 589832 | tf_op jit(solution)/shard_map/ppermute | solution.py:177
  52.1 6.7 %collective-permute-start.14 = (bf16[4,2,48,256]{3,2,1,0:T(8,128)(2,1)S(1)}, bf16[4,2,48,256]{3,2,1,0:T(8,128)(2,1)S(1)}, u32[]{:S(2)}, u32[]{:S(2)}) collective-permute-start(bf16[4,2,48,256]{3,2,1,0:T(8,128)(2,1)S(1)} %get-tuple-element.35), channel_id=1, source_target_pairs={{0,2},{1,3},{2,0},{3,1},{4,6},{5,7},{6,4},{7,5},{8,10},{9,11},{10,... | collective-permute-start | bytes 589832 | tf_op jit(solution)/shard_map/ppermute | solution.py:177
  53.5 6.6 %collective-permute-start.15 = (bf16[4,2,48,256]{3,2,1,0:T(8,128)(2,1)S(1)}, bf16[4,2,48,256]{3,2,1,0:T(8,128)(2,1)S(1)}, u32[]{:S(2)}, u32[]{:S(2)}) collective-permute-start(bf16[4,2,48,256]{3,2,1,0:T(8,128)(2,1)S(1)} %get-tuple-element.36), channel_id=1, source_target_pairs={{0,3},{1,2},{2,1},{3,0},{4,7},{5,6},{6,5},{7,4},{8,11},{9,10},{10,... | collective-permute-start | bytes 589832 | tf_op jit(solution)/shard_map/ppermute | solution.py:177
  54.1 6.0 %collective-permute-start.16 = (bf16[4,2,48,256]{3,2,1,0:T(8,128)(2,1)S(1)}, bf16[4,2,48,256]{3,2,1,0:T(8,128)(2,1)S(1)}, u32[]{:S(2)}, u32[]{:S(2)}) collective-permute-start(bf16[4,2,48,256]{3,2,1,0:T(8,128)(2,1)S(1)} %get-tuple-element.33.refs_0_), channel_id=1, source_target_pairs={{0,16},{1,17},{2,18},{3,19},{4,20},{5,21},{6,22},{7,23},{8,24},{9,... | collective-permute-start | bytes 589832 | tf_op jit(solution)/shard_map/ppermute | solution.py:177
  56.3 3.9 %collective-permute-start.17 = (bf16[4,2,48,256]{3,2,1,0:T(8,128)(2,1)S(1)}, bf16[4,2,48,256]{3,2,1,0:T(8,128)(2,1)S(1)}, u32[]{:S(2)}, u32[]{:S(2)}) collective-permute-start(bf16[4,2,48,256]{3,2,1,0:T(8,128)(2,1)S(1)} %collective-permute-done.13.refs_1_), channel_id=1, source_target_pairs={{0,16},{1,17},{2,18},{3,19},{4,20},{5,21},{6,22},{7,23},{8,24},{9,... | collective-permute-start | bytes 589832 | tf_op jit(solution)/shard_map/ppermute | solution.py:177
  58.9 1.4 %collective-permute-start.18 = (bf16[4,2,48,256]{3,2,1,0:T(8,128)(2,1)S(1)}, bf16[4,2,48,256]{3,2,1,0:T(8,128)(2,1)S(1)}, u32[]{:S(2)}, u32[]{:S(2)}) collective-permute-start(bf16[4,2,48,256]{3,2,1,0:T(8,128)(2,1)S(1)} %collective-permute-done.14.refs_2_), channel_id=1, source_target_pairs={{0,16},{1,17},{2,18},{3,19},{4,20},{5,21},{6,22},{7,23},{8,24},{9,... | collective-permute-start | bytes 589832 | tf_op jit(solution)/shard_map/ppermute | solution.py:177
  60.1 1.4 %collective-permute-start.19 = (bf16[4,2,48,256]{3,2,1,0:T(8,128)(2,1)S(1)}, bf16[4,2,48,256]{3,2,1,0:T(8,128)(2,1)S(1)}, u32[]{:S(2)}, u32[]{:S(2)}) collective-permute-start(bf16[4,2,48,256]{3,2,1,0:T(8,128)(2,1)S(1)} %collective-permute-done.15.refs_3_), channel_id=1, source_target_pairs={{0,16},{1,17},{2,18},{3,19},{4,20},{5,21},{6,22},{7,23},{8,24},{9,... | collective-permute-start | bytes 589832 | tf_op jit(solution)/shard_map/ppermute | solution.py:177

commit v12 on v10

--- a/solution.py
+++ b/solution.py
@@ -399,7 +399,6 @@
         [slab] * 4,
         scratch=[pltpu.VMEM((16, padded, lat_rows), jnp.bfloat16)],
     )
-    weights = [cuts[0]] + [exchange(cuts[deep], deep=deep) for deep in (1, 2, 3)]
 
     held = forward_sums(forward_table, grid_terms, 8)
     block = shape(4, 2, lat_rows, columns)
@@ -415,6 +414,8 @@
 
     taken = exchange(arranged(1, jnp.bfloat16), sec=1)
     keep = arranged(0, jnp.float32)
+    taken, cuts = lax.optimization_barrier((taken, tuple(cuts)))
+    weights = [cuts[0]] + [exchange(cuts[deep], deep=deep) for deep in (1, 2, 3)]
     blocks = call(add_kernel, [keep, taken], [block] * 4, mib=24)
     takes = [blocks[0]] + [exchange(blocks[flat], flat=flat) for flat in (1, 2, 3)]
 

time: 65.4 us -> 65 us (level)
  no operation moved by 1% of the time
where the time goes in v12:
time: 65 us; the launch traced here: 64.9 us
  starting transfers between devices  25.5 us (39%)
  Pallas kernels  21.1 us (32%)
  waiting for transfers between devices  15.8 us (24%)
  local copies, waits for them, and re-layouts  1.7 us (3%)
  between operations  0.79 us (1%)
    ppermute x20, starting transfers between devices, exchange(): return lax.ppermute(array, names, pairs)  25.5 us
    ppermute x20, waiting for transfers between devices, exchange(): return lax.ppermute(array, names, pairs)  15.8 us
    pallas_call x1, Pallas kernels, forward_sums(): pl.pallas_call(forward_kernel, in_specs=[vmem(), anywhere()], out_specs=v...  8.58 us
    pallas_call x1, Pallas kernels, inverse_values(): pl.pallas_call(inverse_kernel, in_specs=[smem()] + [vmem()] * (1 + len(ta...  8.06 us
    pallas_call x8, Pallas kernels, call(): pl.pallas_call(kernel, in_specs=[smem()] * scalars + [vmem()] * (len(oper...  4.51 us
  transfers between devices with their start and end apart: 20, of which 10 were waited for; matrix products, arithmetic and copies ran while one was open for 1% of the time, Pallas kernels for 2%

profile of v12, /device:TPU:0, one launch (start us, length us, event | category | flops | bytes accessed | tf_op | source)
XLA Modules:
  0.0 64.9 jit_solution(3017160294345216700)
XLA Ops:
  0.7 1.0 %copy-done.1 = bf16[2,128,768]{2,1,0:T(8,128)(2,1)S(1)} copy-done((bf16[2,128,768]{2,1,0:T(8,128)(2,1)S(1)}, bf16[2,128,768]{2,1,0:T(8,128)(2,1)}, u32[]{:S(2)}) %copy-start.1) | copy-done | bytes 393240
  1.7 8.6 %shard_map.113.held = f32[6,128,8,128]{3,2,1,0:T(8,128)S(1)} custom-call(bf16[2,128,768]{2,1,0:T(8,128)(2,1)S(1)} %copy-done.1, f32[48,768,128]{2,1,0:T(8,128)} %grid_ref.1), custom_call_target="tpu_custom_call" | custom-call | flops 1207959552 | bytes 18874368 | tf_op jit(solution)/shard_map/pallas_call | solution.py:235
  10.3 0.7 %shard_map.114 = bf16[4,4,2,48,256]{4,3,2,1,0:T(8,128)(2,1)S(1)} custom-call(s32[32]{0:T(128)S(1)} %copy-done.6, f32[6,128,8,128]{3,2,1,0:T(8,128)S(1)} %shard_map.113.held), custom_call_target="tpu_custom_call" | custom-call | tf_op jit(solution)/shard_map/pallas_call | solution.py:140
  11.0 0.5 collective-permute-start
  11.5 0.7 %shard_map.116.keep_ref = f32[4,4,2,48,256]{4,3,2,1,0:T(8,128)S(1)} custom-call(s32[32]{0:T(128)S(1)} %copy-done.6, f32[6,128,8,128]{3,2,1,0:T(8,128)S(1)} %shard_map.113.held), custom_call_target="tpu_custom_call" | custom-call | tf_op jit(solution)/shard_map/pallas_call | solution.py:140
  12.6 0.9 %collective-permute-done.take_ref = bf16[4,4,2,48,256]{4,3,2,1,0:T(8,128)(2,1)S(1)} collective-permute-done((bf16[4,4,2,48,256]{4,3,2,1,0:T(8,128)(2,1)S(1)}, bf16[4,4,2,48,256]{4,3,2,1,0:T(8,128)(2,1)S(1)}, u32[]{:S(2)}, u32[]{:S(2)}) %collective-permute-start) | collective-permute-done | bytes 786464 | tf_op jit(solution)/shard_map/ppermute | solution.py:177
  13.7 2.9 %collective-permute-start.4 = (bf16[4,2,48,256]{3,2,1,0:T(8,128)(2,1)S(1)}, bf16[4,2,48,256]{3,2,1,0:T(8,128)(2,1)S(1)}, u32[]{:S(2)}, u32[]{:S(2)}) collective-permute-start(bf16[4,2,48,256]{3,2,1,0:T(8,128)(2,1)S(1)} %get-tuple-element.35), channel_id=1, source_target_pairs={{0,1},{1,0},{2,3},{3,2},{4,5},{5,4},{6,7},{7,6},{8,9},{9,8},{10,11... | collective-permute-start | bytes 589832 | tf_op jit(solution)/shard_map/ppermute | solution.py:177
  16.6 1.5 %collective-permute-start.5 = (bf16[4,2,48,256]{3,2,1,0:T(8,128)(2,1)S(1)}, bf16[4,2,48,256]{3,2,1,0:T(8,128)(2,1)S(1)}, u32[]{:S(2)}, u32[]{:S(2)}) collective-permute-start(bf16[4,2,48,256]{3,2,1,0:T(8,128)(2,1)S(1)} %get-tuple-element.36), channel_id=1, source_target_pairs={{0,2},{1,3},{2,0},{3,1},{4,6},{5,7},{6,4},{7,5},{8,10},{9,11},{10,... | collective-permute-start | bytes 589832 | tf_op jit(solution)/shard_map/ppermute | solution.py:177
  18.1 2.0 %collective-permute-start.1 = (bf16[72,192]{1,0:T(8,128)(2,1)S(1)}, bf16[72,192]{1,0:T(8,128)(2,1)S(1)}, u32[]{:S(2)}, u32[]{:S(2)}) collective-permute-start(bf16[72,192]{1,0:T(8,128)(2,1)S(1)} %get-tuple-element.30), channel_id=1, source_target_pairs={{0,4},{1,5},{2,6},{3,7},{4,0},{5,1},{6,2},{7,3},{8,12},{9,13},{10,... | collective-permute-start | bytes 82952 | tf_op jit(solution)/shard_map/ppermute | solution.py:177
  20.2 2.6 %collective-permute-start.2 = (bf16[72,192]{1,0:T(8,128)(2,1)S(1)}, bf16[72,192]{1,0:T(8,128)(2,1)S(1)}, u32[]{:S(2)}, u32[]{:S(2)}) collective-permute-start(bf16[72,192]{1,0:T(8,128)(2,1)S(1)} %get-tuple-element.31), channel_id=1, source_target_pairs={{0,8},{1,9},{2,10},{3,11},{4,12},{5,13},{6,14},{7,15},{8,0},{9,1},... | collective-permute-start | bytes 82952 | tf_op jit(solution)/shard_map/ppermute | solution.py:177
  22.8 3.4 %collective-permute-start.3 = (bf16[72,192]{1,0:T(8,128)(2,1)S(1)}, bf16[72,192]{1,0:T(8,128)(2,1)S(1)}, u32[]{:S(2)}, u32[]{:S(2)}) collective-permute-start(bf16[72,192]{1,0:T(8,128)(2,1)S(1)} %get-tuple-element.32), channel_id=1, source_target_pairs={{0,12},{1,13},{2,14},{3,15},{4,8},{5,9},{6,10},{7,11},{8,4},{9,5},... | collective-permute-start | bytes 82952 | tf_op jit(solution)/shard_map/ppermute | solution.py:177
  26.2 2.4 %collective-permute-done.3.refs_3_ = bf16[72,192]{1,0:T(8,128)(2,1)S(1)} collective-permute-done((bf16[72,192]{1,0:T(8,128)(2,1)S(1)}, bf16[72,192]{1,0:T(8,128)(2,1)S(1)}, u32[]{:S(2)}, u32[]{:S(2)}) %collective-permute-start.3) | collective-permute-done | bytes 27680 | tf_op jit(solution)/shard_map/ppermute | solution.py:177
  28.5 0.8 %shard_map.118 = (f32[72,256]{1,0:T(8,128)S(1)}, bf16[72,256]{1,0:T(8,128)(2,1)S(1)}, bf16[72,256]{1,0:T(8,128)(2,1)S(1)}, bf16[72,256]{1,0:T(8,128)(2,1)S(1)}) custom-call(s32[32]{0:T(128)S(1)} %copy-done.6, bf16[72,192]{1,0:T(8,128)(2,1)S(1)} %get-tuple-element.29.refs_0_, bf16[72,192]{1,0:T(8,128)(2,1)S(1)} %collective-permute-done.1.refs_1_, ...), custom_call_target="tpu_custom_call" | custom-call | tf_op jit(solution)/shard_map/pallas_call | solution.py:140
  29.3 3.5 %collective-permute-start.7 = (bf16[72,256]{1,0:T(8,128)(2,1)S(1)}, bf16[72,256]{1,0:T(8,128)(2,1)S(1)}, u32[]{:S(2)}, u32[]{:S(2)}) collective-permute-start(bf16[72,256]{1,0:T(8,128)(2,1)S(1)} %get-tuple-element.39), channel_id=1, source_target_pairs={{0,12},{1,13},{2,14},{3,15},{4,8},{5,9},{6,10},{7,11},{8,4},{9,5},... | collective-permute-start | bytes 110600 | tf_op jit(solution)/shard_map/ppermute | solution.py:177
  32.8 1.0 %collective-permute-start.9 = (bf16[72,256]{1,0:T(8,128)(2,1)S(1)}, bf16[72,256]{1,0:T(8,128)(2,1)S(1)}, u32[]{:S(2)}, u32[]{:S(2)}) collective-permute-start(bf16[72,256]{1,0:T(8,128)(2,1)S(1)} %get-tuple-element.41), channel_id=1, source_target_pairs={{0,4},{1,5},{2,6},{3,7},{4,0},{5,1},{6,2},{7,3},{8,12},{9,13},{10,... | collective-permute-start | bytes 110600 | tf_op jit(solution)/shard_map/ppermute | solution.py:177
  33.8 0.6 shard_map.119.factor_ref
  34.4 0.8 %collective-permute-done.7.two = bf16[72,256]{1,0:T(8,128)(2,1)S(1)} collective-permute-done((bf16[72,256]{1,0:T(8,128)(2,1)S(1)}, bf16[72,256]{1,0:T(8,128)(2,1)S(1)}, u32[]{:S(2)}, u32[]{:S(2)}) %collective-permute-start.7) | collective-permute-done | bytes 36896 | tf_op jit(solution)/shard_map/ppermute | solution.py:177
  35.2 2.5 %collective-permute-done.8.three = bf16[72,256]{1,0:T(8,128)(2,1)S(1)} collective-permute-done((bf16[72,256]{1,0:T(8,128)(2,1)S(1)}, bf16[72,256]{1,0:T(8,128)(2,1)S(1)}, u32[]{:S(2)}, u32[]{:S(2)}) %collective-permute-start.8) | collective-permute-done | bytes 36896 | tf_op jit(solution)/shard_map/ppermute | solution.py:177
  38.0 1.5 %collective-permute-start.12 = (bf16[72,256]{1,0:T(8,128)(2,1)S(1)}, bf16[72,256]{1,0:T(8,128)(2,1)S(1)}, u32[]{:S(2)}, u32[]{:S(2)}) collective-permute-start(bf16[72,256]{1,0:T(8,128)(2,1)S(1)} %shard_map.120.refs_4_), channel_id=1, source_target_pairs={{0,12},{1,13},{2,14},{3,15},{4,8},{5,9},{6,10},{7,11},{8,4},{9,5},... | collective-permute-start | bytes 110600 | tf_op jit(solution)/shard_map/ppermute | solution.py:177
  39.5 0.6 collective-permute-start.11
  40.1 2.3 %collective-permute-start.10 = (bf16[72,256]{1,0:T(8,128)(2,1)S(1)}, bf16[72,256]{1,0:T(8,128)(2,1)S(1)}, u32[]{:S(2)}, u32[]{:S(2)}) collective-permute-start(bf16[72,256]{1,0:T(8,128)(2,1)S(1)} %shard_map.120.refs_4_), channel_id=1, source_target_pairs={{0,4},{1,5},{2,6},{3,7},{4,0},{5,1},{6,2},{7,3},{8,12},{9,13},{10,... | collective-permute-start | bytes 110600 | tf_op jit(solution)/shard_map/ppermute | solution.py:177
  42.4 0.6 slice_bitcast_fusion
  43.0 1.7 %collective-permute-done.10.refs_5_ = bf16[72,256]{1,0:T(8,128)(2,1)S(1)} collective-permute-done((bf16[72,256]{1,0:T(8,128)(2,1)S(1)}, bf16[72,256]{1,0:T(8,128)(2,1)S(1)}, u32[]{:S(2)}, u32[]{:S(2)}) %collective-permute-start.10) | collective-permute-done | bytes 36896 | tf_op jit(solution)/shard_map/ppermute | solution.py:177
  44.7 1.0 %shard_map.121 = (bf16[4,2,48,256]{3,2,1,0:T(8,128)(2,1)S(1)}, bf16[4,2,48,256]{3,2,1,0:T(8,128)(2,1)S(1)}, bf16[4,2,48,256]{3,2,1,0:T(8,128)(2,1)S(1)}, bf16[4,2,48,256]{3,2,1,0:T(8,128)(2,1)S(1)}) custom-call(s32[32]{0:T(128)S(1)} %copy-done.6, bf16[72,192]{1,0:T(8,128)(2,1)S(1)} %get-tuple-element.29.refs_0_, ...), custom_call_target="tpu_custom_call" | custom-call | tf_op jit(solution)/shard_map/pallas_call | solution.py:140
  45.7 1.6 %collective-permute-start.13 = (bf16[4,2,48,256]{3,2,1,0:T(8,128)(2,1)S(1)}, bf16[4,2,48,256]{3,2,1,0:T(8,128)(2,1)S(1)}, u32[]{:S(2)}, u32[]{:S(2)}) collective-permute-start(bf16[4,2,48,256]{3,2,1,0:T(8,128)(2,1)S(1)} %get-tuple-element.44), channel_id=1, source_target_pairs={{0,1},{1,0},{2,3},{3,2},{4,5},{5,4},{6,7},{7,6},{8,9},{9,8},{10,11... | collective-permute-start | bytes 589832 | tf_op jit(solution)/shard_map/ppermute | solution.py:177
  47.3 1.5 %collective-permute-start.14 = (bf16[4,2,48,256]{3,2,1,0:T(8,128)(2,1)S(1)}, bf16[4,2,48,256]{3,2,1,0:T(8,128)(2,1)S(1)}, u32[]{:S(2)}, u32[]{:S(2)}) collective-permute-start(bf16[4,2,48,256]{3,2,1,0:T(8,128)(2,1)S(1)} %get-tuple-element.45), channel_id=1, source_target_pairs={{0,2},{1,3},{2,0},{3,1},{4,6},{5,7},{6,4},{7,5},{8,10},{9,11},{10,... | collective-permute-start | bytes 589832 | tf_op jit(solution)/shard_map/ppermute | solution.py:177
  48.8 0.5 collective-permute-start.15
  49.3 2.2 %collective-permute-done.13.refs_1_ = bf16[4,2,48,256]{3,2,1,0:T(8,128)(2,1)S(1)} collective-permute-done((bf16[4,2,48,256]{3,2,1,0:T(8,128)(2,1)S(1)}, bf16[4,2,48,256]{3,2,1,0:T(8,128)(2,1)S(1)}, u32[]{:S(2)}, u32[]{:S(2)}) %collective-permute-start.13) | collective-permute-done | bytes 196640 | tf_op jit(solution)/shard_map/ppermute | solution.py:177
  51.4 2.7 %collective-permute-done.14.refs_2_ = bf16[4,2,48,256]{3,2,1,0:T(8,128)(2,1)S(1)} collective-permute-done((bf16[4,2,48,256]{3,2,1,0:T(8,128)(2,1)S(1)}, bf16[4,2,48,256]{3,2,1,0:T(8,128)(2,1)S(1)}, u32[]{:S(2)}, u32[]{:S(2)}) %collective-permute-start.14) | collective-permute-done | bytes 196640 | tf_op jit(solution)/shard_map/ppermute | solution.py:177
  54.1 1.2 %collective-permute-done.15.refs_3_ = bf16[4,2,48,256]{3,2,1,0:T(8,128)(2,1)S(1)} collective-permute-done((bf16[4,2,48,256]{3,2,1,0:T(8,128)(2,1)S(1)}, bf16[4,2,48,256]{3,2,1,0:T(8,128)(2,1)S(1)}, u32[]{:S(2)}, u32[]{:S(2)}) %collective-permute-start.15) | collective-permute-done | bytes 196640 | tf_op jit(solution)/shard_map/ppermute | solution.py:177
  55.6 1.2 %collective-permute-done.19.refs_7_ = bf16[4,2,48,256]{3,2,1,0:T(8,128)(2,1)S(1)} collective-permute-done((bf16[4,2,48,256]{3,2,1,0:T(8,128)(2,1)S(1)}, bf16[4,2,48,256]{3,2,1,0:T(8,128)(2,1)S(1)}, u32[]{:S(2)}, u32[]{:S(2)}) %collective-permute-start.19) | collective-permute-done | bytes 196640 | tf_op jit(solution)/shard_map/ppermute | solution.py:177
  56.8 8.1 %shard_map.122 = f32[48,768,128]{2,1,0:T(8,128)} custom-call(s32[32]{0:T(128)S(1)} %copy-done.6, bf16[2,768,128]{2,1,0:T(8,128)(2,1)S(1)} %copy-done, bf16[4,2,48,256]{3,2,1,0:T(8,128)(2,1)S(1)} %get-tuple-element.43.refs_0_, bf16[4,2,48,256]{3,2,1,0:T(8,128)(2,1)S(1)} %collective-permute-done.13.refs_1_, ...), custom_call_target="tpu_custom_call" | custom-call | flops 1207959552 | bytes 18874368 | tf_op jit(solution)/shard_map/pallas_call | solution.py:362
  (37 shorter events, 1.1 us)
Async XLA Ops:
  0.6 33.2 %copy-start.8 = (f32[1,128]{1,0:T(1,128)S(1)}, f32[1,128]{1,0:T(1,128)}, u32[]{:S(2)}) copy-start(f32[1,128]{1,0:T(1,128)} %constant.11.damping_ref) | copy-start | bytes 1540
  0.6 56.2 %copy-start = (bf16[2,768,128]{2,1,0:T(8,128)(2,1)S(1)}, bf16[2,768,128]{2,1,0:T(8,128)(2,1)}, u32[]{:S(2)}) copy-start(bf16[2,768,128]{2,1,0:T(8,128)(2,1)} %constant.7.clone.table_ref) | copy-start | bytes 1179652
  0.7 1.0 %copy-start.1 = (bf16[2,128,768]{2,1,0:T(8,128)(2,1)S(1)}, bf16[2,128,768]{2,1,0:T(8,128)(2,1)}, u32[]{:S(2)}) copy-start(bf16[2,128,768]{2,1,0:T(8,128)(2,1)} %constant.6.clone.table_ref) | copy-start | bytes 1179652
  1.7 8.6 %copy-start.6 = (s32[32]{0:T(128)S(1)}, s32[32]{0:T(128)}, u32[]{:S(2)}) copy-start(s32[32]{0:T(128)} %orders_ref.11) | copy-start | bytes 388
  1.7 10.5 %copy-start.2 = (bf16[1,65,768]{2,1,0:T(8,128)(2,1)S(1)}, bf16[1,65,768]{2,1,0:T(8,128)(2,1)}, u32[]{:S(2)}) copy-start(bf16[1,65,768]{2,1,0:T(8,128)(2,1)} %legendre_ref.1) | copy-start | bytes 299524
  1.7 32.1 %copy-start.7 = (f32[128]{0:T(128)S(1)}, f32[128]{0:T(128)}, u32[]{:S(2)}) copy-start(f32[128]{0:T(128)} %param.14) | copy-start | bytes 1540
  1.7 35.9 %copy-start.3 = (bf16[1,65,256]{2,1,0:T(8,128)(2,1)S(1)}, bf16[1,65,256]{2,1,0:T(8,128)(2,1)}, u32[]{:S(2)}) copy-start(bf16[1,65,256]{2,1,0:T(8,128)(2,1)} %state_ref.1) | copy-start | bytes 99844
  1.7 35.9 %copy-start.4 = (bf16[128,128]{1,0:T(8,128)(2,1)S(1)}, bf16[128,128]{1,0:T(8,128)(2,1)}, u32[]{:S(2)}) copy-start(bf16[128,128]{1,0:T(8,128)(2,1)} %right_ref.1) | copy-start | bytes 98308
  1.7 35.9 %copy-start.5 = (bf16[128,128]{1,0:T(8,128)(2,1)S(1)}, bf16[128,128]{1,0:T(8,128)(2,1)}, u32[]{:S(2)}) copy-start(bf16[128,128]{1,0:T(8,128)(2,1)} %left_ref.1) | copy-start | bytes 98308
  11.0 2.4 %collective-permute-start = (bf16[4,4,2,48,256]{4,3,2,1,0:T(8,128)(2,1)S(1)}, bf16[4,4,2,48,256]{4,3,2,1,0:T(8,128)(2,1)S(1)}, u32[]{:S(2)}, u32[]{:S(2)}) collective-permute-start(bf16[4,4,2,48,256]{4,3,2,1,0:T(8,128)(2,1)S(1)} %shard_map.114), channel_id=1, source_target_pairs={{0,16},{1,17},{2,18},{3,19},{4,20},{5,21},{6,22},{7,23},{8,24},{9,... | collective-permute-start | bytes 2359304 | tf_op jit(solution)/shard_map/ppermute | solution.py:177
  13.7 14.9 %collective-permute-start.4 = (bf16[4,2,48,256]{3,2,1,0:T(8,128)(2,1)S(1)}, bf16[4,2,48,256]{3,2,1,0:T(8,128)(2,1)S(1)}, u32[]{:S(2)}, u32[]{:S(2)}) collective-permute-start(bf16[4,2,48,256]{3,2,1,0:T(8,128)(2,1)S(1)} %get-tuple-element.35), channel_id=1, source_target_pairs={{0,1},{1,0},{2,3},{3,2},{4,5},{5,4},{6,7},{7,6},{8,9},{9,8},{10,11... | collective-permute-start | bytes 589832 | tf_op jit(solution)/shard_map/ppermute | solution.py:177
  16.6 11.9 %collective-permute-start.5 = (bf16[4,2,48,256]{3,2,1,0:T(8,128)(2,1)S(1)}, bf16[4,2,48,256]{3,2,1,0:T(8,128)(2,1)S(1)}, u32[]{:S(2)}, u32[]{:S(2)}) collective-permute-start(bf16[4,2,48,256]{3,2,1,0:T(8,128)(2,1)S(1)} %get-tuple-element.36), channel_id=1, source_target_pairs={{0,2},{1,3},{2,0},{3,1},{4,6},{5,7},{6,4},{7,5},{8,10},{9,11},{10,... | collective-permute-start | bytes 589832 | tf_op jit(solution)/shard_map/ppermute | solution.py:177
  18.1 10.4 %collective-permute-start.6 = (bf16[4,2,48,256]{3,2,1,0:T(8,128)(2,1)S(1)}, bf16[4,2,48,256]{3,2,1,0:T(8,128)(2,1)S(1)}, u32[]{:S(2)}, u32[]{:S(2)}) collective-permute-start(bf16[4,2,48,256]{3,2,1,0:T(8,128)(2,1)S(1)} %get-tuple-element.37), channel_id=1, source_target_pairs={{0,3},{1,2},{2,1},{3,0},{4,7},{5,6},{6,5},{7,4},{8,11},{9,10},{10,... | collective-permute-start | bytes 589832 | tf_op jit(solution)/shard_map/ppermute | solution.py:177
  18.1 4.6 %collective-permute-start.1 = (bf16[72,192]{1,0:T(8,128)(2,1)S(1)}, bf16[72,192]{1,0:T(8,128)(2,1)S(1)}, u32[]{:S(2)}, u32[]{:S(2)}) collective-permute-start(bf16[72,192]{1,0:T(8,128)(2,1)S(1)} %get-tuple-element.30), channel_id=1, source_target_pairs={{0,4},{1,5},{2,6},{3,7},{4,0},{5,1},{6,2},{7,3},{8,12},{9,13},{10,... | collective-permute-start | bytes 82952 | tf_op jit(solution)/shard_map/ppermute | solution.py:177
  20.2 6.0 %collective-permute-start.2 = (bf16[72,192]{1,0:T(8,128)(2,1)S(1)}, bf16[72,192]{1,0:T(8,128)(2,1)S(1)}, u32[]{:S(2)}, u32[]{:S(2)}) collective-permute-start(bf16[72,192]{1,0:T(8,128)(2,1)S(1)} %get-tuple-element.31), channel_id=1, source_target_pairs={{0,8},{1,9},{2,10},{3,11},{4,12},{5,13},{6,14},{7,15},{8,0},{9,1},... | collective-permute-start | bytes 82952 | tf_op jit(solution)/shard_map/ppermute | solution.py:177
  22.8 5.8 %collective-permute-start.3 = (bf16[72,192]{1,0:T(8,128)(2,1)S(1)}, bf16[72,192]{1,0:T(8,128)(2,1)S(1)}, u32[]{:S(2)}, u32[]{:S(2)}) collective-permute-start(bf16[72,192]{1,0:T(8,128)(2,1)S(1)} %get-tuple-element.32), channel_id=1, source_target_pairs={{0,12},{1,13},{2,14},{3,15},{4,8},{5,9},{6,10},{7,11},{8,4},{9,5},... | collective-permute-start | bytes 82952 | tf_op jit(solution)/shard_map/ppermute | solution.py:177
  29.3 5.8 %collective-permute-start.7 = (bf16[72,256]{1,0:T(8,128)(2,1)S(1)}, bf16[72,256]{1,0:T(8,128)(2,1)S(1)}, u32[]{:S(2)}, u32[]{:S(2)}) collective-permute-start(bf16[72,256]{1,0:T(8,128)(2,1)S(1)} %get-tuple-element.39), channel_id=1, source_target_pairs={{0,12},{1,13},{2,14},{3,15},{4,8},{5,9},{6,10},{7,11},{8,4},{9,5},... | collective-permute-start | bytes 110600 | tf_op jit(solution)/shard_map/ppermute | solution.py:177
  32.8 4.9 %collective-permute-start.8 = (bf16[72,256]{1,0:T(8,128)(2,1)S(1)}, bf16[72,256]{1,0:T(8,128)(2,1)S(1)}, u32[]{:S(2)}, u32[]{:S(2)}) collective-permute-start(bf16[72,256]{1,0:T(8,128)(2,1)S(1)} %get-tuple-element.40), channel_id=1, source_target_pairs={{0,8},{1,9},{2,10},{3,11},{4,12},{5,13},{6,14},{7,15},{8,0},{9,1},... | collective-permute-start | bytes 110600 | tf_op jit(solution)/shard_map/ppermute | solution.py:177
  32.8 4.9 %collective-permute-start.9 = (bf16[72,256]{1,0:T(8,128)(2,1)S(1)}, bf16[72,256]{1,0:T(8,128)(2,1)S(1)}, u32[]{:S(2)}, u32[]{:S(2)}) collective-permute-start(bf16[72,256]{1,0:T(8,128)(2,1)S(1)} %get-tuple-element.41), channel_id=1, source_target_pairs={{0,4},{1,5},{2,6},{3,7},{4,0},{5,1},{6,2},{7,3},{8,12},{9,13},{10,... | collective-permute-start | bytes 110600 | tf_op jit(solution)/shard_map/ppermute | solution.py:177
  38.0 6.8 %collective-permute-start.12 = (bf16[72,256]{1,0:T(8,128)(2,1)S(1)}, bf16[72,256]{1,0:T(8,128)(2,1)S(1)}, u32[]{:S(2)}, u32[]{:S(2)}) collective-permute-start(bf16[72,256]{1,0:T(8,128)(2,1)S(1)} %shard_map.120.refs_4_), channel_id=1, source_target_pairs={{0,12},{1,13},{2,14},{3,15},{4,8},{5,9},{6,10},{7,11},{8,4},{9,5},... | collective-permute-start | bytes 110600 | tf_op jit(solution)/shard_map/ppermute | solution.py:177
  39.5 5.3 %collective-permute-start.11 = (bf16[72,256]{1,0:T(8,128)(2,1)S(1)}, bf16[72,256]{1,0:T(8,128)(2,1)S(1)}, u32[]{:S(2)}, u32[]{:S(2)}) collective-permute-start(bf16[72,256]{1,0:T(8,128)(2,1)S(1)} %shard_map.120.refs_4_), channel_id=1, source_target_pairs={{0,8},{1,9},{2,10},{3,11},{4,12},{5,13},{6,14},{7,15},{8,0},{9,1},... | collective-permute-start | bytes 110600 | tf_op jit(solution)/shard_map/ppermute | solution.py:177
  40.1 4.6 %collective-permute-start.10 = (bf16[72,256]{1,0:T(8,128)(2,1)S(1)}, bf16[72,256]{1,0:T(8,128)(2,1)S(1)}, u32[]{:S(2)}, u32[]{:S(2)}) collective-permute-start(bf16[72,256]{1,0:T(8,128)(2,1)S(1)} %shard_map.120.refs_4_), channel_id=1, source_target_pairs={{0,4},{1,5},{2,6},{3,7},{4,0},{5,1},{6,2},{7,3},{8,12},{9,13},{10,... | collective-permute-start | bytes 110600 | tf_op jit(solution)/shard_map/ppermute | solution.py:177
  45.7 5.7 %collective-permute-start.13 = (bf16[4,2,48,256]{3,2,1,0:T(8,128)(2,1)S(1)}, bf16[4,2,48,256]{3,2,1,0:T(8,128)(2,1)S(1)}, u32[]{:S(2)}, u32[]{:S(2)}) collective-permute-start(bf16[4,2,48,256]{3,2,1,0:T(8,128)(2,1)S(1)} %get-tuple-element.44), channel_id=1, source_target_pairs={{0,1},{1,0},{2,3},{3,2},{4,5},{5,4},{6,7},{7,6},{8,9},{9,8},{10,11... | collective-permute-start | bytes 589832 | tf_op jit(solution)/shard_map/ppermute | solution.py:177
  47.3 6.8 %collective-permute-start.14 = (bf16[4,2,48,256]{3,2,1,0:T(8,128)(2,1)S(1)}, bf16[4,2,48,256]{3,2,1,0:T(8,128)(2,1)S(1)}, u32[]{:S(2)}, u32[]{:S(2)}) collective-permute-start(bf16[4,2,48,256]{3,2,1,0:T(8,128)(2,1)S(1)} %get-tuple-element.45), channel_id=1, source_target_pairs={{0,2},{1,3},{2,0},{3,1},{4,6},{5,7},{6,4},{7,5},{8,10},{9,11},{10,... | collective-permute-start | bytes 589832 | tf_op jit(solution)/shard_map/ppermute | solution.py:177
  48.8 6.6 %collective-permute-start.15 = (bf16[4,2,48,256]{3,2,1,0:T(8,128)(2,1)S(1)}, bf16[4,2,48,256]{3,2,1,0:T(8,128)(2,1)S(1)}, u32[]{:S(2)}, u32[]{:S(2)}) collective-permute-start(bf16[4,2,48,256]{3,2,1,0:T(8,128)(2,1)S(1)} %get-tuple-element.46), channel_id=1, source_target_pairs={{0,3},{1,2},{2,1},{3,0},{4,7},{5,6},{6,5},{7,4},{8,11},{9,10},{10,... | collective-permute-start | bytes 589832 | tf_op jit(solution)/shard_map/ppermute | solution.py:177
  49.3 6.1 %collective-permute-start.16 = (bf16[4,2,48,256]{3,2,1,0:T(8,128)(2,1)S(1)}, bf16[4,2,48,256]{3,2,1,0:T(8,128)(2,1)S(1)}, u32[]{:S(2)}, u32[]{:S(2)}) collective-permute-start(bf16[4,2,48,256]{3,2,1,0:T(8,128)(2,1)S(1)} %get-tuple-element.43.refs_0_), channel_id=1, source_target_pairs={{0,16},{1,17},{2,18},{3,19},{4,20},{5,21},{6,22},{7,23},{8,24},{9,... | collective-permute-start | bytes 589832 | tf_op jit(solution)/shard_map/ppermute | solution.py:177
  51.4 3.9 %collective-permute-start.17 = (bf16[4,2,48,256]{3,2,1,0:T(8,128)(2,1)S(1)}, bf16[4,2,48,256]{3,2,1,0:T(8,128)(2,1)S(1)}, u32[]{:S(2)}, u32[]{:S(2)}) collective-permute-start(bf16[4,2,48,256]{3,2,1,0:T(8,128)(2,1)S(1)} %collective-permute-done.13.refs_1_), channel_id=1, source_target_pairs={{0,16},{1,17},{2,18},{3,19},{4,20},{5,21},{6,22},{7,23},{8,24},{9,... | collective-permute-start | bytes 589832 | tf_op jit(solution)/shard_map/ppermute | solution.py:177
  54.1 1.4 %collective-permute-start.18 = (bf16[4,2,48,256]{3,2,1,0:T(8,128)(2,1)S(1)}, bf16[4,2,48,256]{3,2,1,0:T(8,128)(2,1)S(1)}, u32[]{:S(2)}, u32[]{:S(2)}) collective-permute-start(bf16[4,2,48,256]{3,2,1,0:T(8,128)(2,1)S(1)} %collective-permute-done.14.refs_2_), channel_id=1, source_target_pairs={{0,16},{1,17},{2,18},{3,19},{4,20},{5,21},{6,22},{7,23},{8,24},{9,... | collective-permute-start | bytes 589832 | tf_op jit(solution)/shard_map/ppermute | solution.py:177
  55.4 1.4 %collective-permute-start.19 = (bf16[4,2,48,256]{3,2,1,0:T(8,128)(2,1)S(1)}, bf16[4,2,48,256]{3,2,1,0:T(8,128)(2,1)S(1)}, u32[]{:S(2)}, u32[]{:S(2)}) collective-permute-start(bf16[4,2,48,256]{3,2,1,0:T(8,128)(2,1)S(1)} %collective-permute-done.15.refs_3_), channel_id=1, source_target_pairs={{0,16},{1,17},{2,18},{3,19},{4,20},{5,21},{6,22},{7,23},{8,24},{9,... | collective-permute-start | bytes 589832 | tf_op jit(solution)/shard_map/ppermute | solution.py:177
